TPU v7x, 32 devices: a whole 2x2x4 slice. The times are simulated.
32 devices in a mesh: parts: 2 (over y), node: 4 (over z), seg: 2 (over x), feat: 2 (over core).
Axes of the slice: x: 2, y: 2, z: 4, core: 2. Of those that a mesh axis runs over, the one named last changes fastest.
Arguments:
- memory: float32 [4, 8192, 256], P(('parts', 'seg'), 'node', 'feat'), parts along dimension 0, may hold values from -6 to 6
- req_rows: int32 [2, 4, 4, 4, 256], P(None, ('parts', 'seg'), 'node'), parts along dimension 1, may hold values from 0 to 2047, as said below
- req_count: int32 [2, 4, 4, 4], P(None, ('parts', 'seg'), 'node'), parts along dimension 1, may hold values from 85 to 256, as said below
- dst_slot: int32 [2, 4, 4096], P(None, ('parts', 'seg'), 'node'), parts along dimension 1, may hold values from 0 to 1023, as said below
- elapsed: int32 [2, 4, 4096], P(None, ('parts', 'seg'), 'node'), parts along dimension 1, may hold values from 0 to 9999
- edges: bfloat16 [2, 4, 4096, 128], P(None, ('parts', 'seg'), 'node', 'feat'), parts along dimension 1, may hold values from -6 to 6
- upstream: bfloat16 [2, 4, 4096, 256], P(None, ('parts', 'seg'), 'node', 'feat'), parts along dimension 1, may hold values from -0.125 to 0.125
- freq: float32 [128], replicated, may hold values from 0.0001 to 0.1
- phase: float32 [128], replicated, may hold values from -3.140625 to 3.140625
- w_input: bfloat16 [3, 768, 256], P(None, None, 'feat'), may hold values from -0.21875 to 0.21875
- w_hidden: bfloat16 [3, 256, 256], P(None, None, 'feat'), may hold values from -0.375 to 0.375
- bias: float32 [4, 256], P(None, 'feat'), may hold values from -3 to 3
Outputs:
- memory_out: float32 [4, 8192, 256], P(('parts', 'seg'), 'node', 'feat'), parts along dimension 0
- grad_input: float32 [6, 768, 256], P('parts', None, 'feat'), parts along dimension 0
- grad_hidden: float32 [6, 256, 256], P('parts', None, 'feat'), parts along dimension 0
- grad_bias: float32 [8, 256], P('parts', 'feat'), parts along dimension 0
There are 2 independent parts, one for each index of `parts`. A program takes and returns all parts, laid end to end along the dimension named above; an argument that names none is the same for every part. Nothing has to cross between parts.
Inputs may be any that keep to these rules, and one draw needn't show every extreme that they name: `req_rows`: for one batch, segment and owner, the rows named by all requesting devices in their live slots are distinct; slots past the count hold 0. `req_count`: at least one live request from every device to every owner; in every batch and segment some owner receives exactly 256 from every device. `dst_slot`: equals o * 256 + c for some owner o and a live slot c of this device's requests to o.
All inputs are finite; a program needn't handle non-finite values.
Results may differ from a plain program's by a relative error of at most 0.0055.
Values may be sent and summed in bfloat16 or wider, within the bound.
No kernel may reach another device: no remote copies, remote signals or barrier semaphores. Data moves between devices by JAX's collectives and lax.ppermute only.
A program may use at most 64 MiB of HBM per device.

v0:
```python
import jax
import jax.numpy as jnp
from jax import lax
from jax.sharding import PartitionSpec as P


def from_behind(block, axis, distance):
    devices = range(lax.axis_size(axis))
    route = [(i - distance, i) for i in devices if i - distance in devices]
    return lax.ppermute(block, axis, route)


def gate_pass(message, hidden_bf, hidden_own, w_input, w_hidden, bias):
    input_gates = jnp.einsum("ei,gih->geh", message, w_input, preferred_element_type=jnp.float32)
    hidden_gates = jnp.einsum(
        "ei,gih->geh", hidden_bf, w_hidden, preferred_element_type=jnp.float32
    )
    reset_gate = jax.nn.sigmoid(input_gates[0] + hidden_gates[0] + bias[0])
    update = jax.nn.sigmoid(input_gates[1] + hidden_gates[1] + bias[1])
    recur_term = hidden_gates[2] + bias[3]
    candid = jnp.tanh(input_gates[2] + bias[2] + reset_gate * recur_term)
    fresh_rows = (1.0 - update) * candid + update * hidden_own
    return (fresh_rows, reset_gate, update, candid, recur_term)


def gate_grads(message, hidden_bf, hidden_own, cotangent, reset_gate, update, candid, recur_term):
    grad_cand = cotangent * (1.0 - update) * (1.0 - candid * candid)
    grad_upd = cotangent * (hidden_own - candid) * update * (1.0 - update)
    grad_reset = grad_cand * recur_term * reset_gate * (1.0 - reset_gate)
    grad_recur = grad_cand * reset_gate
    gate_in = jnp.stack([grad_reset, grad_upd, grad_cand]).astype(jnp.bfloat16)
    gate_hid = jnp.stack([grad_reset, grad_upd, grad_recur]).astype(jnp.bfloat16)
    grad_in = jnp.einsum("ei,geh->gih", message, gate_in, preferred_element_type=jnp.float32)
    grad_hid = jnp.einsum("ei,geh->gih", hidden_bf, gate_hid, preferred_element_type=jnp.float32)
    grad_b = jnp.stack(
        [
            jnp.sum(grad_reset, 0),
            jnp.sum(grad_upd, 0),
            jnp.sum(grad_cand, 0),
            jnp.sum(grad_recur, 0),
        ]
    )
    return (grad_in, grad_hid, grad_b)


def local(
    memory,
    req_rows,
    req_count,
    dst_slot,
    elapsed,
    edges,
    upstream,
    freq,
    phase,
    w_input,
    w_hidden,
    bias,
):
    memory_now = memory[0]
    node_rows = memory_now.shape[0]
    half_width = memory_now.shape[1]
    slot_count = req_rows.shape[-1]
    batches = req_rows.shape[0]
    first_seg = lax.axis_index("seg") == 0
    totals = None
    summed = None
    for batch_idx in range(batches):
        requested = req_rows[batch_idx, 0, 0]
        counted = req_count[batch_idx, 0, 0][:, None]
        asked_rows, asked_count = (
            lax.all_to_all(requested, "node", split_axis=0, concat_axis=0, tiled=True),
            lax.all_to_all(counted, "node", split_axis=0, concat_axis=0, tiled=True),
        )
        served = jnp.take(memory_now, asked_rows.reshape(-1), axis=0).astype(jnp.bfloat16)
        served = served.reshape(asked_rows.shape[0], slot_count, half_width)
        fetched = lax.all_to_all(served, "node", split_axis=0, concat_axis=0, tiled=True)
        own_rows = fetched.reshape(-1, half_width)
        full_rows, edge_full = (
            lax.all_gather(own_rows, "feat", axis=1, tiled=True),
            lax.all_gather(edges[batch_idx, 0], "feat", axis=1, tiled=True),
        )
        dst_rows = jnp.take(full_rows, dst_slot[batch_idx, 0], axis=0)
        time_code = jnp.cos(
            elapsed[batch_idx, 0].astype(jnp.float32)[:, None] * freq[None, :] + phase[None, :]
        ).astype(jnp.bfloat16)
        message = jnp.concatenate([full_rows, dst_rows, time_code, edge_full], axis=1)
        hidden_own = own_rows.astype(jnp.float32)
        fresh_rows, reset_gate, update, candid, recur_term = gate_pass(
            message, full_rows, hidden_own, w_input, w_hidden, bias
        )
        live_flat = (jnp.arange(slot_count)[None, :] < counted).reshape(-1).astype(jnp.float32)
        cotangent = upstream[batch_idx, 0].astype(jnp.float32) * live_flat[:, None]
        grads_here = gate_grads(
            message, full_rows, hidden_own, cotangent, reset_gate, update, candid, recur_term
        )
        returned = lax.all_to_all(
            fresh_rows.reshape(fetched.shape), "node", split_axis=0, concat_axis=0, tiled=True
        )
        owner_live = jnp.arange(slot_count)[None, :] < asked_count
        places = jnp.where(owner_live, asked_rows, node_rows).reshape(-1)
        values = returned.reshape(-1, half_width)
        memory_now = memory_now.at[places].set(values, mode="drop")
        totals = (
            grads_here
            if totals is None
            else tuple((left + right for left, right in zip(totals, grads_here)))
        )
        if batch_idx + 1 < batches:
            handed = from_behind(memory_now, "seg", 1)
            memory_now = jnp.where(first_seg, memory_now, handed)
    summed = lax.psum(totals, ("node", "seg"))
    return (memory_now[None], summed[0], summed[1], summed[2])


def solution(mesh):
    in_specs = (
        P(("parts", "seg"), "node", "feat"),
        P(None, ("parts", "seg"), "node", None, None),
        P(None, ("parts", "seg"), "node", None),
        P(None, ("parts", "seg"), "node"),
        P(None, ("parts", "seg"), "node"),
        P(None, ("parts", "seg"), "node", "feat"),
        P(None, ("parts", "seg"), "node", "feat"),
        P(),
        P(),
        P(None, None, "feat"),
        P(None, None, "feat"),
        P(None, "feat"),
    )
    out_specs = (
        P(("parts", "seg"), "node", "feat"),
        P("parts", None, "feat"),
        P("parts", None, "feat"),
        P("parts", "feat"),
    )
    return jax.shard_map(local, mesh=mesh, in_specs=in_specs, out_specs=out_specs, check_vma=False)
```

profile of v0, /device:TPU:0, one launch (start us, length us, event | category | flops | bytes accessed | tf_op | source)
XLA Modules:
  0.0 253.0 jit_solution(422010644140952727)
XLA Ops:
  9.1 6.3 %all-to-all-start.1 = ((s32[4,1,256]{2,1,0:T(1,128)}), s32[4,1,256]{2,1,0:T(1,128)S(1)}, u32[]{:S(2)}, u32[]{:S(2)}) async-start(s32[4,1,256]{2,1,0:T(1,128)} %bitcast.273), calls=%async_computation.1 | async-start | bytes 8192 | tf_op jit(solution)/shard_map/all_to_all | solution.py:72
  21.1 2.9 %gather_fusion = bf16[1024,128]{1,0:T(8,128)(2,1)S(1)} fusion(f32[2048,128]{1,0:T(8,128)S(1)} %bitcast.275, s32[1024]{0:T(1024)S(1)} %fusion.66), kind=kCustom, calls=%fused_computation.clone | custom fusion | bytes 528384 | tf_op jit(solution)/shard_map/jit(_take)/gather | solution.py:75
  24.9 3.8 %all-to-all-start.2 = ((bf16[4,256,128]{2,1,0:T(8,128)(2,1)}), bf16[4,256,128]{2,1,0:T(8,128)(2,1)S(1)}, u32[]{:S(2)}, u32[]{:S(2)}) async-start(bf16[4,256,128]{2,1,0:T(8,128)(2,1)} %bitcast.6), calls=%async_computation.2 | async-start | bytes 524288 | tf_op jit(solution)/shard_map/all_to_all | solution.py:77
  28.7 4.4 %cosine_convert_fusion = (bf16[1024,128]{1,0:T(8,128)(2,1)}, bf16[1024,128]{1,0:T(8,128)(2,1)}) fusion(f32[1024]{0:T(1024)S(1)} %bitcast.315, f32[128]{0:T(128)S(1)} %copy-done.41, f32[128]{0:T(128)S(1)} %copy-done.42, f32[1024]{0:T(1024)S(1)} %bitcast.316), kind=kLoop, calls=%fused_computation.115 | loop fusion | flops 786432 | bytes 533504 | tf_op jit(solution)/shard_map/convert_element_type | solution.py:86
  33.1 4.8 %all-to-all-done.2 = bf16[4,256,128]{2,1,0:T(8,128)(2,1)S(1)} async-done(((bf16[4,256,128]{2,1,0:T(8,128)(2,1)}), bf16[4,256,128]{2,1,0:T(8,128)(2,1)S(1)}, u32[]{:S(2)}, u32[]{:S(2)}) %all-to-all-start.2) | async-done | bytes 262176 | tf_op jit(solution)/shard_map/all_to_all | solution.py:77
  37.9 3.2 %all-to-all-start = ((s32[4,1,1]{2,1,0:T(1,128)}), s32[4,1,1]{2,1,0:T(1,128)S(1)}, u32[]{:S(2)}, u32[]{:S(2)}) async-start(s32[4,1,1]{2,1,0:T(1,128)} %copy.36), calls=%async_computation | async-start | bytes 4096 | tf_op jit(solution)/shard_map/all_to_all | solution.py:73
  43.3 3.9 %gather_fusion.1 = bf16[1024,256]{1,0:T(8,128)(2,1)S(1)} fusion(bf16[1024,256]{1,0:T(8,128)(2,1)S(1)} %all_gather.12, s32[1024]{0:T(1024)S(1)} %fusion.67), kind=kCustom, calls=%fused_computation.1.clone | custom fusion | bytes 1052672 | tf_op jit(solution)/shard_map/jit(_take)/gather | solution.py:83
  53.2 5.1 %all-to-all-start.3 = ((f32[4,256,128]{2,1,0:T(8,128)}), f32[4,256,128]{2,1,0:T(8,128)S(1)}, u32[]{:S(2)}, u32[]{:S(2)}) async-start(f32[4,256,128]{2,1,0:T(8,128)} %multiply_add_fusion.1), calls=%async_computation.3 | async-start | bytes 1048576 | tf_op jit(solution)/shard_map/all_to_all | solution.py:97
  58.5 14.5 %all-to-all-done.3 = f32[4,256,128]{2,1,0:T(8,128)S(1)} async-done(((f32[4,256,128]{2,1,0:T(8,128)}), f32[4,256,128]{2,1,0:T(8,128)S(1)}, u32[]{:S(2)}, u32[]{:S(2)}) %all-to-all-start.3) | async-done | bytes 524320 | tf_op jit(solution)/shard_map/all_to_all | solution.py:97
  73.1 3.5 %scatter_fusion = f32[2048,128]{1,0:T(8,128)S(1)} fusion(f32[2048,128]{1,0:T(8,128)S(1)} %bitcast.276, s32[1024]{0:T(1024)S(1)} %bitcast.314, f32[1024,128]{1,0:T(8,128)S(1)} %bitcast.289), kind=kCustom, calls=%fused_computation.4 | custom fusion | bytes 1576960 | tf_op jit(solution)/shard_map/scatter | solution.py:103
  76.6 4.4 %collective-permute-start = (f32[2048,128]{1,0:T(8,128)S(1)}, f32[2048,128]{1,0:T(8,128)}, u32[]{:S(2)}, u32[]{:S(2)}) collective-permute-start(f32[2048,128]{1,0:T(8,128)S(1)} %scatter_fusion), channel_id=1, source_target_pairs={{0,2},{1,3},{4,6},{5,7},{8,10},{9,11},{12,14},{13,15},{16,18},{17,... | collective-permute-start | bytes 3145736 | tf_op jit(solution)/shard_map/ppermute | solution.py:10
  81.5 3.2 %all-to-all-start.5 = ((s32[4,1,256]{2,1,0:T(1,128)}), s32[4,1,256]{2,1,0:T(1,128)S(1)}, u32[]{:S(2)}, u32[]{:S(2)}) async-start(s32[4,1,256]{2,1,0:T(1,128)} %bitcast.272), calls=%async_computation.5 | async-start | bytes 8192 | tf_op jit(solution)/shard_map/all_to_all | solution.py:72
  90.3 3.2 %all-to-all-start.4 = ((s32[4,1,1]{2,1,0:T(1,128)}), s32[4,1,1]{2,1,0:T(1,128)S(1)}, u32[]{:S(2)}, u32[]{:S(2)}) async-start(s32[4,1,1]{2,1,0:T(1,128)} %copy.39), calls=%async_computation.4 | async-start | bytes 4096 | tf_op jit(solution)/shard_map/all_to_all | solution.py:73
  93.6 8.0 %collective-permute-done = f32[2048,128]{1,0:T(8,128)} collective-permute-done((f32[2048,128]{1,0:T(8,128)S(1)}, f32[2048,128]{1,0:T(8,128)}, u32[]{:S(2)}, u32[]{:S(2)}) %collective-permute-start) | collective-permute-done | bytes 1048608 | tf_op jit(solution)/shard_map/ppermute | solution.py:10
  101.7 2.9 %gather_fusion.2 = bf16[1024,128]{1,0:T(8,128)(2,1)S(1)} fusion(f32[2048,128]{1,0:T(8,128)S(1)} %broadcast_select_fusion.2, s32[1024]{0:T(1024)S(1)} %fusion.68), kind=kCustom, calls=%fused_computation.2.clone | custom fusion | bytes 528384 | tf_op jit(solution)/shard_map/jit(_take)/gather | solution.py:75
  105.5 3.4 %all-to-all-start.6 = ((bf16[4,256,128]{2,1,0:T(8,128)(2,1)}), bf16[4,256,128]{2,1,0:T(8,128)(2,1)S(1)}, u32[]{:S(2)}, u32[]{:S(2)}) async-start(bf16[4,256,128]{2,1,0:T(8,128)(2,1)} %bitcast.29), calls=%async_computation.6 | async-start | bytes 524288 | tf_op jit(solution)/shard_map/all_to_all | solution.py:77
  110.0 5.9 %all-to-all-done.6 = bf16[4,256,128]{2,1,0:T(8,128)(2,1)S(1)} async-done(((bf16[4,256,128]{2,1,0:T(8,128)(2,1)}), bf16[4,256,128]{2,1,0:T(8,128)(2,1)S(1)}, u32[]{:S(2)}, u32[]{:S(2)}) %all-to-all-start.6) | async-done | bytes 262176 | tf_op jit(solution)/shard_map/all_to_all | solution.py:77
  119.9 5.0 %gather_fusion.3 = bf16[1024,256]{1,0:T(8,128)(2,1)} fusion(bf16[1024,256]{1,0:T(8,128)(2,1)S(1)} %all_gather.14, s32[1024]{0:T(1024)S(1)} %fusion.69), kind=kCustom, calls=%fused_computation.3.clone | custom fusion | bytes 1052672 | tf_op jit(solution)/shard_map/jit(_take)/gather | solution.py:83
  128.4 3.1 %fusion.39 = (f32[128]{0:T(128)S(1)}, f32[128]{0:T(128)S(1)}, f32[1024,128]{1,0:T(8,128)}, f32[1024,128]{1,0:T(8,128)}, f32[1,1024,128]{2,1,0:T(8,128)S(1)}, /*index=5*/f32[1,1024,128]{2,1,0:T(8,128)S(1)}) fusion(f32[1024]{0:T(1024)S(1)} %bitcast.299, bf16[2,1,1024,128]{3,2,1,0:T(8,128)(2,1)S(1)} %copy-done.13, f32[128]{0:T(128)S(1)} %get-tuple-element.64, ...), kind=kLoop, calls=%fused_computation.59 | loop fusion | flops 5766912 | bytes 8399872 | tf_op jit(solution)/shard_map/reduce_sum | solution.py:38
  143.5 4.1 %all-to-all-start.7 = ((f32[4,256,128]{2,1,0:T(8,128)}), f32[4,256,128]{2,1,0:T(8,128)}, u32[]{:S(2)}, u32[]{:S(2)}) async-start(f32[4,256,128]{2,1,0:T(8,128)} %multiply_add_fusion), calls=%async_computation.7 | async-start | bytes 1048576 | tf_op jit(solution)/shard_map/all_to_all | solution.py:97
  151.4 31.7 %psum.23 = f32[4,128]{1,0:T(4,128)} all-reduce(f32[4,128]{1,0:T(4,128)S(1)} %maximum_add_fusion), channel_id=1, replica_groups=mesh['parts'=2,'node'=4,'seg'=2,'feat'=2] {'node','seg'}, use_global_device_ids=true, to_apply=%region_12.15 | all-reduce | flops 512 | bytes 4096 | tf_op jit(solution)/shard_map/psum | solution.py:112
  183.1 3.9 %scatter_fusion.1 = f32[2048,128]{1,0:T(8,128)S(1)} fusion(f32[2048,128]{1,0:T(8,128)S(1)} %broadcast_select_fusion.2, s32[1024]{0:T(1024)S(1)} %bitcast.313, f32[1024,128]{1,0:T(8,128)} %bitcast.42), kind=kCustom, calls=%fused_computation.5 | custom fusion | bytes 1576960 | tf_op jit(solution)/shard_map/scatter | solution.py:103
  187.0 55.5 %all-reduce.3.cloned.1.call-done = (f32[3,768,128]{1,2,0:T(8,128)}, f32[3,256,128]{1,2,0:T(8,128)}) async-done(((f32[3,768,128]{1,2,0:T(8,128)}, f32[3,256,128]{1,2,0:T(8,128)}), (f32[3,768,128]{1,2,0:T(8,128)}, f32[3,256,128]{1,2,0:T(8,128)})) %all-reduce.3.cloned.1.call-update) | async-done | bytes 1572880 | tf_op jit(solution)/shard_map/psum | solution.py:112
  242.6 2.7 %copy.46 = f32[3,768,128]{2,1,0:T(8,128)} copy(f32[3,768,128]{1,2,0:T(8,128)} %get-tuple-element.29) | data formatting | bytes 2359296
  (155 shorter events, 48.9 us)
Async XLA Ops:
  7.2 40.8 %copy-start = (bf16[3,768,128]{2,1,0:T(8,128)(2,1)S(1)}, bf16[3,768,128]{2,1,0:T(8,128)(2,1)}, u32[]{:S(2)}) copy-start(bf16[3,768,128]{2,1,0:T(8,128)(2,1)} %param.25) | copy-start | bytes 1769476
  7.2 9.0 %copy-start.40 = (s32[2,1,1,4]{3,2,1,0:T(1,128)S(1)}, s32[2,1,1,4]{3,2,1,0:T(1,128)}, u32[]{:S(2)}) copy-start(s32[2,1,1,4]{3,2,1,0:T(1,128)} %param.18) | copy-start | bytes 100
  7.2 8.2 %copy-start.37 = (s32[2,1,1024]{2,1,0:T(1,128)S(1)}, s32[2,1,1024]{2,1,0:T(1,128)}, u32[]{:S(2)}) copy-start(s32[2,1,1024]{2,1,0:T(1,128)} %param.19) | copy-start | bytes 24580
  7.2 8.3 %copy-start.38 = (s32[2,1,1024]{2,1,0:T(1,128)S(1)}, s32[2,1,1024]{2,1,0:T(1,128)}, u32[]{:S(2)}) copy-start(s32[2,1,1024]{2,1,0:T(1,128)} %param.20) | copy-start | bytes 24580
  7.2 8.3 %copy-start.29 = (bf16[2,1,1024,64]{2,3,1,0:T(8,128)(2,1)S(1)}, bf16[2,1,1024,64]{2,3,1,0:T(8,128)(2,1)}, u32[]{:S(2)}) copy-start(bf16[2,1,1024,64]{2,3,1,0:T(8,128)(2,1)} %param.21) | copy-start | bytes 786436
  9.1 11.9 %all-to-all-start.1 = ((s32[4,1,256]{2,1,0:T(1,128)}), s32[4,1,256]{2,1,0:T(1,128)S(1)}, u32[]{:S(2)}, u32[]{:S(2)}) async-start(s32[4,1,256]{2,1,0:T(1,128)} %bitcast.273), calls=%async_computation.1 | async-start | bytes 8192 | tf_op jit(solution)/shard_map/all_to_all | solution.py:72
  21.0 7.7 %copy-start.39 = (f32[4,128]{1,0:T(4,128)S(1)}, f32[4,128]{1,0:T(4,128)}, u32[]{:S(2)}) copy-start(f32[4,128]{1,0:T(4,128)} %param.27) | copy-start | bytes 6148
  21.1 7.7 %copy-start.41 = (f32[128]{0:T(128)S(1)}, f32[128]{0:T(128)}, u32[]{:S(2)}) copy-start(f32[128]{0:T(128)} %param.24) | copy-start | bytes 1540
  21.1 7.7 %copy-start.42 = (f32[128]{0:T(128)S(1)}, f32[128]{0:T(128)}, u32[]{:S(2)}) copy-start(f32[128]{0:T(128)} %param.23) | copy-start | bytes 1540
  24.9 13.1 %all-to-all-start.2 = ((bf16[4,256,128]{2,1,0:T(8,128)(2,1)}), bf16[4,256,128]{2,1,0:T(8,128)(2,1)S(1)}, u32[]{:S(2)}, u32[]{:S(2)}) async-start(bf16[4,256,128]{2,1,0:T(8,128)(2,1)} %bitcast.6), calls=%async_computation.2 | async-start | bytes 524288 | tf_op jit(solution)/shard_map/all_to_all | solution.py:77
  37.9 15.3 %all-to-all-start = ((s32[4,1,1]{2,1,0:T(1,128)}), s32[4,1,1]{2,1,0:T(1,128)S(1)}, u32[]{:S(2)}, u32[]{:S(2)}) async-start(s32[4,1,1]{2,1,0:T(1,128)} %copy.36), calls=%async_computation | async-start | bytes 4096 | tf_op jit(solution)/shard_map/all_to_all | solution.py:73
  43.3 3.9 %copy-start.20 = (bf16[3,256,128]{2,1,0:T(8,128)(2,1)S(1)}, bf16[3,256,128]{2,1,0:T(8,128)(2,1)}, u32[]{:S(2)}) copy-start(bf16[3,256,128]{2,1,0:T(8,128)(2,1)} %param.26) | copy-start | bytes 589828
  53.2 19.8 %all-to-all-start.3 = ((f32[4,256,128]{2,1,0:T(8,128)}), f32[4,256,128]{2,1,0:T(8,128)S(1)}, u32[]{:S(2)}, u32[]{:S(2)}) async-start(f32[4,256,128]{2,1,0:T(8,128)} %multiply_add_fusion.1), calls=%async_computation.3 | async-start | bytes 1048576 | tf_op jit(solution)/shard_map/all_to_all | solution.py:97
  73.1 11.8 %copy-start.24 = (bf16[1,1,1024,64]{2,3,1,0:T(8,128)(2,1)S(1)}, bf16[1,1,1024,64]{2,3,1,0:T(8,128)(2,1)}, u32[]{:S(2)}) copy-start(bf16[1,1,1024,64]{2,3,1,0:T(8,128)(2,1)} %get-tuple-element.55) | copy-start | bytes 393220
  76.6 25.1 %collective-permute-start = (f32[2048,128]{1,0:T(8,128)S(1)}, f32[2048,128]{1,0:T(8,128)}, u32[]{:S(2)}, u32[]{:S(2)}) collective-permute-start(f32[2048,128]{1,0:T(8,128)S(1)} %scatter_fusion), channel_id=1, source_target_pairs={{0,2},{1,3},{4,6},{5,7},{8,10},{9,11},{12,14},{13,15},{16,18},{17,... | collective-permute-start | bytes 3145736 | tf_op jit(solution)/shard_map/ppermute | solution.py:10
  81.5 8.8 %all-to-all-start.5 = ((s32[4,1,256]{2,1,0:T(1,128)}), s32[4,1,256]{2,1,0:T(1,128)S(1)}, u32[]{:S(2)}, u32[]{:S(2)}) async-start(s32[4,1,256]{2,1,0:T(1,128)} %bitcast.272), calls=%async_computation.5 | async-start | bytes 8192 | tf_op jit(solution)/shard_map/all_to_all | solution.py:72
  90.3 15.2 %all-to-all-start.4 = ((s32[4,1,1]{2,1,0:T(1,128)}), s32[4,1,1]{2,1,0:T(1,128)S(1)}, u32[]{:S(2)}, u32[]{:S(2)}) async-start(s32[4,1,1]{2,1,0:T(1,128)} %copy.39), calls=%async_computation.4 | async-start | bytes 4096 | tf_op jit(solution)/shard_map/all_to_all | solution.py:73
  104.6 13.7 %copy-start.21 = (bf16[3,256,128]{2,1,0:T(8,128)(2,1)S(1)}, bf16[3,256,128]{2,1,0:T(8,128)(2,1)}, u32[]{:S(2)}) copy-start(bf16[3,256,128]{2,1,0:T(8,128)(2,1)} %param.26) | copy-start | bytes 589828
  105.5 10.4 %all-to-all-start.6 = ((bf16[4,256,128]{2,1,0:T(8,128)(2,1)}), bf16[4,256,128]{2,1,0:T(8,128)(2,1)S(1)}, u32[]{:S(2)}, u32[]{:S(2)}) async-start(bf16[4,256,128]{2,1,0:T(8,128)(2,1)} %bitcast.29), calls=%async_computation.6 | async-start | bytes 524288 | tf_op jit(solution)/shard_map/all_to_all | solution.py:77
  109.0 133.6 %all-reduce.3.cloned.1.call-start = ((), (), s32[]{:S(2)}) async-start(), calls=%async_computation.8 | async-start | bytes 3145728 | tf_op jit(solution)/shard_map/psum | solution.py:112
  115.9 8.9 %copy-start.14 = (bf16[4,256,128]{2,1,0:T(8,128)(2,1)}, bf16[4,256,128]{2,1,0:T(8,128)(2,1)S(1)}, u32[]{:S(2)}) copy-start(bf16[4,256,128]{2,1,0:T(8,128)(2,1)S(1)} %all-to-all-done.6) | copy-start | bytes 786436
  140.9 6.7 %copy-start.8 = (f32[1,1024,128]{2,1,0:T(8,128)S(1)}, f32[1,1024,128]{2,1,0:T(8,128)}, u32[]{:S(2)}) copy-start(f32[1,1024,128]{2,1,0:T(8,128)} %copy-done.6) | copy-start | bytes 1572868
  143.5 39.6 %all-to-all-start.7 = ((f32[4,256,128]{2,1,0:T(8,128)}), f32[4,256,128]{2,1,0:T(8,128)}, u32[]{:S(2)}, u32[]{:S(2)}) async-start(f32[4,256,128]{2,1,0:T(8,128)} %multiply_add_fusion), calls=%async_computation.7 | async-start | bytes 1048576 | tf_op jit(solution)/shard_map/all_to_all | solution.py:97
  187.0 59.2 %copy-start.1 = (f32[2048,128]{1,0:T(8,128)}, f32[2048,128]{1,0:T(8,128)S(1)}, u32[]{:S(2)}) copy-start(f32[2048,128]{1,0:T(8,128)S(1)} %scatter_fusion.1) | copy-start | bytes 3145732
  (29 other events, 44.4 us)
Sparse Core Ops, SparseCore 0:
  140.0 102.5 all-reduce.2
where the time goes:
time: 254 us; the launch traced here: 253 us
  waiting for transfers between devices  92 us (36%)
  blocking collectives  40.2 us (16%)
  starting transfers between devices  36.9 us (15%)
  local copies, waits for them, and re-layouts  34.8 us (14%)
  other arithmetic  25.1 us (10%)
  between operations  14.6 us (6%)
  matrix products  9.41 us (4%)
    psum x1, waiting for transfers between devices, local(): summed = lax.psum(totals, ('node', 'seg'))  55.5 us
    psum x1, blocking collectives, local(): summed = lax.psum(totals, ('node', 'seg'))  31.7 us
    all_to_all x2, waiting for transfers between devices, local(): lax.all_to_all(fresh_rows.reshape(fetched.shape), 'node', split_axis=0, c...  14.5 us
    all_to_all x2, waiting for transfers between devices, local(): lax.all_to_all(served, 'node', split_axis=0, concat_axis=0, tiled=True)  10.7 us
    all_to_all x2, starting transfers between devices, local(): lax.all_to_all(requested, 'node', split_axis=0, concat_axis=0, tiled=True)  9.56 us
    all_to_all x2, starting transfers between devices, local(): lax.all_to_all(fresh_rows.reshape(fetched.shape), 'node', split_axis=0, c...  9.2 us
    unnamed x95, local copies, waits for them, and re-layouts  9.08 us
    gather x2, local copies, waits for them, and re-layouts, local(): dst_rows = jnp.take(full_rows, dst_slot[batch_idx, 0], axis=0)  8.91 us
  transfers between devices with their start and end apart: 10, of which 7 were waited for; matrix products, arithmetic and copies ran while one was open for 13% of the time, Pallas kernels for 0%

commit v1 on v0

v1 whole, which is shorter than its diff:
```python
import jax
import jax.numpy as jnp
from jax import lax
from jax.experimental import pallas as pl
from jax.experimental.pallas import tpu as pltpu
from jax.sharding import PartitionSpec as P

BF = jnp.bfloat16
F32 = jnp.float32
LANES = 128
VMEM = pl.BlockSpec(memory_space=pltpu.VMEM)
SMEM = pl.BlockSpec(memory_space=pltpu.SMEM)


def run(kernel, outs, smem, args, scratch=(), flops=0):
    args = list(smem) + list(args)
    specs = [SMEM] * len(smem) + [VMEM] * (len(args) - len(smem))
    moved = sum(a.size * a.dtype.itemsize for a in list(args) + list(outs))
    return pl.pallas_call(
        kernel,
        out_shape=list(outs),
        in_specs=specs,
        out_specs=[VMEM] * len(outs),
        scratch_shapes=list(scratch),
        compiler_params=pltpu.CompilerParams(vmem_limit_bytes=40 * 1024 * 1024),
        cost_estimate=pl.CostEstimate(flops=flops, bytes_accessed=moved, transcendentals=0),
    )(*args)


def shape(dims, kind):
    return jax.ShapeDtypeStruct(tuple(dims), kind)


def pick_rows(row, source):
    count = source.shape[0]
    numbers = jnp.transpose(jnp.broadcast_to(row, (LANES, LANES)))
    lane = lax.broadcasted_iota(jnp.int32, (LANES, LANES), 1)
    hot = jnp.concatenate(
        [jnp.where(numbers == lane + k * LANES, 1.0, 0.0).astype(BF) for k in range(count // LANES)],
        axis=1,
    )
    return jnp.dot(hot, source, preferred_element_type=F32).astype(BF)


def serve(rows_ref, source, held, piece_refs):
    for j in range(held.shape[0] // LANES):
        row = rows_ref[:, j * LANES : (j + 1) * LANES]
        held[j * LANES : (j + 1) * LANES, :] = pick_rows(row, source)
    cap = piece_refs[0].shape[0]
    for k, piece in enumerate(piece_refs):
        piece[...] = held[k * cap : (k + 1) * cap, :]


def set_rows(rows_ref, values, base, out_ref):
    events = values.shape[0]
    tall = 256
    wide = jnp.concatenate([values, jnp.ones((events, LANES), BF)], axis=1)
    row = rows_ref[...]
    for i in range(out_ref.shape[0] // tall):
        own = lax.broadcasted_iota(jnp.int32, (tall, events), 0) + i * tall
        hot = jnp.where(own == jnp.broadcast_to(row, (tall, events)), 1.0, 0.0).astype(BF)
        found = jnp.dot(hot, wide, preferred_element_type=F32)
        span = slice(i * tall, (i + 1) * tall)
        out_ref[span, :] = jnp.where(found[:, LANES:] > 0.5, found[:, :LANES], base[span, :])


def ask_kernel(nodes, ids, counts, rows_ref, *pieces):
    z = ids[0]
    batches, _, cap = rows_ref.shape
    slot = lax.broadcasted_iota(jnp.int32, (1, cap), 1)
    for k in range(nodes):
        owner = z ^ k
        for b in range(batches):
            row = rows_ref[b, pl.ds(owner, 1), :]
            pieces[k][b : b + 1, :] = jnp.where(slot < counts[b, owner], row, -1)


def serve_kernel(nodes, rows_ref, memory_ref, *rest):
    pieces, held = rest[:nodes], rest[nodes]
    serve(rows_ref, memory_ref[...].astype(BF), held, pieces)


def next_kernel(nodes, ids, put_ref, ask_ref, own_ref, handed_ref, *rest):
    own_pieces, handed_pieces = rest[:nodes], rest[nodes : 2 * nodes]
    memory_ref = rest[2 * nodes]
    pieces = rest[2 * nodes + 1 : 3 * nodes + 1]
    values, base, held = rest[3 * nodes + 1 :]
    cap = pieces[0].shape[0]

    @pl.when(ids[1] == 0)
    def _():
        base[...] = own_ref[...]
        for k in range(nodes):
            values[k * cap : (k + 1) * cap, :] = own_pieces[k][...]

    @pl.when(ids[1] != 0)
    def _():
        base[...] = handed_ref[...].astype(F32)
        for k in range(nodes):
            values[k * cap : (k + 1) * cap, :] = handed_pieces[k][...]

    set_rows(put_ref, values[...], base, memory_ref)
    serve(ask_ref, memory_ref[...].astype(BF), held, pieces)


def last_kernel(nodes, put_ref, base_ref, *rest):
    pieces, out_ref, values = rest[:nodes], rest[nodes], rest[nodes + 1]
    cap = pieces[0].shape[0]
    for k in range(nodes):
        values[k * cap : (k + 1) * cap, :] = pieces[k][...]
    set_rows(put_ref, values[...], base_ref, out_ref)


def forward_kernel(nodes, ids, dst_ref, time_ref, edge_ref, w_in, w_hid, bias_ref, *rest):
    own_pieces, other_pieces = rest[:nodes], rest[nodes : 2 * nodes]
    fresh_pieces = rest[2 * nodes : 3 * nodes]
    message, reset_ref, update_ref, candid_ref, recur_ref = rest[3 * nodes : 3 * nodes + 5]
    fresh = rest[3 * nodes + 5]
    cap = own_pieces[0].shape[0]
    z, f = ids[0], ids[2]
    mine = pl.multiple_of(f * LANES, LANES)
    other = pl.multiple_of((1 - f) * LANES, LANES)
    for k in range(nodes):
        at = pl.multiple_of((z ^ k) * cap, cap)
        message[pl.ds(at, cap), pl.ds(mine, LANES)] = own_pieces[k][...]
        message[pl.ds(at, cap), pl.ds(other, LANES)] = other_pieces[k][...]
    width = 2 * LANES
    full = message[:, :width]
    events = full.shape[0]
    for j in range(events // LANES):
        row = dst_ref[:, j * LANES : (j + 1) * LANES]
        message[j * LANES : (j + 1) * LANES, width : 2 * width] = pick_rows(row, full)
    message[:, 2 * width : 2 * width + LANES] = time_ref[...]
    message[:, 2 * width + LANES :] = edge_ref[...]
    w_in01 = jnp.concatenate([w_in[0], w_in[1]], axis=1)
    w_hid01 = jnp.concatenate([w_hid[0], w_hid[1]], axis=1)
    tall = 256
    for i in range(events // tall):
        span = slice(i * tall, (i + 1) * tall)
        rows = message[span, :]
        hidden = rows[:, :width]
        both = jnp.dot(rows, w_in01, preferred_element_type=F32) + jnp.dot(
            hidden, w_hid01, preferred_element_type=F32
        )
        own = message[span, pl.ds(mine, LANES)].astype(F32)
        reset_gate = jax.nn.sigmoid(both[:, :LANES] + bias_ref[0:1, :])
        update = jax.nn.sigmoid(both[:, LANES:] + bias_ref[1:2, :])
        recur_term = jnp.dot(hidden, w_hid[2], preferred_element_type=F32) + bias_ref[3:4, :]
        candid = jnp.tanh(
            jnp.dot(rows, w_in[2], preferred_element_type=F32)
            + bias_ref[2:3, :]
            + reset_gate * recur_term
        )
        fresh[span, :] = ((1.0 - update) * candid + update * own).astype(BF)
        reset_ref[span, :] = reset_gate
        update_ref[span, :] = update
        candid_ref[span, :] = candid
        recur_ref[span, :] = recur_term
    for k in range(nodes):
        at = pl.multiple_of((z ^ k) * cap, cap)
        fresh_pieces[k][...] = fresh[pl.ds(at, cap), :]


def backward_kernel(
    nodes, batch, ids, counts, message, reset_ref, update_ref, candid_ref, recur_ref, up_ref, *rest
):
    before = rest[0] if len(rest) == 3 else None
    out_ref, gates = rest[-2:]
    mine = pl.multiple_of(ids[2] * LANES, LANES)
    events = up_ref.shape[0]
    cap = events // nodes
    sums = [jnp.zeros((1, LANES), F32) for _ in range(4)]
    slot = lax.broadcasted_iota(jnp.int32, (cap, LANES), 0)
    for o in range(nodes):
        span = slice(o * cap, (o + 1) * cap)
        cotangent = jnp.where(slot < counts[batch, o], up_ref[span, :].astype(F32), 0.0)
        own = message[span, pl.ds(mine, LANES)].astype(F32)
        reset_gate, update = reset_ref[span, :], update_ref[span, :]
        candid, recur_term = candid_ref[span, :], recur_ref[span, :]
        grad_cand = cotangent * (1.0 - update) * (1.0 - candid * candid)
        grad_upd = cotangent * (own - candid) * update * (1.0 - update)
        grad_reset = grad_cand * recur_term * reset_gate * (1.0 - reset_gate)
        grad_recur = grad_cand * reset_gate
        parts = (grad_reset, grad_upd, grad_cand, grad_recur)
        for g, part in enumerate(parts):
            sums[g] = sums[g] + jnp.sum(part, axis=0, keepdims=True)
            gates[span, g * LANES : (g + 1) * LANES] = part.astype(BF)
    tall = 256
    width = 2 * LANES
    long = message.shape[1]

    def put(start, value):
        stop = start + value.shape[0]
        if before is not None:
            value = value + before[start:stop, :]
        out_ref[start:stop, :] = value.astype(out_ref.dtype)

    for i in range(long // tall):
        rows = message[:, i * tall : (i + 1) * tall]
        columns = gates[...] if i * tall < width else gates[:, : 3 * LANES]
        product = lax.dot_general(
            rows, columns, (((0,), (0,)), ((), ())), preferred_element_type=F32
        )
        for g in range(3):
            put(g * long + i * tall, product[:, g * LANES : (g + 1) * LANES])
        if i * tall < width:
            put(3 * long + i * tall, product[:, 3 * LANES :])
    top = 3 * long + width
    pad = out_ref.shape[0] - top
    tail = jnp.concatenate(sums + [jnp.zeros((pad - 4, LANES), F32)], axis=0)
    put(top, tail)


def unpack_kernel(nodes, segs, long, ids, *rest):
    pieces = rest[:segs]
    grad_in, grad_hid, grad_bias, held = rest[segs:]
    chunk = pieces[0].shape[0] // nodes
    z, s = ids[0], ids[1]
    for x in range(segs):
        for k in range(nodes):
            at = pl.multiple_of(((s ^ x) * nodes + (z ^ k)) * chunk, chunk)
            held[pl.ds(at, chunk), :] = pieces[x][k * chunk : (k + 1) * chunk, :]
    width = grad_hid.shape[1]
    for g in range(3):
        grad_in[g] = held[g * long : (g + 1) * long, :].astype(F32)
    for g in range(2):
        grad_hid[g] = held[g * long : g * long + width, :].astype(F32)
    grad_hid[2] = held[3 * long : 3 * long + width, :].astype(F32)
    top = 3 * long + width
    grad_bias[...] = held[top : top + 16, :].astype(F32)[:4, :]


def local(
    memory, req_rows, req_count, dst_slot, elapsed, edges, upstream, freq, phase, w_input, w_hidden, bias
):
    nodes, segs = lax.axis_size("node"), lax.axis_size("seg")
    z, s, f = lax.axis_index("node"), lax.axis_index("seg"), lax.axis_index("feat")
    ids = jnp.stack([z, s, f]).astype(jnp.int32)
    memory_now = memory[0]
    node_rows, half = memory_now.shape
    batches, cap = req_rows.shape[0], req_rows.shape[-1]
    events = nodes * cap
    counts = req_count[:, 0, 0]
    piece = shape((cap, half), BF)

    def node_swap(block, k):
        return lax.ppermute(block, "node", [(i, i ^ k) for i in range(nodes)])

    def seg_swap(block, x):
        return lax.ppermute(block, "seg", [(i, i ^ x) for i in range(segs)])

    def seg_next(block):
        return lax.ppermute(block, "seg", [(i, i + 1) for i in range(segs - 1)])

    def feat_swap(block):
        return lax.ppermute(block, "feat", [(0, 1), (1, 0)])

    def to_next(block, k):
        route = [
            (i * segs + j, (i ^ k) * segs + j + 1) for i in range(nodes) for j in range(segs - 1)
        ]
        return lax.ppermute(block, ("node", "seg"), route)

    def to_first(block, k):
        route = [(i * segs, (i ^ k) * segs) for i in range(nodes)]
        return lax.ppermute(block, ("node", "seg"), route)

    def exchange(blocks):
        return [blocks[0]] + [node_swap(blocks[k], k) for k in range(1, nodes)]

    wanted = run(
        lambda *refs: ask_kernel(nodes, *refs),
        [shape((batches, cap), jnp.int32)] * nodes,
        [ids, counts],
        [req_rows[:, 0, 0]],
    )
    asked = jnp.concatenate(exchange(wanted), axis=1)
    asked_before = seg_next(asked)

    edge_other = feat_swap(edges[:, 0])
    edge_full = jnp.where(
        f == 0,
        jnp.concatenate([edges[:, 0], edge_other], axis=-1),
        jnp.concatenate([edge_other, edges[:, 0]], axis=-1),
    )
    time_code = jnp.cos(
        elapsed[:, 0].astype(F32)[:, :, None] * freq[None, None, :] + phase[None, None, :]
    ).astype(BF)

    long = w_input.shape[1]
    held = pltpu.VMEM((events, half), BF)
    total_rows = 3 * long + w_hidden.shape[1] + 16
    chunk = -(-total_rows // (16 * nodes * segs)) * 16
    total_rows = chunk * nodes * segs
    totals = None
    served = run(
        lambda *refs: serve_kernel(nodes, *refs),
        [piece] * nodes,
        [],
        [asked[0:1], memory_now],
        [held],
    )
    for b in range(batches):
        final = b + 1 == batches
        own_pieces = exchange(served)
        if not final:
            memory_before = seg_next(memory_now.astype(BF))
        other_pieces = [feat_swap(p) for p in own_pieces]
        gate = shape((events, half), F32)
        outs = run(
            lambda *refs: forward_kernel(nodes, *refs),
            [piece] * nodes + [shape((events, long), BF)] + [gate] * 4,
            [ids],
            [dst_slot[b], time_code[b], edge_full[b], w_input, w_hidden, bias]
            + own_pieces
            + other_pieces,
            [held],
        )
        fresh, kept = outs[:nodes], outs[nodes:]
        if final:
            returned = exchange(fresh)
        else:
            handed = [to_next(fresh[k], k) for k in range(nodes)]
            stayed = [fresh[0]] + [to_first(fresh[k], k) for k in range(1, nodes)]
        totals = run(
            lambda *refs, b=b: backward_kernel(nodes, b, *refs),
            [shape((total_rows, half), BF if final else F32)],
            [ids, counts],
            list(kept) + [upstream[b, 0]] + ([] if totals is None else [totals]),
            [pltpu.VMEM((events, 4 * half), BF)],
        )[0]
        if final:
            memory_out = run(
                lambda *refs: last_kernel(nodes, *refs),
                [shape((node_rows, half), F32)],
                [],
                [asked[b : b + 1], memory_now] + returned,
                [held],
            )[0]
        else:
            put = jnp.where(s == 0, asked[b : b + 1], asked_before[b : b + 1])
            outs = run(
                lambda *refs: next_kernel(nodes, *refs),
                [shape((node_rows, half), F32)] + [piece] * nodes,
                [ids],
                [put, asked[b + 1 : b + 2], memory_now, memory_before] + stayed + handed,
                [held, pltpu.VMEM((node_rows, half), F32), held],
            )
            memory_now, served = outs[0], outs[1:]

    def at(blocks, i):
        return lax.dynamic_index_in_dim(blocks, i, 0, keepdims=False)

    blocks = totals.reshape(segs, nodes * chunk, half)
    got = [seg_swap(at(blocks, s ^ x), x) for x in range(1, segs)]
    summed = sum((g.astype(F32) for g in got), at(blocks, s).astype(F32)).astype(BF)
    blocks = summed.reshape(nodes, chunk, half)
    got = [node_swap(at(blocks, z ^ k), k) for k in range(1, nodes)]
    summed = sum((g.astype(F32) for g in got), at(blocks, z).astype(F32)).astype(BF)
    gathered = jnp.concatenate([summed] + [node_swap(summed, k) for k in range(1, nodes)], axis=0)
    gathered = [gathered] + [seg_swap(gathered, x) for x in range(1, segs)]
    grads = run(
        lambda *refs: unpack_kernel(nodes, segs, long, *refs),
        [shape(w_input.shape, F32), shape(w_hidden.shape, F32), shape(bias.shape, F32)],
        [ids],
        gathered,
        [pltpu.VMEM((total_rows, half), BF)],
    )
    return (memory_out[None], *grads)


def solution(mesh):
    in_specs = (
        P(("parts", "seg"), "node", "feat"),
        P(None, ("parts", "seg"), "node", None, None),
        P(None, ("parts", "seg"), "node", None),
        P(None, ("parts", "seg"), "node"),
        P(None, ("parts", "seg"), "node"),
        P(None, ("parts", "seg"), "node", "feat"),
        P(None, ("parts", "seg"), "node", "feat"),
        P(),
        P(),
        P(None, None, "feat"),
        P(None, None, "feat"),
        P(None, "feat"),
    )
    out_specs = (
        P(("parts", "seg"), "node", "feat"),
        P("parts", None, "feat"),
        P("parts", None, "feat"),
        P("parts", "feat"),
    )
    return jax.shard_map(local, mesh=mesh, in_specs=in_specs, out_specs=out_specs, check_vma=False)
```

time: 254 us -> 144 us (0.57)
  waiting for transfers between devices: 92 us -> 41.6 us
  blocking collectives: 40.2 us -> 0 us
  Pallas kernels: 0 us -> 19.9 us
  starting transfers between devices: 36.9 us -> 54.8 us
  local copies, waits for them, and re-layouts: 34.8 us -> 17.4 us
  other arithmetic: 25.1 us -> 7.94 us
  between operations: 14.6 us -> 1.18 us
  matrix products: 9.41 us -> 0 us
    psum x1 -> x0, waiting for transfers between devices: 55.5 us -> none  [local(): summed = lax.psum(totals, ('node', 'seg'))]
    ppermute x1 -> x38, starting transfers between devices: 4.38 us -> 54.8 us  [the longest x18 27.8 us: node_swap(): return lax.ppermute(block, 'node', [(i, i ^ k) for i in range(nodes)])]
    ppermute x1 -> x38, waiting for transfers between devices: 8.03 us -> 41.6 us  [the longest x18 25.2 us: node_swap(): return lax.ppermute(block, 'node', [(i, i ^ k) for i in range(nodes)])]
    all_to_all x8 -> x0, starting transfers between devices: 32.4 us -> none  [the longest x2 9.56 us: local(): lax.all_to_all(requested, 'node', split_axis=0, concat_axis=0, tiled=True)]
    psum x1 -> x0, blocking collectives: 31.7 us -> none  [local(): summed = lax.psum(totals, ('node', 'seg'))]
    all_to_all x8 -> x0, waiting for transfers between devices: 28.5 us -> none  [the longest x2 14.5 us: local(): lax.all_to_all(fresh_rows.reshape(fetched.shape), 'node', split_axis=0, c...]
    pallas_call x0 -> x9, Pallas kernels: none -> 19.9 us  [run(): pl.pallas_call(kernel, out_shape=list(outs), in_specs=specs, out_specs=[V...]
    gather x4 -> x0, local copies, waits for them, and re-layouts: 14.7 us -> none  [the longest x2 8.91 us: local(): dst_rows = jnp.take(full_rows, dst_slot[batch_idx, 0], axis=0)]
  transfers between devices with their start and end apart: 10 -> 38, of which waited for: 7 -> 15; matrix products, arithmetic and copies ran while one was open for 13% -> 8% of each run, Pallas kernels for 0% -> 6%
where the time goes in v1:
time: 144 us; the launch traced here: 143 us
  starting transfers between devices  54.8 us (38%)
  waiting for transfers between devices  41.6 us (29%)
  Pallas kernels  19.9 us (14%)
  local copies, waits for them, and re-layouts  17.4 us (12%)
  other arithmetic  7.94 us (6%)
    ppermute x18, starting transfers between devices, node_swap(): return lax.ppermute(block, 'node', [(i, i ^ k) for i in range(nodes)])  27.8 us
    ppermute x18, waiting for transfers between devices, node_swap(): return lax.ppermute(block, 'node', [(i, i ^ k) for i in range(nodes)])  25.2 us
    pallas_call x9, Pallas kernels, run(): pl.pallas_call(kernel, out_shape=list(outs), in_specs=specs, out_specs=[V...  19.9 us
    unnamed x71, local copies, waits for them, and re-layouts  15.2 us
    ppermute x3, starting transfers between devices, to_first(): return lax.ppermute(block, ('node', 'seg'), route)  10.1 us
    ppermute x2, waiting for transfers between devices, seg_swap(): return lax.ppermute(block, 'seg', [(i, i ^ x) for i in range(segs)])  8.73 us
    ppermute x2, starting transfers between devices, seg_next(): return lax.ppermute(block, 'seg', [(i, i + 1) for i in range(segs - 1)])  5.85 us
    ppermute x2, waiting for transfers between devices, seg_next(): return lax.ppermute(block, 'seg', [(i, i + 1) for i in range(segs - 1)])  5.42 us
  transfers between devices with their start and end apart: 38, of which 15 were waited for; matrix products, arithmetic and copies ran while one was open for 8% of the time, Pallas kernels for 6%

profile of v1, /device:TPU:0, one launch (start us, length us, event | category | flops | bytes accessed | tf_op | source)
XLA Modules:
  0.0 142.8 jit_solution(11538196619451194267)
XLA Ops:
  2.7 3.1 %collective-permute-start = (s32[2,256]{1,0:T(2,128)S(1)}, s32[2,256]{1,0:T(2,128)S(1)}, u32[]{:S(2)}, u32[]{:S(2)}) collective-permute-start(s32[2,256]{1,0:T(2,128)S(1)} %get-tuple-element.39), channel_id=1, source_target_pairs={{0,4},{4,0},{8,12},{12,8},{1,5},{5,1},{9,13},{13,9},{2,6},{6,2},{1... | collective-permute-start | bytes 6152 | tf_op jit(solution)/shard_map/ppermute | solution.py:247
  5.8 2.6 %collective-permute-start.1 = (s32[2,256]{1,0:T(2,128)S(1)}, s32[2,256]{1,0:T(2,128)S(1)}, u32[]{:S(2)}, u32[]{:S(2)}) collective-permute-start(s32[2,256]{1,0:T(2,128)S(1)} %get-tuple-element.40), channel_id=1, source_target_pairs={{0,8},{4,12},{8,0},{12,4},{1,9},{5,13},{9,1},{13,5},{2,10},{6,14},... | collective-permute-start | bytes 6152 | tf_op jit(solution)/shard_map/ppermute | solution.py:247
  9.7 2.1 %bitcast_convert_fusion = bf16[2048,128]{1,0:T(8,128)(2,1)} fusion(f32[1,2048,128]{2,1,0:T(8,128)} %param.12), kind=kLoop, calls=%fused_computation.28 | loop fusion | flops 262144 | bytes 1572864 | tf_op jit(solution)/shard_map/convert_element_type | solution.py:307
  11.9 4.6 %collective-permute-start.4 = (bf16[2048,128]{1,0:T(8,128)(2,1)}, bf16[2048,128]{1,0:T(8,128)(2,1)}, u32[]{:S(2)}, u32[]{:S(2)}) collective-permute-start(bf16[2048,128]{1,0:T(8,128)(2,1)} %bitcast_convert_fusion), channel_id=1, source_target_pairs={{0,2},{1,3},{4,6},{5,7},{8,10},{9,11},{12,14},{13,15},{16,18},{17,... | collective-permute-start | bytes 1572872 | tf_op jit(solution)/shard_map/ppermute | solution.py:253
  16.5 3.8 %cosine_convert_fusion = bf16[2,1024,128]{2,1,0:T(8,128)(2,1)S(1)} fusion(f32[128]{0:T(128)S(1)} %copy-done.31, f32[128]{0:T(128)S(1)} %copy-done.32, f32[2,1024]{1,0:T(2,128)S(1)} %bitcast.57), kind=kLoop, calls=%fused_computation | loop fusion | flops 786432 | bytes 533504 | tf_op jit(solution)/shard_map/convert_element_type | solution.py:288
  22.3 5.4 %collective-permute-done.3 = s32[2,1024]{1,0:T(2,128)S(1)} collective-permute-done((s32[2,1024]{1,0:T(2,128)S(1)}, s32[2,1024]{1,0:T(2,128)S(1)}, u32[]{:S(2)}, u32[]{:S(2)}) %collective-permute-start.3) | collective-permute-done | bytes 8224 | tf_op jit(solution)/shard_map/ppermute | solution.py:253
  30.0 3.5 %collective-permute-start.7 = (bf16[256,128]{1,0:T(8,128)(2,1)S(1)}, bf16[256,128]{1,0:T(8,128)(2,1)S(1)}, u32[]{:S(2)}, u32[]{:S(2)}) collective-permute-start(bf16[256,128]{1,0:T(8,128)(2,1)S(1)} %get-tuple-element.44), channel_id=1, source_target_pairs={{0,8},{4,12},{8,0},{12,4},{1,9},{5,13},{9,1},{13,5},{2,10},{6,14},... | collective-permute-start | bytes 196616 | tf_op jit(solution)/shard_map/ppermute | solution.py:247
  34.3 3.6 %collective-permute-done.7.refs_9_ = bf16[256,128]{1,0:T(8,128)(2,1)S(1)} collective-permute-done((bf16[256,128]{1,0:T(8,128)(2,1)S(1)}, bf16[256,128]{1,0:T(8,128)(2,1)S(1)}, u32[]{:S(2)}, u32[]{:S(2)}) %collective-permute-start.7) | collective-permute-done | bytes 65568 | tf_op jit(solution)/shard_map/ppermute | solution.py:247
  47.8 2.8 %shard_map.149 = (bf16[256,128]{1,0:T(8,128)(2,1)S(1)}, bf16[256,128]{1,0:T(8,128)(2,1)S(1)}, bf16[256,128]{1,0:T(8,128)(2,1)S(1)}, bf16[256,128]{1,0:T(8,128)(2...) custom-call(s32[3]{0:T(128)S(1)} %pad_add_fusion.refs_0_, ...), custom_call_target="tpu_custom_call" | custom-call | bytes 5773324 | tf_op jit(solution)/shard_map/pallas_call | solution.py:19
  52.1 1.9 %collective-permute-start.13 = (bf16[256,128]{1,0:T(8,128)(2,1)S(1)}, bf16[256,128]{1,0:T(8,128)(2,1)S(1)}, u32[]{:S(2)}, u32[]{:S(2)}) collective-permute-start(bf16[256,128]{1,0:T(8,128)(2,1)S(1)} %get-tuple-element.47), channel_id=1, source_target_pairs={{0,4},{4,0},{8,12},{12,8},{1,5},{5,1},{9,13},{13,9},{16,20},{20,16... | collective-permute-start | bytes 196616 | tf_op jit(solution)/shard_map/ppermute | solution.py:266
  54.1 4.0 %collective-permute-start.14 = (bf16[256,128]{1,0:T(8,128)(2,1)S(1)}, bf16[256,128]{1,0:T(8,128)(2,1)S(1)}, u32[]{:S(2)}, u32[]{:S(2)}) collective-permute-start(bf16[256,128]{1,0:T(8,128)(2,1)S(1)} %get-tuple-element.48), channel_id=1, source_target_pairs={{0,8},{4,12},{8,0},{12,4},{1,9},{5,13},{9,1},{13,5},{16,24},{20,28... | collective-permute-start | bytes 196616 | tf_op jit(solution)/shard_map/ppermute | solution.py:266
  58.1 4.2 %collective-permute-start.15 = (bf16[256,128]{1,0:T(8,128)(2,1)S(1)}, bf16[256,128]{1,0:T(8,128)(2,1)S(1)}, u32[]{:S(2)}, u32[]{:S(2)}) collective-permute-start(bf16[256,128]{1,0:T(8,128)(2,1)S(1)} %get-tuple-element.49), channel_id=1, source_target_pairs={{0,12},{4,8},{8,4},{12,0},{1,13},{5,9},{9,5},{13,1},{16,28},{20,24... | collective-permute-start | bytes 196616 | tf_op jit(solution)/shard_map/ppermute | solution.py:266
  69.7 4.3 %shard_map.150 = (f32[2048,128]{1,0:T(8,128)S(1)}, bf16[256,128]{1,0:T(8,128)(2,1)S(1)}, bf16[256,128]{1,0:T(8,128)(2,1)S(1)}, bf16[256,128]{1,0:T(8,128)(2,1)S(1)}, bf16[256,128]{1,0:T(8,128)(2,1)S(1)}) custom-call(s32[3]{0:T(128)S(1)} %pad_add_fusion.refs_0_, s32[1,1024]{1,0:T(1,128)S(1)} %get-tuple-element.84.refs_1_, ...), custom_call_target="tpu_custom_call" | custom-call | bytes 3416076 | tf_op jit(solution)/shard_map/pallas_call | solution.py:19
  79.9 2.7 %collective-permute-done.21.refs_9_ = bf16[256,128]{1,0:T(8,128)(2,1)S(1)} collective-permute-done((bf16[256,128]{1,0:T(8,128)(2,1)S(1)}, bf16[256,128]{1,0:T(8,128)(2,1)S(1)}, u32[]{:S(2)}, u32[]{:S(2)}) %collective-permute-start.21) | collective-permute-done | bytes 65568 | tf_op jit(solution)/shard_map/ppermute | solution.py:247
  89.1 2.0 %shard_map.153.refs_8_ = f32[2688,128]{1,0:T(8,128)S(1)} custom-call(s32[3]{0:T(128)S(1)} %pad_add_fusion.refs_0_, s32[2,4]{1,0:T(2,128)S(1)} %bitcast.49, bf16[1024,768]{1,0:T(8,128)(2,1)S(1)} %get-tuple-element.64.refs_2_, f32[1024,128]{1,0:T(8,128)S(1)} %copy-done.9, f32[1024,128]{1,0:T(8,128)S(1)} %copy-done.11, f32[1024,128]{1,0:T(8,128)S(1)} %copy-done.13, ...), custom_call_target="tpu_custom_call" | custom-call | bytes 5308460 | tf_op jit(solution)/shard_map/pallas_call | solution.py:19
  91.1 2.8 %shard_map.151 = (bf16[256,128]{1,0:T(8,128)(2,1)S(1)}, bf16[256,128]{1,0:T(8,128)(2,1)S(1)}, bf16[256,128]{1,0:T(8,128)(2,1)S(1)}, bf16[256,128]{1,0:T(8,128)(2...) custom-call(s32[3]{0:T(128)S(1)} %pad_add_fusion.refs_0_, ...), custom_call_target="tpu_custom_call" | custom-call | bytes 5773324 | tf_op jit(solution)/shard_map/pallas_call | solution.py:19
  94.0 2.0 %shard_map.154 = bf16[2688,128]{1,0:T(8,128)(2,1)S(1)} custom-call(s32[3]{0:T(128)S(1)} %pad_add_fusion.refs_0_, s32[2,4]{1,0:T(2,128)S(1)} %bitcast.50, bf16[1024,768]{1,0:T(8,128)(2,1)S(1)} %get-tuple-element.59.refs_2_, f32[1024,128]{1,0:T(8,128)S(1)} %get-tuple-element.60.refs_3_, f32[1024,128]{1,0:T(8,128)S(1)} %get-tuple-element.61.refs_4_, ...), custom_call_target="tpu_custom_call" | custom-call | bytes 5996588 | tf_op jit(solution)/shard_map/pallas_call | solution.py:19
  96.0 3.3 %collective-permute-start.30 = (bf16[1344,128]{1,0:T(8,128)(2,1)S(1)}, bf16[1344,128]{1,0:T(8,128)(2,1)S(1)}, u32[]{:S(2)}, u32[]{:S(2)}) collective-permute-start(bf16[1344,128]{1,0:T(8,128)(2,1)S(1)} %dynamic-slice_bitcast_fusion), channel_id=1, source_target_pairs={{0,2},{2,0},{1,3},{3,1},{4,6},{6,4},{5,7},{7,5},{8,10},{10,8},{9,1... | collective-permute-start | bytes 1032200 | tf_op jit(solution)/shard_map/ppermute | solution.py:250
  99.3 8.7 %collective-permute-done.30 = bf16[1344,128]{1,0:T(8,128)(2,1)S(1)} collective-permute-done((bf16[1344,128]{1,0:T(8,128)(2,1)S(1)}, bf16[1344,128]{1,0:T(8,128)(2,1)S(1)}, u32[]{:S(2)}, u32[]{:S(2)}) %collective-permute-start.30) | collective-permute-done | bytes 344096 | tf_op jit(solution)/shard_map/ppermute | solution.py:250
  108.9 2.3 %collective-permute-start.32 = (bf16[336,128]{1,0:T(8,128)(2,1)S(1)}, bf16[336,128]{1,0:T(8,128)(2,1)S(1)}, u32[]{:S(2)}, u32[]{:S(2)}) collective-permute-start(bf16[336,128]{1,0:T(8,128)(2,1)S(1)} %get-tuple-element.80), channel_id=1, source_target_pairs={{0,8},{4,12},{8,0},{12,4},{1,9},{5,13},{9,1},{13,5},{2,10},{6,14},... | collective-permute-start | bytes 258056 | tf_op jit(solution)/shard_map/ppermute | solution.py:247
  113.7 4.8 %collective-permute-done.32 = bf16[336,128]{1,0:T(8,128)(2,1)S(1)} collective-permute-done((bf16[336,128]{1,0:T(8,128)(2,1)S(1)}, bf16[336,128]{1,0:T(8,128)(2,1)S(1)}, u32[]{:S(2)}, u32[]{:S(2)}) %collective-permute-start.32) | collective-permute-done | bytes 86048 | tf_op jit(solution)/shard_map/ppermute | solution.py:247
  123.5 5.0 %collective-permute-done.35 = bf16[336,128]{1,0:T(8,128)(2,1)S(1)} collective-permute-done((bf16[336,128]{1,0:T(8,128)(2,1)S(1)}, bf16[336,128]{1,0:T(8,128)(2,1)S(1)}, u32[]{:S(2)}, u32[]{:S(2)}) %collective-permute-start.35) | collective-permute-done | bytes 86048 | tf_op jit(solution)/shard_map/ppermute | solution.py:247
  134.4 3.0 %collective-permute-done.28.refs_4_ = bf16[256,128]{1,0:T(8,128)(2,1)S(1)} collective-permute-done((bf16[256,128]{1,0:T(8,128)(2,1)S(1)}, bf16[256,128]{1,0:T(8,128)(2,1)S(1)}, u32[]{:S(2)}, u32[]{:S(2)}) %collective-permute-start.28) | collective-permute-done | bytes 65568 | tf_op jit(solution)/shard_map/ppermute | solution.py:247
  138.7 2.2 %shard_map.152 = f32[2048,128]{1,0:T(8,128)} custom-call(s32[1,1024]{1,0:T(1,128)S(1)} %get-tuple-element.85.refs_2_.refs_0_, f32[2048,128]{1,0:T(8,128)S(1)} %copy-done.3, bf16[256,128]{1,0:T(8,128)(2,1)S(1)} %get-tuple-element.55.refs_2_, bf16[256,128]{1,0:T(8,128)(2,1)S(1)} %collective-permute-done.27.refs_3_, ...), custom_call_target="tpu_custom_call" | custom-call | bytes 2363392 | tf_op jit(solution)/shard_map/pallas_call | solution.py:19
  (148 shorter events, 57.0 us)
Async XLA Ops:
  2.7 17.5 %collective-permute-start = (s32[2,256]{1,0:T(2,128)S(1)}, s32[2,256]{1,0:T(2,128)S(1)}, u32[]{:S(2)}, u32[]{:S(2)}) collective-permute-start(s32[2,256]{1,0:T(2,128)S(1)} %get-tuple-element.39), channel_id=1, source_target_pairs={{0,4},{4,0},{8,12},{12,8},{1,5},{5,1},{9,13},{13,9},{2,6},{6,2},{1... | collective-permute-start | bytes 6152 | tf_op jit(solution)/shard_map/ppermute | solution.py:247
  5.8 14.5 %collective-permute-start.1 = (s32[2,256]{1,0:T(2,128)S(1)}, s32[2,256]{1,0:T(2,128)S(1)}, u32[]{:S(2)}, u32[]{:S(2)}) collective-permute-start(s32[2,256]{1,0:T(2,128)S(1)} %get-tuple-element.40), channel_id=1, source_target_pairs={{0,8},{4,12},{8,0},{12,4},{1,9},{5,13},{9,1},{13,5},{2,10},{6,14},... | collective-permute-start | bytes 6152 | tf_op jit(solution)/shard_map/ppermute | solution.py:247
  8.4 11.9 %collective-permute-start.2 = (s32[2,256]{1,0:T(2,128)S(1)}, s32[2,256]{1,0:T(2,128)S(1)}, u32[]{:S(2)}, u32[]{:S(2)}) collective-permute-start(s32[2,256]{1,0:T(2,128)S(1)} %get-tuple-element.41), channel_id=1, source_target_pairs={{0,12},{4,8},{8,4},{12,0},{1,13},{5,9},{9,5},{13,1},{2,14},{6,10},... | collective-permute-start | bytes 6152 | tf_op jit(solution)/shard_map/ppermute | solution.py:247
  9.6 29.9 %collective-permute-start.5 = (bf16[2,1024,64]{2,1,0:T(8,128)(2,1)S(1)}, bf16[2,1024,64]{2,1,0:T(8,128)(2,1)}, u32[]{:S(2)}, u32[]{:S(2)}) collective-permute-start(bf16[2,1024,64]{2,1,0:T(8,128)(2,1)S(1)} %bitcast.52), channel_id=1, source_target_pairs={{0,1},{1,0},{2,3},{3,2},{4,5},{5,4},{6,7},{7,6},{8,9},{9,8},{10,11... | collective-permute-start | bytes 786440 | tf_op jit(solution)/shard_map/ppermute | solution.py:256
  11.9 57.9 %collective-permute-start.4 = (bf16[2048,128]{1,0:T(8,128)(2,1)}, bf16[2048,128]{1,0:T(8,128)(2,1)}, u32[]{:S(2)}, u32[]{:S(2)}) collective-permute-start(bf16[2048,128]{1,0:T(8,128)(2,1)} %bitcast_convert_fusion), channel_id=1, source_target_pairs={{0,2},{1,3},{4,6},{5,7},{8,10},{9,11},{12,14},{13,15},{16,18},{17,... | collective-permute-start | bytes 1572872 | tf_op jit(solution)/shard_map/ppermute | solution.py:253
  20.3 7.5 %collective-permute-start.3 = (s32[2,1024]{1,0:T(2,128)S(1)}, s32[2,1024]{1,0:T(2,128)S(1)}, u32[]{:S(2)}, u32[]{:S(2)}) collective-permute-start(s32[2,1024]{1,0:T(2,128)S(1)} %constant_dynamic-update-slice_fusion), channel_id=1, source_target_pairs={{0,2},{1,3},{4,6},{5,7},{8,10},{9,11},{12,14},{13,15},{16,18},{17,... | collective-permute-start | bytes 24584 | tf_op jit(solution)/shard_map/ppermute | solution.py:253
  30.0 7.9 %collective-permute-start.7 = (bf16[256,128]{1,0:T(8,128)(2,1)S(1)}, bf16[256,128]{1,0:T(8,128)(2,1)S(1)}, u32[]{:S(2)}, u32[]{:S(2)}) collective-permute-start(bf16[256,128]{1,0:T(8,128)(2,1)S(1)} %get-tuple-element.44), channel_id=1, source_target_pairs={{0,8},{4,12},{8,0},{12,4},{1,9},{5,13},{9,1},{13,5},{2,10},{6,14},... | collective-permute-start | bytes 196616 | tf_op jit(solution)/shard_map/ppermute | solution.py:247
  33.5 6.1 %collective-permute-start.8 = (bf16[256,128]{1,0:T(8,128)(2,1)S(1)}, bf16[256,128]{1,0:T(8,128)(2,1)S(1)}, u32[]{:S(2)}, u32[]{:S(2)}) collective-permute-start(bf16[256,128]{1,0:T(8,128)(2,1)S(1)} %get-tuple-element.45), channel_id=1, source_target_pairs={{0,12},{4,8},{8,4},{12,0},{1,13},{5,9},{9,5},{13,1},{2,14},{6,10},... | collective-permute-start | bytes 196616 | tf_op jit(solution)/shard_map/ppermute | solution.py:247
  34.3 8.3 %collective-permute-start.9 = (bf16[256,128]{1,0:T(8,128)(2,1)S(1)}, bf16[256,128]{1,0:T(8,128)(2,1)S(1)}, u32[]{:S(2)}, u32[]{:S(2)}) collective-permute-start(bf16[256,128]{1,0:T(8,128)(2,1)S(1)} %get-tuple-element.42.refs_7_), channel_id=1, source_target_pairs={{0,1},{1,0},{2,3},{3,2},{4,5},{5,4},{6,7},{7,6},{8,9},{9,8},{10,11... | collective-permute-start | bytes 196616 | tf_op jit(solution)/shard_map/ppermute | solution.py:256
  52.1 11.4 %collective-permute-start.13 = (bf16[256,128]{1,0:T(8,128)(2,1)S(1)}, bf16[256,128]{1,0:T(8,128)(2,1)S(1)}, u32[]{:S(2)}, u32[]{:S(2)}) collective-permute-start(bf16[256,128]{1,0:T(8,128)(2,1)S(1)} %get-tuple-element.47), channel_id=1, source_target_pairs={{0,4},{4,0},{8,12},{12,8},{1,5},{5,1},{9,13},{13,9},{16,20},{20,16... | collective-permute-start | bytes 196616 | tf_op jit(solution)/shard_map/ppermute | solution.py:266
  54.1 10.8 %collective-permute-start.14 = (bf16[256,128]{1,0:T(8,128)(2,1)S(1)}, bf16[256,128]{1,0:T(8,128)(2,1)S(1)}, u32[]{:S(2)}, u32[]{:S(2)}) collective-permute-start(bf16[256,128]{1,0:T(8,128)(2,1)S(1)} %get-tuple-element.48), channel_id=1, source_target_pairs={{0,8},{4,12},{8,0},{12,4},{1,9},{5,13},{9,1},{13,5},{16,24},{20,28... | collective-permute-start | bytes 196616 | tf_op jit(solution)/shard_map/ppermute | solution.py:266
  58.1 8.4 %collective-permute-start.15 = (bf16[256,128]{1,0:T(8,128)(2,1)S(1)}, bf16[256,128]{1,0:T(8,128)(2,1)S(1)}, u32[]{:S(2)}, u32[]{:S(2)}) collective-permute-start(bf16[256,128]{1,0:T(8,128)(2,1)S(1)} %get-tuple-element.49), channel_id=1, source_target_pairs={{0,12},{4,8},{8,4},{12,0},{1,13},{5,9},{9,5},{13,1},{16,28},{20,24... | collective-permute-start | bytes 196616 | tf_op jit(solution)/shard_map/ppermute | solution.py:266
  78.0 6.2 %collective-permute-start.22 = (bf16[256,128]{1,0:T(8,128)(2,1)S(1)}, bf16[256,128]{1,0:T(8,128)(2,1)S(1)}, u32[]{:S(2)}, u32[]{:S(2)}) collective-permute-start(bf16[256,128]{1,0:T(8,128)(2,1)S(1)} %get-tuple-element.54), channel_id=1, source_target_pairs={{0,12},{4,8},{8,4},{12,0},{1,13},{5,9},{9,5},{13,1},{2,14},{6,10},... | collective-permute-start | bytes 196616 | tf_op jit(solution)/shard_map/ppermute | solution.py:247
  79.4 11.7 %collective-permute-start.23 = (bf16[256,128]{1,0:T(8,128)(2,1)S(1)}, bf16[256,128]{1,0:T(8,128)(2,1)S(1)}, u32[]{:S(2)}, u32[]{:S(2)}) collective-permute-start(bf16[256,128]{1,0:T(8,128)(2,1)S(1)} %get-tuple-element.51.refs_7_), channel_id=1, source_target_pairs={{0,1},{1,0},{2,3},{3,2},{4,5},{5,4},{6,7},{7,6},{8,9},{9,8},{10,11... | collective-permute-start | bytes 196616 | tf_op jit(solution)/shard_map/ppermute | solution.py:256
  79.4 11.7 %collective-permute-start.24 = (bf16[256,128]{1,0:T(8,128)(2,1)S(1)}, bf16[256,128]{1,0:T(8,128)(2,1)S(1)}, u32[]{:S(2)}, u32[]{:S(2)}) collective-permute-start(bf16[256,128]{1,0:T(8,128)(2,1)S(1)} %collective-permute-done.20.refs_8_), channel_id=1, source_target_pairs={{0,1},{1,0},{2,3},{3,2},{4,5},{5,4},{6,7},{7,6},{8,9},{9,8},{10,11... | collective-permute-start | bytes 196616 | tf_op jit(solution)/shard_map/ppermute | solution.py:256
  82.6 8.5 %collective-permute-start.25 = (bf16[256,128]{1,0:T(8,128)(2,1)S(1)}, bf16[256,128]{1,0:T(8,128)(2,1)S(1)}, u32[]{:S(2)}, u32[]{:S(2)}) collective-permute-start(bf16[256,128]{1,0:T(8,128)(2,1)S(1)} %collective-permute-done.21.refs_9_), channel_id=1, source_target_pairs={{0,1},{1,0},{2,3},{3,2},{4,5},{5,4},{6,7},{7,6},{8,9},{9,8},{10,11... | collective-permute-start | bytes 196616 | tf_op jit(solution)/shard_map/ppermute | solution.py:256
  84.2 6.9 %collective-permute-start.26 = (bf16[256,128]{1,0:T(8,128)(2,1)S(1)}, bf16[256,128]{1,0:T(8,128)(2,1)S(1)}, u32[]{:S(2)}, u32[]{:S(2)}) collective-permute-start(bf16[256,128]{1,0:T(8,128)(2,1)S(1)} %collective-permute-done.22.refs_10_), channel_id=1, source_target_pairs={{0,1},{1,0},{2,3},{3,2},{4,5},{5,4},{6,7},{7,6},{8,9},{9,8},{10,11... | collective-permute-start | bytes 196616 | tf_op jit(solution)/shard_map/ppermute | solution.py:256
  96.0 12.0 %collective-permute-start.30 = (bf16[1344,128]{1,0:T(8,128)(2,1)S(1)}, bf16[1344,128]{1,0:T(8,128)(2,1)S(1)}, u32[]{:S(2)}, u32[]{:S(2)}) collective-permute-start(bf16[1344,128]{1,0:T(8,128)(2,1)S(1)} %dynamic-slice_bitcast_fusion), channel_id=1, source_target_pairs={{0,2},{2,0},{1,3},{3,1},{4,6},{6,4},{5,7},{7,5},{8,10},{10,8},{9,1... | collective-permute-start | bytes 1032200 | tf_op jit(solution)/shard_map/ppermute | solution.py:250
  108.9 9.6 %collective-permute-start.32 = (bf16[336,128]{1,0:T(8,128)(2,1)S(1)}, bf16[336,128]{1,0:T(8,128)(2,1)S(1)}, u32[]{:S(2)}, u32[]{:S(2)}) collective-permute-start(bf16[336,128]{1,0:T(8,128)(2,1)S(1)} %get-tuple-element.80), channel_id=1, source_target_pairs={{0,8},{4,12},{8,0},{12,4},{1,9},{5,13},{9,1},{13,5},{2,10},{6,14},... | collective-permute-start | bytes 258056 | tf_op jit(solution)/shard_map/ppermute | solution.py:247
  111.2 7.3 %collective-permute-start.33 = (bf16[336,128]{1,0:T(8,128)(2,1)S(1)}, bf16[336,128]{1,0:T(8,128)(2,1)S(1)}, u32[]{:S(2)}, u32[]{:S(2)}) collective-permute-start(bf16[336,128]{1,0:T(8,128)(2,1)S(1)} %get-tuple-element.79), channel_id=1, source_target_pairs={{0,12},{4,8},{8,4},{12,0},{1,13},{5,9},{9,5},{13,1},{2,14},{6,10},... | collective-permute-start | bytes 258056 | tf_op jit(solution)/shard_map/ppermute | solution.py:247
  120.1 8.4 %collective-permute-start.35 = (bf16[336,128]{1,0:T(8,128)(2,1)S(1)}, bf16[336,128]{1,0:T(8,128)(2,1)S(1)}, u32[]{:S(2)}, u32[]{:S(2)}) collective-permute-start(bf16[336,128]{1,0:T(8,128)(2,1)S(1)} %fusion.3), channel_id=1, source_target_pairs={{0,8},{4,12},{8,0},{12,4},{1,9},{5,13},{9,1},{13,5},{2,10},{6,14},... | collective-permute-start | bytes 258056 | tf_op jit(solution)/shard_map/ppermute | solution.py:247
  121.3 7.2 %collective-permute-start.36 = (bf16[336,128]{1,0:T(8,128)(2,1)S(1)}, bf16[336,128]{1,0:T(8,128)(2,1)S(1)}, u32[]{:S(2)}, u32[]{:S(2)}) collective-permute-start(bf16[336,128]{1,0:T(8,128)(2,1)S(1)} %fusion.3), channel_id=1, source_target_pairs={{0,12},{4,8},{8,4},{12,0},{1,13},{5,9},{9,5},{13,1},{2,14},{6,10},... | collective-permute-start | bytes 258056 | tf_op jit(solution)/shard_map/ppermute | solution.py:247
  128.5 12.5 %collective-permute-start.37 = (bf16[1344,128]{1,0:T(8,128)(2,1)S(1)}, bf16[1344,128]{1,0:T(8,128)(2,1)S(1)}, u32[]{:S(2)}, u32[]{:S(2)}) collective-permute-start(bf16[1344,128]{1,0:T(8,128)(2,1)S(1)} %pad_maximum_fusion.refs_1_), channel_id=1, source_target_pairs={{0,2},{2,0},{1,3},{3,1},{4,6},{6,4},{5,7},{7,5},{8,10},{10,8},{9,1... | collective-permute-start | bytes 1032200 | tf_op jit(solution)/shard_map/ppermute | solution.py:250
  132.7 6.1 %collective-permute-start.29 = (bf16[256,128]{1,0:T(8,128)(2,1)S(1)}, bf16[256,128]{1,0:T(8,128)(2,1)S(1)}, u32[]{:S(2)}, u32[]{:S(2)}) collective-permute-start(bf16[256,128]{1,0:T(8,128)(2,1)S(1)} %get-tuple-element.58), channel_id=1, source_target_pairs={{0,12},{4,8},{8,4},{12,0},{1,13},{5,9},{9,5},{13,1},{2,14},{6,10},... | collective-permute-start | bytes 196616 | tf_op jit(solution)/shard_map/ppermute | solution.py:247
  (47 other events, 352.1 us)

commit v2 on v1

v2 whole, which is shorter than its diff:
```python
import jax
import jax.numpy as jnp
from jax import lax
from jax.experimental import pallas as pl
from jax.experimental.pallas import tpu as pltpu
from jax.sharding import PartitionSpec as P

BF = jnp.bfloat16
F32 = jnp.float32
I32 = jnp.int32
LANES = 128
VMEM = pl.BlockSpec(memory_space=pltpu.VMEM)
SMEM = pl.BlockSpec(memory_space=pltpu.SMEM)
ANY = pl.BlockSpec(memory_space=pl.ANY)


def shape(dims, kind):
    return jax.ShapeDtypeStruct(tuple(dims), kind)


def run(kernel, outs, args, smem=(), scratch=(), copies=1, flops=0):
    counts = (len(smem), len(args), len(outs))

    def body(*refs):
        a, b, c = counts
        scalars, given, made = refs[:a], refs[a : a + b], refs[a + b : a + b + c]
        kernel(refs[-1], scalars, given, made, refs[a + b + c : -1])

    moved = sum(a.size * a.dtype.itemsize for a in list(args) + list(outs))
    return pl.pallas_call(
        body,
        out_shape=list(outs),
        in_specs=[SMEM] * len(smem) + [ANY] * len(args),
        out_specs=[VMEM] * len(outs),
        scratch_shapes=list(scratch) + [pltpu.SemaphoreType.DMA((copies,))],
        compiler_params=pltpu.CompilerParams(vmem_limit_bytes=32 * 1024 * 1024),
        cost_estimate=pl.CostEstimate(flops=flops, bytes_accessed=moved, transcendentals=0),
    )(*smem, *args)


def begin(sems, pairs, first=0):
    copies = [
        pltpu.make_async_copy(source, target, sems.at[first + i])
        for i, (source, target) in enumerate(pairs)
    ]
    for copy in copies:
        copy.start()
    return copies


def end(copies):
    for copy in copies:
        copy.wait()


def down(row):
    return jnp.transpose(jnp.broadcast_to(row, (LANES, LANES)))


def ones_at(where):
    return jnp.where(where, 1.0, 0.0).astype(BF)


def pick_rows(row, source):
    numbers = down(row)
    lane = lax.broadcasted_iota(I32, (LANES, LANES), 1)
    hot = jnp.concatenate(
        [ones_at(numbers == lane + k * LANES) for k in range(source.shape[0] // LANES)], axis=1
    )
    return jnp.dot(hot, source, preferred_element_type=F32).astype(BF)


def set_rows(row, values, base_ref, out_ref):
    events = values.shape[0]
    tall = 256
    wide = jnp.concatenate([values, jnp.ones((events, LANES), BF)], axis=1)
    for i in range(out_ref.shape[0] // tall):
        own = lax.broadcasted_iota(I32, (tall, events), 0) + i * tall
        hot = ones_at(own == jnp.broadcast_to(row, (tall, events)))
        found = jnp.dot(hot, wide, preferred_element_type=F32)
        span = slice(i * tall, (i + 1) * tall)
        out_ref[span, :] = jnp.where(found[:, LANES:] > 0.5, found[:, :LANES], base_ref[span, :])


def padded(cap):
    return -(-cap // LANES) * LANES


def ask_kernel(sems, smem, given, pieces, scratch):
    (ids, counts), (rows_any,), (rows_ref,) = smem, given, scratch
    end(begin(sems, [(rows_any, rows_ref)]))
    batches, _, cap = rows_ref.shape
    slot = lax.broadcasted_iota(I32, (1, cap), 1)
    for k, piece in enumerate(pieces):
        owner = ids[0] ^ k
        if piece.shape[1] != cap:
            piece[...] = jnp.full(piece.shape, -1, I32)
        for b in range(batches):
            row = rows_ref[b, pl.ds(owner, 1), :]
            piece[b : b + 1, :cap] = jnp.where(slot < counts[b, owner], row, -1)


def give(held, pieces):
    cap = pieces[0].shape[0]
    room = padded(cap)
    for k, piece in enumerate(pieces):
        piece[...] = held[k * room : k * room + cap, :]


def serve_kernel(sems, smem, given, made, scratch):
    *asked_pieces, memory_any = given
    asked_ref, narrow_ref, *pieces = made
    memory_ref, held = scratch
    nodes, room = len(asked_pieces), asked_pieces[0].shape[1]
    pairs = [(memory_any, memory_ref)]
    for k, piece in enumerate(asked_pieces):
        pairs.append((piece, asked_ref.at[:, k * room : (k + 1) * room]))
    end(begin(sems, pairs))
    narrow_ref[...] = memory_ref[...].astype(BF)
    for j in range(nodes * room // LANES):
        span = slice(j * LANES, (j + 1) * LANES)
        held[span, :] = pick_rows(asked_ref[0:1, span], narrow_ref[...])
    give(held, pieces)


def base_kernel(batch, sems, smem, given, made, scratch):
    (ids,) = smem
    asked_any, before_any, memory_any, handed_any = given
    base_ref, put_ref, rows_ref = made
    asked, before, handed, narrow = scratch
    begun = begin(
        sems,
        [(asked_any, asked), (before_any, before), (memory_any, base_ref), (handed_any, handed)],
    )
    end(begun)
    row = slice(batch, batch + 1)
    put_ref[...] = jnp.where(ids[1] == 0, asked[row, :], before[row, :])

    @pl.when(ids[1] != 0)
    def _():
        base_ref[...] = handed[...].astype(F32)

    narrow[...] = base_ref[...].astype(BF)
    for j in range(rows_ref.shape[0] // LANES):
        span = slice(j * LANES, (j + 1) * LANES)
        rows_ref[span, :] = pick_rows(asked[batch + 1 : batch + 2, span], narrow[...])


def gather_values(values, cap, pieces, sems, first):
    room = padded(cap)
    if room != cap:
        values[...] = jnp.zeros(values.shape, values.dtype)
    pairs = [(piece, values.at[k * room : k * room + cap, :]) for k, piece in enumerate(pieces)]
    return begin(sems, pairs, first)


def next_kernel(nodes, batch, sems, smem, given, made, scratch):
    (ids,) = smem
    asked_any, put_any, rows_any = given[:3]
    stayed, handed = given[3 : 3 + nodes], given[3 + nodes :]
    values_ref, pieces = made[0], made[1:]
    asked, put, rows, held = scratch
    cap = pieces[0].shape[0]
    begun = begin(sems, [(asked_any, asked), (put_any, put), (rows_any, rows)])

    @pl.when(ids[1] == 0)
    def _():
        end(gather_values(values_ref, cap, stayed, sems, 3))

    @pl.when(ids[1] != 0)
    def _():
        end(gather_values(values_ref, cap, handed, sems, 3))

    end(begun)
    events = values_ref.shape[0]
    wide = jnp.concatenate([values_ref[...], jnp.ones((events, LANES), BF)], axis=1)
    written = jnp.where(put[...] < 0, -2, put[...])
    for j in range(events // LANES):
        span = slice(j * LANES, (j + 1) * LANES)
        numbers = down(asked[batch + 1 : batch + 2, span])
        hot = jnp.concatenate(
            [
                ones_at(
                    numbers
                    == jnp.broadcast_to(written[:, i * LANES : (i + 1) * LANES], (LANES, LANES))
                )
                for i in range(events // LANES)
            ],
            axis=1,
        )
        found = jnp.dot(hot, wide, preferred_element_type=F32)
        kept = rows[span, :].astype(F32)
        held[span, :] = jnp.where(found[:, LANES:] > 0.5, found[:, :LANES], kept).astype(BF)
    give(held, pieces)


def update_kernel(sems, smem, given, made, scratch):
    put_any, values_any, base_any = given
    put, values, base = scratch
    end(begin(sems, [(put_any, put), (values_any, values), (base_any, base)]))
    set_rows(put[...], values[...], base, made[0])


def last_kernel(batch, sems, smem, given, made, scratch):
    asked_any, base_any, *pieces = given
    asked, values, base = scratch
    begun = begin(sems, [(asked_any, asked), (base_any, base)])
    end(gather_values(values, pieces[0].shape[0], pieces, sems, 2))
    end(begun)
    set_rows(asked[batch : batch + 1, :], values[...], base, made[0])


def batch_kernel(nodes, batch, forward, backward, prior, sems, smem, given, made, scratch):
    ids, counts = smem
    dst_any, time_any, edge_any, w_in_any, w_hid_any, bias_any = given[:6]
    own_pieces, other_pieces = given[6 : 6 + nodes], given[6 + nodes : 6 + 2 * nodes]
    rest = given[6 + 2 * nodes :]
    message, dst, w_in, w_hid, bias_ref, fresh = scratch[:6]
    cap = own_pieces[0].shape[0]
    events = nodes * cap
    z, f = ids[0], ids[2]
    mine = pl.multiple_of(f * LANES, LANES)
    other = pl.multiple_of((1 - f) * LANES, LANES)
    width = 2 * LANES
    long = message.shape[1]
    pairs = [(dst_any.at[batch], dst)]
    for k in range(nodes):
        at = pl.ds(pl.multiple_of((z ^ k) * cap, cap), cap)
        pairs.append((own_pieces[k], message.at[at, pl.ds(mine, LANES)]))
        pairs.append((other_pieces[k], message.at[at, pl.ds(other, LANES)]))
    rows_begun = begin(sems, pairs)
    pairs2 = [
        (w_in_any, w_in),
        (w_hid_any, w_hid),
        (bias_any, bias_ref),
        (time_any.at[batch], message.at[:, 2 * width : 2 * width + LANES]),
        (edge_any.at[batch], message.at[:, 2 * width + LANES :]),
    ]
    begun = begin(sems, pairs2, len(pairs))
    if backward:
        gates, up = scratch[6:8]
        last_pairs = [(rest[0].at[batch], up)]
        if prior:
            before = scratch[8]
            last_pairs.append((rest[1], before))
        last_begun = begin(sems, last_pairs, len(pairs) + len(pairs2))
    end(rows_begun)
    full = message[:, :width]
    for j in range(events // LANES):
        span = slice(j * LANES, (j + 1) * LANES)
        message[span, width : 2 * width] = pick_rows(dst[:, span], full)
    end(begun)
    w_in01 = jnp.concatenate([w_in[0], w_in[1]], axis=1)
    w_hid01 = jnp.concatenate([w_hid[0], w_hid[1]], axis=1)
    sums = [jnp.zeros((1, LANES), F32) for _ in range(4)]
    if backward:
        end(last_begun)
    tall = 256
    for i in range(events // tall):
        span = slice(i * tall, (i + 1) * tall)
        rows = message[span, :]
        hidden = rows[:, :width]
        both = jnp.dot(rows, w_in01, preferred_element_type=F32) + jnp.dot(
            hidden, w_hid01, preferred_element_type=F32
        )
        own = message[span, pl.ds(mine, LANES)].astype(F32)
        reset_gate = jax.nn.sigmoid(both[:, :LANES] + bias_ref[0:1, :])
        update = jax.nn.sigmoid(both[:, LANES:] + bias_ref[1:2, :])
        recur_term = jnp.dot(hidden, w_hid[2], preferred_element_type=F32) + bias_ref[3:4, :]
        candid = jnp.tanh(
            jnp.dot(rows, w_in[2], preferred_element_type=F32)
            + bias_ref[2:3, :]
            + reset_gate * recur_term
        )
        if forward:
            fresh[span, :] = ((1.0 - update) * candid + update * own).astype(BF)
        if backward:
            number = lax.broadcasted_iota(I32, (tall, LANES), 0) + i * tall
            live = number < 0
            for o in range(nodes):
                if o * cap < (i + 1) * tall and (o + 1) * cap > i * tall:
                    live = live | (
                        (number >= o * cap) & (number < o * cap + counts[batch, o])
                    )
            cotangent = jnp.where(live, up[span, :].astype(F32), 0.0)
            grad_cand = cotangent * (1.0 - update) * (1.0 - candid * candid)
            grad_upd = cotangent * (own - candid) * update * (1.0 - update)
            grad_reset = grad_cand * recur_term * reset_gate * (1.0 - reset_gate)
            grad_recur = grad_cand * reset_gate
            for g, part in enumerate((grad_reset, grad_upd, grad_cand, grad_recur)):
                sums[g] = sums[g] + jnp.sum(part, axis=0, keepdims=True)
                gates[span, g * LANES : (g + 1) * LANES] = part.astype(BF)
    if forward:
        for k in range(nodes):
            made[k][...] = fresh[pl.ds(pl.multiple_of((z ^ k) * cap, cap), cap), :]
    if not backward:
        return
    out_ref = made[-1]

    def put(start, value):
        stop = start + value.shape[0]
        if prior:
            value = value + before[start:stop, :]
        out_ref[start:stop, :] = value.astype(out_ref.dtype)

    for i in range(long // tall):
        rows = message[:, i * tall : (i + 1) * tall]
        columns = gates[...] if i * tall < width else gates[:, : 3 * LANES]
        product = lax.dot_general(
            rows, columns, (((0,), (0,)), ((), ())), preferred_element_type=F32
        )
        for g in range(3):
            put(g * long + i * tall, product[:, g * LANES : (g + 1) * LANES])
        if i * tall < width:
            put(3 * long + i * tall, product[:, 3 * LANES :])
    top = 3 * long + width
    pad = out_ref.shape[0] - top
    tail = jnp.concatenate(sums + [jnp.zeros((pad - 4, LANES), F32)], axis=0)
    put(top, tail)


def middle_kernel(segs, sems, smem, given, made, scratch):
    (ids,) = smem
    totals, got = given[0], given[1:segs]
    rows = scratch[:segs]
    whole = scratch[segs]
    nodes, chunk = len(made), made[0].shape[0]
    share = nodes * chunk
    at = pl.ds(pl.multiple_of(ids[1] * share, share), share)
    pairs = [(totals.at[at, :], rows[0])] + list(zip(got, rows[1:]))
    end(begin(sems, pairs))
    total = rows[0][...].astype(F32)
    for x in range(1, segs):
        total = total + rows[x][...].astype(F32)
    whole[...] = total.astype(BF)
    for k in range(nodes):
        made[k][...] = whole[pl.ds(pl.multiple_of((ids[0] ^ k) * chunk, chunk), chunk), :]


def unpack_kernel(nodes, segs, long, sems, smem, pieces, made, scratch):
    (ids,) = smem
    grad_in, grad_hid, grad_bias = made
    (held,) = scratch
    chunk = pieces[0].shape[0] // nodes
    z, s = ids[0], ids[1]
    pairs = []
    for x in range(segs):
        for k in range(nodes):
            at = pl.multiple_of(((s ^ x) * nodes + (z ^ k)) * chunk, chunk)
            pairs.append((pieces[x].at[k * chunk : (k + 1) * chunk, :], held.at[pl.ds(at, chunk), :]))
    end(begin(sems, pairs))
    width = grad_hid.shape[1]
    for g in range(3):
        grad_in[g] = held[g * long : (g + 1) * long, :].astype(F32)
    for g in range(2):
        grad_hid[g] = held[g * long : g * long + width, :].astype(F32)
    grad_hid[2] = held[3 * long : 3 * long + width, :].astype(F32)
    top = 3 * long + width
    grad_bias[...] = held[top : top + 16, :].astype(F32)[:4, :]


def local(
    memory, req_rows, req_count, dst_slot, elapsed, edges, upstream, freq, phase, w_input, w_hidden, bias
):
    nodes, segs = lax.axis_size("node"), lax.axis_size("seg")
    z, s, f = lax.axis_index("node"), lax.axis_index("seg"), lax.axis_index("feat")
    ids = jnp.stack([z, s, f]).astype(I32)
    memory_now = memory[0]
    node_rows, half = memory_now.shape
    batches, cap = req_rows.shape[0], req_rows.shape[-1]
    events = nodes * cap
    room = padded(cap)
    spread = nodes * room
    counts = req_count[:, 0, 0]
    piece = shape((cap, half), BF)
    long, width = w_input.shape[1], w_hidden.shape[1]

    def node_swap(block, k):
        return lax.ppermute(block, "node", [(i, i ^ k) for i in range(nodes)])

    def seg_swap(block, x):
        return lax.ppermute(block, "seg", [(i, i ^ x) for i in range(segs)])

    def seg_next(block):
        return lax.ppermute(block, "seg", [(i, i + 1) for i in range(segs - 1)])

    def feat_swap(block):
        return lax.ppermute(block, "feat", [(0, 1), (1, 0)])

    def to_next(block, k):
        route = [
            (i * segs + j, (i ^ k) * segs + j + 1) for i in range(nodes) for j in range(segs - 1)
        ]
        return lax.ppermute(block, ("node", "seg"), route)

    def to_first(block, k):
        route = [(i * segs, (i ^ k) * segs) for i in range(nodes)]
        return lax.ppermute(block, ("node", "seg"), route)

    def exchange(blocks):
        return [blocks[0]] + [node_swap(blocks[k], k) for k in range(1, nodes)]

    wanted = run(
        ask_kernel,
        [shape((batches, room), I32)] * nodes,
        [req_rows[:, 0, 0]],
        [ids, counts],
        [pltpu.VMEM((batches, nodes, cap), I32)],
    )
    wide_rows = pltpu.VMEM((spread, half), BF)
    asked, narrow, *served = run(
        serve_kernel,
        [shape((batches, spread), I32), shape((node_rows, half), BF)] + [piece] * nodes,
        exchange(wanted) + [memory_now],
        [],
        [pltpu.VMEM((node_rows, half), F32), wide_rows],
        nodes + 1,
    )
    asked_before = seg_next(asked)

    edge_other = feat_swap(edges[:, 0])
    edge_full = jnp.where(
        f == 0,
        jnp.concatenate([edges[:, 0], edge_other], axis=-1),
        jnp.concatenate([edge_other, edges[:, 0]], axis=-1),
    )
    time_code = jnp.cos(
        elapsed[:, 0].astype(F32)[:, :, None] * freq[None, None, :] + phase[None, None, :]
    ).astype(BF)

    chunk = -(-(3 * long + width + 16) // (16 * nodes * segs)) * 16
    total_rows = chunk * nodes * segs
    numbers = pltpu.VMEM((batches, spread), I32)
    line = pltpu.VMEM((1, spread), I32)
    block = pltpu.VMEM((node_rows, half), F32)
    totals = None
    for b in range(batches):
        final = b + 1 == batches
        own_pieces = exchange(served)
        if not final:
            handed_memory = seg_next(narrow)
        other_pieces = [feat_swap(p) for p in own_pieces]
        given = [dst_slot, time_code, edge_full, w_input, w_hidden, bias]
        given = given + own_pieces + other_pieces
        rooms = [
            pltpu.VMEM((events, long), BF),
            pltpu.VMEM((1, events), I32),
            pltpu.VMEM(w_input.shape, BF),
            pltpu.VMEM(w_hidden.shape, BF),
            pltpu.VMEM(bias.shape, F32),
            pltpu.VMEM((events, half), BF),
        ]
        more = [pltpu.VMEM((events, 4 * half), BF), pltpu.VMEM((events, half), BF)]
        if totals is not None:
            more.append(pltpu.VMEM((total_rows, half), F32))
        copies = 8 + 2 * nodes
        prior = [] if totals is None else [totals]
        if not final:
            fresh = run(
                lambda *a, b=b: batch_kernel(nodes, b, True, False, False, *a),
                [piece] * nodes,
                given,
                [ids, counts],
                rooms,
                copies,
            )
            handed = [to_next(fresh[k], k) for k in range(nodes)]
            stayed = [fresh[0]] + [to_first(fresh[k], k) for k in range(1, nodes)]
            base, put, rows = run(
                lambda *a, b=b: base_kernel(b, *a),
                [shape((node_rows, half), F32), shape((1, spread), I32), shape((spread, half), BF)],
                [asked, asked_before, memory_now, handed_memory],
                [ids],
                [numbers, numbers, pltpu.VMEM((node_rows, half), BF)] + [pltpu.VMEM((node_rows, half), BF)],
                4,
            )
            values, *served = run(
                lambda *a, b=b: next_kernel(nodes, b, *a),
                [shape((spread, half), BF)] + [piece] * nodes,
                [asked, put, rows] + stayed + handed,
                [ids],
                [numbers, line, wide_rows, wide_rows],
                3 + nodes,
            )
            memory_now = run(
                update_kernel,
                [shape((node_rows, half), F32)],
                [put, values, base],
                [],
                [line, wide_rows, block],
                3,
            )[0]
            narrow = memory_now.astype(BF)
            totals = run(
                lambda *a, b=b, p=prior: batch_kernel(nodes, b, False, True, len(p) > 0, *a),
                [shape((total_rows, half), F32)],
                given + [upstream[:, 0]] + prior + [handed[0]],
                [ids, counts],
                rooms + more,
                copies,
            )[0]
        else:
            *fresh, totals = run(
                lambda *a, b=b, p=prior: batch_kernel(nodes, b, True, True, len(p) > 0, *a),
                [piece] * nodes + [shape((total_rows, half), BF)],
                given + [upstream[:, 0]] + prior,
                [ids, counts],
                rooms + more,
                copies,
            )
            returned = exchange(fresh)
            memory_out = run(
                lambda *a, b=b: last_kernel(b, *a),
                [shape((node_rows, half), F32)],
                [asked, memory_now] + returned,
                [],
                [numbers, wide_rows, block],
                2 + nodes,
            )[0]

    def at(blocks, i):
        return lax.dynamic_index_in_dim(blocks, i, 0, keepdims=False)

    blocks = totals.reshape(segs, nodes * chunk, half)
    got = [seg_swap(at(blocks, s ^ x), x) for x in range(1, segs)]
    share = pltpu.VMEM((nodes * chunk, half), BF)
    parts = run(
        lambda *a: middle_kernel(segs, *a),
        [shape((chunk, half), BF)] * nodes,
        [totals] + got + returned[1:],
        [ids],
        [share] * (segs + 1),
        segs,
    )
    got = [node_swap(parts[k], k) for k in range(1, nodes)]
    summed = sum((g.astype(F32) for g in got), parts[0].astype(F32)).astype(BF)
    gathered = jnp.concatenate([summed] + [node_swap(summed, k) for k in range(1, nodes)], axis=0)
    gathered = [gathered] + [seg_swap(gathered, x) for x in range(1, segs)]
    grads = run(
        lambda *a: unpack_kernel(nodes, segs, long, *a),
        [shape(w_input.shape, F32), shape(w_hidden.shape, F32), shape(bias.shape, F32)],
        gathered,
        [ids],
        [pltpu.VMEM((total_rows, half), BF)],
        nodes * segs,
    )
    return (memory_out[None], *grads)


def solution(mesh):
    in_specs = (
        P(("parts", "seg"), "node", "feat"),
        P(None, ("parts", "seg"), "node", None, None),
        P(None, ("parts", "seg"), "node", None),
        P(None, ("parts", "seg"), "node"),
        P(None, ("parts", "seg"), "node"),
        P(None, ("parts", "seg"), "node", "feat"),
        P(None, ("parts", "seg"), "node", "feat"),
        P(),
        P(),
        P(None, None, "feat"),
        P(None, None, "feat"),
        P(None, "feat"),
    )
    out_specs = (
        P(("parts", "seg"), "node", "feat"),
        P("parts", None, "feat"),
        P("parts", None, "feat"),
        P("parts", "feat"),
    )
    return jax.shard_map(local, mesh=mesh, in_specs=in_specs, out_specs=out_specs, check_vma=False)
```

time: 144 us -> 135 us (0.938)
  waiting for transfers between devices: 41.6 us -> 30.6 us
  Pallas kernels: 19.9 us -> 27.2 us
  other arithmetic: 7.94 us -> 6.12 us
  local copies, waits for them, and re-layouts: 17.4 us -> 15.7 us
  starting transfers between devices: 54.8 us -> 53.1 us
    pallas_call x9 -> x11, Pallas kernels: 19.9 us -> 27.2 us  [run(): pl.pallas_call(body, out_shape=list(outs), in_specs=[SMEM] * len(smem) +...]
    ppermute x2, waiting for transfers between devices: 5.42 us -> 0.01 us  [seg_next(): return lax.ppermute(block, 'seg', [(i, i + 1) for i in range(segs - 1)])]
    ppermute x2, starting transfers between devices: 4.77 us -> 1.25 us  [seg_swap(): return lax.ppermute(block, 'seg', [(i, i ^ x) for i in range(segs)])]
    ppermute x2, waiting for transfers between devices: 8.73 us -> 5.37 us  [seg_swap(): return lax.ppermute(block, 'seg', [(i, i ^ x) for i in range(segs)])]
    ppermute x4, starting transfers between devices: 5.16 us -> 8.12 us  [to_next(): return lax.ppermute(block, ('node', 'seg'), route)]
    convert_element_type x3 -> x1, other arithmetic: 2.29 us -> 0.05 us  [local(): summed = sum((g.astype(F32) for g in got), parts[0].astype(F32)).astype(BF)]
    squeeze x4 -> x0, local copies, waits for them, and re-layouts: 2.11 us -> none  [the longest x1 0.75 us: local(): edge_full[b]]
    ppermute x4, waiting for transfers between devices: 1.87 us -> 0.01 us  [to_next(): return lax.ppermute(block, ('node', 'seg'), route)]
  transfers between devices with their start and end apart: 38 -> 38, of which waited for: 15 -> 15; matrix products, arithmetic and copies ran while one was open for 8% -> 5% of each run, Pallas kernels for 6% -> 10%
where the time goes in v2:
time: 135 us; the launch traced here: 134 us
  starting transfers between devices  53.1 us (39%)
  waiting for transfers between devices  30.6 us (23%)
  Pallas kernels  27.2 us (20%)
  local copies, waits for them, and re-layouts  15.7 us (12%)
  other arithmetic  6.12 us (5%)
  between operations  1.52 us (1%)
    ppermute x18, starting transfers between devices, node_swap(): return lax.ppermute(block, 'node', [(i, i ^ k) for i in range(nodes)])  27.9 us
    pallas_call x11, Pallas kernels, run(): pl.pallas_call(body, out_shape=list(outs), in_specs=[SMEM] * len(smem) +...  27.2 us
    ppermute x18, waiting for transfers between devices, node_swap(): return lax.ppermute(block, 'node', [(i, i ^ k) for i in range(nodes)])  24.4 us
    unnamed x80, local copies, waits for them, and re-layouts  15.6 us
    ppermute x3, starting transfers between devices, to_first(): return lax.ppermute(block, ('node', 'seg'), route)  9.78 us
    ppermute x4, starting transfers between devices, to_next(): return lax.ppermute(block, ('node', 'seg'), route)  8.12 us
    ppermute x2, waiting for transfers between devices, seg_swap(): return lax.ppermute(block, 'seg', [(i, i ^ x) for i in range(segs)])  5.37 us
    ppermute x2, starting transfers between devices, seg_next(): return lax.ppermute(block, 'seg', [(i, i + 1) for i in range(segs - 1)])  4.85 us
  transfers between devices with their start and end apart: 38, of which 15 were waited for; matrix products, arithmetic and copies ran while one was open for 5% of the time, Pallas kernels for 10%

profile of v2, /device:TPU:0, one launch (start us, length us, event | category | flops | bytes accessed | tf_op | source)
XLA Modules:
  0.0 134.2 jit_solution(2708188779953044350)
XLA Ops:
  2.7 3.1 %collective-permute-start = (s32[2,256]{1,0:T(2,128)S(1)}, s32[2,256]{1,0:T(2,128)S(1)}, u32[]{:S(2)}, u32[]{:S(2)}) collective-permute-start(s32[2,256]{1,0:T(2,128)S(1)} %get-tuple-element.39), channel_id=1, source_target_pairs={{0,4},{4,0},{8,12},{12,8},{1,5},{5,1},{9,13},{13,9},{2,6},{6,2},{1... | collective-permute-start | bytes 6152 | tf_op jit(solution)/shard_map/ppermute | solution.py:379
  5.8 2.6 %collective-permute-start.1 = (s32[2,256]{1,0:T(2,128)S(1)}, s32[2,256]{1,0:T(2,128)S(1)}, u32[]{:S(2)}, u32[]{:S(2)}) collective-permute-start(s32[2,256]{1,0:T(2,128)S(1)} %get-tuple-element.40), channel_id=1, source_target_pairs={{0,8},{4,12},{8,0},{12,4},{1,9},{5,13},{9,1},{13,5},{2,10},{6,14},... | collective-permute-start | bytes 6152 | tf_op jit(solution)/shard_map/ppermute | solution.py:379
  10.3 3.5 %collective-permute-done.2.refs_3_ = s32[2,256]{1,0:T(2,128)S(1)} collective-permute-done((s32[2,256]{1,0:T(2,128)S(1)}, s32[2,256]{1,0:T(2,128)S(1)}, u32[]{:S(2)}, u32[]{:S(2)}) %collective-permute-start.2) | collective-permute-done | bytes 2080 | tf_op jit(solution)/shard_map/ppermute | solution.py:379
  16.7 3.6 %collective-permute-start.4 = (bf16[2048,128]{1,0:T(8,128)(2,1)S(1)}, bf16[2048,128]{1,0:T(8,128)(2,1)S(1)}, u32[]{:S(2)}, u32[]{:S(2)}) collective-permute-start(bf16[2048,128]{1,0:T(8,128)(2,1)S(1)} %get-tuple-element.43), channel_id=1, source_target_pairs={{0,2},{1,3},{4,6},{5,7},{8,10},{9,11},{12,14},{13,15},{16,18},{17,... | collective-permute-start | bytes 1572872 | tf_op jit(solution)/shard_map/ppermute | solution.py:385
  22.5 3.6 %collective-permute-start.8 = (bf16[256,128]{1,0:T(8,128)(2,1)S(1)}, bf16[256,128]{1,0:T(8,128)(2,1)S(1)}, u32[]{:S(2)}, u32[]{:S(2)}) collective-permute-start(bf16[256,128]{1,0:T(8,128)(2,1)S(1)} %get-tuple-element.49), channel_id=1, source_target_pairs={{0,12},{4,8},{8,4},{12,0},{1,13},{5,9},{9,5},{13,1},{2,14},{6,10},... | collective-permute-start | bytes 196616 | tf_op jit(solution)/shard_map/ppermute | solution.py:379
  26.1 3.7 %cosine_convert_fusion.refs_3_ = bf16[2,1024,128]{2,1,0:T(8,128)(2,1)S(1)} fusion(f32[128]{0:T(128)S(1)} %copy-done.37, f32[128]{0:T(128)S(1)} %copy-done.38, f32[2,1024]{1,0:T(2,128)S(1)} %bitcast.28), kind=kLoop, calls=%fused_computation | loop fusion | flops 786432 | bytes 533504 | tf_op jit(solution)/shard_map/convert_element_type | solution.py:429
  33.4 3.4 %shard_map.150 = (bf16[256,128]{1,0:T(8,128)(2,1)S(1)}, bf16[256,128]{1,0:T(8,128)(2,1)S(1)}, bf16[256,128]{1,0:T(8,128)(2,1)S(1)}, bf16[256,128]{1,0:T(8,128)(2,1)S(1)}) custom-call(s32[3]{0:T(128)S(1)} %pad_add_fusion.refs_0_, s32[2,4]{1,0:T(2,128)S(1)} %bitcast.21, s32[2,1,1024]{2,1,0:T(1,128)S(1)} %copy-done.23, ...), custom_call_target="tpu_custom_call" | custom-call | bytes 2631680 | tf_op jit(solution)/shard_map/pallas_call | solution.py:30
  41.7 2.5 %collective-permute-start.13 = (bf16[256,128]{1,0:T(8,128)(2,1)S(1)}, bf16[256,128]{1,0:T(8,128)(2,1)S(1)}, u32[]{:S(2)}, u32[]{:S(2)}) collective-permute-start(bf16[256,128]{1,0:T(8,128)(2,1)S(1)} %get-tuple-element.51), channel_id=1, source_target_pairs={{0,4},{4,0},{8,12},{12,8},{1,5},{5,1},{9,13},{13,9},{16,20},{20,16... | collective-permute-start | bytes 196616 | tf_op jit(solution)/shard_map/ppermute | solution.py:398
  44.2 3.2 %collective-permute-start.18 = (bf16[256,128]{1,0:T(8,128)(2,1)S(1)}, bf16[256,128]{1,0:T(8,128)(2,1)S(1)}, u32[]{:S(2)}, u32[]{:S(2)}) collective-permute-start(bf16[256,128]{1,0:T(8,128)(2,1)S(1)} %get-tuple-element.52), channel_id=1, source_target_pairs={{0,10},{4,14},{8,2},{12,6},{1,11},{5,15},{9,3},{13,7},{16,26},{20,... | collective-permute-start | bytes 196616 | tf_op jit(solution)/shard_map/ppermute | solution.py:394
  47.5 4.0 %collective-permute-start.14 = (bf16[256,128]{1,0:T(8,128)(2,1)S(1)}, bf16[256,128]{1,0:T(8,128)(2,1)S(1)}, u32[]{:S(2)}, u32[]{:S(2)}) collective-permute-start(bf16[256,128]{1,0:T(8,128)(2,1)S(1)} %get-tuple-element.52), channel_id=1, source_target_pairs={{0,8},{4,12},{8,0},{12,4},{1,9},{5,13},{9,1},{13,5},{16,24},{20,28... | collective-permute-start | bytes 196616 | tf_op jit(solution)/shard_map/ppermute | solution.py:398
  53.7 3.2 %collective-permute-start.15 = (bf16[256,128]{1,0:T(8,128)(2,1)S(1)}, bf16[256,128]{1,0:T(8,128)(2,1)S(1)}, u32[]{:S(2)}, u32[]{:S(2)}) collective-permute-start(bf16[256,128]{1,0:T(8,128)(2,1)S(1)} %get-tuple-element.53), channel_id=1, source_target_pairs={{0,12},{4,8},{8,4},{12,0},{1,13},{5,9},{9,5},{13,1},{16,28},{20,24... | collective-permute-start | bytes 196616 | tf_op jit(solution)/shard_map/ppermute | solution.py:398
  61.6 2.5 %shard_map.151 = (bf16[1024,128]{1,0:T(8,128)(2,1)S(1)}, bf16[256,128]{1,0:T(8,128)(2,1)}, bf16[256,128]{1,0:T(8,128)(2,1)S(1)}, bf16[256,128]{1,0:T(8,128)(2,1)S(1)}, bf16[256,128]{1,0:T(8,128)(2,1)S(1)}) custom-call(s32[3]{0:T(128)S(1)} %copy-done.25, s32[2,1024]{1,0:T(2,128)S(1)} %get-tuple-element.42.refs_1_.refs_0_, ...), custom_call_target="tpu_custom_call" | custom-call | bytes 1323008 | tf_op jit(solution)/shard_map/pallas_call | solution.py:30
  71.4 2.5 %collective-permute-done.22.refs_11_ = bf16[256,128]{1,0:T(8,128)(2,1)} collective-permute-done((bf16[256,128]{1,0:T(8,128)(2,1)S(1)}, bf16[256,128]{1,0:T(8,128)(2,1)}, u32[]{:S(2)}, u32[]{:S(2)}) %collective-permute-start.22) | collective-permute-done | bytes 65568 | tf_op jit(solution)/shard_map/ppermute | solution.py:379
  81.8 4.3 %shard_map.153.refs_17_ = f32[2688,128]{1,0:T(8,128)S(1)} custom-call(s32[3]{0:T(128)S(1)} %copy-done.26, s32[2,4]{1,0:T(2,128)S(1)} %bitcast.22, s32[2,1,1024]{2,1,0:T(1,128)S(1)} %copy-done.23, bf16[2,1024,128]{2,1,0:T(8,128)(2,1)S(1)} %cosine_convert_fusion.refs_3_, bf16[2,1024,128]{2,1,0:T(8,128)(2,1)S(1)} %maximum_select_fusion.refs_4_, ...), custom_call_target="tpu_custom_call" | custom-call | bytes 4335616 | tf_op jit(solution)/shard_map/pallas_call | solution.py:30
  86.2 5.0 %shard_map.154 = (bf16[256,128]{1,0:T(8,128)(2,1)S(1)}, bf16[256,128]{1,0:T(8,128)(2,1)S(1)}, bf16[256,128]{1,0:T(8,128)(2,1)S(1)}, bf16[256,128]{1,0:T(8,128)(2,1)S(1)}, bf16[2688,128]{1,0:T(8,128)(2,1)S(1)}) custom-call(s32[3]{0:T(128)S(1)} %copy-done.26, s32[2,4]{1,0:T(2,128)S(1)} %bitcast.23, s32[2,1,1024]{2,1,0:T(1,128)S(1)} %copy-done.23, ...), custom_call_target="tpu_custom_call" | custom-call | bytes 5220352 | tf_op jit(solution)/shard_map/pallas_call | solution.py:30
  91.3 2.7 %collective-permute-start.28 = (bf16[256,128]{1,0:T(8,128)(2,1)S(1)}, bf16[256,128]{1,0:T(8,128)(2,1)S(1)}, u32[]{:S(2)}, u32[]{:S(2)}) collective-permute-start(bf16[256,128]{1,0:T(8,128)(2,1)S(1)} %get-tuple-element.62), channel_id=1, source_target_pairs={{0,8},{4,12},{8,0},{12,4},{1,9},{5,13},{9,1},{13,5},{2,10},{6,14},... | collective-permute-start | bytes 196616 | tf_op jit(solution)/shard_map/ppermute | solution.py:379
  96.9 2.4 %collective-permute-done.28.refs_4_ = bf16[256,128]{1,0:T(8,128)(2,1)S(1)} collective-permute-done((bf16[256,128]{1,0:T(8,128)(2,1)S(1)}, bf16[256,128]{1,0:T(8,128)(2,1)S(1)}, u32[]{:S(2)}, u32[]{:S(2)}) %collective-permute-start.28) | collective-permute-done | bytes 65568 | tf_op jit(solution)/shard_map/ppermute | solution.py:379
  102.8 2.7 %collective-permute-start.32 = (bf16[336,128]{1,0:T(8,128)(2,1)S(1)}, bf16[336,128]{1,0:T(8,128)(2,1)S(1)}, u32[]{:S(2)}, u32[]{:S(2)}) collective-permute-start(bf16[336,128]{1,0:T(8,128)(2,1)S(1)} %get-tuple-element.67), channel_id=1, source_target_pairs={{0,8},{4,12},{8,0},{12,4},{1,9},{5,13},{9,1},{13,5},{2,10},{6,14},... | collective-permute-start | bytes 258056 | tf_op jit(solution)/shard_map/ppermute | solution.py:379
  108.0 4.6 %collective-permute-done.32 = bf16[336,128]{1,0:T(8,128)(2,1)S(1)} collective-permute-done((bf16[336,128]{1,0:T(8,128)(2,1)S(1)}, bf16[336,128]{1,0:T(8,128)(2,1)S(1)}, u32[]{:S(2)}, u32[]{:S(2)}) %collective-permute-start.32) | collective-permute-done | bytes 86048 | tf_op jit(solution)/shard_map/ppermute | solution.py:379
  117.1 2.4 %collective-permute-done.36 = bf16[336,128]{1,0:T(8,128)(2,1)S(1)} collective-permute-done((bf16[336,128]{1,0:T(8,128)(2,1)S(1)}, bf16[336,128]{1,0:T(8,128)(2,1)S(1)}, u32[]{:S(2)}, u32[]{:S(2)}) %collective-permute-start.36) | collective-permute-done | bytes 86048 | tf_op jit(solution)/shard_map/ppermute | solution.py:379
  119.5 2.7 %collective-permute-done.35 = bf16[336,128]{1,0:T(8,128)(2,1)S(1)} collective-permute-done((bf16[336,128]{1,0:T(8,128)(2,1)S(1)}, bf16[336,128]{1,0:T(8,128)(2,1)S(1)}, u32[]{:S(2)}, u32[]{:S(2)}) %collective-permute-start.35) | collective-permute-done | bytes 86048 | tf_op jit(solution)/shard_map/ppermute | solution.py:379
  124.8 2.7 %shard_map.155 = f32[2048,128]{1,0:T(8,128)} custom-call(s32[2,1024]{1,0:T(2,128)S(1)} %get-tuple-element.42.refs_1_.refs_0_, f32[2048,128]{1,0:T(8,128)S(1)} %shard_map.152.refs_1_, bf16[256,128]{1,0:T(8,128)(2,1)S(1)} %get-tuple-element.60.refs_2_, bf16[256,128]{1,0:T(8,128)(2,1)S(1)} %collective-permute-done.27.refs_3_, ...), custom_call_target="tpu_custom_call" | custom-call | bytes 2367488 | tf_op jit(solution)/shard_map/pallas_call | solution.py:30
  127.5 3.8 %collective-permute-done.37.refs_2_ = bf16[1344,128]{1,0:T(8,128)(2,1)S(1)} collective-permute-done((bf16[1344,128]{1,0:T(8,128)(2,1)S(1)}, bf16[1344,128]{1,0:T(8,128)(2,1)S(1)}, u32[]{:S(2)}, u32[]{:S(2)}) %collective-permute-start.37) | collective-permute-done | bytes 344096 | tf_op jit(solution)/shard_map/ppermute | solution.py:382
  131.3 2.7 %shard_map.157 = (f32[3,768,128]{2,1,0:T(8,128)}, f32[3,256,128]{2,1,0:T(8,128)}, f32[4,128]{1,0:T(4,128)}) custom-call(s32[3]{0:T(128)S(1)} %copy-done.26, bf16[1344,128]{1,0:T(8,128)(2,1)S(1)} %pad_maximum_fusion.refs_1_, bf16[1344,128]{1,0:T(8,128)(2,1)S(1)} %collective-permute-done.37.refs_2_), custom_call_target="tpu_custom_call" | custom-call | bytes 2263040 | tf_op jit(solution)/shard_map/pallas_call | solution.py:30
  (150 shorter events, 55.3 us)
Async XLA Ops:
  16.7 36.2 %collective-permute-start.4 = (bf16[2048,128]{1,0:T(8,128)(2,1)S(1)}, bf16[2048,128]{1,0:T(8,128)(2,1)S(1)}, u32[]{:S(2)}, u32[]{:S(2)}) collective-permute-start(bf16[2048,128]{1,0:T(8,128)(2,1)S(1)} %get-tuple-element.43), channel_id=1, source_target_pairs={{0,2},{1,3},{4,6},{5,7},{8,10},{9,11},{12,14},{13,15},{16,18},{17,... | collective-permute-start | bytes 1572872 | tf_op jit(solution)/shard_map/ppermute | solution.py:385
  21.5 9.4 %collective-permute-start.5 = (bf16[2,1024,64]{2,1,0:T(8,128)(2,1)S(1)}, bf16[2,1024,64]{2,1,0:T(8,128)(2,1)}, u32[]{:S(2)}, u32[]{:S(2)}) collective-permute-start(bf16[2,1024,64]{2,1,0:T(8,128)(2,1)S(1)} %bitcast.25), channel_id=1, source_target_pairs={{0,1},{1,0},{2,3},{3,2},{4,5},{5,4},{6,7},{7,6},{8,9},{9,8},{10,11... | collective-permute-start | bytes 786440 | tf_op jit(solution)/shard_map/ppermute | solution.py:388
  21.6 8.2 %collective-permute-start.6 = (bf16[256,128]{1,0:T(8,128)(2,1)S(1)}, bf16[256,128]{1,0:T(8,128)(2,1)S(1)}, u32[]{:S(2)}, u32[]{:S(2)}) collective-permute-start(bf16[256,128]{1,0:T(8,128)(2,1)S(1)} %get-tuple-element.47), channel_id=1, source_target_pairs={{0,4},{4,0},{8,12},{12,8},{1,5},{5,1},{9,13},{13,9},{2,6},{6,2},{1... | collective-permute-start | bytes 196616 | tf_op jit(solution)/shard_map/ppermute | solution.py:379
  21.7 8.7 %collective-permute-start.7 = (bf16[256,128]{1,0:T(8,128)(2,1)S(1)}, bf16[256,128]{1,0:T(8,128)(2,1)S(1)}, u32[]{:S(2)}, u32[]{:S(2)}) collective-permute-start(bf16[256,128]{1,0:T(8,128)(2,1)S(1)} %get-tuple-element.48), channel_id=1, source_target_pairs={{0,8},{4,12},{8,0},{12,4},{1,9},{5,13},{9,1},{13,5},{2,10},{6,14},... | collective-permute-start | bytes 196616 | tf_op jit(solution)/shard_map/ppermute | solution.py:379
  22.5 8.0 %collective-permute-start.8 = (bf16[256,128]{1,0:T(8,128)(2,1)S(1)}, bf16[256,128]{1,0:T(8,128)(2,1)S(1)}, u32[]{:S(2)}, u32[]{:S(2)}) collective-permute-start(bf16[256,128]{1,0:T(8,128)(2,1)S(1)} %get-tuple-element.49), channel_id=1, source_target_pairs={{0,12},{4,8},{8,4},{12,0},{1,13},{5,9},{9,5},{13,1},{2,14},{6,10},... | collective-permute-start | bytes 196616 | tf_op jit(solution)/shard_map/ppermute | solution.py:379
  36.8 10.7 %collective-permute-start.16 = (bf16[256,128]{1,0:T(8,128)(2,1)S(1)}, bf16[256,128]{1,0:T(8,128)(2,1)S(1)}, u32[]{:S(2)}, u32[]{:S(2)}) collective-permute-start(bf16[256,128]{1,0:T(8,128)(2,1)S(1)} %get-tuple-element.50.refs_4_), channel_id=1, source_target_pairs={{0,2},{4,6},{8,10},{12,14},{1,3},{5,7},{9,11},{13,15},{16,18},{20,... | collective-permute-start | bytes 196616 | tf_op jit(solution)/shard_map/ppermute | solution.py:394
  38.2 13.3 %collective-permute-start.17 = (bf16[256,128]{1,0:T(8,128)(2,1)S(1)}, bf16[256,128]{1,0:T(8,128)(2,1)S(1)}, u32[]{:S(2)}, u32[]{:S(2)}) collective-permute-start(bf16[256,128]{1,0:T(8,128)(2,1)S(1)} %get-tuple-element.51), channel_id=1, source_target_pairs={{0,6},{4,2},{8,14},{12,10},{1,7},{5,3},{9,15},{13,11},{16,22},{20,... | collective-permute-start | bytes 196616 | tf_op jit(solution)/shard_map/ppermute | solution.py:394
  41.7 19.1 %collective-permute-start.13 = (bf16[256,128]{1,0:T(8,128)(2,1)S(1)}, bf16[256,128]{1,0:T(8,128)(2,1)S(1)}, u32[]{:S(2)}, u32[]{:S(2)}) collective-permute-start(bf16[256,128]{1,0:T(8,128)(2,1)S(1)} %get-tuple-element.51), channel_id=1, source_target_pairs={{0,4},{4,0},{8,12},{12,8},{1,5},{5,1},{9,13},{13,9},{16,20},{20,16... | collective-permute-start | bytes 196616 | tf_op jit(solution)/shard_map/ppermute | solution.py:398
  44.2 16.5 %collective-permute-start.18 = (bf16[256,128]{1,0:T(8,128)(2,1)S(1)}, bf16[256,128]{1,0:T(8,128)(2,1)S(1)}, u32[]{:S(2)}, u32[]{:S(2)}) collective-permute-start(bf16[256,128]{1,0:T(8,128)(2,1)S(1)} %get-tuple-element.52), channel_id=1, source_target_pairs={{0,10},{4,14},{8,2},{12,6},{1,11},{5,15},{9,3},{13,7},{16,26},{20,... | collective-permute-start | bytes 196616 | tf_op jit(solution)/shard_map/ppermute | solution.py:394
  47.5 13.3 %collective-permute-start.14 = (bf16[256,128]{1,0:T(8,128)(2,1)S(1)}, bf16[256,128]{1,0:T(8,128)(2,1)S(1)}, u32[]{:S(2)}, u32[]{:S(2)}) collective-permute-start(bf16[256,128]{1,0:T(8,128)(2,1)S(1)} %get-tuple-element.52), channel_id=1, source_target_pairs={{0,8},{4,12},{8,0},{12,4},{1,9},{5,13},{9,1},{13,5},{16,24},{20,28... | collective-permute-start | bytes 196616 | tf_op jit(solution)/shard_map/ppermute | solution.py:398
  51.5 9.3 %collective-permute-start.19 = (bf16[256,128]{1,0:T(8,128)(2,1)S(1)}, bf16[256,128]{1,0:T(8,128)(2,1)S(1)}, u32[]{:S(2)}, u32[]{:S(2)}) collective-permute-start(bf16[256,128]{1,0:T(8,128)(2,1)S(1)} %get-tuple-element.53), channel_id=1, source_target_pairs={{0,14},{4,10},{8,6},{12,2},{1,15},{5,11},{9,7},{13,3},{16,30},{20,... | collective-permute-start | bytes 196616 | tf_op jit(solution)/shard_map/ppermute | solution.py:394
  53.7 7.9 %collective-permute-start.15 = (bf16[256,128]{1,0:T(8,128)(2,1)S(1)}, bf16[256,128]{1,0:T(8,128)(2,1)S(1)}, u32[]{:S(2)}, u32[]{:S(2)}) collective-permute-start(bf16[256,128]{1,0:T(8,128)(2,1)S(1)} %get-tuple-element.53), channel_id=1, source_target_pairs={{0,12},{4,8},{8,4},{12,0},{1,13},{5,9},{9,5},{13,1},{16,28},{20,24... | collective-permute-start | bytes 196616 | tf_op jit(solution)/shard_map/ppermute | solution.py:398
  69.8 16.3 %collective-permute-start.23 = (bf16[256,128]{1,0:T(8,128)(2,1)}, bf16[256,128]{1,0:T(8,128)(2,1)}, u32[]{:S(2)}, u32[]{:S(2)}) collective-permute-start(bf16[256,128]{1,0:T(8,128)(2,1)} %get-tuple-element.56.refs_8_), channel_id=1, source_target_pairs={{0,1},{1,0},{2,3},{3,2},{4,5},{5,4},{6,7},{7,6},{8,9},{9,8},{10,11... | collective-permute-start | bytes 196616 | tf_op jit(solution)/shard_map/ppermute | solution.py:388
  69.8 16.3 %collective-permute-start.24 = (bf16[256,128]{1,0:T(8,128)(2,1)}, bf16[256,128]{1,0:T(8,128)(2,1)}, u32[]{:S(2)}, u32[]{:S(2)}) collective-permute-start(bf16[256,128]{1,0:T(8,128)(2,1)} %collective-permute-done.20.refs_9_), channel_id=1, source_target_pairs={{0,1},{1,0},{2,3},{3,2},{4,5},{5,4},{6,7},{7,6},{8,9},{9,8},{10,11... | collective-permute-start | bytes 196616 | tf_op jit(solution)/shard_map/ppermute | solution.py:388
  71.4 14.7 %collective-permute-start.25 = (bf16[256,128]{1,0:T(8,128)(2,1)}, bf16[256,128]{1,0:T(8,128)(2,1)}, u32[]{:S(2)}, u32[]{:S(2)}) collective-permute-start(bf16[256,128]{1,0:T(8,128)(2,1)} %collective-permute-done.21.refs_10_), channel_id=1, source_target_pairs={{0,1},{1,0},{2,3},{3,2},{4,5},{5,4},{6,7},{7,6},{8,9},{9,8},{10,11... | collective-permute-start | bytes 196616 | tf_op jit(solution)/shard_map/ppermute | solution.py:388
  73.9 12.3 %collective-permute-start.26 = (bf16[256,128]{1,0:T(8,128)(2,1)}, bf16[256,128]{1,0:T(8,128)(2,1)}, u32[]{:S(2)}, u32[]{:S(2)}) collective-permute-start(bf16[256,128]{1,0:T(8,128)(2,1)} %collective-permute-done.22.refs_11_), channel_id=1, source_target_pairs={{0,1},{1,0},{2,3},{3,2},{4,5},{5,4},{6,7},{7,6},{8,9},{9,8},{10,11... | collective-permute-start | bytes 196616 | tf_op jit(solution)/shard_map/ppermute | solution.py:388
  91.2 10.5 %collective-permute-start.30 = (bf16[1344,128]{1,0:T(8,128)(2,1)S(1)}, bf16[1344,128]{1,0:T(8,128)(2,1)S(1)}, u32[]{:S(2)}, u32[]{:S(2)}) collective-permute-start(bf16[1344,128]{1,0:T(8,128)(2,1)S(1)} %dynamic-slice_bitcast_fusion), channel_id=1, source_target_pairs={{0,2},{2,0},{1,3},{3,1},{4,6},{6,4},{5,7},{7,5},{8,10},{10,8},{9,1... | collective-permute-start | bytes 1032200 | tf_op jit(solution)/shard_map/ppermute | solution.py:382
  91.3 8.0 %collective-permute-start.28 = (bf16[256,128]{1,0:T(8,128)(2,1)S(1)}, bf16[256,128]{1,0:T(8,128)(2,1)S(1)}, u32[]{:S(2)}, u32[]{:S(2)}) collective-permute-start(bf16[256,128]{1,0:T(8,128)(2,1)S(1)} %get-tuple-element.62), channel_id=1, source_target_pairs={{0,8},{4,12},{8,0},{12,4},{1,9},{5,13},{9,1},{13,5},{2,10},{6,14},... | collective-permute-start | bytes 196616 | tf_op jit(solution)/shard_map/ppermute | solution.py:379
  102.8 9.8 %collective-permute-start.32 = (bf16[336,128]{1,0:T(8,128)(2,1)S(1)}, bf16[336,128]{1,0:T(8,128)(2,1)S(1)}, u32[]{:S(2)}, u32[]{:S(2)}) collective-permute-start(bf16[336,128]{1,0:T(8,128)(2,1)S(1)} %get-tuple-element.67), channel_id=1, source_target_pairs={{0,8},{4,12},{8,0},{12,4},{1,9},{5,13},{9,1},{13,5},{2,10},{6,14},... | collective-permute-start | bytes 258056 | tf_op jit(solution)/shard_map/ppermute | solution.py:379
  105.5 7.1 %collective-permute-start.33 = (bf16[336,128]{1,0:T(8,128)(2,1)S(1)}, bf16[336,128]{1,0:T(8,128)(2,1)S(1)}, u32[]{:S(2)}, u32[]{:S(2)}) collective-permute-start(bf16[336,128]{1,0:T(8,128)(2,1)S(1)} %get-tuple-element.68), channel_id=1, source_target_pairs={{0,12},{4,8},{8,4},{12,0},{1,13},{5,9},{9,5},{13,1},{2,14},{6,10},... | collective-permute-start | bytes 258056 | tf_op jit(solution)/shard_map/ppermute | solution.py:379
  112.6 6.9 %collective-permute-start.36 = (bf16[336,128]{1,0:T(8,128)(2,1)S(1)}, bf16[336,128]{1,0:T(8,128)(2,1)S(1)}, u32[]{:S(2)}, u32[]{:S(2)}) collective-permute-start(bf16[336,128]{1,0:T(8,128)(2,1)S(1)} %add_convert_fusion), channel_id=1, source_target_pairs={{0,12},{4,8},{8,4},{12,0},{1,13},{5,9},{9,5},{13,1},{2,14},{6,10},... | collective-permute-start | bytes 258056 | tf_op jit(solution)/shard_map/ppermute | solution.py:379
  114.8 7.4 %collective-permute-start.35 = (bf16[336,128]{1,0:T(8,128)(2,1)S(1)}, bf16[336,128]{1,0:T(8,128)(2,1)S(1)}, u32[]{:S(2)}, u32[]{:S(2)}) collective-permute-start(bf16[336,128]{1,0:T(8,128)(2,1)S(1)} %add_convert_fusion), channel_id=1, source_target_pairs={{0,8},{4,12},{8,0},{12,4},{1,9},{5,13},{9,1},{13,5},{2,10},{6,14},... | collective-permute-start | bytes 258056 | tf_op jit(solution)/shard_map/ppermute | solution.py:379
  115.7 6.6 %collective-permute-start.34 = (bf16[336,128]{1,0:T(8,128)(2,1)S(1)}, bf16[336,128]{1,0:T(8,128)(2,1)S(1)}, u32[]{:S(2)}, u32[]{:S(2)}) collective-permute-start(bf16[336,128]{1,0:T(8,128)(2,1)S(1)} %add_convert_fusion), channel_id=1, source_target_pairs={{0,4},{4,0},{8,12},{12,8},{1,5},{5,1},{9,13},{13,9},{2,6},{6,2},{1... | collective-permute-start | bytes 258056 | tf_op jit(solution)/shard_map/ppermute | solution.py:379
  122.3 9.0 %collective-permute-start.37 = (bf16[1344,128]{1,0:T(8,128)(2,1)S(1)}, bf16[1344,128]{1,0:T(8,128)(2,1)S(1)}, u32[]{:S(2)}, u32[]{:S(2)}) collective-permute-start(bf16[1344,128]{1,0:T(8,128)(2,1)S(1)} %pad_maximum_fusion.refs_1_), channel_id=1, source_target_pairs={{0,2},{2,0},{1,3},{3,1},{4,6},{6,4},{5,7},{7,5},{8,10},{10,8},{9,1... | collective-permute-start | bytes 1032200 | tf_op jit(solution)/shard_map/ppermute | solution.py:382
  (53 other events, 512.6 us)

commit v3 on v2

--- a/solution.py
+++ b/solution.py
@@ -10,7 +10,6 @@
 I32 = jnp.int32
 LANES = 128
 VMEM = pl.BlockSpec(memory_space=pltpu.VMEM)
-SMEM = pl.BlockSpec(memory_space=pltpu.SMEM)
 ANY = pl.BlockSpec(memory_space=pl.ANY)
 
 
@@ -18,24 +17,22 @@
     return jax.ShapeDtypeStruct(tuple(dims), kind)
 
 
-def run(kernel, outs, args, smem=(), scratch=(), copies=1, flops=0):
-    counts = (len(smem), len(args), len(outs))
+def run(kernel, outs, args, scratch=(), copies=1, flops=0):
+    b, c = len(args), len(outs)
 
     def body(*refs):
-        a, b, c = counts
-        scalars, given, made = refs[:a], refs[a : a + b], refs[a + b : a + b + c]
-        kernel(refs[-1], scalars, given, made, refs[a + b + c : -1])
+        kernel(refs[-1], refs[:b], refs[b : b + c], refs[b + c : -1])
 
     moved = sum(a.size * a.dtype.itemsize for a in list(args) + list(outs))
     return pl.pallas_call(
         body,
         out_shape=list(outs),
-        in_specs=[SMEM] * len(smem) + [ANY] * len(args),
+        in_specs=[ANY] * len(args),
         out_specs=[VMEM] * len(outs),
         scratch_shapes=list(scratch) + [pltpu.SemaphoreType.DMA((copies,))],
-        compiler_params=pltpu.CompilerParams(vmem_limit_bytes=32 * 1024 * 1024),
+        compiler_params=pltpu.CompilerParams(vmem_limit_bytes=56 * 1024 * 1024),
         cost_estimate=pl.CostEstimate(flops=flops, bytes_accessed=moved, transcendentals=0),
-    )(*smem, *args)
+    )(*args)
 
 
 def begin(sems, pairs, first=0):
@@ -86,13 +83,15 @@
     return -(-cap // LANES) * LANES
 
 
-def ask_kernel(sems, smem, given, pieces, scratch):
-    (ids, counts), (rows_any,), (rows_ref,) = smem, given, scratch
-    end(begin(sems, [(rows_any, rows_ref)]))
+def ask_kernel(sems, given, pieces, scratch):
+    rows_any, counts_any = given
+    rows_ref, counts = scratch
+    end(begin(sems, [(rows_any, rows_ref), (counts_any, counts)]))
+    z = lax.axis_index("node")
     batches, _, cap = rows_ref.shape
     slot = lax.broadcasted_iota(I32, (1, cap), 1)
     for k, piece in enumerate(pieces):
-        owner = ids[0] ^ k
+        owner = z ^ k
         if piece.shape[1] != cap:
             piece[...] = jnp.full(piece.shape, -1, I32)
         for b in range(batches):
@@ -107,7 +106,7 @@
         piece[...] = held[k * room : k * room + cap, :]
 
 
-def serve_kernel(sems, smem, given, made, scratch):
+def serve_kernel(sems, given, made, scratch):
     *asked_pieces, memory_any = given
     asked_ref, narrow_ref, *pieces = made
     memory_ref, held = scratch
@@ -123,8 +122,7 @@
     give(held, pieces)
 
 
-def base_kernel(batch, sems, smem, given, made, scratch):
-    (ids,) = smem
+def base_kernel(batch, sems, given, made, scratch):
     asked_any, before_any, memory_any, handed_any = given
     base_ref, put_ref, rows_ref = made
     asked, before, handed, narrow = scratch
@@ -134,9 +132,9 @@
     )
     end(begun)
     row = slice(batch, batch + 1)
-    put_ref[...] = jnp.where(ids[1] == 0, asked[row, :], before[row, :])
-
-    @pl.when(ids[1] != 0)
+    put_ref[...] = jnp.where(lax.axis_index("seg") == 0, asked[row, :], before[row, :])
+
+    @pl.when(lax.axis_index("seg") != 0)
     def _():
         base_ref[...] = handed[...].astype(F32)
 
@@ -154,23 +152,33 @@
     return begin(sems, pairs, first)
 
 
-def next_kernel(nodes, batch, sems, smem, given, made, scratch):
-    (ids,) = smem
+def handed_kernel(sems, given, pieces, scratch):
+    z = lax.axis_index("node")
+    cap = pieces[0].shape[0]
+
+    def send(source):
+        pairs = []
+        for k, piece in enumerate(pieces):
+            at = pl.multiple_of((z ^ k) * cap, cap)
+            pairs.append((source.at[pl.ds(at, cap), :], piece))
+        end(begin(sems, pairs))
+
+    @pl.when(lax.axis_index("seg") == 0)
+    def _():
+        send(given[0])
+
+    @pl.when(lax.axis_index("seg") != 0)
+    def _():
+        send(given[1])
+
+
+def next_kernel(batch, sems, given, made, scratch):
     asked_any, put_any, rows_any = given[:3]
-    stayed, handed = given[3 : 3 + nodes], given[3 + nodes :]
     values_ref, pieces = made[0], made[1:]
     asked, put, rows, held = scratch
     cap = pieces[0].shape[0]
     begun = begin(sems, [(asked_any, asked), (put_any, put), (rows_any, rows)])
-
-    @pl.when(ids[1] == 0)
-    def _():
-        end(gather_values(values_ref, cap, stayed, sems, 3))
-
-    @pl.when(ids[1] != 0)
-    def _():
-        end(gather_values(values_ref, cap, handed, sems, 3))
-
+    end(gather_values(values_ref, cap, given[3:], sems, 3))
     end(begun)
     events = values_ref.shape[0]
     wide = jnp.concatenate([values_ref[...], jnp.ones((events, LANES), BF)], axis=1)
@@ -194,14 +202,14 @@
     give(held, pieces)
 
 
-def update_kernel(sems, smem, given, made, scratch):
+def update_kernel(sems, given, made, scratch):
     put_any, values_any, base_any = given
     put, values, base = scratch
     end(begin(sems, [(put_any, put), (values_any, values), (base_any, base)]))
     set_rows(put[...], values[...], base, made[0])
 
 
-def last_kernel(batch, sems, smem, given, made, scratch):
+def last_kernel(batch, sems, given, made, scratch):
     asked_any, base_any, *pieces = given
     asked, values, base = scratch
     begun = begin(sems, [(asked_any, asked), (base_any, base)])
@@ -210,51 +218,74 @@
     set_rows(asked[batch : batch + 1, :], values[...], base, made[0])
 
 
-def batch_kernel(nodes, batch, forward, backward, prior, sems, smem, given, made, scratch):
-    ids, counts = smem
-    dst_any, time_any, edge_any, w_in_any, w_hid_any, bias_any = given[:6]
-    own_pieces, other_pieces = given[6 : 6 + nodes], given[6 + nodes : 6 + 2 * nodes]
-    rest = given[6 + 2 * nodes :]
-    message, dst, w_in, w_hid, bias_ref, fresh = scratch[:6]
+def cosine(x):
+    turns = jnp.round(x * 0.3183098861837907)
+    r = x - turns * 3.140625
+    r = r - turns * 0.0009670257568359375
+    r = r - turns * 6.278329573009626e-07
+    odd = turns - 2.0 * jnp.floor(turns * 0.5)
+    q = r * r
+    p = 2.08767569878681e-09 - q * 1.1470745597729725e-11
+    p = q * p - 2.7557319223985893e-07
+    p = q * p + 2.48015873015873e-05
+    p = q * p - 0.001388888888888889
+    p = q * p + 0.041666666666666664
+    p = q * p - 0.5
+    p = q * p + 1.0
+    return p * (1.0 - 2.0 * odd)
+
+
+def batch_kernel(nodes, batch, final, sems, given, made, scratch):
+    dst_any, elapsed_any, edge_any, edge_other_any, w_in_any, w_hid_any, bias_any = given[:7]
+    freq_any, phase_any, counts_any, up_any = given[7:11]
+    own_pieces, other_pieces = given[11 : 11 + nodes], given[11 + nodes : 11 + 2 * nodes]
+    rest = given[11 + 2 * nodes :]
+    prior = len(rest) > 0
+    message, dst, elapsed, edge, w_in, w_hid, bias_ref, freq, phase, counts = scratch[:10]
+    gates, up, fresh = scratch[10:13]
     cap = own_pieces[0].shape[0]
     events = nodes * cap
-    z, f = ids[0], ids[2]
+    z, f = lax.axis_index("node"), lax.axis_index("feat")
     mine = pl.multiple_of(f * LANES, LANES)
     other = pl.multiple_of((1 - f) * LANES, LANES)
     width = 2 * LANES
     long = message.shape[1]
+    thin = edge_any.shape[1]
     pairs = [(dst_any.at[batch], dst)]
     for k in range(nodes):
         at = pl.ds(pl.multiple_of((z ^ k) * cap, cap), cap)
         pairs.append((own_pieces[k], message.at[at, pl.ds(mine, LANES)]))
         pairs.append((other_pieces[k], message.at[at, pl.ds(other, LANES)]))
+    early = [
+        (elapsed_any.at[batch], elapsed),
+        (freq_any, freq),
+        (phase_any, phase),
+        (edge_any.at[batch], edge.at[pl.ds(pl.multiple_of(f * thin, thin), thin), :]),
+        (edge_other_any.at[batch], edge.at[pl.ds(pl.multiple_of((1 - f) * thin, thin), thin), :]),
+    ]
+    late = [(w_in_any, w_in), (w_hid_any, w_hid), (bias_any, bias_ref), (counts_any, counts)]
+    late.append((up_any.at[batch], up))
+    if prior:
+        before = scratch[13]
+        late.append((rest[0], before))
     rows_begun = begin(sems, pairs)
-    pairs2 = [
-        (w_in_any, w_in),
-        (w_hid_any, w_hid),
-        (bias_any, bias_ref),
-        (time_any.at[batch], message.at[:, 2 * width : 2 * width + LANES]),
-        (edge_any.at[batch], message.at[:, 2 * width + LANES :]),
-    ]
-    begun = begin(sems, pairs2, len(pairs))
-    if backward:
-        gates, up = scratch[6:8]
-        last_pairs = [(rest[0].at[batch], up)]
-        if prior:
-            before = scratch[8]
-            last_pairs.append((rest[1], before))
-        last_begun = begin(sems, last_pairs, len(pairs) + len(pairs2))
+    early_begun = begin(sems, early, len(pairs))
+    late_begun = begin(sems, late, len(pairs) + len(early))
+    end(early_begun)
+    for j in range(events // LANES):
+        span = slice(j * LANES, (j + 1) * LANES)
+        angle = down(elapsed[:, span].astype(F32)) * freq[...] + phase[...]
+        message[span, 2 * width : 2 * width + LANES] = cosine(angle).astype(BF)
+        message[span, 2 * width + LANES :] = jnp.transpose(edge[:, span].astype(F32)).astype(BF)
     end(rows_begun)
     full = message[:, :width]
     for j in range(events // LANES):
         span = slice(j * LANES, (j + 1) * LANES)
         message[span, width : 2 * width] = pick_rows(dst[:, span], full)
-    end(begun)
+    end(late_begun)
     w_in01 = jnp.concatenate([w_in[0], w_in[1]], axis=1)
     w_hid01 = jnp.concatenate([w_hid[0], w_hid[1]], axis=1)
     sums = [jnp.zeros((1, LANES), F32) for _ in range(4)]
-    if backward:
-        end(last_begun)
     tall = 256
     for i in range(events // tall):
         span = slice(i * tall, (i + 1) * tall)
@@ -272,29 +303,25 @@
             + bias_ref[2:3, :]
             + reset_gate * recur_term
         )
-        if forward:
-            fresh[span, :] = ((1.0 - update) * candid + update * own).astype(BF)
-        if backward:
-            number = lax.broadcasted_iota(I32, (tall, LANES), 0) + i * tall
-            live = number < 0
-            for o in range(nodes):
-                if o * cap < (i + 1) * tall and (o + 1) * cap > i * tall:
-                    live = live | (
-                        (number >= o * cap) & (number < o * cap + counts[batch, o])
-                    )
-            cotangent = jnp.where(live, up[span, :].astype(F32), 0.0)
-            grad_cand = cotangent * (1.0 - update) * (1.0 - candid * candid)
-            grad_upd = cotangent * (own - candid) * update * (1.0 - update)
-            grad_reset = grad_cand * recur_term * reset_gate * (1.0 - reset_gate)
-            grad_recur = grad_cand * reset_gate
-            for g, part in enumerate((grad_reset, grad_upd, grad_cand, grad_recur)):
-                sums[g] = sums[g] + jnp.sum(part, axis=0, keepdims=True)
-                gates[span, g * LANES : (g + 1) * LANES] = part.astype(BF)
-    if forward:
+        fresh[span, :] = ((1.0 - update) * candid + update * own).astype(BF)
+        number = lax.broadcasted_iota(I32, (tall, LANES), 0) + i * tall
+        live = number < 0
+        for o in range(nodes):
+            if o * cap < (i + 1) * tall and (o + 1) * cap > i * tall:
+                live = live | ((number >= o * cap) & (number < o * cap + counts[batch, o]))
+        cotangent = jnp.where(live, up[span, :].astype(F32), 0.0)
+        grad_cand = cotangent * (1.0 - update) * (1.0 - candid * candid)
+        grad_upd = cotangent * (own - candid) * update * (1.0 - update)
+        grad_reset = grad_cand * recur_term * reset_gate * (1.0 - reset_gate)
+        grad_recur = grad_cand * reset_gate
+        for g, part in enumerate((grad_reset, grad_upd, grad_cand, grad_recur)):
+            sums[g] = sums[g] + jnp.sum(part, axis=0, keepdims=True)
+            gates[span, g * LANES : (g + 1) * LANES] = part.astype(BF)
+    if final:
         for k in range(nodes):
             made[k][...] = fresh[pl.ds(pl.multiple_of((z ^ k) * cap, cap), cap), :]
-    if not backward:
-        return
+    else:
+        made[0][...] = fresh[...]
     out_ref = made[-1]
 
     def put(start, value):
@@ -319,14 +346,13 @@
     put(top, tail)
 
 
-def middle_kernel(segs, sems, smem, given, made, scratch):
-    (ids,) = smem
+def middle_kernel(segs, sems, given, made, scratch):
     totals, got = given[0], given[1:segs]
     rows = scratch[:segs]
     whole = scratch[segs]
     nodes, chunk = len(made), made[0].shape[0]
     share = nodes * chunk
-    at = pl.ds(pl.multiple_of(ids[1] * share, share), share)
+    at = pl.ds(pl.multiple_of(lax.axis_index("seg") * share, share), share)
     pairs = [(totals.at[at, :], rows[0])] + list(zip(got, rows[1:]))
     end(begin(sems, pairs))
     total = rows[0][...].astype(F32)
@@ -334,15 +360,14 @@
         total = total + rows[x][...].astype(F32)
     whole[...] = total.astype(BF)
     for k in range(nodes):
-        made[k][...] = whole[pl.ds(pl.multiple_of((ids[0] ^ k) * chunk, chunk), chunk), :]
-
-
-def unpack_kernel(nodes, segs, long, sems, smem, pieces, made, scratch):
-    (ids,) = smem
+        made[k][...] = whole[pl.ds(pl.multiple_of((lax.axis_index("node") ^ k) * chunk, chunk), chunk), :]
+
+
+def unpack_kernel(nodes, segs, long, sems, pieces, made, scratch):
     grad_in, grad_hid, grad_bias = made
     (held,) = scratch
     chunk = pieces[0].shape[0] // nodes
-    z, s = ids[0], ids[1]
+    z, s = lax.axis_index("node"), lax.axis_index("seg")
     pairs = []
     for x in range(segs):
         for k in range(nodes):
@@ -363,8 +388,7 @@
     memory, req_rows, req_count, dst_slot, elapsed, edges, upstream, freq, phase, w_input, w_hidden, bias
 ):
     nodes, segs = lax.axis_size("node"), lax.axis_size("seg")
-    z, s, f = lax.axis_index("node"), lax.axis_index("seg"), lax.axis_index("feat")
-    ids = jnp.stack([z, s, f]).astype(I32)
+    z, s = lax.axis_index("node"), lax.axis_index("seg")
     memory_now = memory[0]
     node_rows, half = memory_now.shape
     batches, cap = req_rows.shape[0], req_rows.shape[-1]
@@ -387,46 +411,28 @@
     def feat_swap(block):
         return lax.ppermute(block, "feat", [(0, 1), (1, 0)])
 
-    def to_next(block, k):
-        route = [
-            (i * segs + j, (i ^ k) * segs + j + 1) for i in range(nodes) for j in range(segs - 1)
-        ]
-        return lax.ppermute(block, ("node", "seg"), route)
-
-    def to_first(block, k):
-        route = [(i * segs, (i ^ k) * segs) for i in range(nodes)]
-        return lax.ppermute(block, ("node", "seg"), route)
-
     def exchange(blocks):
         return [blocks[0]] + [node_swap(blocks[k], k) for k in range(1, nodes)]
 
     wanted = run(
         ask_kernel,
         [shape((batches, room), I32)] * nodes,
-        [req_rows[:, 0, 0]],
-        [ids, counts],
-        [pltpu.VMEM((batches, nodes, cap), I32)],
+        [req_rows[:, 0, 0], counts],
+        [pltpu.VMEM((batches, nodes, cap), I32), pltpu.SMEM((batches, nodes), I32)],
+        2,
     )
     wide_rows = pltpu.VMEM((spread, half), BF)
     asked, narrow, *served = run(
         serve_kernel,
         [shape((batches, spread), I32), shape((node_rows, half), BF)] + [piece] * nodes,
         exchange(wanted) + [memory_now],
-        [],
         [pltpu.VMEM((node_rows, half), F32), wide_rows],
         nodes + 1,
     )
     asked_before = seg_next(asked)
 
-    edge_other = feat_swap(edges[:, 0])
-    edge_full = jnp.where(
-        f == 0,
-        jnp.concatenate([edges[:, 0], edge_other], axis=-1),
-        jnp.concatenate([edge_other, edges[:, 0]], axis=-1),
-    )
-    time_code = jnp.cos(
-        elapsed[:, 0].astype(F32)[:, :, None] * freq[None, None, :] + phase[None, None, :]
-    ).astype(BF)
+    edge_own = jnp.swapaxes(edges[:, 0], 1, 2)
+    edge_other = feat_swap(edge_own)
 
     chunk = -(-(3 * long + width + 16) // (16 * nodes * segs)) * 16
     total_rows = chunk * nodes * segs
@@ -440,45 +446,49 @@
         if not final:
             handed_memory = seg_next(narrow)
         other_pieces = [feat_swap(p) for p in own_pieces]
-        given = [dst_slot, time_code, edge_full, w_input, w_hidden, bias]
-        given = given + own_pieces + other_pieces
+        given = [dst_slot, elapsed, edge_own, edge_other, w_input, w_hidden, bias]
+        given = given + [freq[None], phase[None], counts, upstream[:, 0]]
+        given = given + own_pieces + other_pieces + ([] if totals is None else [totals])
         rooms = [
             pltpu.VMEM((events, long), BF),
             pltpu.VMEM((1, events), I32),
+            pltpu.VMEM((1, events), I32),
+            pltpu.VMEM((2 * edges.shape[-1], events), BF),
             pltpu.VMEM(w_input.shape, BF),
             pltpu.VMEM(w_hidden.shape, BF),
             pltpu.VMEM(bias.shape, F32),
+            pltpu.VMEM((1, freq.shape[0]), F32),
+            pltpu.VMEM((1, freq.shape[0]), F32),
+            pltpu.SMEM((batches, nodes), I32),
+            pltpu.VMEM((events, 4 * half), BF),
+            pltpu.VMEM((events, half), BF),
             pltpu.VMEM((events, half), BF),
         ]
-        more = [pltpu.VMEM((events, 4 * half), BF), pltpu.VMEM((events, half), BF)]
         if totals is not None:
-            more.append(pltpu.VMEM((total_rows, half), F32))
-        copies = 8 + 2 * nodes
-        prior = [] if totals is None else [totals]
+            rooms.append(pltpu.VMEM((total_rows, half), F32))
+        copies = 12 + 2 * nodes
+        *fresh, totals = run(
+            lambda *a, b=b, last=final: batch_kernel(nodes, b, last, *a),
+            ([piece] * nodes if final else [shape((events, half), BF)])
+            + [shape((total_rows, half), BF if final else F32)],
+            given,
+            rooms,
+            copies,
+        )
         if not final:
-            fresh = run(
-                lambda *a, b=b: batch_kernel(nodes, b, True, False, False, *a),
-                [piece] * nodes,
-                given,
-                [ids, counts],
-                rooms,
-                copies,
-            )
-            handed = [to_next(fresh[k], k) for k in range(nodes)]
-            stayed = [fresh[0]] + [to_first(fresh[k], k) for k in range(1, nodes)]
+            values = run(handed_kernel, [piece] * nodes, [fresh[0], seg_next(fresh[0])], [], nodes)
+            values = exchange(values)
             base, put, rows = run(
                 lambda *a, b=b: base_kernel(b, *a),
                 [shape((node_rows, half), F32), shape((1, spread), I32), shape((spread, half), BF)],
                 [asked, asked_before, memory_now, handed_memory],
-                [ids],
-                [numbers, numbers, pltpu.VMEM((node_rows, half), BF)] + [pltpu.VMEM((node_rows, half), BF)],
+                [numbers, numbers] + [pltpu.VMEM((node_rows, half), BF)] * 2,
                 4,
             )
             values, *served = run(
-                lambda *a, b=b: next_kernel(nodes, b, *a),
+                lambda *a, b=b: next_kernel(b, *a),
                 [shape((spread, half), BF)] + [piece] * nodes,
-                [asked, put, rows] + stayed + handed,
-                [ids],
+                [asked, put, rows] + values,
                 [numbers, line, wide_rows, wide_rows],
                 3 + nodes,
             )
@@ -486,34 +496,16 @@
                 update_kernel,
                 [shape((node_rows, half), F32)],
                 [put, values, base],
-                [],
                 [line, wide_rows, block],
                 3,
             )[0]
             narrow = memory_now.astype(BF)
-            totals = run(
-                lambda *a, b=b, p=prior: batch_kernel(nodes, b, False, True, len(p) > 0, *a),
-                [shape((total_rows, half), F32)],
-                given + [upstream[:, 0]] + prior + [handed[0]],
-                [ids, counts],
-                rooms + more,
-                copies,
-            )[0]
         else:
-            *fresh, totals = run(
-                lambda *a, b=b, p=prior: batch_kernel(nodes, b, True, True, len(p) > 0, *a),
-                [piece] * nodes + [shape((total_rows, half), BF)],
-                given + [upstream[:, 0]] + prior,
-                [ids, counts],
-                rooms + more,
-                copies,
-            )
             returned = exchange(fresh)
             memory_out = run(
                 lambda *a, b=b: last_kernel(b, *a),
                 [shape((node_rows, half), F32)],
                 [asked, memory_now] + returned,
-                [],
                 [numbers, wide_rows, block],
                 2 + nodes,
             )[0]
@@ -528,7 +520,6 @@
         lambda *a: middle_kernel(segs, *a),
         [shape((chunk, half), BF)] * nodes,
         [totals] + got + returned[1:],
-        [ids],
         [share] * (segs + 1),
         segs,
     )
@@ -540,7 +531,6 @@
         lambda *a: unpack_kernel(nodes, segs, long, *a),
         [shape(w_input.shape, F32), shape(w_hidden.shape, F32), shape(bias.shape, F32)],
         gathered,
-        [ids],
         [pltpu.VMEM((total_rows, half), BF)],
         nodes * segs,
     )

time: 135 us -> 133 us (0.985)
  waiting for transfers between devices: 30.6 us -> 40.1 us
  Pallas kernels: 27.2 us -> 36.6 us
  local copies, waits for them, and re-layouts: 15.7 us -> 7.69 us
  starting transfers between devices: 53.1 us -> 46 us
  other arithmetic: 6.12 us -> 0.96 us
    ppermute x7 -> x0, starting transfers between devices: 17.9 us -> none  [the longest x3 9.78 us: to_first(): return lax.ppermute(block, ('node', 'seg'), route)]
    pallas_call x11, Pallas kernels: 27.2 us -> 36.6 us  [run(): pl.pallas_call(body, out_shape=list(outs), in_specs=[ANY] * len(args), ou...]
    unnamed x80 -> x62, local copies, waits for them, and re-layouts: 15.6 us -> 6.68 us
    ppermute x2 -> x3, waiting for transfers between devices: 0.01 us -> 8 us  [seg_next(): return lax.ppermute(block, 'seg', [(i, i + 1) for i in range(segs - 1)])]
    ppermute x2 -> x3, starting transfers between devices: 4.85 us -> 9 us  [seg_next(): return lax.ppermute(block, 'seg', [(i, i + 1) for i in range(segs - 1)])]
    ppermute x18 -> x21, starting transfers between devices: 27.9 us -> 31.9 us  [node_swap(): return lax.ppermute(block, 'node', [(i, i ^ k) for i in range(nodes)])]
    ppermute x18 -> x21, waiting for transfers between devices: 24.4 us -> 28.3 us  [node_swap(): return lax.ppermute(block, 'node', [(i, i ^ k) for i in range(nodes)])]
    convert_element_type x2 -> x0, other arithmetic: 3.75 us -> none  [the longest x1 3.74 us: local(): time_code = jnp.cos(elapsed[:, 0].astype(F32)[:, :, None] * freq[None, No...]
  transfers between devices with their start and end apart: 38 -> 35, of which waited for: 15 -> 19; matrix products, arithmetic and copies ran while one was open for 5% -> 0% of each run, Pallas kernels for 10% -> 18%
where the time goes in v3:
time: 133 us; the launch traced here: 132 us
  starting transfers between devices  46 us (35%)
  waiting for transfers between devices  40.1 us (30%)
  Pallas kernels  36.6 us (28%)
  local copies, waits for them, and re-layouts  7.69 us (6%)
    pallas_call x11, Pallas kernels, run(): pl.pallas_call(body, out_shape=list(outs), in_specs=[ANY] * len(args), ou...  36.6 us
    ppermute x21, starting transfers between devices, node_swap(): return lax.ppermute(block, 'node', [(i, i ^ k) for i in range(nodes)])  31.9 us
    ppermute x21, waiting for transfers between devices, node_swap(): return lax.ppermute(block, 'node', [(i, i ^ k) for i in range(nodes)])  28.3 us
    ppermute x3, starting transfers between devices, seg_next(): return lax.ppermute(block, 'seg', [(i, i + 1) for i in range(segs - 1)])  9 us
    ppermute x3, waiting for transfers between devices, seg_next(): return lax.ppermute(block, 'seg', [(i, i + 1) for i in range(segs - 1)])  8 us
    unnamed x62, local copies, waits for them, and re-layouts  6.68 us
    ppermute x2, starting transfers between devices, seg_swap(): return lax.ppermute(block, 'seg', [(i, i ^ x) for i in range(segs)])  3.71 us
  transfers between devices with their start and end apart: 35, of which 19 were waited for; matrix products, arithmetic and copies ran while one was open for 0% of the time, Pallas kernels for 18%

profile of v3, /device:TPU:0, one launch (start us, length us, event | category | flops | bytes accessed | tf_op | source)
XLA Modules:
  0.0 132.5 jit_solution(10306821168095541040)
XLA Ops:
  2.6 2.7 %collective-permute-start = (s32[2,256]{1,0:T(2,128)}, s32[2,256]{1,0:T(2,128)S(1)}, u32[]{:S(2)}, u32[]{:S(2)}) collective-permute-start(s32[2,256]{1,0:T(2,128)} %get-tuple-element.41), channel_id=1, source_target_pairs={{0,4},{4,0},{8,12},{12,8},{1,5},{5,1},{9,13},{13,9},{2,6},{6,2},{1... | collective-permute-start | bytes 6152 | tf_op jit(solution)/shard_map/ppermute | solution.py:403
  5.3 2.6 %collective-permute-start.1 = (s32[2,256]{1,0:T(2,128)}, s32[2,256]{1,0:T(2,128)S(1)}, u32[]{:S(2)}, u32[]{:S(2)}) collective-permute-start(s32[2,256]{1,0:T(2,128)} %get-tuple-element.42), channel_id=1, source_target_pairs={{0,8},{4,12},{8,0},{12,4},{1,9},{5,13},{9,1},{13,5},{2,10},{6,14},... | collective-permute-start | bytes 6152 | tf_op jit(solution)/shard_map/ppermute | solution.py:403
  10.0 3.5 %collective-permute-done.2.refs_3_ = s32[2,256]{1,0:T(2,128)S(1)} collective-permute-done((s32[2,256]{1,0:T(2,128)}, s32[2,256]{1,0:T(2,128)S(1)}, u32[]{:S(2)}, u32[]{:S(2)}) %collective-permute-start.2) | collective-permute-done | bytes 2080 | tf_op jit(solution)/shard_map/ppermute | solution.py:403
  14.0 3.4 %shard_map.148 = (s32[2,1024]{1,0:T(2,128)}, bf16[2048,128]{1,0:T(8,128)(2,1)}, bf16[256,128]{1,0:T(8,128)(2,1)}, bf16[256,128]{1,0:T(8,128)(2,1)}, bf16[256,128]{1,0:T(8,128)(2,1)}, /*index=5*/bf16[256,128]{1,0:T(8,128)(2,1)}) custom-call(s32[2,256]{1,0:T(2,128)} %get-tuple-element.40.refs_0_, s32[2,256]{1,0:T(2,128)} %copy-done.28, s32[2,256]{1,0:T(2,128)} %copy-done.29, ...), custom_call_target="tpu_custom_call" | custom-call | bytes 1851392 | tf_op jit(solution)/shard_map/pallas_call | solution.py:27
  17.5 3.4 %collective-permute-start.4 = (bf16[2048,128]{1,0:T(8,128)(2,1)}, bf16[2048,128]{1,0:T(8,128)(2,1)S(1)}, u32[]{:S(2)}, u32[]{:S(2)}) collective-permute-start(bf16[2048,128]{1,0:T(8,128)(2,1)} %get-tuple-element.45), channel_id=1, source_target_pairs={{0,2},{1,3},{4,6},{5,7},{8,10},{9,11},{12,14},{13,15},{16,18},{17,... | collective-permute-start | bytes 1572872 | tf_op jit(solution)/shard_map/ppermute | solution.py:409
  21.7 3.6 %collective-permute-start.8 = (bf16[256,128]{1,0:T(8,128)(2,1)}, bf16[256,128]{1,0:T(8,128)(2,1)S(1)}, u32[]{:S(2)}, u32[]{:S(2)}) collective-permute-start(bf16[256,128]{1,0:T(8,128)(2,1)} %get-tuple-element.51), channel_id=1, source_target_pairs={{0,12},{4,8},{8,4},{12,0},{1,13},{5,9},{9,5},{13,1},{2,14},{6,10},... | collective-permute-start | bytes 196616 | tf_op jit(solution)/shard_map/ppermute | solution.py:403
  30.8 6.4 %shard_map.150 = (bf16[1024,128]{1,0:T(8,128)(2,1)}, f32[2688,128]{1,0:T(8,128)}) custom-call(s32[2,1,1024]{2,1,0:T(1,128)} %refs_0_.3, s32[2,1,1024]{2,1,0:T(1,128)} %refs_1_.3, bf16[2,64,1024]{2,1,0:T(8,128)(2,1)} %bitcast.19, bf16[2,64,1024]{2,1,0:T(8,128)(2,1)} %copy-done.1, bf16[3,768,128]{2,1,0:T(8,128)(2,1)} %refs_4_.3, bf16[3,256,128]{2,1,0:T(8,128)(2,1)} %refs_5_.3, ...), custom_call_target="tpu_custom_call" | custom-call | bytes 4017184 | tf_op jit(solution)/shard_map/pallas_call | solution.py:27
  38.5 6.6 %collective-permute-done.13.refs_1_ = bf16[1024,128]{1,0:T(8,128)(2,1)S(1)} collective-permute-done((bf16[1024,128]{1,0:T(8,128)(2,1)}, bf16[1024,128]{1,0:T(8,128)(2,1)S(1)}, u32[]{:S(2)}, u32[]{:S(2)}) %collective-permute-start.13) | collective-permute-done | bytes 262176 | tf_op jit(solution)/shard_map/ppermute | solution.py:409
  48.4 2.8 %collective-permute-start.15 = (bf16[256,128]{1,0:T(8,128)(2,1)}, bf16[256,128]{1,0:T(8,128)(2,1)S(1)}, u32[]{:S(2)}, u32[]{:S(2)}) collective-permute-start(bf16[256,128]{1,0:T(8,128)(2,1)} %get-tuple-element.55), channel_id=1, source_target_pairs={{0,8},{4,12},{8,0},{12,4},{1,9},{5,13},{9,1},{13,5},{2,10},{6,14},... | collective-permute-start | bytes 196616 | tf_op jit(solution)/shard_map/ppermute | solution.py:403
  52.0 4.3 %collective-permute-start.3 = (s32[2,1024]{1,0:T(2,128)S(1)}, s32[2,1024]{1,0:T(2,128)S(1)}, u32[]{:S(2)}, u32[]{:S(2)}) collective-permute-start(s32[2,1024]{1,0:T(2,128)S(1)} %copy-done.9), channel_id=1, source_target_pairs={{0,2},{1,3},{4,6},{5,7},{8,10},{9,11},{12,14},{13,15},{16,18},{17,... | collective-permute-start | bytes 24584 | tf_op jit(solution)/shard_map/ppermute | solution.py:409
  59.0 3.5 %shard_map.149 = (f32[2048,128]{1,0:T(8,128)}, s32[1,1024]{1,0:T(1,128)}, bf16[1024,128]{1,0:T(8,128)(2,1)}) custom-call(s32[2,1024]{1,0:T(2,128)} %get-tuple-element.44.refs_0_, s32[2,1024]{1,0:T(2,128)} %copy-done.27, f32[2048,128]{1,0:T(8,128)} %bitcast.14, bf16[2048,128]{1,0:T(8,128)(2,1)} %copy-done.2), custom_call_target="tpu_custom_call" | custom-call | bytes 2904064 | tf_op jit(solution)/shard_map/pallas_call | solution.py:27
  63.2 2.5 %shard_map.152 = (bf16[1024,128]{1,0:T(8,128)(2,1)}, bf16[256,128]{1,0:T(8,128)(2,1)}, bf16[256,128]{1,0:T(8,128)(2,1)}, bf16[256,128]{1,0:T(8,128)(2,1)}, bf16[256,128]{1,0:T(8,128)(2,1)}) custom-call(s32[2,1024]{1,0:T(2,128)} %get-tuple-element.44.refs_0_, s32[1,1024]{1,0:T(1,128)} %get-tuple-element.46.refs_1_.refs_0_, ...), custom_call_target="tpu_custom_call" | custom-call | bytes 1060864 | tf_op jit(solution)/shard_map/pallas_call | solution.py:27
  65.8 3.6 %collective-permute-start.18 = (bf16[256,128]{1,0:T(8,128)(2,1)}, bf16[256,128]{1,0:T(8,128)(2,1)S(1)}, u32[]{:S(2)}, u32[]{:S(2)}) collective-permute-start(bf16[256,128]{1,0:T(8,128)(2,1)} %get-tuple-element.61), channel_id=1, source_target_pairs={{0,8},{4,12},{8,0},{12,4},{1,9},{5,13},{9,1},{13,5},{2,10},{6,14},... | collective-permute-start | bytes 196616 | tf_op jit(solution)/shard_map/ppermute | solution.py:403
  70.7 2.5 %collective-permute-done.18.refs_13_ = bf16[256,128]{1,0:T(8,128)(2,1)S(1)} collective-permute-done((bf16[256,128]{1,0:T(8,128)(2,1)}, bf16[256,128]{1,0:T(8,128)(2,1)S(1)}, u32[]{:S(2)}, u32[]{:S(2)}) %collective-permute-start.18) | collective-permute-done | bytes 65568 | tf_op jit(solution)/shard_map/ppermute | solution.py:403
  77.6 6.1 %shard_map.154 = (bf16[256,128]{1,0:T(8,128)(2,1)}, bf16[256,128]{1,0:T(8,128)(2,1)}, bf16[256,128]{1,0:T(8,128)(2,1)}, bf16[256,128]{1,0:T(8,128)(2,1)}, bf16[2688,128]{1,0:T(8,128)(2,1)}) custom-call(s32[2,1,1024]{2,1,0:T(1,128)} %refs_0_.3, s32[2,1,1024]{2,1,0:T(1,128)} %refs_1_.3, bf16[2,64,1024]{2,1,0:T(8,128)(2,1)} %bitcast.20, ...), custom_call_target="tpu_custom_call" | custom-call | bytes 4705312 | tf_op jit(solution)/shard_map/pallas_call | solution.py:27
  84.7 2.6 %collective-permute-start.27 = (bf16[1344,128]{1,0:T(8,128)(2,1)S(1)}, bf16[1344,128]{1,0:T(8,128)(2,1)S(1)}, u32[]{:S(2)}, u32[]{:S(2)}) collective-permute-start(bf16[1344,128]{1,0:T(8,128)(2,1)S(1)} %dynamic-slice_bitcast_fusion), channel_id=1, source_target_pairs={{0,2},{2,0},{1,3},{3,1},{4,6},{6,4},{5,7},{7,5},{8,10},{10,8},{9,1... | collective-permute-start | bytes 1032200 | tf_op jit(solution)/shard_map/ppermute | solution.py:406
  88.6 3.0 %collective-permute-start.26 = (bf16[256,128]{1,0:T(8,128)(2,1)}, bf16[256,128]{1,0:T(8,128)(2,1)S(1)}, u32[]{:S(2)}, u32[]{:S(2)}) collective-permute-start(bf16[256,128]{1,0:T(8,128)(2,1)} %get-tuple-element.67), channel_id=1, source_target_pairs={{0,12},{4,8},{8,4},{12,0},{1,13},{5,9},{9,5},{13,1},{2,14},{6,10},... | collective-permute-start | bytes 196616 | tf_op jit(solution)/shard_map/ppermute | solution.py:403
  92.3 3.4 %collective-permute-done.25.refs_4_.refs_3_ = bf16[256,128]{1,0:T(8,128)(2,1)S(1)} collective-permute-done((bf16[256,128]{1,0:T(8,128)(2,1)}, bf16[256,128]{1,0:T(8,128)(2,1)S(1)}, u32[]{:S(2)}, u32[]{:S(2)}) %collective-permute-start.25) | collective-permute-done | bytes 65568 | tf_op jit(solution)/shard_map/ppermute | solution.py:403
  103.6 2.9 %collective-permute-done.30 = bf16[336,128]{1,0:T(8,128)(2,1)S(1)} collective-permute-done((bf16[336,128]{1,0:T(8,128)(2,1)}, bf16[336,128]{1,0:T(8,128)(2,1)S(1)}, u32[]{:S(2)}, u32[]{:S(2)}) %collective-permute-start.30) | collective-permute-done | bytes 86048 | tf_op jit(solution)/shard_map/ppermute | solution.py:403
  106.5 2.7 %collective-permute-done.29 = bf16[336,128]{1,0:T(8,128)(2,1)S(1)} collective-permute-done((bf16[336,128]{1,0:T(8,128)(2,1)}, bf16[336,128]{1,0:T(8,128)(2,1)S(1)}, u32[]{:S(2)}, u32[]{:S(2)}) %collective-permute-start.29) | collective-permute-done | bytes 86048 | tf_op jit(solution)/shard_map/ppermute | solution.py:403
  111.7 2.9 %collective-permute-start.31 = (bf16[336,128]{1,0:T(8,128)(2,1)S(1)}, bf16[336,128]{1,0:T(8,128)(2,1)S(1)}, u32[]{:S(2)}, u32[]{:S(2)}) collective-permute-start(bf16[336,128]{1,0:T(8,128)(2,1)S(1)} %add_convert_fusion), channel_id=1, source_target_pairs={{0,4},{4,0},{8,12},{12,8},{1,5},{5,1},{9,13},{13,9},{2,6},{6,2},{1... | collective-permute-start | bytes 258056 | tf_op jit(solution)/shard_map/ppermute | solution.py:403
  114.6 2.7 %collective-permute-done.33 = bf16[336,128]{1,0:T(8,128)(2,1)S(1)} collective-permute-done((bf16[336,128]{1,0:T(8,128)(2,1)S(1)}, bf16[336,128]{1,0:T(8,128)(2,1)S(1)}, u32[]{:S(2)}, u32[]{:S(2)}) %collective-permute-start.33) | collective-permute-done | bytes 86048 | tf_op jit(solution)/shard_map/ppermute | solution.py:403
  120.4 3.6 %shard_map.153.refs_1_ = f32[2048,128]{1,0:T(8,128)} custom-call(s32[1,1024]{1,0:T(1,128)} %get-tuple-element.46.refs_1_.refs_0_, bf16[1024,128]{1,0:T(8,128)(2,1)} %get-tuple-element.57.refs_1_, f32[2048,128]{1,0:T(8,128)} %get-tuple-element.58.refs_2_), custom_call_target="tpu_custom_call" | custom-call | bytes 2363392 | tf_op jit(solution)/shard_map/pallas_call | solution.py:27
  124.0 3.5 %shard_map.155 = f32[2048,128]{1,0:T(8,128)} custom-call(s32[2,1024]{1,0:T(2,128)} %get-tuple-element.44.refs_0_, f32[2048,128]{1,0:T(8,128)} %shard_map.153.refs_1_, bf16[256,128]{1,0:T(8,128)(2,1)} %get-tuple-element.64.refs_2_, bf16[256,128]{1,0:T(8,128)(2,1)} %copy-done.5, bf16[256,128]{1,0:T(8,128)(2,1)} %copy-done.6, bf16[256,128]{1,0:T(8,128)(2,1)} %copy-done.7), custom_call_target="tpu_custom_call" | custom-call | bytes 2367488 | tf_op jit(solution)/shard_map/pallas_call | solution.py:27
  (122 shorter events, 46.6 us)
Async XLA Ops:
  0.6 29.4 %collective-permute-start.5 = (bf16[2,64,1024]{2,1,0:T(8,128)(2,1)}, bf16[2,64,1024]{2,1,0:T(8,128)(2,1)S(1)}, u32[]{:S(2)}, u32[]{:S(2)}) collective-permute-start(bf16[2,64,1024]{2,1,0:T(8,128)(2,1)} %bitcast.18), channel_id=1, source_target_pairs={{0,1},{1,0},{2,3},{3,2},{4,5},{5,4},{6,7},{7,6},{8,9},{9,8},{10,11... | collective-permute-start | bytes 786440 | tf_op jit(solution)/shard_map/ppermute | solution.py:412
  7.8 5.6 %collective-permute-start.2 = (s32[2,256]{1,0:T(2,128)}, s32[2,256]{1,0:T(2,128)S(1)}, u32[]{:S(2)}, u32[]{:S(2)}) collective-permute-start(s32[2,256]{1,0:T(2,128)} %get-tuple-element.43), channel_id=1, source_target_pairs={{0,12},{4,8},{8,4},{12,0},{1,13},{5,9},{9,5},{13,1},{2,14},{6,10},... | collective-permute-start | bytes 6152 | tf_op jit(solution)/shard_map/ppermute | solution.py:403
  17.4 7.9 %collective-permute-start.6 = (bf16[256,128]{1,0:T(8,128)(2,1)}, bf16[256,128]{1,0:T(8,128)(2,1)S(1)}, u32[]{:S(2)}, u32[]{:S(2)}) collective-permute-start(bf16[256,128]{1,0:T(8,128)(2,1)} %get-tuple-element.49), channel_id=1, source_target_pairs={{0,4},{4,0},{8,12},{12,8},{1,5},{5,1},{9,13},{13,9},{2,6},{6,2},{1... | collective-permute-start | bytes 196616 | tf_op jit(solution)/shard_map/ppermute | solution.py:403
  17.5 40.2 %collective-permute-start.4 = (bf16[2048,128]{1,0:T(8,128)(2,1)}, bf16[2048,128]{1,0:T(8,128)(2,1)S(1)}, u32[]{:S(2)}, u32[]{:S(2)}) collective-permute-start(bf16[2048,128]{1,0:T(8,128)(2,1)} %get-tuple-element.45), channel_id=1, source_target_pairs={{0,2},{1,3},{4,6},{5,7},{8,10},{9,11},{12,14},{13,15},{16,18},{17,... | collective-permute-start | bytes 1572872 | tf_op jit(solution)/shard_map/ppermute | solution.py:409
  20.9 5.8 %collective-permute-start.7 = (bf16[256,128]{1,0:T(8,128)(2,1)}, bf16[256,128]{1,0:T(8,128)(2,1)S(1)}, u32[]{:S(2)}, u32[]{:S(2)}) collective-permute-start(bf16[256,128]{1,0:T(8,128)(2,1)} %get-tuple-element.50), channel_id=1, source_target_pairs={{0,8},{4,12},{8,0},{12,4},{1,9},{5,13},{9,1},{13,5},{2,10},{6,14},... | collective-permute-start | bytes 196616 | tf_op jit(solution)/shard_map/ppermute | solution.py:403
  21.7 6.9 %collective-permute-start.8 = (bf16[256,128]{1,0:T(8,128)(2,1)}, bf16[256,128]{1,0:T(8,128)(2,1)S(1)}, u32[]{:S(2)}, u32[]{:S(2)}) collective-permute-start(bf16[256,128]{1,0:T(8,128)(2,1)} %get-tuple-element.51), channel_id=1, source_target_pairs={{0,12},{4,8},{8,4},{12,0},{1,13},{5,9},{9,5},{13,1},{2,14},{6,10},... | collective-permute-start | bytes 196616 | tf_op jit(solution)/shard_map/ppermute | solution.py:403
  37.2 8.0 %collective-permute-start.13 = (bf16[1024,128]{1,0:T(8,128)(2,1)}, bf16[1024,128]{1,0:T(8,128)(2,1)S(1)}, u32[]{:S(2)}, u32[]{:S(2)}) collective-permute-start(bf16[1024,128]{1,0:T(8,128)(2,1)} %get-tuple-element.52.refs_0_), channel_id=1, source_target_pairs={{0,2},{1,3},{4,6},{5,7},{8,10},{9,11},{12,14},{13,15},{16,18},{17,... | collective-permute-start | bytes 786440 | tf_op jit(solution)/shard_map/ppermute | solution.py:409
  47.6 15.0 %collective-permute-start.14 = (bf16[256,128]{1,0:T(8,128)(2,1)}, bf16[256,128]{1,0:T(8,128)(2,1)S(1)}, u32[]{:S(2)}, u32[]{:S(2)}) collective-permute-start(bf16[256,128]{1,0:T(8,128)(2,1)} %get-tuple-element.54), channel_id=1, source_target_pairs={{0,4},{4,0},{8,12},{12,8},{1,5},{5,1},{9,13},{13,9},{2,6},{6,2},{1... | collective-permute-start | bytes 196616 | tf_op jit(solution)/shard_map/ppermute | solution.py:403
  48.4 14.2 %collective-permute-start.15 = (bf16[256,128]{1,0:T(8,128)(2,1)}, bf16[256,128]{1,0:T(8,128)(2,1)S(1)}, u32[]{:S(2)}, u32[]{:S(2)}) collective-permute-start(bf16[256,128]{1,0:T(8,128)(2,1)} %get-tuple-element.55), channel_id=1, source_target_pairs={{0,8},{4,12},{8,0},{12,4},{1,9},{5,13},{9,1},{13,5},{2,10},{6,14},... | collective-permute-start | bytes 196616 | tf_op jit(solution)/shard_map/ppermute | solution.py:403
  51.2 11.4 %collective-permute-start.16 = (bf16[256,128]{1,0:T(8,128)(2,1)}, bf16[256,128]{1,0:T(8,128)(2,1)S(1)}, u32[]{:S(2)}, u32[]{:S(2)}) collective-permute-start(bf16[256,128]{1,0:T(8,128)(2,1)} %get-tuple-element.56), channel_id=1, source_target_pairs={{0,12},{4,8},{8,4},{12,0},{1,13},{5,9},{9,5},{13,1},{2,14},{6,10},... | collective-permute-start | bytes 196616 | tf_op jit(solution)/shard_map/ppermute | solution.py:403
  52.0 5.6 %collective-permute-start.3 = (s32[2,1024]{1,0:T(2,128)S(1)}, s32[2,1024]{1,0:T(2,128)S(1)}, u32[]{:S(2)}, u32[]{:S(2)}) collective-permute-start(s32[2,1024]{1,0:T(2,128)S(1)} %copy-done.9), channel_id=1, source_target_pairs={{0,2},{1,3},{4,6},{5,7},{8,10},{9,11},{12,14},{13,15},{16,18},{17,... | collective-permute-start | bytes 24584 | tf_op jit(solution)/shard_map/ppermute | solution.py:409
  65.8 7.4 %collective-permute-start.18 = (bf16[256,128]{1,0:T(8,128)(2,1)}, bf16[256,128]{1,0:T(8,128)(2,1)S(1)}, u32[]{:S(2)}, u32[]{:S(2)}) collective-permute-start(bf16[256,128]{1,0:T(8,128)(2,1)} %get-tuple-element.61), channel_id=1, source_target_pairs={{0,8},{4,12},{8,0},{12,4},{1,9},{5,13},{9,1},{13,5},{2,10},{6,14},... | collective-permute-start | bytes 196616 | tf_op jit(solution)/shard_map/ppermute | solution.py:403
  69.4 6.3 %collective-permute-start.19 = (bf16[256,128]{1,0:T(8,128)(2,1)}, bf16[256,128]{1,0:T(8,128)(2,1)S(1)}, u32[]{:S(2)}, u32[]{:S(2)}) collective-permute-start(bf16[256,128]{1,0:T(8,128)(2,1)} %get-tuple-element.62), channel_id=1, source_target_pairs={{0,12},{4,8},{8,4},{12,0},{1,13},{5,9},{9,5},{13,1},{2,14},{6,10},... | collective-permute-start | bytes 196616 | tf_op jit(solution)/shard_map/ppermute | solution.py:403
  70.2 5.5 %collective-permute-start.20 = (bf16[256,128]{1,0:T(8,128)(2,1)}, bf16[256,128]{1,0:T(8,128)(2,1)S(1)}, u32[]{:S(2)}, u32[]{:S(2)}) collective-permute-start(bf16[256,128]{1,0:T(8,128)(2,1)} %get-tuple-element.59.refs_11_), channel_id=1, source_target_pairs={{0,1},{1,0},{2,3},{3,2},{4,5},{5,4},{6,7},{7,6},{8,9},{9,8},{10,11... | collective-permute-start | bytes 196616 | tf_op jit(solution)/shard_map/ppermute | solution.py:412
  84.7 11.1 %collective-permute-start.27 = (bf16[1344,128]{1,0:T(8,128)(2,1)S(1)}, bf16[1344,128]{1,0:T(8,128)(2,1)S(1)}, u32[]{:S(2)}, u32[]{:S(2)}) collective-permute-start(bf16[1344,128]{1,0:T(8,128)(2,1)S(1)} %dynamic-slice_bitcast_fusion), channel_id=1, source_target_pairs={{0,2},{2,0},{1,3},{3,1},{4,6},{6,4},{5,7},{7,5},{8,10},{10,8},{9,1... | collective-permute-start | bytes 1032200 | tf_op jit(solution)/shard_map/ppermute | solution.py:406
  87.2 8.5 %collective-permute-start.25 = (bf16[256,128]{1,0:T(8,128)(2,1)}, bf16[256,128]{1,0:T(8,128)(2,1)S(1)}, u32[]{:S(2)}, u32[]{:S(2)}) collective-permute-start(bf16[256,128]{1,0:T(8,128)(2,1)} %get-tuple-element.66), channel_id=1, source_target_pairs={{0,8},{4,12},{8,0},{12,4},{1,9},{5,13},{9,1},{13,5},{2,10},{6,14},... | collective-permute-start | bytes 196616 | tf_op jit(solution)/shard_map/ppermute | solution.py:403
  88.6 7.1 %collective-permute-start.26 = (bf16[256,128]{1,0:T(8,128)(2,1)}, bf16[256,128]{1,0:T(8,128)(2,1)S(1)}, u32[]{:S(2)}, u32[]{:S(2)}) collective-permute-start(bf16[256,128]{1,0:T(8,128)(2,1)} %get-tuple-element.67), channel_id=1, source_target_pairs={{0,12},{4,8},{8,4},{12,0},{1,13},{5,9},{9,5},{13,1},{2,14},{6,10},... | collective-permute-start | bytes 196616 | tf_op jit(solution)/shard_map/ppermute | solution.py:403
  99.2 7.3 %collective-permute-start.30 = (bf16[336,128]{1,0:T(8,128)(2,1)}, bf16[336,128]{1,0:T(8,128)(2,1)S(1)}, u32[]{:S(2)}, u32[]{:S(2)}) collective-permute-start(bf16[336,128]{1,0:T(8,128)(2,1)} %get-tuple-element.72), channel_id=1, source_target_pairs={{0,12},{4,8},{8,4},{12,0},{1,13},{5,9},{9,5},{13,1},{2,14},{6,10},... | collective-permute-start | bytes 258056 | tf_op jit(solution)/shard_map/ppermute | solution.py:403
  101.5 7.7 %collective-permute-start.29 = (bf16[336,128]{1,0:T(8,128)(2,1)}, bf16[336,128]{1,0:T(8,128)(2,1)S(1)}, u32[]{:S(2)}, u32[]{:S(2)}) collective-permute-start(bf16[336,128]{1,0:T(8,128)(2,1)} %get-tuple-element.71), channel_id=1, source_target_pairs={{0,8},{4,12},{8,0},{12,4},{1,9},{5,13},{9,1},{13,5},{2,10},{6,14},... | collective-permute-start | bytes 258056 | tf_op jit(solution)/shard_map/ppermute | solution.py:403
  101.9 7.2 %collective-permute-start.28 = (bf16[336,128]{1,0:T(8,128)(2,1)}, bf16[336,128]{1,0:T(8,128)(2,1)S(1)}, u32[]{:S(2)}, u32[]{:S(2)}) collective-permute-start(bf16[336,128]{1,0:T(8,128)(2,1)} %get-tuple-element.70), channel_id=1, source_target_pairs={{0,4},{4,0},{8,12},{12,8},{1,5},{5,1},{9,13},{13,9},{2,6},{6,2},{1... | collective-permute-start | bytes 258056 | tf_op jit(solution)/shard_map/ppermute | solution.py:403
  110.1 7.1 %collective-permute-start.33 = (bf16[336,128]{1,0:T(8,128)(2,1)S(1)}, bf16[336,128]{1,0:T(8,128)(2,1)S(1)}, u32[]{:S(2)}, u32[]{:S(2)}) collective-permute-start(bf16[336,128]{1,0:T(8,128)(2,1)S(1)} %add_convert_fusion), channel_id=1, source_target_pairs={{0,12},{4,8},{8,4},{12,0},{1,13},{5,9},{9,5},{13,1},{2,14},{6,10},... | collective-permute-start | bytes 258056 | tf_op jit(solution)/shard_map/ppermute | solution.py:403
  111.7 7.6 %collective-permute-start.32 = (bf16[336,128]{1,0:T(8,128)(2,1)S(1)}, bf16[336,128]{1,0:T(8,128)(2,1)S(1)}, u32[]{:S(2)}, u32[]{:S(2)}) collective-permute-start(bf16[336,128]{1,0:T(8,128)(2,1)S(1)} %add_convert_fusion), channel_id=1, source_target_pairs={{0,8},{4,12},{8,0},{12,4},{1,9},{5,13},{9,1},{13,5},{2,10},{6,14},... | collective-permute-start | bytes 258056 | tf_op jit(solution)/shard_map/ppermute | solution.py:403
  111.7 7.6 %collective-permute-start.31 = (bf16[336,128]{1,0:T(8,128)(2,1)S(1)}, bf16[336,128]{1,0:T(8,128)(2,1)S(1)}, u32[]{:S(2)}, u32[]{:S(2)}) collective-permute-start(bf16[336,128]{1,0:T(8,128)(2,1)S(1)} %add_convert_fusion), channel_id=1, source_target_pairs={{0,4},{4,0},{8,12},{12,8},{1,5},{5,1},{9,13},{13,9},{2,6},{6,2},{1... | collective-permute-start | bytes 258056 | tf_op jit(solution)/shard_map/ppermute | solution.py:403
  119.3 9.9 %collective-permute-start.34 = (bf16[1344,128]{1,0:T(8,128)(2,1)S(1)}, bf16[1344,128]{1,0:T(8,128)(2,1)S(1)}, u32[]{:S(2)}, u32[]{:S(2)}) collective-permute-start(bf16[1344,128]{1,0:T(8,128)(2,1)S(1)} %pad_maximum_fusion.refs_0_), channel_id=1, source_target_pairs={{0,2},{2,0},{1,3},{3,1},{4,6},{6,4},{5,7},{7,5},{8,10},{10,8},{9,1... | collective-permute-start | bytes 1032200 | tf_op jit(solution)/shard_map/ppermute | solution.py:406
  (42 other events, 116.0 us)

commit v4 on v3

--- a/solution.py
+++ b/solution.py
@@ -11,13 +11,14 @@
 LANES = 128
 VMEM = pl.BlockSpec(memory_space=pltpu.VMEM)
 ANY = pl.BlockSpec(memory_space=pl.ANY)
+HBM = pl.BlockSpec(memory_space=pltpu.HBM)
 
 
 def shape(dims, kind):
     return jax.ShapeDtypeStruct(tuple(dims), kind)
 
 
-def run(kernel, outs, args, scratch=(), copies=1, flops=0):
+def run(kernel, outs, args, scratch=(), copies=1, far=()):
     b, c = len(args), len(outs)
 
     def body(*refs):
@@ -27,11 +28,11 @@
     return pl.pallas_call(
         body,
         out_shape=list(outs),
-        in_specs=[ANY] * len(args),
+        in_specs=[HBM if i in far else ANY for i in range(len(args))],
         out_specs=[VMEM] * len(outs),
         scratch_shapes=list(scratch) + [pltpu.SemaphoreType.DMA((copies,))],
-        compiler_params=pltpu.CompilerParams(vmem_limit_bytes=56 * 1024 * 1024),
-        cost_estimate=pl.CostEstimate(flops=flops, bytes_accessed=moved, transcendentals=0),
+        compiler_params=pltpu.CompilerParams(vmem_limit_bytes=24 * 1024 * 1024),
+        cost_estimate=pl.CostEstimate(flops=0, bytes_accessed=moved, transcendentals=0),
     )(*args)
 
 
@@ -83,22 +84,6 @@
     return -(-cap // LANES) * LANES
 
 
-def ask_kernel(sems, given, pieces, scratch):
-    rows_any, counts_any = given
-    rows_ref, counts = scratch
-    end(begin(sems, [(rows_any, rows_ref), (counts_any, counts)]))
-    z = lax.axis_index("node")
-    batches, _, cap = rows_ref.shape
-    slot = lax.broadcasted_iota(I32, (1, cap), 1)
-    for k, piece in enumerate(pieces):
-        owner = z ^ k
-        if piece.shape[1] != cap:
-            piece[...] = jnp.full(piece.shape, -1, I32)
-        for b in range(batches):
-            row = rows_ref[b, pl.ds(owner, 1), :]
-            piece[b : b + 1, :cap] = jnp.where(slot < counts[b, owner], row, -1)
-
-
 def give(held, pieces):
     cap = pieces[0].shape[0]
     room = padded(cap)
@@ -106,39 +91,69 @@
         piece[...] = held[k * room : k * room + cap, :]
 
 
+def narrow_kernel(sems, given, made, scratch):
+    end(begin(sems, [(given[0], scratch[0])]))
+    made[0][...] = scratch[0][...].astype(BF)
+
+
+def bundle_kernel(batch, sems, given, made, scratch):
+    narrow_any, asked_any = given
+    (out_ref,), (asked,) = made, scratch
+    rows = narrow_any.shape[0]
+    end(begin(sems, [(narrow_any, out_ref.at[:rows, :]), (asked_any, asked)]))
+    lines = (out_ref.shape[0] - rows) // 2
+    number = jnp.concatenate(
+        [asked[batch : batch + 1, j * LANES : (j + 1) * LANES] for j in range(lines)], axis=0
+    )
+    high = jnp.floor(number.astype(F32) * (1.0 / 64.0))
+    low = number.astype(F32) - 64.0 * high
+    out_ref[rows:, :] = jnp.concatenate([high, low], axis=0).astype(BF)
+
+
 def serve_kernel(sems, given, made, scratch):
-    *asked_pieces, memory_any = given
-    asked_ref, narrow_ref, *pieces = made
-    memory_ref, held = scratch
+    *asked_pieces, narrow_any = given
+    asked_ref, *pieces = made
+    narrow, held = scratch
     nodes, room = len(asked_pieces), asked_pieces[0].shape[1]
-    pairs = [(memory_any, memory_ref)]
+    pairs = [(narrow_any, narrow)]
     for k, piece in enumerate(asked_pieces):
         pairs.append((piece, asked_ref.at[:, k * room : (k + 1) * room]))
     end(begin(sems, pairs))
-    narrow_ref[...] = memory_ref[...].astype(BF)
     for j in range(nodes * room // LANES):
         span = slice(j * LANES, (j + 1) * LANES)
-        held[span, :] = pick_rows(asked_ref[0:1, span], narrow_ref[...])
+        held[span, :] = pick_rows(asked_ref[0:1, span], narrow[...])
     give(held, pieces)
 
 
-def base_kernel(batch, sems, given, made, scratch):
-    asked_any, before_any, memory_any, handed_any = given
-    base_ref, put_ref, rows_ref = made
-    asked, before, handed, narrow = scratch
-    begun = begin(
-        sems,
-        [(asked_any, asked), (before_any, before), (memory_any, base_ref), (handed_any, handed)],
-    )
-    end(begun)
-    row = slice(batch, batch + 1)
-    put_ref[...] = jnp.where(lax.axis_index("seg") == 0, asked[row, :], before[row, :])
+def pick_base(sems, memory_any, handed_any, base_ref, handed_ref, first):
+    @pl.when(lax.axis_index("seg") == 0)
+    def _():
+        end(begin(sems, [(memory_any, base_ref)], first))
 
     @pl.when(lax.axis_index("seg") != 0)
     def _():
-        base_ref[...] = handed[...].astype(F32)
-
-    narrow[...] = base_ref[...].astype(BF)
+        end(begin(sems, [(handed_any, handed_ref)], first))
+        base_ref[...] = handed_ref[: base_ref.shape[0], :].astype(base_ref.dtype)
+
+
+def base_kernel(batch, sems, given, made, scratch):
+    asked_any, narrow_any, handed_any = given
+    put_ref, rows_ref = made
+    asked, handed, narrow = scratch
+    begun = begin(sems, [(asked_any, asked)])
+    pick_base(sems, narrow_any, handed_any, narrow, handed, 1)
+    end(begun)
+    put_ref[...] = asked[batch : batch + 1, :]
+
+    @pl.when(lax.axis_index("seg") != 0)
+    def _():
+        top = narrow.shape[0]
+        lines = (handed.shape[0] - top) // 2
+        digits = handed[top:, :].astype(F32)
+        number = digits[:lines, :] * 64.0 + digits[lines:, :]
+        for j in range(lines):
+            put_ref[:, j * LANES : (j + 1) * LANES] = number[j : j + 1, :].astype(I32)
+
     for j in range(rows_ref.shape[0] // LANES):
         span = slice(j * LANES, (j + 1) * LANES)
         rows_ref[span, :] = pick_rows(asked[batch + 1 : batch + 2, span], narrow[...])
@@ -203,9 +218,11 @@
 
 
 def update_kernel(sems, given, made, scratch):
-    put_any, values_any, base_any = given
-    put, values, base = scratch
-    end(begin(sems, [(put_any, put), (values_any, values), (base_any, base)]))
+    put_any, values_any, memory_any, handed_any = given
+    put, values, base, handed = scratch
+    begun = begin(sems, [(put_any, put), (values_any, values)])
+    pick_base(sems, memory_any, handed_any, base, handed, 2)
+    end(begun)
     set_rows(put[...], values[...], base, made[0])
 
 
@@ -235,14 +252,11 @@
     return p * (1.0 - 2.0 * odd)
 
 
-def batch_kernel(nodes, batch, final, sems, given, made, scratch):
-    dst_any, elapsed_any, edge_any, edge_other_any, w_in_any, w_hid_any, bias_any = given[:7]
-    freq_any, phase_any, counts_any, up_any = given[7:11]
-    own_pieces, other_pieces = given[11 : 11 + nodes], given[11 + nodes : 11 + 2 * nodes]
-    rest = given[11 + 2 * nodes :]
-    prior = len(rest) > 0
-    message, dst, elapsed, edge, w_in, w_hid, bias_ref, freq, phase, counts = scratch[:10]
-    gates, up, fresh = scratch[10:13]
+def batch_kernel(nodes, batch, final, prior, sems, given, made, scratch):
+    facts_any, edge_any, edge_other_any, w_in_any, w_hid_any, up_any = given[:6]
+    own_pieces, other_pieces = given[6 : 6 + nodes], given[6 + nodes : 6 + 2 * nodes]
+    rest = given[6 + 2 * nodes :]
+    message, facts, edge, w_in, w_hid, gates, up, fresh = scratch[:8]
     cap = own_pieces[0].shape[0]
     events = nodes * cap
     z, f = lax.axis_index("node"), lax.axis_index("feat")
@@ -251,37 +265,40 @@
     width = 2 * LANES
     long = message.shape[1]
     thin = edge_any.shape[1]
-    pairs = [(dst_any.at[batch], dst)]
+    pairs = []
     for k in range(nodes):
         at = pl.ds(pl.multiple_of((z ^ k) * cap, cap), cap)
         pairs.append((own_pieces[k], message.at[at, pl.ds(mine, LANES)]))
         pairs.append((other_pieces[k], message.at[at, pl.ds(other, LANES)]))
     early = [
-        (elapsed_any.at[batch], elapsed),
-        (freq_any, freq),
-        (phase_any, phase),
+        (facts_any, facts),
         (edge_any.at[batch], edge.at[pl.ds(pl.multiple_of(f * thin, thin), thin), :]),
         (edge_other_any.at[batch], edge.at[pl.ds(pl.multiple_of((1 - f) * thin, thin), thin), :]),
     ]
-    late = [(w_in_any, w_in), (w_hid_any, w_hid), (bias_any, bias_ref), (counts_any, counts)]
-    late.append((up_any.at[batch], up))
+    late = [(w_in_any, w_in), (w_hid_any, w_hid), (up_any.at[batch], up)]
     if prior:
-        before = scratch[13]
+        before = scratch[8]
         late.append((rest[0], before))
     rows_begun = begin(sems, pairs)
     early_begun = begin(sems, early, len(pairs))
     late_begun = begin(sems, late, len(pairs) + len(early))
     end(early_begun)
-    for j in range(events // LANES):
+    lines = events // LANES
+    top = facts.shape[0] - 8
+    bias_ref = facts[top : top + 4, :]
+    freq, phase = facts[top + 4 : top + 5, :], facts[top + 5 : top + 6, :]
+    dst = [facts[2 * lines * batch + j : 2 * lines * batch + j + 1, :] for j in range(lines)]
+    start = 2 * lines * batch + lines
+    for j in range(lines):
         span = slice(j * LANES, (j + 1) * LANES)
-        angle = down(elapsed[:, span].astype(F32)) * freq[...] + phase[...]
+        angle = down(facts[start + j : start + j + 1, :]) * freq + phase
         message[span, 2 * width : 2 * width + LANES] = cosine(angle).astype(BF)
         message[span, 2 * width + LANES :] = jnp.transpose(edge[:, span].astype(F32)).astype(BF)
     end(rows_begun)
     full = message[:, :width]
     for j in range(events // LANES):
         span = slice(j * LANES, (j + 1) * LANES)
-        message[span, width : 2 * width] = pick_rows(dst[:, span], full)
+        message[span, width : 2 * width] = pick_rows(dst[j].astype(I32), full)
     end(late_begun)
     w_in01 = jnp.concatenate([w_in[0], w_in[1]], axis=1)
     w_hid01 = jnp.concatenate([w_hid[0], w_hid[1]], axis=1)
@@ -304,11 +321,8 @@
             + reset_gate * recur_term
         )
         fresh[span, :] = ((1.0 - update) * candid + update * own).astype(BF)
-        number = lax.broadcasted_iota(I32, (tall, LANES), 0) + i * tall
-        live = number < 0
-        for o in range(nodes):
-            if o * cap < (i + 1) * tall and (o + 1) * cap > i * tall:
-                live = live | ((number >= o * cap) & (number < o * cap + counts[batch, o]))
+        numbers = [down(dst[j]) for j in range(i * tall // LANES, (i + 1) * tall // LANES)]
+        live = jnp.concatenate(numbers, axis=0) >= 0.0
         cotangent = jnp.where(live, up[span, :].astype(F32), 0.0)
         grad_cand = cotangent * (1.0 - update) * (1.0 - candid * candid)
         grad_upd = cotangent * (own - candid) * update * (1.0 - update)
@@ -414,25 +428,37 @@
     def exchange(blocks):
         return [blocks[0]] + [node_swap(blocks[k], k) for k in range(1, nodes)]
 
-    wanted = run(
-        ask_kernel,
-        [shape((batches, room), I32)] * nodes,
-        [req_rows[:, 0, 0], counts],
-        [pltpu.VMEM((batches, nodes, cap), I32), pltpu.SMEM((batches, nodes), I32)],
-        2,
+    live = jnp.arange(cap)[None, None, :] < counts[:, :, None]
+    masked = jnp.where(live, req_rows[:, 0, 0], -1)
+    masked = jnp.pad(masked, ((0, 0), (0, 0), (0, room - cap)), constant_values=-1)
+    wanted = exchange(
+        [lax.dynamic_index_in_dim(masked, z ^ k, 1, keepdims=False) for k in range(nodes)]
     )
     wide_rows = pltpu.VMEM((spread, half), BF)
-    asked, narrow, *served = run(
-        serve_kernel,
-        [shape((batches, spread), I32), shape((node_rows, half), BF)] + [piece] * nodes,
-        exchange(wanted) + [memory_now],
-        [pltpu.VMEM((node_rows, half), F32), wide_rows],
-        nodes + 1,
-    )
-    asked_before = seg_next(asked)
-
     edge_own = jnp.swapaxes(edges[:, 0], 1, 2)
     edge_other = feat_swap(edge_own)
+    lines = events // LANES
+    named = jnp.where(live, dst_slot[:, 0].reshape(live.shape), -1)
+    facts = jnp.stack([named.reshape(batches, events), elapsed[:, 0]], axis=1).astype(F32)
+    facts = facts.reshape(batches * 2 * lines, LANES)
+    rest = jnp.zeros((2, half), F32)
+    facts = jnp.concatenate([facts, bias, freq[None], phase[None], rest], axis=0)
+
+    narrow = run(
+        narrow_kernel,
+        [shape((node_rows, half), BF)],
+        [memory_now, wanted[1], facts],
+        [pltpu.VMEM((node_rows, half), F32)],
+        1,
+        (0,),
+    )[0]
+    asked, *served = run(
+        serve_kernel,
+        [shape((batches, spread), I32)] + [piece] * nodes,
+        wanted + [narrow],
+        [pltpu.VMEM((node_rows, half), BF), wide_rows],
+        nodes + 1,
+    )
 
     chunk = -(-(3 * long + width + 16) // (16 * nodes * segs)) * 16
     total_rows = chunk * nodes * segs
@@ -444,47 +470,52 @@
         final = b + 1 == batches
         own_pieces = exchange(served)
         if not final:
-            handed_memory = seg_next(narrow)
+            bundle = run(
+                lambda *a, b=b: bundle_kernel(b, *a),
+                [shape((node_rows + 2 * spread // LANES, half), BF)],
+                [narrow, asked],
+                [numbers],
+                2,
+            )[0]
+            handed_memory = seg_next(bundle)
         other_pieces = [feat_swap(p) for p in own_pieces]
-        given = [dst_slot, elapsed, edge_own, edge_other, w_input, w_hidden, bias]
-        given = given + [freq[None], phase[None], counts, upstream[:, 0]]
+        given = [facts, edge_own, edge_other, w_input, w_hidden, upstream[:, 0]]
         given = given + own_pieces + other_pieces + ([] if totals is None else [totals])
         rooms = [
             pltpu.VMEM((events, long), BF),
-            pltpu.VMEM((1, events), I32),
-            pltpu.VMEM((1, events), I32),
+            pltpu.VMEM(facts.shape, F32),
             pltpu.VMEM((2 * edges.shape[-1], events), BF),
             pltpu.VMEM(w_input.shape, BF),
             pltpu.VMEM(w_hidden.shape, BF),
-            pltpu.VMEM(bias.shape, F32),
-            pltpu.VMEM((1, freq.shape[0]), F32),
-            pltpu.VMEM((1, freq.shape[0]), F32),
-            pltpu.SMEM((batches, nodes), I32),
             pltpu.VMEM((events, 4 * half), BF),
             pltpu.VMEM((events, half), BF),
             pltpu.VMEM((events, half), BF),
         ]
         if totals is not None:
             rooms.append(pltpu.VMEM((total_rows, half), F32))
-        copies = 12 + 2 * nodes
+        copies = 7 + 2 * nodes
         *fresh, totals = run(
-            lambda *a, b=b, last=final: batch_kernel(nodes, b, last, *a),
+            lambda *a, b=b, last=final, p=totals is not None: batch_kernel(nodes, b, last, p, *a),
             ([piece] * nodes if final else [shape((events, half), BF)])
             + [shape((total_rows, half), BF if final else F32)],
             given,
             rooms,
             copies,
+            (1, 3, 4, 5),
         )
         if not final:
-            values = run(handed_kernel, [piece] * nodes, [fresh[0], seg_next(fresh[0])], [], nodes)
+            hop = seg_next(fresh[0])
+            put, rows = run(
+                lambda *a, b=b: base_kernel(b, *a),
+                [shape((1, spread), I32), shape((spread, half), BF)],
+                [asked, narrow, handed_memory],
+                [numbers, pltpu.VMEM(bundle.shape, BF), pltpu.VMEM((node_rows, half), BF)],
+                2,
+            )
+            values = run(
+                handed_kernel, [piece] * nodes, [fresh[0], hop, rows], [], nodes
+            )
             values = exchange(values)
-            base, put, rows = run(
-                lambda *a, b=b: base_kernel(b, *a),
-                [shape((node_rows, half), F32), shape((1, spread), I32), shape((spread, half), BF)],
-                [asked, asked_before, memory_now, handed_memory],
-                [numbers, numbers] + [pltpu.VMEM((node_rows, half), BF)] * 2,
-                4,
-            )
             values, *served = run(
                 lambda *a, b=b: next_kernel(b, *a),
                 [shape((spread, half), BF)] + [piece] * nodes,
@@ -495,11 +526,12 @@
             memory_now = run(
                 update_kernel,
                 [shape((node_rows, half), F32)],
-                [put, values, base],
-                [line, wide_rows, block],
+                [put, values, memory_now, handed_memory],
+                [line, wide_rows, block, pltpu.VMEM(bundle.shape, BF)],
                 3,
             )[0]
-            narrow = memory_now.astype(BF)
+            if b + 2 < batches:
+                narrow = memory_now.astype(BF)
         else:
             returned = exchange(fresh)
             memory_out = run(

time: 133 us -> 117 us (0.88)
  Pallas kernels: 36.6 us -> 22.1 us
  starting transfers between devices: 46 us -> 40.7 us
  waiting for transfers between devices: 40.1 us -> 44.4 us
  local copies, waits for them, and re-layouts: 7.69 us -> 5.9 us
    pallas_call x11 -> x12, Pallas kernels: 36.6 us -> 22.1 us  [run(): pl.pallas_call(body, out_shape=list(outs), in_specs=[HBM if i in far else...]
    ppermute x3 -> x2, starting transfers between devices: 9 us -> 4.73 us  [seg_next(): return lax.ppermute(block, 'seg', [(i, i + 1) for i in range(segs - 1)])]
    ppermute x2, waiting for transfers between devices: 1.64 us -> 5.79 us  [seg_swap(): return lax.ppermute(block, 'seg', [(i, i ^ x) for i in range(segs)])]
    ppermute x3 -> x2, waiting for transfers between devices: 8 us -> 4.9 us  [seg_next(): return lax.ppermute(block, 'seg', [(i, i + 1) for i in range(segs - 1)])]
    ppermute x21, waiting for transfers between devices: 28.3 us -> 31.2 us  [node_swap(): return lax.ppermute(block, 'node', [(i, i ^ k) for i in range(nodes)])]
    unnamed x62 -> x30, local copies, waits for them, and re-layouts: 6.68 us -> 4.34 us
    select_n x0 -> x2, other arithmetic: none -> 1.48 us  [the longest x1 0.77 us: local(): masked = jnp.where(live, req_rows[:, 0, 0], -1)]
  transfers between devices with their start and end apart: 35 -> 34, of which waited for: 19 -> 20; matrix products, arithmetic and copies ran while one was open for 0% -> 3% of each run, Pallas kernels for 18% -> 9%
where the time goes in v4:
time: 117 us
  waiting for transfers between devices  44.4 us (38%)
  starting transfers between devices  40.7 us (35%)
  Pallas kernels  22.1 us (19%)
  local copies, waits for them, and re-layouts  5.9 us (5%)
  other arithmetic  2.28 us (2%)
    ppermute x21, starting transfers between devices, node_swap(): return lax.ppermute(block, 'node', [(i, i ^ k) for i in range(nodes)])  32.3 us
    ppermute x21, waiting for transfers between devices, node_swap(): return lax.ppermute(block, 'node', [(i, i ^ k) for i in range(nodes)])  31.2 us
    pallas_call x12, Pallas kernels, run(): pl.pallas_call(body, out_shape=list(outs), in_specs=[HBM if i in far else...  22.1 us
    ppermute x2, waiting for transfers between devices, seg_swap(): return lax.ppermute(block, 'seg', [(i, i ^ x) for i in range(segs)])  5.79 us
    ppermute x2, waiting for transfers between devices, seg_next(): return lax.ppermute(block, 'seg', [(i, i + 1) for i in range(segs - 1)])  4.9 us
    ppermute x2, starting transfers between devices, seg_next(): return lax.ppermute(block, 'seg', [(i, i + 1) for i in range(segs - 1)])  4.73 us
    unnamed x30, local copies, waits for them, and re-layouts  4.34 us
    ppermute x2, starting transfers between devices, seg_swap(): return lax.ppermute(block, 'seg', [(i, i ^ x) for i in range(segs)])  2.61 us
  transfers between devices with their start and end apart: 34, of which 20 were waited for; matrix products, arithmetic and copies ran while one was open for 3% of the time, Pallas kernels for 9%

profile of v4, /device:TPU:0, one launch (start us, length us, event | category | flops | bytes accessed | tf_op | source)
XLA Modules:
  0.0 116.5 jit_solution(10960571146604425516)
XLA Ops:
  1.5 3.1 %collective-permute-start = (s32[2,256]{1,0:T(2,128)S(1)}, s32[2,256]{1,0:T(2,128)S(1)}, u32[]{:S(2)}, u32[]{:S(2)}) collective-permute-start(s32[2,256]{1,0:T(2,128)S(1)} %bitcast.42), channel_id=1, source_target_pairs={{0,4},{4,0},{8,12},{12,8},{1,5},{5,1},{9,13},{13,9},{2,6},{6,2},{1... | collective-permute-start | bytes 6152 | tf_op jit(solution)/shard_map/ppermute | solution.py:417
  4.5 2.6 %collective-permute-start.1 = (s32[2,256]{1,0:T(2,128)S(1)}, s32[2,256]{1,0:T(2,128)S(1)}, u32[]{:S(2)}, u32[]{:S(2)}) collective-permute-start(s32[2,256]{1,0:T(2,128)S(1)} %bitcast.43), channel_id=1, source_target_pairs={{0,8},{4,12},{8,0},{12,4},{1,9},{5,13},{9,1},{13,5},{2,10},{6,14},... | collective-permute-start | bytes 6152 | tf_op jit(solution)/shard_map/ppermute | solution.py:417
  14.1 3.4 %collective-permute-start.3 = (bf16[2064,128]{1,0:T(8,128)(2,1)S(1)}, bf16[2064,128]{1,0:T(8,128)(2,1)S(1)}, u32[]{:S(2)}, u32[]{:S(2)}) collective-permute-start(bf16[2064,128]{1,0:T(8,128)(2,1)S(1)} %shard_map.149), channel_id=1, source_target_pairs={{0,2},{1,3},{4,6},{5,7},{8,10},{9,11},{12,14},{13,15},{16,18},{17,... | collective-permute-start | bytes 1585160 | tf_op jit(solution)/shard_map/ppermute | solution.py:423
  17.7 3.4 %collective-permute-start.6 = (bf16[256,128]{1,0:T(8,128)(2,1)S(1)}, bf16[256,128]{1,0:T(8,128)(2,1)S(1)}, u32[]{:S(2)}, u32[]{:S(2)}) collective-permute-start(bf16[256,128]{1,0:T(8,128)(2,1)S(1)} %get-tuple-element.39), channel_id=1, source_target_pairs={{0,8},{4,12},{8,0},{12,4},{1,9},{5,13},{9,1},{13,5},{2,10},{6,14},... | collective-permute-start | bytes 196616 | tf_op jit(solution)/shard_map/ppermute | solution.py:417
  22.2 3.2 %collective-permute-done.6.refs_8_ = bf16[256,128]{1,0:T(8,128)(2,1)S(1)} collective-permute-done((bf16[256,128]{1,0:T(8,128)(2,1)S(1)}, bf16[256,128]{1,0:T(8,128)(2,1)S(1)}, u32[]{:S(2)}, u32[]{:S(2)}) %collective-permute-start.6) | collective-permute-done | bytes 65568 | tf_op jit(solution)/shard_map/ppermute | solution.py:417
  25.4 1.9 %collective-permute-done.7.refs_9_ = bf16[256,128]{1,0:T(8,128)(2,1)S(1)} collective-permute-done((bf16[256,128]{1,0:T(8,128)(2,1)S(1)}, bf16[256,128]{1,0:T(8,128)(2,1)S(1)}, u32[]{:S(2)}, u32[]{:S(2)}) %collective-permute-start.7) | collective-permute-done | bytes 65568 | tf_op jit(solution)/shard_map/ppermute | solution.py:417
  29.4 5.0 %shard_map.151 = (bf16[1024,128]{1,0:T(8,128)(2,1)S(1)}, f32[2688,128]{1,0:T(8,128)S(1)}) custom-call(f32[40,128]{1,0:T(8,128)S(1)} %copy-done.8, bf16[2,64,1024]{2,1,0:T(8,128)(2,1)S(1)} %bitcast.35, bf16[2,64,1024]{2,1,0:T(8,128)(2,1)S(1)} %collective-permute-done.4.refs_2_, bf16[3,768,128]{2,1,0:T(8,128)(2,1)S(1)} %copy-done.2, ...), custom_call_target="tpu_custom_call" | custom-call | bytes 4018176 | tf_op jit(solution)/shard_map/pallas_call | solution.py:28
  37.2 4.9 %collective-permute-done.12.refs_1_ = bf16[1024,128]{1,0:T(8,128)(2,1)S(1)} collective-permute-done((bf16[1024,128]{1,0:T(8,128)(2,1)S(1)}, bf16[1024,128]{1,0:T(8,128)(2,1)S(1)}, u32[]{:S(2)}, u32[]{:S(2)}) %collective-permute-start.12) | collective-permute-done | bytes 262176 | tf_op jit(solution)/shard_map/ppermute | solution.py:423
  47.5 4.2 %collective-permute-done.14.refs_5_ = bf16[256,128]{1,0:T(8,128)(2,1)S(1)} collective-permute-done((bf16[256,128]{1,0:T(8,128)(2,1)S(1)}, bf16[256,128]{1,0:T(8,128)(2,1)S(1)}, u32[]{:S(2)}, u32[]{:S(2)}) %collective-permute-start.14) | collective-permute-done | bytes 65568 | tf_op jit(solution)/shard_map/ppermute | solution.py:417
  51.7 1.7 %shard_map.153 = (bf16[1024,128]{1,0:T(8,128)(2,1)S(1)}, bf16[256,128]{1,0:T(8,128)(2,1)}, bf16[256,128]{1,0:T(8,128)(2,1)S(1)}, bf16[256,128]{1,0:T(8,128)(2,1)S(1)}, bf16[256,128]{1,0:T(8,128)(2,1)S(1)}) custom-call(s32[2,1024]{1,0:T(2,128)S(1)} %get-tuple-element.34.refs_1_.refs_0_, s32[1,1024]{1,0:T(1,128)S(1)} %get-tuple-element.35.refs_1_.refs_0_, ...), custom_call_target="tpu_custom_call" | custom-call | bytes 1060864 | tf_op jit(solution)/shard_map/pallas_call | solution.py:28
  55.4 1.7 %collective-permute-start.17 = (bf16[256,128]{1,0:T(8,128)(2,1)S(1)}, bf16[256,128]{1,0:T(8,128)(2,1)}, u32[]{:S(2)}, u32[]{:S(2)}) collective-permute-start(bf16[256,128]{1,0:T(8,128)(2,1)S(1)} %get-tuple-element.49), channel_id=1, source_target_pairs={{0,8},{4,12},{8,0},{12,4},{1,9},{5,13},{9,1},{13,5},{2,10},{6,14},... | collective-permute-start | bytes 196616 | tf_op jit(solution)/shard_map/ppermute | solution.py:417
  59.0 2.8 %collective-permute-done.17.refs_8_ = bf16[256,128]{1,0:T(8,128)(2,1)} collective-permute-done((bf16[256,128]{1,0:T(8,128)(2,1)S(1)}, bf16[256,128]{1,0:T(8,128)(2,1)}, u32[]{:S(2)}, u32[]{:S(2)}) %collective-permute-start.17) | collective-permute-done | bytes 65568 | tf_op jit(solution)/shard_map/ppermute | solution.py:417
  66.5 5.0 %shard_map.155 = (bf16[256,128]{1,0:T(8,128)(2,1)S(1)}, bf16[256,128]{1,0:T(8,128)(2,1)S(1)}, bf16[256,128]{1,0:T(8,128)(2,1)S(1)}, bf16[256,128]{1,0:T(8,128)(2,1)S(1)}, bf16[2688,128]{1,0:T(8,128)(2,1)S(1)}) custom-call(f32[40,128]{1,0:T(8,128)S(1)} %copy-done.9, bf16[2,64,1024]{2,1,0:T(8,128)(2,1)S(1)} %bitcast.36, ...), custom_call_target="tpu_custom_call" | custom-call | bytes 4706304 | tf_op jit(solution)/shard_map/pallas_call | solution.py:28
  71.6 2.5 %collective-permute-start.26 = (bf16[1344,128]{1,0:T(8,128)(2,1)S(1)}, bf16[1344,128]{1,0:T(8,128)(2,1)S(1)}, u32[]{:S(2)}, u32[]{:S(2)}) collective-permute-start(bf16[1344,128]{1,0:T(8,128)(2,1)S(1)} %dynamic-slice_bitcast_fusion), channel_id=1, source_target_pairs={{0,2},{2,0},{1,3},{3,1},{4,6},{6,4},{5,7},{7,5},{8,10},{10,8},{9,1... | collective-permute-start | bytes 1032200 | tf_op jit(solution)/shard_map/ppermute | solution.py:420
  74.1 2.1 %collective-permute-start.24 = (bf16[256,128]{1,0:T(8,128)(2,1)S(1)}, bf16[256,128]{1,0:T(8,128)(2,1)S(1)}, u32[]{:S(2)}, u32[]{:S(2)}) collective-permute-start(bf16[256,128]{1,0:T(8,128)(2,1)S(1)} %get-tuple-element.54), channel_id=1, source_target_pairs={{0,8},{4,12},{8,0},{12,4},{1,9},{5,13},{9,1},{13,5},{2,10},{6,14},... | collective-permute-start | bytes 196616 | tf_op jit(solution)/shard_map/ppermute | solution.py:417
  76.2 2.2 %collective-permute-start.25 = (bf16[256,128]{1,0:T(8,128)(2,1)S(1)}, bf16[256,128]{1,0:T(8,128)(2,1)S(1)}, u32[]{:S(2)}, u32[]{:S(2)}) collective-permute-start(bf16[256,128]{1,0:T(8,128)(2,1)S(1)} %get-tuple-element.55), channel_id=1, source_target_pairs={{0,12},{4,8},{8,4},{12,0},{1,13},{5,9},{9,5},{13,1},{2,14},{6,10},... | collective-permute-start | bytes 196616 | tf_op jit(solution)/shard_map/ppermute | solution.py:417
  79.1 3.6 %collective-permute-done.24.refs_4_.refs_3_ = bf16[256,128]{1,0:T(8,128)(2,1)S(1)} collective-permute-done((bf16[256,128]{1,0:T(8,128)(2,1)S(1)}, bf16[256,128]{1,0:T(8,128)(2,1)S(1)}, u32[]{:S(2)}, u32[]{:S(2)}) %collective-permute-start.24) | collective-permute-done | bytes 65568 | tf_op jit(solution)/shard_map/ppermute | solution.py:417
  87.8 5.7 %collective-permute-done.28 = bf16[336,128]{1,0:T(8,128)(2,1)S(1)} collective-permute-done((bf16[336,128]{1,0:T(8,128)(2,1)S(1)}, bf16[336,128]{1,0:T(8,128)(2,1)S(1)}, u32[]{:S(2)}, u32[]{:S(2)}) %collective-permute-start.28) | collective-permute-done | bytes 86048 | tf_op jit(solution)/shard_map/ppermute | solution.py:417
  93.5 2.1 %collective-permute-start.32 = (bf16[336,128]{1,0:T(8,128)(2,1)S(1)}, bf16[336,128]{1,0:T(8,128)(2,1)S(1)}, u32[]{:S(2)}, u32[]{:S(2)}) collective-permute-start(bf16[336,128]{1,0:T(8,128)(2,1)S(1)} %add_convert_fusion), channel_id=1, source_target_pairs={{0,12},{4,8},{8,4},{12,0},{1,13},{5,9},{9,5},{13,1},{2,14},{6,10},... | collective-permute-start | bytes 258056 | tf_op jit(solution)/shard_map/ppermute | solution.py:417
  98.0 2.8 %collective-permute-done.32 = bf16[336,128]{1,0:T(8,128)(2,1)S(1)} collective-permute-done((bf16[336,128]{1,0:T(8,128)(2,1)S(1)}, bf16[336,128]{1,0:T(8,128)(2,1)S(1)}, u32[]{:S(2)}, u32[]{:S(2)}) %collective-permute-start.32) | collective-permute-done | bytes 86048 | tf_op jit(solution)/shard_map/ppermute | solution.py:417
  100.7 3.5 %collective-permute-done.31 = bf16[336,128]{1,0:T(8,128)(2,1)S(1)} collective-permute-done((bf16[336,128]{1,0:T(8,128)(2,1)S(1)}, bf16[336,128]{1,0:T(8,128)(2,1)S(1)}, u32[]{:S(2)}, u32[]{:S(2)}) %collective-permute-start.31) | collective-permute-done | bytes 86048 | tf_op jit(solution)/shard_map/ppermute | solution.py:417
  105.8 2.7 %shard_map.156 = f32[2048,128]{1,0:T(8,128)} custom-call(s32[2,1024]{1,0:T(2,128)S(1)} %get-tuple-element.34.refs_1_.refs_0_, f32[2048,128]{1,0:T(8,128)S(1)} %shard_map.154.refs_1_, bf16[256,128]{1,0:T(8,128)(2,1)S(1)} %get-tuple-element.52.refs_2_, bf16[256,128]{1,0:T(8,128)(2,1)S(1)} %collective-permute-done.23.refs_3_.refs_2_, ...), custom_call_target="tpu_custom_call" | custom-call | bytes 2367488 | tf_op jit(solution)/shard_map/pallas_call | solution.py:28
  108.5 5.8 %collective-permute-done.33.refs_1_ = bf16[1344,128]{1,0:T(8,128)(2,1)S(1)} collective-permute-done((bf16[1344,128]{1,0:T(8,128)(2,1)S(1)}, bf16[1344,128]{1,0:T(8,128)(2,1)S(1)}, u32[]{:S(2)}, u32[]{:S(2)}) %collective-permute-start.33) | collective-permute-done | bytes 344096 | tf_op jit(solution)/shard_map/ppermute | solution.py:420
  114.3 2.1 %shard_map.158 = (f32[3,768,128]{2,1,0:T(8,128)}, f32[3,256,128]{2,1,0:T(8,128)}, f32[4,128]{1,0:T(4,128)}) custom-call(bf16[1344,128]{1,0:T(8,128)(2,1)S(1)} %pad_maximum_fusion.refs_0_, bf16[1344,128]{1,0:T(8,128)(2,1)S(1)} %collective-permute-done.33.refs_1_), custom_call_target="tpu_custom_call" | custom-call | bytes 2263040 | tf_op jit(solution)/shard_map/pallas_call | solution.py:28
  (98 shorter events, 37.4 us)
Async XLA Ops:
  1.5 8.7 %collective-permute-start = (s32[2,256]{1,0:T(2,128)S(1)}, s32[2,256]{1,0:T(2,128)S(1)}, u32[]{:S(2)}, u32[]{:S(2)}) collective-permute-start(s32[2,256]{1,0:T(2,128)S(1)} %bitcast.42), channel_id=1, source_target_pairs={{0,4},{4,0},{8,12},{12,8},{1,5},{5,1},{9,13},{13,9},{2,6},{6,2},{1... | collective-permute-start | bytes 6152 | tf_op jit(solution)/shard_map/ppermute | solution.py:417
  4.5 7.0 %collective-permute-start.1 = (s32[2,256]{1,0:T(2,128)S(1)}, s32[2,256]{1,0:T(2,128)S(1)}, u32[]{:S(2)}, u32[]{:S(2)}) collective-permute-start(s32[2,256]{1,0:T(2,128)S(1)} %bitcast.43), channel_id=1, source_target_pairs={{0,8},{4,12},{8,0},{12,4},{1,9},{5,13},{9,1},{13,5},{2,10},{6,14},... | collective-permute-start | bytes 6152 | tf_op jit(solution)/shard_map/ppermute | solution.py:417
  7.1 5.4 %collective-permute-start.2 = (s32[2,256]{1,0:T(2,128)S(1)}, s32[2,256]{1,0:T(2,128)S(1)}, u32[]{:S(2)}, u32[]{:S(2)}) collective-permute-start(s32[2,256]{1,0:T(2,128)S(1)} %bitcast.44), channel_id=1, source_target_pairs={{0,12},{4,8},{8,4},{12,0},{1,13},{5,9},{9,5},{13,1},{2,14},{6,10},... | collective-permute-start | bytes 6152 | tf_op jit(solution)/shard_map/ppermute | solution.py:417
  14.1 21.6 %collective-permute-start.3 = (bf16[2064,128]{1,0:T(8,128)(2,1)S(1)}, bf16[2064,128]{1,0:T(8,128)(2,1)S(1)}, u32[]{:S(2)}, u32[]{:S(2)}) collective-permute-start(bf16[2064,128]{1,0:T(8,128)(2,1)S(1)} %shard_map.149), channel_id=1, source_target_pairs={{0,2},{1,3},{4,6},{5,7},{8,10},{9,11},{12,14},{13,15},{16,18},{17,... | collective-permute-start | bytes 1585160 | tf_op jit(solution)/shard_map/ppermute | solution.py:423
  17.6 11.1 %collective-permute-start.4 = (bf16[2,64,1024]{2,1,0:T(8,128)(2,1)S(1)}, bf16[2,64,1024]{2,1,0:T(8,128)(2,1)S(1)}, u32[]{:S(2)}, u32[]{:S(2)}) collective-permute-start(bf16[2,64,1024]{2,1,0:T(8,128)(2,1)S(1)} %bitcast.34), channel_id=1, source_target_pairs={{0,1},{1,0},{2,3},{3,2},{4,5},{5,4},{6,7},{7,6},{8,9},{9,8},{10,11... | collective-permute-start | bytes 786440 | tf_op jit(solution)/shard_map/ppermute | solution.py:426
  17.7 7.6 %collective-permute-start.6 = (bf16[256,128]{1,0:T(8,128)(2,1)S(1)}, bf16[256,128]{1,0:T(8,128)(2,1)S(1)}, u32[]{:S(2)}, u32[]{:S(2)}) collective-permute-start(bf16[256,128]{1,0:T(8,128)(2,1)S(1)} %get-tuple-element.39), channel_id=1, source_target_pairs={{0,8},{4,12},{8,0},{12,4},{1,9},{5,13},{9,1},{13,5},{2,10},{6,14},... | collective-permute-start | bytes 196616 | tf_op jit(solution)/shard_map/ppermute | solution.py:417
  21.1 6.1 %collective-permute-start.7 = (bf16[256,128]{1,0:T(8,128)(2,1)S(1)}, bf16[256,128]{1,0:T(8,128)(2,1)S(1)}, u32[]{:S(2)}, u32[]{:S(2)}) collective-permute-start(bf16[256,128]{1,0:T(8,128)(2,1)S(1)} %get-tuple-element.40), channel_id=1, source_target_pairs={{0,12},{4,8},{8,4},{12,0},{1,13},{5,9},{9,5},{13,1},{2,14},{6,10},... | collective-permute-start | bytes 196616 | tf_op jit(solution)/shard_map/ppermute | solution.py:417
  22.2 5.1 %collective-permute-start.8 = (bf16[256,128]{1,0:T(8,128)(2,1)S(1)}, bf16[256,128]{1,0:T(8,128)(2,1)S(1)}, u32[]{:S(2)}, u32[]{:S(2)}) collective-permute-start(bf16[256,128]{1,0:T(8,128)(2,1)S(1)} %get-tuple-element.37.refs_6_), channel_id=1, source_target_pairs={{0,1},{1,0},{2,3},{3,2},{4,5},{5,4},{6,7},{7,6},{8,9},{9,8},{10,11... | collective-permute-start | bytes 196616 | tf_op jit(solution)/shard_map/ppermute | solution.py:426
  34.4 7.7 %collective-permute-start.12 = (bf16[1024,128]{1,0:T(8,128)(2,1)S(1)}, bf16[1024,128]{1,0:T(8,128)(2,1)S(1)}, u32[]{:S(2)}, u32[]{:S(2)}) collective-permute-start(bf16[1024,128]{1,0:T(8,128)(2,1)S(1)} %get-tuple-element.41.refs_0_), channel_id=1, source_target_pairs={{0,2},{1,3},{4,6},{5,7},{8,10},{9,11},{12,14},{13,15},{16,18},{17,... | collective-permute-start | bytes 786440 | tf_op jit(solution)/shard_map/ppermute | solution.py:423
  42.6 4.9 %collective-permute-start.13 = (bf16[256,128]{1,0:T(8,128)(2,1)S(1)}, bf16[256,128]{1,0:T(8,128)(2,1)S(1)}, u32[]{:S(2)}, u32[]{:S(2)}) collective-permute-start(bf16[256,128]{1,0:T(8,128)(2,1)S(1)} %get-tuple-element.43), channel_id=1, source_target_pairs={{0,4},{4,0},{8,12},{12,8},{1,5},{5,1},{9,13},{13,9},{2,6},{6,2},{1... | collective-permute-start | bytes 196616 | tf_op jit(solution)/shard_map/ppermute | solution.py:417
  43.7 7.9 %collective-permute-start.14 = (bf16[256,128]{1,0:T(8,128)(2,1)S(1)}, bf16[256,128]{1,0:T(8,128)(2,1)S(1)}, u32[]{:S(2)}, u32[]{:S(2)}) collective-permute-start(bf16[256,128]{1,0:T(8,128)(2,1)S(1)} %get-tuple-element.44), channel_id=1, source_target_pairs={{0,8},{4,12},{8,0},{12,4},{1,9},{5,13},{9,1},{13,5},{2,10},{6,14},... | collective-permute-start | bytes 196616 | tf_op jit(solution)/shard_map/ppermute | solution.py:417
  45.4 6.3 %collective-permute-start.15 = (bf16[256,128]{1,0:T(8,128)(2,1)S(1)}, bf16[256,128]{1,0:T(8,128)(2,1)S(1)}, u32[]{:S(2)}, u32[]{:S(2)}) collective-permute-start(bf16[256,128]{1,0:T(8,128)(2,1)S(1)} %get-tuple-element.45), channel_id=1, source_target_pairs={{0,12},{4,8},{8,4},{12,0},{1,13},{5,9},{9,5},{13,1},{2,14},{6,10},... | collective-permute-start | bytes 196616 | tf_op jit(solution)/shard_map/ppermute | solution.py:417
  55.4 6.4 %collective-permute-start.17 = (bf16[256,128]{1,0:T(8,128)(2,1)S(1)}, bf16[256,128]{1,0:T(8,128)(2,1)}, u32[]{:S(2)}, u32[]{:S(2)}) collective-permute-start(bf16[256,128]{1,0:T(8,128)(2,1)S(1)} %get-tuple-element.49), channel_id=1, source_target_pairs={{0,8},{4,12},{8,0},{12,4},{1,9},{5,13},{9,1},{13,5},{2,10},{6,14},... | collective-permute-start | bytes 196616 | tf_op jit(solution)/shard_map/ppermute | solution.py:417
  57.0 6.2 %collective-permute-start.18 = (bf16[256,128]{1,0:T(8,128)(2,1)S(1)}, bf16[256,128]{1,0:T(8,128)(2,1)}, u32[]{:S(2)}, u32[]{:S(2)}) collective-permute-start(bf16[256,128]{1,0:T(8,128)(2,1)S(1)} %get-tuple-element.50), channel_id=1, source_target_pairs={{0,12},{4,8},{8,4},{12,0},{1,13},{5,9},{9,5},{13,1},{2,14},{6,10},... | collective-permute-start | bytes 196616 | tf_op jit(solution)/shard_map/ppermute | solution.py:417
  71.6 11.1 %collective-permute-start.26 = (bf16[1344,128]{1,0:T(8,128)(2,1)S(1)}, bf16[1344,128]{1,0:T(8,128)(2,1)S(1)}, u32[]{:S(2)}, u32[]{:S(2)}) collective-permute-start(bf16[1344,128]{1,0:T(8,128)(2,1)S(1)} %dynamic-slice_bitcast_fusion), channel_id=1, source_target_pairs={{0,2},{2,0},{1,3},{3,1},{4,6},{6,4},{5,7},{7,5},{8,10},{10,8},{9,1... | collective-permute-start | bytes 1032200 | tf_op jit(solution)/shard_map/ppermute | solution.py:420
  74.1 5.0 %collective-permute-start.23 = (bf16[256,128]{1,0:T(8,128)(2,1)S(1)}, bf16[256,128]{1,0:T(8,128)(2,1)S(1)}, u32[]{:S(2)}, u32[]{:S(2)}) collective-permute-start(bf16[256,128]{1,0:T(8,128)(2,1)S(1)} %get-tuple-element.53), channel_id=1, source_target_pairs={{0,4},{4,0},{8,12},{12,8},{1,5},{5,1},{9,13},{13,9},{2,6},{6,2},{1... | collective-permute-start | bytes 196616 | tf_op jit(solution)/shard_map/ppermute | solution.py:417
  74.1 8.5 %collective-permute-start.24 = (bf16[256,128]{1,0:T(8,128)(2,1)S(1)}, bf16[256,128]{1,0:T(8,128)(2,1)S(1)}, u32[]{:S(2)}, u32[]{:S(2)}) collective-permute-start(bf16[256,128]{1,0:T(8,128)(2,1)S(1)} %get-tuple-element.54), channel_id=1, source_target_pairs={{0,8},{4,12},{8,0},{12,4},{1,9},{5,13},{9,1},{13,5},{2,10},{6,14},... | collective-permute-start | bytes 196616 | tf_op jit(solution)/shard_map/ppermute | solution.py:417
  76.2 6.4 %collective-permute-start.25 = (bf16[256,128]{1,0:T(8,128)(2,1)S(1)}, bf16[256,128]{1,0:T(8,128)(2,1)S(1)}, u32[]{:S(2)}, u32[]{:S(2)}) collective-permute-start(bf16[256,128]{1,0:T(8,128)(2,1)S(1)} %get-tuple-element.55), channel_id=1, source_target_pairs={{0,12},{4,8},{8,4},{12,0},{1,13},{5,9},{9,5},{13,1},{2,14},{6,10},... | collective-permute-start | bytes 196616 | tf_op jit(solution)/shard_map/ppermute | solution.py:417
  84.6 8.9 %collective-permute-start.28 = (bf16[336,128]{1,0:T(8,128)(2,1)S(1)}, bf16[336,128]{1,0:T(8,128)(2,1)S(1)}, u32[]{:S(2)}, u32[]{:S(2)}) collective-permute-start(bf16[336,128]{1,0:T(8,128)(2,1)S(1)} %get-tuple-element.59), channel_id=1, source_target_pairs={{0,8},{4,12},{8,0},{12,4},{1,9},{5,13},{9,1},{13,5},{2,10},{6,14},... | collective-permute-start | bytes 258056 | tf_op jit(solution)/shard_map/ppermute | solution.py:417
  85.9 7.6 %collective-permute-start.29 = (bf16[336,128]{1,0:T(8,128)(2,1)S(1)}, bf16[336,128]{1,0:T(8,128)(2,1)S(1)}, u32[]{:S(2)}, u32[]{:S(2)}) collective-permute-start(bf16[336,128]{1,0:T(8,128)(2,1)S(1)} %get-tuple-element.60), channel_id=1, source_target_pairs={{0,12},{4,8},{8,4},{12,0},{1,13},{5,9},{9,5},{13,1},{2,14},{6,10},... | collective-permute-start | bytes 258056 | tf_op jit(solution)/shard_map/ppermute | solution.py:417
  93.5 7.2 %collective-permute-start.32 = (bf16[336,128]{1,0:T(8,128)(2,1)S(1)}, bf16[336,128]{1,0:T(8,128)(2,1)S(1)}, u32[]{:S(2)}, u32[]{:S(2)}) collective-permute-start(bf16[336,128]{1,0:T(8,128)(2,1)S(1)} %add_convert_fusion), channel_id=1, source_target_pairs={{0,12},{4,8},{8,4},{12,0},{1,13},{5,9},{9,5},{13,1},{2,14},{6,10},... | collective-permute-start | bytes 258056 | tf_op jit(solution)/shard_map/ppermute | solution.py:417
  95.6 8.6 %collective-permute-start.31 = (bf16[336,128]{1,0:T(8,128)(2,1)S(1)}, bf16[336,128]{1,0:T(8,128)(2,1)S(1)}, u32[]{:S(2)}, u32[]{:S(2)}) collective-permute-start(bf16[336,128]{1,0:T(8,128)(2,1)S(1)} %add_convert_fusion), channel_id=1, source_target_pairs={{0,8},{4,12},{8,0},{12,4},{1,9},{5,13},{9,1},{13,5},{2,10},{6,14},... | collective-permute-start | bytes 258056 | tf_op jit(solution)/shard_map/ppermute | solution.py:417
  96.8 7.4 %collective-permute-start.30 = (bf16[336,128]{1,0:T(8,128)(2,1)S(1)}, bf16[336,128]{1,0:T(8,128)(2,1)S(1)}, u32[]{:S(2)}, u32[]{:S(2)}) collective-permute-start(bf16[336,128]{1,0:T(8,128)(2,1)S(1)} %add_convert_fusion), channel_id=1, source_target_pairs={{0,4},{4,0},{8,12},{12,8},{1,5},{5,1},{9,13},{13,9},{2,6},{6,2},{1... | collective-permute-start | bytes 258056 | tf_op jit(solution)/shard_map/ppermute | solution.py:417
  104.3 10.0 %collective-permute-start.33 = (bf16[1344,128]{1,0:T(8,128)(2,1)S(1)}, bf16[1344,128]{1,0:T(8,128)(2,1)S(1)}, u32[]{:S(2)}, u32[]{:S(2)}) collective-permute-start(bf16[1344,128]{1,0:T(8,128)(2,1)S(1)} %pad_maximum_fusion.refs_0_), channel_id=1, source_target_pairs={{0,2},{2,0},{1,3},{3,1},{4,6},{6,4},{5,7},{7,5},{8,10},{10,8},{9,1... | collective-permute-start | bytes 1032200 | tf_op jit(solution)/shard_map/ppermute | solution.py:420
  (22 other events, 163.4 us)

commit v5 on v4

--- a/solution.py
+++ b/solution.py
@@ -167,14 +167,14 @@
     return begin(sems, pairs, first)
 
 
-def handed_kernel(sems, given, pieces, scratch):
+def handed_kernel(first, sems, given, pieces, scratch):
     z = lax.axis_index("node")
-    cap = pieces[0].shape[0]
+    cap, few = pieces[0].shape[0], len(pieces)
 
     def send(source):
         pairs = []
         for k, piece in enumerate(pieces):
-            at = pl.multiple_of((z ^ k) * cap, cap)
+            at = pl.multiple_of(((z ^ (first + k)) % few) * cap, cap)
             pairs.append((source.at[pl.ds(at, cap), :], piece))
         end(begin(sems, pairs))
 
@@ -335,7 +335,10 @@
         for k in range(nodes):
             made[k][...] = fresh[pl.ds(pl.multiple_of((z ^ k) * cap, cap), cap), :]
     else:
-        made[0][...] = fresh[...]
+        few = events // 2
+        upper = z // (nodes // 2)
+        made[0][...] = fresh[pl.ds(pl.multiple_of((1 - upper) * few, few), few), :]
+        made[1][...] = fresh[pl.ds(pl.multiple_of(upper * few, few), few), :]
     out_ref = made[-1]
 
     def put(start, value):
@@ -360,33 +363,41 @@
     put(top, tail)
 
 
-def middle_kernel(segs, sems, given, made, scratch):
+def middle_kernel(nodes, segs, first, sems, given, made, scratch):
     totals, got = given[0], given[1:segs]
     rows = scratch[:segs]
     whole = scratch[segs]
-    nodes, chunk = len(made), made[0].shape[0]
-    share = nodes * chunk
-    at = pl.ds(pl.multiple_of(lax.axis_index("seg") * share, share), share)
+    few, chunk = len(made), made[0].shape[0]
+    z = lax.axis_index("node")
+    side = (z ^ first) // few
+    share = few * chunk
+    at = pl.ds(pl.multiple_of((lax.axis_index("seg") * 2 + side) * share, share), share)
     pairs = [(totals.at[at, :], rows[0])] + list(zip(got, rows[1:]))
     end(begin(sems, pairs))
     total = rows[0][...].astype(F32)
     for x in range(1, segs):
         total = total + rows[x][...].astype(F32)
     whole[...] = total.astype(BF)
-    for k in range(nodes):
-        made[k][...] = whole[pl.ds(pl.multiple_of((lax.axis_index("node") ^ k) * chunk, chunk), chunk), :]
+    for k in range(few):
+        at = pl.multiple_of(((z ^ (first + k)) % few) * chunk, chunk)
+        made[k][...] = whole[pl.ds(at, chunk), :]
 
 
 def unpack_kernel(nodes, segs, long, sems, pieces, made, scratch):
     grad_in, grad_hid, grad_bias = made
     (held,) = scratch
-    chunk = pieces[0].shape[0] // nodes
+    few = nodes // 2
+    chunk = pieces[0].shape[0] // few
     z, s = lax.axis_index("node"), lax.axis_index("seg")
     pairs = []
     for x in range(segs):
         for k in range(nodes):
             at = pl.multiple_of(((s ^ x) * nodes + (z ^ k)) * chunk, chunk)
-            pairs.append((pieces[x].at[k * chunk : (k + 1) * chunk, :], held.at[pl.ds(at, chunk), :]))
+            source = pieces[2 * x + k // few]
+            i = k % few
+            pairs.append(
+                (source.at[i * chunk : (i + 1) * chunk, :], held.at[pl.ds(at, chunk), :])
+            )
     end(begin(sems, pairs))
     width = grad_hid.shape[1]
     for g in range(3):
@@ -496,7 +507,7 @@
         copies = 7 + 2 * nodes
         *fresh, totals = run(
             lambda *a, b=b, last=final, p=totals is not None: batch_kernel(nodes, b, last, p, *a),
-            ([piece] * nodes if final else [shape((events, half), BF)])
+            ([piece] * nodes if final else [shape((events // 2, half), BF)] * 2)
             + [shape((total_rows, half), BF if final else F32)],
             given,
             rooms,
@@ -504,7 +515,7 @@
             (1, 3, 4, 5),
         )
         if not final:
-            hop = seg_next(fresh[0])
+            hops = [seg_next(side) for side in fresh]
             put, rows = run(
                 lambda *a, b=b: base_kernel(b, *a),
                 [shape((1, spread), I32), shape((spread, half), BF)],
@@ -512,9 +523,16 @@
                 [numbers, pltpu.VMEM(bundle.shape, BF), pltpu.VMEM((node_rows, half), BF)],
                 2,
             )
-            values = run(
-                handed_kernel, [piece] * nodes, [fresh[0], hop, rows], [], nodes
-            )
+            few = nodes // 2
+            values = [None] * nodes
+            for side, first in ((0, few), (1, 0)):
+                values[first : first + few] = run(
+                    lambda *a, first=first: handed_kernel(first, *a),
+                    [piece] * few,
+                    [fresh[side], hops[side]] + ([rows] if side == 1 else []),
+                    [],
+                    few,
+                )
             values = exchange(values)
             values, *served = run(
                 lambda *a, b=b: next_kernel(b, *a),
@@ -545,20 +563,30 @@
     def at(blocks, i):
         return lax.dynamic_index_in_dim(blocks, i, 0, keepdims=False)
 
-    blocks = totals.reshape(segs, nodes * chunk, half)
-    got = [seg_swap(at(blocks, s ^ x), x) for x in range(1, segs)]
-    share = pltpu.VMEM((nodes * chunk, half), BF)
-    parts = run(
-        lambda *a: middle_kernel(segs, *a),
-        [shape((chunk, half), BF)] * nodes,
-        [totals] + got + returned[1:],
-        [share] * (segs + 1),
-        segs,
-    )
-    got = [node_swap(parts[k], k) for k in range(1, nodes)]
-    summed = sum((g.astype(F32) for g in got), parts[0].astype(F32)).astype(BF)
-    gathered = jnp.concatenate([summed] + [node_swap(summed, k) for k in range(1, nodes)], axis=0)
-    gathered = [gathered] + [seg_swap(gathered, x) for x in range(1, segs)]
+    few = nodes // 2
+    upper = z // few
+    blocks = totals.reshape(segs, 2, few * chunk, half)
+    got = [
+        [seg_swap(at(at(blocks, s ^ x), side), x) for x in range(1, segs)]
+        for side in (1 - upper, upper)
+    ]
+    share = pltpu.VMEM((few * chunk, half), BF)
+    parts = [None] * nodes
+    for side, first in ((0, few), (1, 0)):
+        parts[first : first + few] = run(
+            lambda *a, first=first: middle_kernel(nodes, segs, first, *a),
+            [shape((chunk, half), BF)] * few,
+            [totals] + got[side] + (returned[1:] if side else []),
+            [share] * (segs + 1),
+            segs,
+        )
+    parts = exchange(parts)
+    summed = sum((g.astype(F32) for g in parts[1:]), parts[0].astype(F32)).astype(BF)
+    around = [summed] + [node_swap(summed, k) for k in range(1, nodes)]
+    sides = [jnp.concatenate(around[:few], axis=0), jnp.concatenate(around[few:], axis=0)]
+    gathered = list(sides)
+    for x in range(1, segs):
+        gathered += [seg_swap(side, x) for side in sides]
     grads = run(
         lambda *a: unpack_kernel(nodes, segs, long, *a),
         [shape(w_input.shape, F32), shape(w_hidden.shape, F32), shape(bias.shape, F32)],

time: 117 us -> 110 us (0.940)
  waiting for transfers between devices: 44.4 us -> 34 us
  starting transfers between devices: 40.7 us -> 43.2 us
    ppermute x2 -> x4, waiting for transfers between devices: 5.79 us -> 1.11 us  [seg_swap(): return lax.ppermute(block, 'seg', [(i, i ^ x) for i in range(segs)])]
    ppermute x21, waiting for transfers between devices: 31.2 us -> 27.8 us  [node_swap(): return lax.ppermute(block, 'node', [(i, i ^ k) for i in range(nodes)])]
    ppermute x2 -> x4, starting transfers between devices: 2.61 us -> 5.13 us  [seg_swap(): return lax.ppermute(block, 'seg', [(i, i ^ x) for i in range(segs)])]
    ppermute x2 -> x3, waiting for transfers between devices: 4.9 us -> 2.56 us  [seg_next(): return lax.ppermute(block, 'seg', [(i, i + 1) for i in range(segs - 1)])]
    ppermute x21, starting transfers between devices: 32.3 us -> 31 us  [node_swap(): return lax.ppermute(block, 'node', [(i, i ^ k) for i in range(nodes)])]
    ppermute x2 -> x3, starting transfers between devices: 4.73 us -> 6.02 us  [seg_next(): return lax.ppermute(block, 'seg', [(i, i + 1) for i in range(segs - 1)])]
    pallas_call x12 -> x14, Pallas kernels: 22.1 us -> 22.7 us  [run(): pl.pallas_call(body, out_shape=list(outs), in_specs=[HBM if i in far else...]
    unnamed x30 -> x31, local copies, waits for them, and re-layouts: 4.34 us -> 4.35 us
  transfers between devices with their start and end apart: 34 -> 37, of which waited for: 20 -> 20; matrix products, arithmetic and copies ran while one was open for 3% -> 3% of each run, Pallas kernels for 9% -> 11%
where the time goes in v5:
time: 110 us; the launch traced here: 109 us
  starting transfers between devices  43.2 us (39%)
  waiting for transfers between devices  34 us (31%)
  Pallas kernels  22.7 us (21%)
  local copies, waits for them, and re-layouts  5.92 us (5%)
  other arithmetic  2.27 us (2%)
  between operations  1.16 us (1%)
    ppermute x21, starting transfers between devices, node_swap(): return lax.ppermute(block, 'node', [(i, i ^ k) for i in range(nodes)])  31 us
    ppermute x21, waiting for transfers between devices, node_swap(): return lax.ppermute(block, 'node', [(i, i ^ k) for i in range(nodes)])  27.8 us
    pallas_call x14, Pallas kernels, run(): pl.pallas_call(body, out_shape=list(outs), in_specs=[HBM if i in far else...  22.7 us
    ppermute x3, starting transfers between devices, seg_next(): return lax.ppermute(block, 'seg', [(i, i + 1) for i in range(segs - 1)])  6.02 us
    ppermute x4, starting transfers between devices, seg_swap(): return lax.ppermute(block, 'seg', [(i, i ^ x) for i in range(segs)])  5.13 us
    unnamed x31, local copies, waits for them, and re-layouts  4.35 us
    ppermute x3, waiting for transfers between devices, seg_next(): return lax.ppermute(block, 'seg', [(i, i + 1) for i in range(segs - 1)])  2.56 us
    ppermute x9, waiting for transfers between devices, feat_swap(): return lax.ppermute(block, 'feat', [(0, 1), (1, 0)])  2.49 us
  transfers between devices with their start and end apart: 37, of which 20 were waited for; matrix products, arithmetic and copies ran while one was open for 3% of the time, Pallas kernels for 11%

profile of v5, /device:TPU:0, one launch (start us, length us, event | category | flops | bytes accessed | tf_op | source)
XLA Modules:
  0.0 109.2 jit_solution(1736951726713670784)
XLA Ops:
  1.5 3.1 %collective-permute-start = (s32[2,256]{1,0:T(2,128)S(1)}, s32[2,256]{1,0:T(2,128)S(1)}, u32[]{:S(2)}, u32[]{:S(2)}) collective-permute-start(s32[2,256]{1,0:T(2,128)S(1)} %bitcast.44), channel_id=1, source_target_pairs={{0,4},{4,0},{8,12},{12,8},{1,5},{5,1},{9,13},{13,9},{2,6},{6,2},{1... | collective-permute-start | bytes 6152 | tf_op jit(solution)/shard_map/ppermute | solution.py:428
  4.5 2.6 %collective-permute-start.1 = (s32[2,256]{1,0:T(2,128)S(1)}, s32[2,256]{1,0:T(2,128)S(1)}, u32[]{:S(2)}, u32[]{:S(2)}) collective-permute-start(s32[2,256]{1,0:T(2,128)S(1)} %bitcast.45), channel_id=1, source_target_pairs={{0,8},{4,12},{8,0},{12,4},{1,9},{5,13},{9,1},{13,5},{2,10},{6,14},... | collective-permute-start | bytes 6152 | tf_op jit(solution)/shard_map/ppermute | solution.py:428
  14.2 3.4 %collective-permute-start.3 = (bf16[2064,128]{1,0:T(8,128)(2,1)S(1)}, bf16[2064,128]{1,0:T(8,128)(2,1)S(1)}, u32[]{:S(2)}, u32[]{:S(2)}) collective-permute-start(bf16[2064,128]{1,0:T(8,128)(2,1)S(1)} %shard_map.149), channel_id=1, source_target_pairs={{0,2},{1,3},{4,6},{5,7},{8,10},{9,11},{12,14},{13,15},{16,18},{17,... | collective-permute-start | bytes 1585160 | tf_op jit(solution)/shard_map/ppermute | solution.py:434
  17.8 3.4 %collective-permute-start.6 = (bf16[256,128]{1,0:T(8,128)(2,1)S(1)}, bf16[256,128]{1,0:T(8,128)(2,1)S(1)}, u32[]{:S(2)}, u32[]{:S(2)}) collective-permute-start(bf16[256,128]{1,0:T(8,128)(2,1)S(1)} %get-tuple-element.40), channel_id=1, source_target_pairs={{0,8},{4,12},{8,0},{12,4},{1,9},{5,13},{9,1},{13,5},{2,10},{6,14},... | collective-permute-start | bytes 196616 | tf_op jit(solution)/shard_map/ppermute | solution.py:428
  22.2 3.2 %collective-permute-done.6.refs_8_ = bf16[256,128]{1,0:T(8,128)(2,1)S(1)} collective-permute-done((bf16[256,128]{1,0:T(8,128)(2,1)S(1)}, bf16[256,128]{1,0:T(8,128)(2,1)S(1)}, u32[]{:S(2)}, u32[]{:S(2)}) %collective-permute-start.6) | collective-permute-done | bytes 65568 | tf_op jit(solution)/shard_map/ppermute | solution.py:428
  25.4 1.9 %collective-permute-done.7.refs_9_ = bf16[256,128]{1,0:T(8,128)(2,1)S(1)} collective-permute-done((bf16[256,128]{1,0:T(8,128)(2,1)S(1)}, bf16[256,128]{1,0:T(8,128)(2,1)S(1)}, u32[]{:S(2)}, u32[]{:S(2)}) %collective-permute-start.7) | collective-permute-done | bytes 65568 | tf_op jit(solution)/shard_map/ppermute | solution.py:428
  29.4 4.9 %shard_map.151 = (bf16[512,128]{1,0:T(8,128)(2,1)S(1)}, bf16[512,128]{1,0:T(8,128)(2,1)S(1)}, f32[2688,128]{1,0:T(8,128)S(1)}) custom-call(f32[40,128]{1,0:T(8,128)S(1)} %copy-done.8, bf16[2,64,1024]{2,1,0:T(8,128)(2,1)S(1)} %bitcast.37, bf16[2,64,1024]{2,1,0:T(8,128)(2,1)S(1)} %collective-permute-done.4.refs_2_, bf16[3,768,128]{2,1,0:T(8,128)(2,1)S(1)} %copy-done.2, ...), custom_call_target="tpu_custom_call" | custom-call | bytes 4018176 | tf_op jit(solution)/shard_map/pallas_call | solution.py:28
  37.0 2.6 %collective-permute-done.14.refs_1_ = bf16[512,128]{1,0:T(8,128)(2,1)S(1)} collective-permute-done((bf16[512,128]{1,0:T(8,128)(2,1)S(1)}, bf16[512,128]{1,0:T(8,128)(2,1)S(1)}, u32[]{:S(2)}, u32[]{:S(2)}) %collective-permute-start.14) | collective-permute-done | bytes 131104 | tf_op jit(solution)/shard_map/ppermute | solution.py:434
  39.7 2.0 %collective-permute-start.15 = (bf16[256,128]{1,0:T(8,128)(2,1)S(1)}, bf16[256,128]{1,0:T(8,128)(2,1)S(1)}, u32[]{:S(2)}, u32[]{:S(2)}) collective-permute-start(bf16[256,128]{1,0:T(8,128)(2,1)S(1)} %get-tuple-element.46), channel_id=1, source_target_pairs={{0,8},{4,12},{8,0},{12,4},{1,9},{5,13},{9,1},{13,5},{2,10},{6,14},... | collective-permute-start | bytes 196616 | tf_op jit(solution)/shard_map/ppermute | solution.py:428
  45.2 1.9 %collective-permute-done.15.refs_5_ = bf16[256,128]{1,0:T(8,128)(2,1)S(1)} collective-permute-done((bf16[256,128]{1,0:T(8,128)(2,1)S(1)}, bf16[256,128]{1,0:T(8,128)(2,1)S(1)}, u32[]{:S(2)}, u32[]{:S(2)}) %collective-permute-start.15) | collective-permute-done | bytes 65568 | tf_op jit(solution)/shard_map/ppermute | solution.py:428
  51.9 2.8 %collective-permute-start.18 = (bf16[256,128]{1,0:T(8,128)(2,1)S(1)}, bf16[256,128]{1,0:T(8,128)(2,1)}, u32[]{:S(2)}, u32[]{:S(2)}) collective-permute-start(bf16[256,128]{1,0:T(8,128)(2,1)S(1)} %get-tuple-element.51), channel_id=1, source_target_pairs={{0,8},{4,12},{8,0},{12,4},{1,9},{5,13},{9,1},{13,5},{2,10},{6,14},... | collective-permute-start | bytes 196616 | tf_op jit(solution)/shard_map/ppermute | solution.py:428
  56.7 2.0 %collective-permute-done.18.refs_8_ = bf16[256,128]{1,0:T(8,128)(2,1)} collective-permute-done((bf16[256,128]{1,0:T(8,128)(2,1)S(1)}, bf16[256,128]{1,0:T(8,128)(2,1)}, u32[]{:S(2)}, u32[]{:S(2)}) %collective-permute-start.18) | collective-permute-done | bytes 65568 | tf_op jit(solution)/shard_map/ppermute | solution.py:428
  58.7 2.2 %collective-permute-done.19.refs_9_ = bf16[256,128]{1,0:T(8,128)(2,1)} collective-permute-done((bf16[256,128]{1,0:T(8,128)(2,1)S(1)}, bf16[256,128]{1,0:T(8,128)(2,1)}, u32[]{:S(2)}, u32[]{:S(2)}) %collective-permute-start.19) | collective-permute-done | bytes 65568 | tf_op jit(solution)/shard_map/ppermute | solution.py:428
  64.1 5.0 %shard_map.156 = (bf16[256,128]{1,0:T(8,128)(2,1)S(1)}, bf16[256,128]{1,0:T(8,128)(2,1)S(1)}, bf16[256,128]{1,0:T(8,128)(2,1)S(1)}, bf16[256,128]{1,0:T(8,128)(2,1)S(1)}, bf16[2688,128]{1,0:T(8,128)(2,1)S(1)}) custom-call(f32[40,128]{1,0:T(8,128)S(1)} %copy-done.9, bf16[2,64,1024]{2,1,0:T(8,128)(2,1)S(1)} %bitcast.38, ...), custom_call_target="tpu_custom_call" | custom-call | bytes 4706304 | tf_op jit(solution)/shard_map/pallas_call | solution.py:28
  69.2 2.6 %collective-permute-start.27 = (bf16[672,128]{1,0:T(8,128)(2,1)S(1)}, bf16[672,128]{1,0:T(8,128)(2,1)S(1)}, u32[]{:S(2)}, u32[]{:S(2)}) collective-permute-start(bf16[672,128]{1,0:T(8,128)(2,1)S(1)} %get-tuple-element.66), channel_id=1, source_target_pairs={{0,2},{2,0},{1,3},{3,1},{4,6},{6,4},{5,7},{7,5},{8,10},{10,8},{9,1... | collective-permute-start | bytes 516104 | tf_op jit(solution)/shard_map/ppermute | solution.py:431
  71.9 2.1 %collective-permute-start.25 = (bf16[256,128]{1,0:T(8,128)(2,1)S(1)}, bf16[256,128]{1,0:T(8,128)(2,1)S(1)}, u32[]{:S(2)}, u32[]{:S(2)}) collective-permute-start(bf16[256,128]{1,0:T(8,128)(2,1)S(1)} %get-tuple-element.56), channel_id=1, source_target_pairs={{0,8},{4,12},{8,0},{12,4},{1,9},{5,13},{9,1},{13,5},{2,10},{6,14},... | collective-permute-start | bytes 196616 | tf_op jit(solution)/shard_map/ppermute | solution.py:428
  74.0 2.3 %collective-permute-start.26 = (bf16[256,128]{1,0:T(8,128)(2,1)S(1)}, bf16[256,128]{1,0:T(8,128)(2,1)S(1)}, u32[]{:S(2)}, u32[]{:S(2)}) collective-permute-start(bf16[256,128]{1,0:T(8,128)(2,1)S(1)} %get-tuple-element.57), channel_id=1, source_target_pairs={{0,12},{4,8},{8,4},{12,0},{1,13},{5,9},{9,5},{13,1},{2,14},{6,10},... | collective-permute-start | bytes 196616 | tf_op jit(solution)/shard_map/ppermute | solution.py:428
  76.8 3.4 %collective-permute-done.25.refs_4_.refs_3_ = bf16[256,128]{1,0:T(8,128)(2,1)S(1)} collective-permute-done((bf16[256,128]{1,0:T(8,128)(2,1)S(1)}, bf16[256,128]{1,0:T(8,128)(2,1)S(1)}, u32[]{:S(2)}, u32[]{:S(2)}) %collective-permute-start.25) | collective-permute-done | bytes 65568 | tf_op jit(solution)/shard_map/ppermute | solution.py:428
  85.8 3.7 %collective-permute-done.30 = bf16[336,128]{1,0:T(8,128)(2,1)S(1)} collective-permute-done((bf16[336,128]{1,0:T(8,128)(2,1)S(1)}, bf16[336,128]{1,0:T(8,128)(2,1)S(1)}, u32[]{:S(2)}, u32[]{:S(2)}) %collective-permute-start.30) | collective-permute-done | bytes 86048 | tf_op jit(solution)/shard_map/ppermute | solution.py:428
  92.0 2.6 %collective-permute-start.34 = (bf16[336,128]{1,0:T(8,128)(2,1)S(1)}, bf16[336,128]{1,0:T(8,128)(2,1)S(1)}, u32[]{:S(2)}, u32[]{:S(2)}) collective-permute-start(bf16[336,128]{1,0:T(8,128)(2,1)S(1)} %add_convert_fusion), channel_id=1, source_target_pairs={{0,12},{4,8},{8,4},{12,0},{1,13},{5,9},{9,5},{13,1},{2,14},{6,10},... | collective-permute-start | bytes 258056 | tf_op jit(solution)/shard_map/ppermute | solution.py:428
  96.1 2.1 %collective-permute-start.35 = (bf16[672,128]{1,0:T(8,128)(2,1)S(1)}, bf16[672,128]{1,0:T(8,128)(2,1)S(1)}, u32[]{:S(2)}, u32[]{:S(2)}) collective-permute-start(bf16[672,128]{1,0:T(8,128)(2,1)S(1)} %pad_maximum_fusion.refs_0_), channel_id=1, source_target_pairs={{0,2},{2,0},{1,3},{3,1},{4,6},{6,4},{5,7},{7,5},{8,10},{10,8},{9,1... | collective-permute-start | bytes 516104 | tf_op jit(solution)/shard_map/ppermute | solution.py:431
  98.2 3.1 %collective-permute-done.33 = bf16[336,128]{1,0:T(8,128)(2,1)S(1)} collective-permute-done((bf16[336,128]{1,0:T(8,128)(2,1)S(1)}, bf16[336,128]{1,0:T(8,128)(2,1)S(1)}, u32[]{:S(2)}, u32[]{:S(2)}) %collective-permute-start.33) | collective-permute-done | bytes 86048 | tf_op jit(solution)/shard_map/ppermute | solution.py:428
  103.1 2.7 %shard_map.157 = f32[2048,128]{1,0:T(8,128)} custom-call(s32[2,1024]{1,0:T(2,128)S(1)} %get-tuple-element.35.refs_1_.refs_0_, f32[2048,128]{1,0:T(8,128)S(1)} %shard_map.155.refs_1_, bf16[256,128]{1,0:T(8,128)(2,1)S(1)} %get-tuple-element.54.refs_2_, bf16[256,128]{1,0:T(8,128)(2,1)S(1)} %collective-permute-done.24.refs_3_.refs_2_, ...), custom_call_target="tpu_custom_call" | custom-call | bytes 2367488 | tf_op jit(solution)/shard_map/pallas_call | solution.py:28
  106.9 2.1 %shard_map.160 = (f32[3,768,128]{2,1,0:T(8,128)}, f32[3,256,128]{2,1,0:T(8,128)}, f32[4,128]{1,0:T(4,128)}) custom-call(bf16[672,128]{1,0:T(8,128)(2,1)S(1)} %pad_maximum_fusion.refs_0_, bf16[672,128]{1,0:T(8,128)(2,1)S(1)} %constant_dynamic-update-slice_fusion.refs_1_, bf16[672,128]{1,0:T(8,128)(2,1)S(1)} %collective-permute-done.35.refs_2_, ...), custom_call_target="tpu_custom_call" | custom-call | bytes 2263040 | tf_op jit(solution)/shard_map/pallas_call | solution.py:28
  (108 shorter events, 40.4 us)
Async XLA Ops:
  1.5 8.7 %collective-permute-start = (s32[2,256]{1,0:T(2,128)S(1)}, s32[2,256]{1,0:T(2,128)S(1)}, u32[]{:S(2)}, u32[]{:S(2)}) collective-permute-start(s32[2,256]{1,0:T(2,128)S(1)} %bitcast.44), channel_id=1, source_target_pairs={{0,4},{4,0},{8,12},{12,8},{1,5},{5,1},{9,13},{13,9},{2,6},{6,2},{1... | collective-permute-start | bytes 6152 | tf_op jit(solution)/shard_map/ppermute | solution.py:428
  4.5 7.0 %collective-permute-start.1 = (s32[2,256]{1,0:T(2,128)S(1)}, s32[2,256]{1,0:T(2,128)S(1)}, u32[]{:S(2)}, u32[]{:S(2)}) collective-permute-start(s32[2,256]{1,0:T(2,128)S(1)} %bitcast.45), channel_id=1, source_target_pairs={{0,8},{4,12},{8,0},{12,4},{1,9},{5,13},{9,1},{13,5},{2,10},{6,14},... | collective-permute-start | bytes 6152 | tf_op jit(solution)/shard_map/ppermute | solution.py:428
  7.1 5.4 %collective-permute-start.2 = (s32[2,256]{1,0:T(2,128)S(1)}, s32[2,256]{1,0:T(2,128)S(1)}, u32[]{:S(2)}, u32[]{:S(2)}) collective-permute-start(s32[2,256]{1,0:T(2,128)S(1)} %bitcast.46), channel_id=1, source_target_pairs={{0,12},{4,8},{8,4},{12,0},{1,13},{5,9},{9,5},{13,1},{2,14},{6,10},... | collective-permute-start | bytes 6152 | tf_op jit(solution)/shard_map/ppermute | solution.py:428
  14.2 29.1 %collective-permute-start.3 = (bf16[2064,128]{1,0:T(8,128)(2,1)S(1)}, bf16[2064,128]{1,0:T(8,128)(2,1)S(1)}, u32[]{:S(2)}, u32[]{:S(2)}) collective-permute-start(bf16[2064,128]{1,0:T(8,128)(2,1)S(1)} %shard_map.149), channel_id=1, source_target_pairs={{0,2},{1,3},{4,6},{5,7},{8,10},{9,11},{12,14},{13,15},{16,18},{17,... | collective-permute-start | bytes 1585160 | tf_op jit(solution)/shard_map/ppermute | solution.py:434
  17.6 11.1 %collective-permute-start.4 = (bf16[2,64,1024]{2,1,0:T(8,128)(2,1)S(1)}, bf16[2,64,1024]{2,1,0:T(8,128)(2,1)S(1)}, u32[]{:S(2)}, u32[]{:S(2)}) collective-permute-start(bf16[2,64,1024]{2,1,0:T(8,128)(2,1)S(1)} %bitcast.36), channel_id=1, source_target_pairs={{0,1},{1,0},{2,3},{3,2},{4,5},{5,4},{6,7},{7,6},{8,9},{9,8},{10,11... | collective-permute-start | bytes 786440 | tf_op jit(solution)/shard_map/ppermute | solution.py:437
  17.8 7.6 %collective-permute-start.6 = (bf16[256,128]{1,0:T(8,128)(2,1)S(1)}, bf16[256,128]{1,0:T(8,128)(2,1)S(1)}, u32[]{:S(2)}, u32[]{:S(2)}) collective-permute-start(bf16[256,128]{1,0:T(8,128)(2,1)S(1)} %get-tuple-element.40), channel_id=1, source_target_pairs={{0,8},{4,12},{8,0},{12,4},{1,9},{5,13},{9,1},{13,5},{2,10},{6,14},... | collective-permute-start | bytes 196616 | tf_op jit(solution)/shard_map/ppermute | solution.py:428
  21.2 6.1 %collective-permute-start.7 = (bf16[256,128]{1,0:T(8,128)(2,1)S(1)}, bf16[256,128]{1,0:T(8,128)(2,1)S(1)}, u32[]{:S(2)}, u32[]{:S(2)}) collective-permute-start(bf16[256,128]{1,0:T(8,128)(2,1)S(1)} %get-tuple-element.41), channel_id=1, source_target_pairs={{0,12},{4,8},{8,4},{12,0},{1,13},{5,9},{9,5},{13,1},{2,14},{6,10},... | collective-permute-start | bytes 196616 | tf_op jit(solution)/shard_map/ppermute | solution.py:428
  34.4 5.2 %collective-permute-start.14 = (bf16[512,128]{1,0:T(8,128)(2,1)S(1)}, bf16[512,128]{1,0:T(8,128)(2,1)S(1)}, u32[]{:S(2)}, u32[]{:S(2)}) collective-permute-start(bf16[512,128]{1,0:T(8,128)(2,1)S(1)} %get-tuple-element.45.refs_0_), channel_id=1, source_target_pairs={{0,2},{1,3},{4,6},{5,7},{8,10},{9,11},{12,14},{13,15},{16,18},{17,... | collective-permute-start | bytes 393224 | tf_op jit(solution)/shard_map/ppermute | solution.py:434
  35.7 8.9 %collective-permute-start.12 = (bf16[512,128]{1,0:T(8,128)(2,1)S(1)}, bf16[512,128]{1,0:T(8,128)(2,1)S(1)}, u32[]{:S(2)}, u32[]{:S(2)}) collective-permute-start(bf16[512,128]{1,0:T(8,128)(2,1)S(1)} %get-tuple-element.42.refs_0_), channel_id=1, source_target_pairs={{0,2},{1,3},{4,6},{5,7},{8,10},{9,11},{12,14},{13,15},{16,18},{17,... | collective-permute-start | bytes 393224 | tf_op jit(solution)/shard_map/ppermute | solution.py:434
  39.7 7.3 %collective-permute-start.15 = (bf16[256,128]{1,0:T(8,128)(2,1)S(1)}, bf16[256,128]{1,0:T(8,128)(2,1)S(1)}, u32[]{:S(2)}, u32[]{:S(2)}) collective-permute-start(bf16[256,128]{1,0:T(8,128)(2,1)S(1)} %get-tuple-element.46), channel_id=1, source_target_pairs={{0,8},{4,12},{8,0},{12,4},{1,9},{5,13},{9,1},{13,5},{2,10},{6,14},... | collective-permute-start | bytes 196616 | tf_op jit(solution)/shard_map/ppermute | solution.py:428
  41.7 6.6 %collective-permute-start.16 = (bf16[256,128]{1,0:T(8,128)(2,1)S(1)}, bf16[256,128]{1,0:T(8,128)(2,1)S(1)}, u32[]{:S(2)}, u32[]{:S(2)}) collective-permute-start(bf16[256,128]{1,0:T(8,128)(2,1)S(1)} %get-tuple-element.47), channel_id=1, source_target_pairs={{0,12},{4,8},{8,4},{12,0},{1,13},{5,9},{9,5},{13,1},{2,14},{6,10},... | collective-permute-start | bytes 196616 | tf_op jit(solution)/shard_map/ppermute | solution.py:428
  51.9 6.9 %collective-permute-start.18 = (bf16[256,128]{1,0:T(8,128)(2,1)S(1)}, bf16[256,128]{1,0:T(8,128)(2,1)}, u32[]{:S(2)}, u32[]{:S(2)}) collective-permute-start(bf16[256,128]{1,0:T(8,128)(2,1)S(1)} %get-tuple-element.51), channel_id=1, source_target_pairs={{0,8},{4,12},{8,0},{12,4},{1,9},{5,13},{9,1},{13,5},{2,10},{6,14},... | collective-permute-start | bytes 196616 | tf_op jit(solution)/shard_map/ppermute | solution.py:428
  54.7 6.2 %collective-permute-start.19 = (bf16[256,128]{1,0:T(8,128)(2,1)S(1)}, bf16[256,128]{1,0:T(8,128)(2,1)}, u32[]{:S(2)}, u32[]{:S(2)}) collective-permute-start(bf16[256,128]{1,0:T(8,128)(2,1)S(1)} %get-tuple-element.52), channel_id=1, source_target_pairs={{0,12},{4,8},{8,4},{12,0},{1,13},{5,9},{9,5},{13,1},{2,14},{6,10},... | collective-permute-start | bytes 196616 | tf_op jit(solution)/shard_map/ppermute | solution.py:428
  69.2 11.0 %collective-permute-start.27 = (bf16[672,128]{1,0:T(8,128)(2,1)S(1)}, bf16[672,128]{1,0:T(8,128)(2,1)S(1)}, u32[]{:S(2)}, u32[]{:S(2)}) collective-permute-start(bf16[672,128]{1,0:T(8,128)(2,1)S(1)} %get-tuple-element.66), channel_id=1, source_target_pairs={{0,2},{2,0},{1,3},{3,1},{4,6},{6,4},{5,7},{7,5},{8,10},{10,8},{9,1... | collective-permute-start | bytes 516104 | tf_op jit(solution)/shard_map/ppermute | solution.py:431
  71.8 10.2 %collective-permute-start.29 = (bf16[672,128]{1,0:T(8,128)(2,1)S(1)}, bf16[672,128]{1,0:T(8,128)(2,1)S(1)}, u32[]{:S(2)}, u32[]{:S(2)}) collective-permute-start(bf16[672,128]{1,0:T(8,128)(2,1)S(1)} %get-tuple-element.67), channel_id=1, source_target_pairs={{0,2},{2,0},{1,3},{3,1},{4,6},{6,4},{5,7},{7,5},{8,10},{10,8},{9,1... | collective-permute-start | bytes 516104 | tf_op jit(solution)/shard_map/ppermute | solution.py:431
  71.9 8.3 %collective-permute-start.25 = (bf16[256,128]{1,0:T(8,128)(2,1)S(1)}, bf16[256,128]{1,0:T(8,128)(2,1)S(1)}, u32[]{:S(2)}, u32[]{:S(2)}) collective-permute-start(bf16[256,128]{1,0:T(8,128)(2,1)S(1)} %get-tuple-element.56), channel_id=1, source_target_pairs={{0,8},{4,12},{8,0},{12,4},{1,9},{5,13},{9,1},{13,5},{2,10},{6,14},... | collective-permute-start | bytes 196616 | tf_op jit(solution)/shard_map/ppermute | solution.py:428
  74.0 6.2 %collective-permute-start.26 = (bf16[256,128]{1,0:T(8,128)(2,1)S(1)}, bf16[256,128]{1,0:T(8,128)(2,1)S(1)}, u32[]{:S(2)}, u32[]{:S(2)}) collective-permute-start(bf16[256,128]{1,0:T(8,128)(2,1)S(1)} %get-tuple-element.57), channel_id=1, source_target_pairs={{0,12},{4,8},{8,4},{12,0},{1,13},{5,9},{9,5},{13,1},{2,14},{6,10},... | collective-permute-start | bytes 196616 | tf_op jit(solution)/shard_map/ppermute | solution.py:428
  82.6 6.9 %collective-permute-start.30 = (bf16[336,128]{1,0:T(8,128)(2,1)S(1)}, bf16[336,128]{1,0:T(8,128)(2,1)S(1)}, u32[]{:S(2)}, u32[]{:S(2)}) collective-permute-start(bf16[336,128]{1,0:T(8,128)(2,1)S(1)} %get-tuple-element.61), channel_id=1, source_target_pairs={{0,8},{4,12},{8,0},{12,4},{1,9},{5,13},{9,1},{13,5},{2,10},{6,14},... | collective-permute-start | bytes 258056 | tf_op jit(solution)/shard_map/ppermute | solution.py:428
  84.2 6.4 %collective-permute-start.31 = (bf16[336,128]{1,0:T(8,128)(2,1)S(1)}, bf16[336,128]{1,0:T(8,128)(2,1)S(1)}, u32[]{:S(2)}, u32[]{:S(2)}) collective-permute-start(bf16[336,128]{1,0:T(8,128)(2,1)S(1)} %get-tuple-element.62), channel_id=1, source_target_pairs={{0,12},{4,8},{8,4},{12,0},{1,13},{5,9},{9,5},{13,1},{2,14},{6,10},... | collective-permute-start | bytes 258056 | tf_op jit(solution)/shard_map/ppermute | solution.py:428
  90.6 5.5 %collective-permute-start.32 = (bf16[336,128]{1,0:T(8,128)(2,1)S(1)}, bf16[336,128]{1,0:T(8,128)(2,1)S(1)}, u32[]{:S(2)}, u32[]{:S(2)}) collective-permute-start(bf16[336,128]{1,0:T(8,128)(2,1)S(1)} %add_convert_fusion), channel_id=1, source_target_pairs={{0,4},{4,0},{8,12},{12,8},{1,5},{5,1},{9,13},{13,9},{2,6},{6,2},{1... | collective-permute-start | bytes 258056 | tf_op jit(solution)/shard_map/ppermute | solution.py:428
  92.0 9.3 %collective-permute-start.34 = (bf16[336,128]{1,0:T(8,128)(2,1)S(1)}, bf16[336,128]{1,0:T(8,128)(2,1)S(1)}, u32[]{:S(2)}, u32[]{:S(2)}) collective-permute-start(bf16[336,128]{1,0:T(8,128)(2,1)S(1)} %add_convert_fusion), channel_id=1, source_target_pairs={{0,12},{4,8},{8,4},{12,0},{1,13},{5,9},{9,5},{13,1},{2,14},{6,10},... | collective-permute-start | bytes 258056 | tf_op jit(solution)/shard_map/ppermute | solution.py:428
  94.6 6.7 %collective-permute-start.33 = (bf16[336,128]{1,0:T(8,128)(2,1)S(1)}, bf16[336,128]{1,0:T(8,128)(2,1)S(1)}, u32[]{:S(2)}, u32[]{:S(2)}) collective-permute-start(bf16[336,128]{1,0:T(8,128)(2,1)S(1)} %add_convert_fusion), channel_id=1, source_target_pairs={{0,8},{4,12},{8,0},{12,4},{1,9},{5,13},{9,1},{13,5},{2,10},{6,14},... | collective-permute-start | bytes 258056 | tf_op jit(solution)/shard_map/ppermute | solution.py:428
  96.1 9.7 %collective-permute-start.35 = (bf16[672,128]{1,0:T(8,128)(2,1)S(1)}, bf16[672,128]{1,0:T(8,128)(2,1)S(1)}, u32[]{:S(2)}, u32[]{:S(2)}) collective-permute-start(bf16[672,128]{1,0:T(8,128)(2,1)S(1)} %pad_maximum_fusion.refs_0_), channel_id=1, source_target_pairs={{0,2},{2,0},{1,3},{3,1},{4,6},{6,4},{5,7},{7,5},{8,10},{10,8},{9,1... | collective-permute-start | bytes 516104 | tf_op jit(solution)/shard_map/ppermute | solution.py:431
  101.3 5.6 %collective-permute-start.36 = (bf16[672,128]{1,0:T(8,128)(2,1)S(1)}, bf16[672,128]{1,0:T(8,128)(2,1)S(1)}, u32[]{:S(2)}, u32[]{:S(2)}) collective-permute-start(bf16[672,128]{1,0:T(8,128)(2,1)S(1)} %constant_dynamic-update-slice_fusion.refs_1_), channel_id=1, source_target_pairs={{0,2},{2,0},{1,3},{3,1},{4,6},{6,4},{5,7},{7,5},{8,10},{10,8},{9,1... | collective-permute-start | bytes 516104 | tf_op jit(solution)/shard_map/ppermute | solution.py:431
  (25 other events, 168.5 us)

commit v6 on v5

--- a/solution.py
+++ b/solution.py
@@ -18,7 +18,7 @@
     return jax.ShapeDtypeStruct(tuple(dims), kind)
 
 
-def run(kernel, outs, args, scratch=(), copies=1, far=()):
+def run(kernel, outs, args, scratch=(), copies=1, far=(), here=()):
     b, c = len(args), len(outs)
 
     def body(*refs):
@@ -28,7 +28,7 @@
     return pl.pallas_call(
         body,
         out_shape=list(outs),
-        in_specs=[HBM if i in far else ANY for i in range(len(args))],
+        in_specs=[HBM if i in far else VMEM if i in here else ANY for i in range(len(args))],
         out_specs=[VMEM] * len(outs),
         scratch_shapes=list(scratch) + [pltpu.SemaphoreType.DMA((copies,))],
         compiler_params=pltpu.CompilerParams(vmem_limit_bytes=24 * 1024 * 1024),
@@ -193,7 +193,7 @@
     asked, put, rows, held = scratch
     cap = pieces[0].shape[0]
     begun = begin(sems, [(asked_any, asked), (put_any, put), (rows_any, rows)])
-    end(gather_values(values_ref, cap, given[3:], sems, 3))
+    end(gather_values(values_ref, cap, given[3:-1], sems, 3))
     end(begun)
     events = values_ref.shape[0]
     wide = jnp.concatenate([values_ref[...], jnp.ones((events, LANES), BF)], axis=1)
@@ -252,11 +252,44 @@
     return p * (1.0 - 2.0 * odd)
 
 
+def products(message, gates, sums, before, out_ref):
+    long, width = message.shape[1], 2 * LANES
+    tall = 256
+
+    def put(start, value):
+        stop = start + value.shape[0]
+        if before is not None:
+            value = value + before[start:stop, :]
+        out_ref[start:stop, :] = value.astype(out_ref.dtype)
+
+    for i in range(long // tall):
+        rows = message[:, i * tall : (i + 1) * tall]
+        columns = gates[...] if i * tall < width else gates[:, : 3 * LANES]
+        product = lax.dot_general(
+            rows, columns, (((0,), (0,)), ((), ())), preferred_element_type=F32
+        )
+        for g in range(3):
+            put(g * long + i * tall, product[:, g * LANES : (g + 1) * LANES])
+        if i * tall < width:
+            put(3 * long + i * tall, product[:, 3 * LANES :])
+    top = 3 * long + width
+    pad = out_ref.shape[0] - top
+    tail = jnp.concatenate(sums + [jnp.zeros((pad - 4, LANES), F32)], axis=0)
+    put(top, tail)
+
+
+def grads_kernel(sems, given, made, scratch):
+    message, gates, sums = given
+    products(message, gates, [sums[g : g + 1, :] for g in range(4)], None, made[0])
+
+
 def batch_kernel(nodes, batch, final, prior, sems, given, made, scratch):
     facts_any, edge_any, edge_other_any, w_in_any, w_hid_any, up_any = given[:6]
     own_pieces, other_pieces = given[6 : 6 + nodes], given[6 + nodes : 6 + 2 * nodes]
     rest = given[6 + 2 * nodes :]
     message, facts, edge, w_in, w_hid, gates, up, fresh = scratch[:8]
+    if not final:
+        message, gates = made[2:4]
     cap = own_pieces[0].shape[0]
     events = nodes * cap
     z, f = lax.axis_index("node"), lax.axis_index("feat")
@@ -339,28 +372,10 @@
         upper = z // (nodes // 2)
         made[0][...] = fresh[pl.ds(pl.multiple_of((1 - upper) * few, few), few), :]
         made[1][...] = fresh[pl.ds(pl.multiple_of(upper * few, few), few), :]
-    out_ref = made[-1]
-
-    def put(start, value):
-        stop = start + value.shape[0]
-        if prior:
-            value = value + before[start:stop, :]
-        out_ref[start:stop, :] = value.astype(out_ref.dtype)
-
-    for i in range(long // tall):
-        rows = message[:, i * tall : (i + 1) * tall]
-        columns = gates[...] if i * tall < width else gates[:, : 3 * LANES]
-        product = lax.dot_general(
-            rows, columns, (((0,), (0,)), ((), ())), preferred_element_type=F32
-        )
-        for g in range(3):
-            put(g * long + i * tall, product[:, g * LANES : (g + 1) * LANES])
-        if i * tall < width:
-            put(3 * long + i * tall, product[:, 3 * LANES :])
-    top = 3 * long + width
-    pad = out_ref.shape[0] - top
-    tail = jnp.concatenate(sums + [jnp.zeros((pad - 4, LANES), F32)], axis=0)
-    put(top, tail)
+    if final:
+        products(message, gates, sums, before if prior else None, made[-1])
+    else:
+        made[4][...] = jnp.concatenate(sums + [jnp.zeros((4, LANES), F32)], axis=0)
 
 
 def middle_kernel(nodes, segs, first, sems, given, made, scratch):
@@ -505,15 +520,27 @@
         if totals is not None:
             rooms.append(pltpu.VMEM((total_rows, half), F32))
         copies = 7 + 2 * nodes
-        *fresh, totals = run(
+        before_grads = [shape((events // 2, half), BF)] * 2 + [
+            shape((events, long), BF),
+            shape((events, 4 * half), BF),
+            shape((8, half), F32),
+        ]
+        outs = run(
             lambda *a, b=b, last=final, p=totals is not None: batch_kernel(nodes, b, last, p, *a),
-            ([piece] * nodes if final else [shape((events // 2, half), BF)] * 2)
-            + [shape((total_rows, half), BF if final else F32)],
+            [piece] * nodes + [shape((total_rows, half), BF)] if final else before_grads,
             given,
             rooms,
             copies,
             (1, 3, 4, 5),
         )
+        if final:
+            fresh, totals = outs[:-1], outs[-1]
+        else:
+            assert b == 0
+            fresh = outs[:2]
+            totals = run(
+                grads_kernel, [shape((total_rows, half), F32)], outs[2:], [], 1, (), (0, 1, 2)
+            )[0]
         if not final:
             hops = [seg_next(side) for side in fresh]
             put, rows = run(
@@ -537,7 +564,7 @@
             values, *served = run(
                 lambda *a, b=b: next_kernel(b, *a),
                 [shape((spread, half), BF)] + [piece] * nodes,
-                [asked, put, rows] + values,
+                [asked, put, rows] + values + [totals],
                 [numbers, line, wide_rows, wide_rows],
                 3 + nodes,
             )
@@ -576,7 +603,7 @@
         parts[first : first + few] = run(
             lambda *a, first=first: middle_kernel(nodes, segs, first, *a),
             [shape((chunk, half), BF)] * few,
-            [totals] + got[side] + (returned[1:] if side else []),
+            [totals] + got[side] + ([] if side else returned[1:]),
             [share] * (segs + 1),
             segs,
         )

time: 110 us -> 107 us (0.973)
  starting transfers between devices: 43.2 us -> 40.6 us
    ppermute x21, starting transfers between devices: 31 us -> 28.3 us  [node_swap(): return lax.ppermute(block, 'node', [(i, i ^ k) for i in range(nodes)])]
    unnamed x31 -> x29, local copies, waits for them, and re-layouts: 4.35 us -> 3.62 us
    pallas_call x14 -> x15, Pallas kernels: 22.7 us -> 23 us  [run(): pl.pallas_call(body, out_shape=list(outs), in_specs=[HBM if i in far else...]
  transfers between devices with their start and end apart: 37 -> 37, of which waited for: 20 -> 19; matrix products, arithmetic and copies ran while one was open for 3% -> 3% of each run, Pallas kernels for 11% -> 12%
where the time goes in v6:
time: 107 us; the launch traced here: 106 us
  starting transfers between devices  40.6 us (38%)
  waiting for transfers between devices  33.9 us (32%)
  Pallas kernels  23 us (21%)
  local copies, waits for them, and re-layouts  5.2 us (5%)
  other arithmetic  2.27 us (2%)
  between operations  1.18 us (1%)
    ppermute x21, starting transfers between devices, node_swap(): return lax.ppermute(block, 'node', [(i, i ^ k) for i in range(nodes)])  28.3 us
    ppermute x21, waiting for transfers between devices, node_swap(): return lax.ppermute(block, 'node', [(i, i ^ k) for i in range(nodes)])  26.9 us
    pallas_call x15, Pallas kernels, run(): pl.pallas_call(body, out_shape=list(outs), in_specs=[HBM if i in far else...  23 us
    ppermute x3, starting transfers between devices, seg_next(): return lax.ppermute(block, 'seg', [(i, i + 1) for i in range(segs - 1)])  6.02 us
    ppermute x4, starting transfers between devices, seg_swap(): return lax.ppermute(block, 'seg', [(i, i ^ x) for i in range(segs)])  4.82 us
    unnamed x29, local copies, waits for them, and re-layouts  3.62 us
    ppermute x9, waiting for transfers between devices, feat_swap(): return lax.ppermute(block, 'feat', [(0, 1), (1, 0)])  2.79 us
    ppermute x3, waiting for transfers between devices, seg_next(): return lax.ppermute(block, 'seg', [(i, i + 1) for i in range(segs - 1)])  2.48 us
  transfers between devices with their start and end apart: 37, of which 19 were waited for; matrix products, arithmetic and copies ran while one was open for 3% of the time, Pallas kernels for 12%

profile of v6, /device:TPU:0, one launch (start us, length us, event | category | flops | bytes accessed | tf_op | source)
XLA Modules:
  0.0 106.2 jit_solution(13789852112237115802)
XLA Ops:
  1.5 3.1 %collective-permute-start = (s32[2,256]{1,0:T(2,128)S(1)}, s32[2,256]{1,0:T(2,128)S(1)}, u32[]{:S(2)}, u32[]{:S(2)}) collective-permute-start(s32[2,256]{1,0:T(2,128)S(1)} %bitcast.44), channel_id=1, source_target_pairs={{0,4},{4,0},{8,12},{12,8},{1,5},{5,1},{9,13},{13,9},{2,6},{6,2},{1... | collective-permute-start | bytes 6152 | tf_op jit(solution)/shard_map/ppermute | solution.py:443
  4.5 2.6 %collective-permute-start.1 = (s32[2,256]{1,0:T(2,128)S(1)}, s32[2,256]{1,0:T(2,128)S(1)}, u32[]{:S(2)}, u32[]{:S(2)}) collective-permute-start(s32[2,256]{1,0:T(2,128)S(1)} %bitcast.45), channel_id=1, source_target_pairs={{0,8},{4,12},{8,0},{12,4},{1,9},{5,13},{9,1},{13,5},{2,10},{6,14},... | collective-permute-start | bytes 6152 | tf_op jit(solution)/shard_map/ppermute | solution.py:443
  14.2 3.4 %collective-permute-start.3 = (bf16[2064,128]{1,0:T(8,128)(2,1)S(1)}, bf16[2064,128]{1,0:T(8,128)(2,1)S(1)}, u32[]{:S(2)}, u32[]{:S(2)}) collective-permute-start(bf16[2064,128]{1,0:T(8,128)(2,1)S(1)} %shard_map.149), channel_id=1, source_target_pairs={{0,2},{1,3},{4,6},{5,7},{8,10},{9,11},{12,14},{13,15},{16,18},{17,... | collective-permute-start | bytes 1585160 | tf_op jit(solution)/shard_map/ppermute | solution.py:449
  18.7 2.0 %collective-permute-start.7 = (bf16[256,128]{1,0:T(8,128)(2,1)S(1)}, bf16[256,128]{1,0:T(8,128)(2,1)S(1)}, u32[]{:S(2)}, u32[]{:S(2)}) collective-permute-start(bf16[256,128]{1,0:T(8,128)(2,1)S(1)} %get-tuple-element.43), channel_id=1, source_target_pairs={{0,12},{4,8},{8,4},{12,0},{1,13},{5,9},{9,5},{13,1},{2,14},{6,10},... | collective-permute-start | bytes 196616 | tf_op jit(solution)/shard_map/ppermute | solution.py:443
  21.2 5.0 %collective-permute-done.6.refs_8_ = bf16[256,128]{1,0:T(8,128)(2,1)S(1)} collective-permute-done((bf16[256,128]{1,0:T(8,128)(2,1)S(1)}, bf16[256,128]{1,0:T(8,128)(2,1)S(1)}, u32[]{:S(2)}, u32[]{:S(2)}) %collective-permute-start.6) | collective-permute-done | bytes 65568 | tf_op jit(solution)/shard_map/ppermute | solution.py:443
  28.8 4.3 %shard_map.151 = (bf16[512,128]{1,0:T(8,128)(2,1)S(1)}, bf16[512,128]{1,0:T(8,128)(2,1)S(1)}, bf16[1024,768]{1,0:T(8,128)(2,1)S(1)}, bf16[1024,512]{1,0:T(8,128)(2,1)S(1)}, f32[8,128]{1,0:T(8,128)S(1)}) custom-call(f32[40,128]{1,0:T(8,128)S(1)} %concatenate.9.refs_2_.refs_0_, bf16[2,64,1024]{2,1,0:T(8,128)(2,1)S(1)} %bitcast.37, ...), custom_call_target="tpu_custom_call" | custom-call | bytes 5267456 | tf_op jit(solution)/shard_map/pallas_call | solution.py:28
  35.7 2.5 %collective-permute-done.14.refs_1_ = bf16[512,128]{1,0:T(8,128)(2,1)S(1)} collective-permute-done((bf16[512,128]{1,0:T(8,128)(2,1)S(1)}, bf16[512,128]{1,0:T(8,128)(2,1)S(1)}, u32[]{:S(2)}, u32[]{:S(2)}) %collective-permute-start.14) | collective-permute-done | bytes 131104 | tf_op jit(solution)/shard_map/ppermute | solution.py:449
  39.7 2.0 %collective-permute-start.16 = (bf16[256,128]{1,0:T(8,128)(2,1)S(1)}, bf16[256,128]{1,0:T(8,128)(2,1)S(1)}, u32[]{:S(2)}, u32[]{:S(2)}) collective-permute-start(bf16[256,128]{1,0:T(8,128)(2,1)S(1)} %get-tuple-element.49), channel_id=1, source_target_pairs={{0,12},{4,8},{8,4},{12,0},{1,13},{5,9},{9,5},{13,1},{2,14},{6,10},... | collective-permute-start | bytes 196616 | tf_op jit(solution)/shard_map/ppermute | solution.py:443
  47.9 1.7 %shard_map.155 = (bf16[1024,128]{1,0:T(8,128)(2,1)S(1)}, bf16[256,128]{1,0:T(8,128)(2,1)}, bf16[256,128]{1,0:T(8,128)(2,1)S(1)}, bf16[256,128]{1,0:T(8,128)(2,1)S(1)}, bf16[256,128]{1,0:T(8,128)(2,1)S(1)}) custom-call(s32[2,1024]{1,0:T(2,128)S(1)} %get-tuple-element.37.refs_1_.refs_0_, s32[1,1024]{1,0:T(1,128)S(1)} %get-tuple-element.38.refs_1_.refs_0_, ...), custom_call_target="tpu_custom_call" | custom-call | bytes 2437120 | tf_op jit(solution)/shard_map/pallas_call | solution.py:28
  50.5 2.2 %collective-permute-start.18 = (bf16[256,128]{1,0:T(8,128)(2,1)S(1)}, bf16[256,128]{1,0:T(8,128)(2,1)}, u32[]{:S(2)}, u32[]{:S(2)}) collective-permute-start(bf16[256,128]{1,0:T(8,128)(2,1)S(1)} %get-tuple-element.56), channel_id=1, source_target_pairs={{0,8},{4,12},{8,0},{12,4},{1,9},{5,13},{9,1},{13,5},{2,10},{6,14},... | collective-permute-start | bytes 196616 | tf_op jit(solution)/shard_map/ppermute | solution.py:443
  52.7 2.0 %collective-permute-start.19 = (bf16[256,128]{1,0:T(8,128)(2,1)S(1)}, bf16[256,128]{1,0:T(8,128)(2,1)}, u32[]{:S(2)}, u32[]{:S(2)}) collective-permute-start(bf16[256,128]{1,0:T(8,128)(2,1)S(1)} %get-tuple-element.57), channel_id=1, source_target_pairs={{0,12},{4,8},{8,4},{12,0},{1,13},{5,9},{9,5},{13,1},{2,14},{6,10},... | collective-permute-start | bytes 196616 | tf_op jit(solution)/shard_map/ppermute | solution.py:443
  55.2 1.9 %collective-permute-done.18.refs_8_ = bf16[256,128]{1,0:T(8,128)(2,1)} collective-permute-done((bf16[256,128]{1,0:T(8,128)(2,1)S(1)}, bf16[256,128]{1,0:T(8,128)(2,1)}, u32[]{:S(2)}, u32[]{:S(2)}) %collective-permute-start.18) | collective-permute-done | bytes 65568 | tf_op jit(solution)/shard_map/ppermute | solution.py:443
  62.1 5.0 %shard_map.157 = (bf16[256,128]{1,0:T(8,128)(2,1)S(1)}, bf16[256,128]{1,0:T(8,128)(2,1)S(1)}, bf16[256,128]{1,0:T(8,128)(2,1)S(1)}, bf16[256,128]{1,0:T(8,128)(2,1)S(1)}, bf16[2688,128]{1,0:T(8,128)(2,1)S(1)}) custom-call(f32[40,128]{1,0:T(8,128)S(1)} %copy-done.8, bf16[2,64,1024]{2,1,0:T(8,128)(2,1)S(1)} %bitcast.38, ...), custom_call_target="tpu_custom_call" | custom-call | bytes 4706304 | tf_op jit(solution)/shard_map/pallas_call | solution.py:28
  67.2 2.6 %collective-permute-start.27 = (bf16[672,128]{1,0:T(8,128)(2,1)S(1)}, bf16[672,128]{1,0:T(8,128)(2,1)S(1)}, u32[]{:S(2)}, u32[]{:S(2)}) collective-permute-start(bf16[672,128]{1,0:T(8,128)(2,1)S(1)} %get-tuple-element.70), channel_id=1, source_target_pairs={{0,2},{2,0},{1,3},{3,1},{4,6},{6,4},{5,7},{7,5},{8,10},{10,8},{9,1... | collective-permute-start | bytes 516104 | tf_op jit(solution)/shard_map/ppermute | solution.py:446
  69.9 2.6 %collective-permute-start.25 = (bf16[256,128]{1,0:T(8,128)(2,1)S(1)}, bf16[256,128]{1,0:T(8,128)(2,1)S(1)}, u32[]{:S(2)}, u32[]{:S(2)}) collective-permute-start(bf16[256,128]{1,0:T(8,128)(2,1)S(1)} %get-tuple-element.60), channel_id=1, source_target_pairs={{0,8},{4,12},{8,0},{12,4},{1,9},{5,13},{9,1},{13,5},{2,10},{6,14},... | collective-permute-start | bytes 196616 | tf_op jit(solution)/shard_map/ppermute | solution.py:443
  72.5 1.8 %collective-permute-start.26 = (bf16[256,128]{1,0:T(8,128)(2,1)S(1)}, bf16[256,128]{1,0:T(8,128)(2,1)S(1)}, u32[]{:S(2)}, u32[]{:S(2)}) collective-permute-start(bf16[256,128]{1,0:T(8,128)(2,1)S(1)} %get-tuple-element.61), channel_id=1, source_target_pairs={{0,12},{4,8},{8,4},{12,0},{1,13},{5,9},{9,5},{13,1},{2,14},{6,10},... | collective-permute-start | bytes 196616 | tf_op jit(solution)/shard_map/ppermute | solution.py:443
  75.5 2.2 %collective-permute-done.25.refs_4_.refs_3_ = bf16[256,128]{1,0:T(8,128)(2,1)S(1)} collective-permute-done((bf16[256,128]{1,0:T(8,128)(2,1)S(1)}, bf16[256,128]{1,0:T(8,128)(2,1)S(1)}, u32[]{:S(2)}, u32[]{:S(2)}) %collective-permute-start.25) | collective-permute-done | bytes 65568 | tf_op jit(solution)/shard_map/ppermute | solution.py:443
  80.4 1.9 %collective-permute-start.31 = (bf16[336,128]{1,0:T(8,128)(2,1)S(1)}, bf16[336,128]{1,0:T(8,128)(2,1)S(1)}, u32[]{:S(2)}, u32[]{:S(2)}) collective-permute-start(bf16[336,128]{1,0:T(8,128)(2,1)S(1)} %get-tuple-element.66), channel_id=1, source_target_pairs={{0,12},{4,8},{8,4},{12,0},{1,13},{5,9},{9,5},{13,1},{2,14},{6,10},... | collective-permute-start | bytes 258056 | tf_op jit(solution)/shard_map/ppermute | solution.py:443
  82.3 5.3 %collective-permute-done.30 = bf16[336,128]{1,0:T(8,128)(2,1)S(1)} collective-permute-done((bf16[336,128]{1,0:T(8,128)(2,1)S(1)}, bf16[336,128]{1,0:T(8,128)(2,1)S(1)}, u32[]{:S(2)}, u32[]{:S(2)}) %collective-permute-start.30) | collective-permute-done | bytes 86048 | tf_op jit(solution)/shard_map/ppermute | solution.py:443
  87.7 2.0 %collective-permute-start.33 = (bf16[336,128]{1,0:T(8,128)(2,1)S(1)}, bf16[336,128]{1,0:T(8,128)(2,1)S(1)}, u32[]{:S(2)}, u32[]{:S(2)}) collective-permute-start(bf16[336,128]{1,0:T(8,128)(2,1)S(1)} %add_convert_fusion), channel_id=1, source_target_pairs={{0,8},{4,12},{8,0},{12,4},{1,9},{5,13},{9,1},{13,5},{2,10},{6,14},... | collective-permute-start | bytes 258056 | tf_op jit(solution)/shard_map/ppermute | solution.py:443
  89.7 2.1 %collective-permute-start.34 = (bf16[336,128]{1,0:T(8,128)(2,1)S(1)}, bf16[336,128]{1,0:T(8,128)(2,1)S(1)}, u32[]{:S(2)}, u32[]{:S(2)}) collective-permute-start(bf16[336,128]{1,0:T(8,128)(2,1)S(1)} %add_convert_fusion), channel_id=1, source_target_pairs={{0,12},{4,8},{8,4},{12,0},{1,13},{5,9},{9,5},{13,1},{2,14},{6,10},... | collective-permute-start | bytes 258056 | tf_op jit(solution)/shard_map/ppermute | solution.py:443
  91.8 4.7 %collective-permute-done.33 = bf16[336,128]{1,0:T(8,128)(2,1)S(1)} collective-permute-done((bf16[336,128]{1,0:T(8,128)(2,1)S(1)}, bf16[336,128]{1,0:T(8,128)(2,1)S(1)}, u32[]{:S(2)}, u32[]{:S(2)}) %collective-permute-start.33) | collective-permute-done | bytes 86048 | tf_op jit(solution)/shard_map/ppermute | solution.py:443
  100.1 2.7 %shard_map.158 = f32[2048,128]{1,0:T(8,128)} custom-call(s32[2,1024]{1,0:T(2,128)S(1)} %get-tuple-element.37.refs_1_.refs_0_, f32[2048,128]{1,0:T(8,128)S(1)} %shard_map.156.refs_1_, bf16[256,128]{1,0:T(8,128)(2,1)S(1)} %get-tuple-element.58.refs_2_, bf16[256,128]{1,0:T(8,128)(2,1)S(1)} %collective-permute-done.24.refs_3_.refs_2_, ...), custom_call_target="tpu_custom_call" | custom-call | bytes 2367488 | tf_op jit(solution)/shard_map/pallas_call | solution.py:28
  103.9 2.1 %shard_map.161 = (f32[3,768,128]{2,1,0:T(8,128)}, f32[3,256,128]{2,1,0:T(8,128)}, f32[4,128]{1,0:T(4,128)}) custom-call(bf16[672,128]{1,0:T(8,128)(2,1)S(1)} %pad_maximum_fusion.refs_0_, bf16[672,128]{1,0:T(8,128)(2,1)S(1)} %constant_dynamic-update-slice_fusion.refs_1_, bf16[672,128]{1,0:T(8,128)(2,1)S(1)} %collective-permute-done.35.refs_2_, ...), custom_call_target="tpu_custom_call" | custom-call | bytes 2263040 | tf_op jit(solution)/shard_map/pallas_call | solution.py:28
  (107 shorter events, 37.2 us)
Async XLA Ops:
  1.5 8.7 %collective-permute-start = (s32[2,256]{1,0:T(2,128)S(1)}, s32[2,256]{1,0:T(2,128)S(1)}, u32[]{:S(2)}, u32[]{:S(2)}) collective-permute-start(s32[2,256]{1,0:T(2,128)S(1)} %bitcast.44), channel_id=1, source_target_pairs={{0,4},{4,0},{8,12},{12,8},{1,5},{5,1},{9,13},{13,9},{2,6},{6,2},{1... | collective-permute-start | bytes 6152 | tf_op jit(solution)/shard_map/ppermute | solution.py:443
  4.5 7.0 %collective-permute-start.1 = (s32[2,256]{1,0:T(2,128)S(1)}, s32[2,256]{1,0:T(2,128)S(1)}, u32[]{:S(2)}, u32[]{:S(2)}) collective-permute-start(s32[2,256]{1,0:T(2,128)S(1)} %bitcast.45), channel_id=1, source_target_pairs={{0,8},{4,12},{8,0},{12,4},{1,9},{5,13},{9,1},{13,5},{2,10},{6,14},... | collective-permute-start | bytes 6152 | tf_op jit(solution)/shard_map/ppermute | solution.py:443
  14.2 27.6 %collective-permute-start.3 = (bf16[2064,128]{1,0:T(8,128)(2,1)S(1)}, bf16[2064,128]{1,0:T(8,128)(2,1)S(1)}, u32[]{:S(2)}, u32[]{:S(2)}) collective-permute-start(bf16[2064,128]{1,0:T(8,128)(2,1)S(1)} %shard_map.149), channel_id=1, source_target_pairs={{0,2},{1,3},{4,6},{5,7},{8,10},{9,11},{12,14},{13,15},{16,18},{17,... | collective-permute-start | bytes 1585160 | tf_op jit(solution)/shard_map/ppermute | solution.py:449
  17.6 11.1 %collective-permute-start.4 = (bf16[2,64,1024]{2,1,0:T(8,128)(2,1)S(1)}, bf16[2,64,1024]{2,1,0:T(8,128)(2,1)S(1)}, u32[]{:S(2)}, u32[]{:S(2)}) collective-permute-start(bf16[2,64,1024]{2,1,0:T(8,128)(2,1)S(1)} %bitcast.36), channel_id=1, source_target_pairs={{0,1},{1,0},{2,3},{3,2},{4,5},{5,4},{6,7},{7,6},{8,9},{9,8},{10,11... | collective-permute-start | bytes 786440 | tf_op jit(solution)/shard_map/ppermute | solution.py:452
  17.7 8.5 %collective-permute-start.6 = (bf16[256,128]{1,0:T(8,128)(2,1)S(1)}, bf16[256,128]{1,0:T(8,128)(2,1)S(1)}, u32[]{:S(2)}, u32[]{:S(2)}) collective-permute-start(bf16[256,128]{1,0:T(8,128)(2,1)S(1)} %get-tuple-element.42), channel_id=1, source_target_pairs={{0,8},{4,12},{8,0},{12,4},{1,9},{5,13},{9,1},{13,5},{2,10},{6,14},... | collective-permute-start | bytes 196616 | tf_op jit(solution)/shard_map/ppermute | solution.py:443
  18.7 7.6 %collective-permute-start.7 = (bf16[256,128]{1,0:T(8,128)(2,1)S(1)}, bf16[256,128]{1,0:T(8,128)(2,1)S(1)}, u32[]{:S(2)}, u32[]{:S(2)}) collective-permute-start(bf16[256,128]{1,0:T(8,128)(2,1)S(1)} %get-tuple-element.43), channel_id=1, source_target_pairs={{0,12},{4,8},{8,4},{12,0},{1,13},{5,9},{9,5},{13,1},{2,14},{6,10},... | collective-permute-start | bytes 196616 | tf_op jit(solution)/shard_map/ppermute | solution.py:443
  20.7 6.6 %collective-permute-start.5 = (bf16[256,128]{1,0:T(8,128)(2,1)S(1)}, bf16[256,128]{1,0:T(8,128)(2,1)S(1)}, u32[]{:S(2)}, u32[]{:S(2)}) collective-permute-start(bf16[256,128]{1,0:T(8,128)(2,1)S(1)} %get-tuple-element.41), channel_id=1, source_target_pairs={{0,4},{4,0},{8,12},{12,8},{1,5},{5,1},{9,13},{13,9},{2,6},{6,2},{1... | collective-permute-start | bytes 196616 | tf_op jit(solution)/shard_map/ppermute | solution.py:443
  34.4 8.7 %collective-permute-start.12 = (bf16[512,128]{1,0:T(8,128)(2,1)S(1)}, bf16[512,128]{1,0:T(8,128)(2,1)S(1)}, u32[]{:S(2)}, u32[]{:S(2)}) collective-permute-start(bf16[512,128]{1,0:T(8,128)(2,1)S(1)} %get-tuple-element.44.refs_0_), channel_id=1, source_target_pairs={{0,2},{1,3},{4,6},{5,7},{8,10},{9,11},{12,14},{13,15},{16,18},{17,... | collective-permute-start | bytes 393224 | tf_op jit(solution)/shard_map/ppermute | solution.py:449
  38.3 7.7 %collective-permute-start.15 = (bf16[256,128]{1,0:T(8,128)(2,1)S(1)}, bf16[256,128]{1,0:T(8,128)(2,1)S(1)}, u32[]{:S(2)}, u32[]{:S(2)}) collective-permute-start(bf16[256,128]{1,0:T(8,128)(2,1)S(1)} %get-tuple-element.48), channel_id=1, source_target_pairs={{0,8},{4,12},{8,0},{12,4},{1,9},{5,13},{9,1},{13,5},{2,10},{6,14},... | collective-permute-start | bytes 196616 | tf_op jit(solution)/shard_map/ppermute | solution.py:443
  39.7 6.7 %collective-permute-start.16 = (bf16[256,128]{1,0:T(8,128)(2,1)S(1)}, bf16[256,128]{1,0:T(8,128)(2,1)S(1)}, u32[]{:S(2)}, u32[]{:S(2)}) collective-permute-start(bf16[256,128]{1,0:T(8,128)(2,1)S(1)} %get-tuple-element.49), channel_id=1, source_target_pairs={{0,12},{4,8},{8,4},{12,0},{1,13},{5,9},{9,5},{13,1},{2,14},{6,10},... | collective-permute-start | bytes 196616 | tf_op jit(solution)/shard_map/ppermute | solution.py:443
  50.5 6.7 %collective-permute-start.18 = (bf16[256,128]{1,0:T(8,128)(2,1)S(1)}, bf16[256,128]{1,0:T(8,128)(2,1)}, u32[]{:S(2)}, u32[]{:S(2)}) collective-permute-start(bf16[256,128]{1,0:T(8,128)(2,1)S(1)} %get-tuple-element.56), channel_id=1, source_target_pairs={{0,8},{4,12},{8,0},{12,4},{1,9},{5,13},{9,1},{13,5},{2,10},{6,14},... | collective-permute-start | bytes 196616 | tf_op jit(solution)/shard_map/ppermute | solution.py:443
  52.7 6.2 %collective-permute-start.19 = (bf16[256,128]{1,0:T(8,128)(2,1)S(1)}, bf16[256,128]{1,0:T(8,128)(2,1)}, u32[]{:S(2)}, u32[]{:S(2)}) collective-permute-start(bf16[256,128]{1,0:T(8,128)(2,1)S(1)} %get-tuple-element.57), channel_id=1, source_target_pairs={{0,12},{4,8},{8,4},{12,0},{1,13},{5,9},{9,5},{13,1},{2,14},{6,10},... | collective-permute-start | bytes 196616 | tf_op jit(solution)/shard_map/ppermute | solution.py:443
  67.2 7.7 %collective-permute-start.27 = (bf16[672,128]{1,0:T(8,128)(2,1)S(1)}, bf16[672,128]{1,0:T(8,128)(2,1)S(1)}, u32[]{:S(2)}, u32[]{:S(2)}) collective-permute-start(bf16[672,128]{1,0:T(8,128)(2,1)S(1)} %get-tuple-element.70), channel_id=1, source_target_pairs={{0,2},{2,0},{1,3},{3,1},{4,6},{6,4},{5,7},{7,5},{8,10},{10,8},{9,1... | collective-permute-start | bytes 516104 | tf_op jit(solution)/shard_map/ppermute | solution.py:446
  69.8 9.5 %collective-permute-start.29 = (bf16[672,128]{1,0:T(8,128)(2,1)S(1)}, bf16[672,128]{1,0:T(8,128)(2,1)S(1)}, u32[]{:S(2)}, u32[]{:S(2)}) collective-permute-start(bf16[672,128]{1,0:T(8,128)(2,1)S(1)} %get-tuple-element.71), channel_id=1, source_target_pairs={{0,2},{2,0},{1,3},{3,1},{4,6},{6,4},{5,7},{7,5},{8,10},{10,8},{9,1... | collective-permute-start | bytes 516104 | tf_op jit(solution)/shard_map/ppermute | solution.py:446
  69.9 7.8 %collective-permute-start.25 = (bf16[256,128]{1,0:T(8,128)(2,1)S(1)}, bf16[256,128]{1,0:T(8,128)(2,1)S(1)}, u32[]{:S(2)}, u32[]{:S(2)}) collective-permute-start(bf16[256,128]{1,0:T(8,128)(2,1)S(1)} %get-tuple-element.60), channel_id=1, source_target_pairs={{0,8},{4,12},{8,0},{12,4},{1,9},{5,13},{9,1},{13,5},{2,10},{6,14},... | collective-permute-start | bytes 196616 | tf_op jit(solution)/shard_map/ppermute | solution.py:443
  72.5 6.8 %collective-permute-start.26 = (bf16[256,128]{1,0:T(8,128)(2,1)S(1)}, bf16[256,128]{1,0:T(8,128)(2,1)S(1)}, u32[]{:S(2)}, u32[]{:S(2)}) collective-permute-start(bf16[256,128]{1,0:T(8,128)(2,1)S(1)} %get-tuple-element.61), channel_id=1, source_target_pairs={{0,12},{4,8},{8,4},{12,0},{1,13},{5,9},{9,5},{13,1},{2,14},{6,10},... | collective-permute-start | bytes 196616 | tf_op jit(solution)/shard_map/ppermute | solution.py:443
  75.5 6.9 %collective-permute-start.28 = (bf16[336,128]{1,0:T(8,128)(2,1)S(1)}, bf16[336,128]{1,0:T(8,128)(2,1)S(1)}, u32[]{:S(2)}, u32[]{:S(2)}) collective-permute-start(bf16[336,128]{1,0:T(8,128)(2,1)S(1)} %get-tuple-element.64), channel_id=1, source_target_pairs={{0,4},{4,0},{8,12},{12,8},{1,5},{5,1},{9,13},{13,9},{2,6},{6,2},{1... | collective-permute-start | bytes 258056 | tf_op jit(solution)/shard_map/ppermute | solution.py:443
  79.8 7.9 %collective-permute-start.30 = (bf16[336,128]{1,0:T(8,128)(2,1)S(1)}, bf16[336,128]{1,0:T(8,128)(2,1)S(1)}, u32[]{:S(2)}, u32[]{:S(2)}) collective-permute-start(bf16[336,128]{1,0:T(8,128)(2,1)S(1)} %get-tuple-element.65), channel_id=1, source_target_pairs={{0,8},{4,12},{8,0},{12,4},{1,9},{5,13},{9,1},{13,5},{2,10},{6,14},... | collective-permute-start | bytes 258056 | tf_op jit(solution)/shard_map/ppermute | solution.py:443
  80.4 7.2 %collective-permute-start.31 = (bf16[336,128]{1,0:T(8,128)(2,1)S(1)}, bf16[336,128]{1,0:T(8,128)(2,1)S(1)}, u32[]{:S(2)}, u32[]{:S(2)}) collective-permute-start(bf16[336,128]{1,0:T(8,128)(2,1)S(1)} %get-tuple-element.66), channel_id=1, source_target_pairs={{0,12},{4,8},{8,4},{12,0},{1,13},{5,9},{9,5},{13,1},{2,14},{6,10},... | collective-permute-start | bytes 258056 | tf_op jit(solution)/shard_map/ppermute | solution.py:443
  87.7 8.8 %collective-permute-start.33 = (bf16[336,128]{1,0:T(8,128)(2,1)S(1)}, bf16[336,128]{1,0:T(8,128)(2,1)S(1)}, u32[]{:S(2)}, u32[]{:S(2)}) collective-permute-start(bf16[336,128]{1,0:T(8,128)(2,1)S(1)} %add_convert_fusion), channel_id=1, source_target_pairs={{0,8},{4,12},{8,0},{12,4},{1,9},{5,13},{9,1},{13,5},{2,10},{6,14},... | collective-permute-start | bytes 258056 | tf_op jit(solution)/shard_map/ppermute | solution.py:443
  89.7 6.9 %collective-permute-start.34 = (bf16[336,128]{1,0:T(8,128)(2,1)S(1)}, bf16[336,128]{1,0:T(8,128)(2,1)S(1)}, u32[]{:S(2)}, u32[]{:S(2)}) collective-permute-start(bf16[336,128]{1,0:T(8,128)(2,1)S(1)} %add_convert_fusion), channel_id=1, source_target_pairs={{0,12},{4,8},{8,4},{12,0},{1,13},{5,9},{9,5},{13,1},{2,14},{6,10},... | collective-permute-start | bytes 258056 | tf_op jit(solution)/shard_map/ppermute | solution.py:443
  91.8 6.1 %collective-permute-start.32 = (bf16[336,128]{1,0:T(8,128)(2,1)S(1)}, bf16[336,128]{1,0:T(8,128)(2,1)S(1)}, u32[]{:S(2)}, u32[]{:S(2)}) collective-permute-start(bf16[336,128]{1,0:T(8,128)(2,1)S(1)} %add_convert_fusion), channel_id=1, source_target_pairs={{0,4},{4,0},{8,12},{12,8},{1,5},{5,1},{9,13},{13,9},{2,6},{6,2},{1... | collective-permute-start | bytes 258056 | tf_op jit(solution)/shard_map/ppermute | solution.py:443
  96.5 6.3 %collective-permute-start.36 = (bf16[672,128]{1,0:T(8,128)(2,1)S(1)}, bf16[672,128]{1,0:T(8,128)(2,1)S(1)}, u32[]{:S(2)}, u32[]{:S(2)}) collective-permute-start(bf16[672,128]{1,0:T(8,128)(2,1)S(1)} %constant_dynamic-update-slice_fusion.refs_1_), channel_id=1, source_target_pairs={{0,2},{2,0},{1,3},{3,1},{4,6},{6,4},{5,7},{7,5},{8,10},{10,8},{9,1... | collective-permute-start | bytes 516104 | tf_op jit(solution)/shard_map/ppermute | solution.py:446
  97.9 6.0 %collective-permute-start.35 = (bf16[672,128]{1,0:T(8,128)(2,1)S(1)}, bf16[672,128]{1,0:T(8,128)(2,1)S(1)}, u32[]{:S(2)}, u32[]{:S(2)}) collective-permute-start(bf16[672,128]{1,0:T(8,128)(2,1)S(1)} %pad_maximum_fusion.refs_0_), channel_id=1, source_target_pairs={{0,2},{2,0},{1,3},{3,1},{4,6},{6,4},{5,7},{7,5},{8,10},{10,8},{9,1... | collective-permute-start | bytes 516104 | tf_op jit(solution)/shard_map/ppermute | solution.py:446
  (24 other events, 175.0 us)

commit v7 on v6

--- a/solution.py
+++ b/solution.py
@@ -18,7 +18,7 @@
     return jax.ShapeDtypeStruct(tuple(dims), kind)
 
 
-def run(kernel, outs, args, scratch=(), copies=1, far=(), here=()):
+def run(kernel, outs, args, scratch=(), copies=1, far=(), here=(), flops=0):
     b, c = len(args), len(outs)
 
     def body(*refs):
@@ -32,7 +32,7 @@
         out_specs=[VMEM] * len(outs),
         scratch_shapes=list(scratch) + [pltpu.SemaphoreType.DMA((copies,))],
         compiler_params=pltpu.CompilerParams(vmem_limit_bytes=24 * 1024 * 1024),
-        cost_estimate=pl.CostEstimate(flops=0, bytes_accessed=moved, transcendentals=0),
+        cost_estimate=pl.CostEstimate(flops=flops, bytes_accessed=moved, transcendentals=0),
     )(*args)
 
 
@@ -233,6 +233,7 @@
     end(gather_values(values, pieces[0].shape[0], pieces, sems, 2))
     end(begun)
     set_rows(asked[batch : batch + 1, :], values[...], base, made[0])
+    made[1][...] = jnp.zeros(made[1].shape, F32)
 
 
 def cosine(x):
@@ -283,11 +284,37 @@
     products(message, gates, [sums[g : g + 1, :] for g in range(4)], None, made[0])
 
 
+def side_kernel(batch, sems, given, made, scratch):
+    facts_any, edge_any, edge_other_any = given
+    facts, edge = scratch
+    (side_ref,) = made
+    events = side_ref.shape[0]
+    thin = edge_any.shape[1]
+    f = lax.axis_index("feat")
+    own = pl.ds(pl.multiple_of(f * thin, thin), thin)
+    other = pl.ds(pl.multiple_of((1 - f) * thin, thin), thin)
+    pairs = [
+        (facts_any, facts),
+        (edge_any.at[batch], edge.at[own, :]),
+        (edge_other_any.at[batch], edge.at[other, :]),
+    ]
+    end(begin(sems, pairs))
+    lines = events // LANES
+    top = facts.shape[0] - 8
+    freq, phase = facts[top + 4 : top + 5, :], facts[top + 5 : top + 6, :]
+    start = 2 * lines * batch + lines
+    for j in range(lines):
+        span = slice(j * LANES, (j + 1) * LANES)
+        angle = down(facts[start + j : start + j + 1, :]) * freq + phase
+        side_ref[span, :LANES] = cosine(angle).astype(BF)
+        side_ref[span, LANES:] = jnp.transpose(edge[:, span].astype(F32)).astype(BF)
+
+
 def batch_kernel(nodes, batch, final, prior, sems, given, made, scratch):
-    facts_any, edge_any, edge_other_any, w_in_any, w_hid_any, up_any = given[:6]
-    own_pieces, other_pieces = given[6 : 6 + nodes], given[6 + nodes : 6 + 2 * nodes]
-    rest = given[6 + 2 * nodes :]
-    message, facts, edge, w_in, w_hid, gates, up, fresh = scratch[:8]
+    facts_any, side_any, w_in_any, w_hid_any, up_any = given[:5]
+    own_pieces, other_pieces = given[5 : 5 + nodes], given[5 + nodes : 5 + 2 * nodes]
+    rest = given[5 + 2 * nodes :]
+    message, facts, w_in, w_hid, gates, up, fresh = scratch[:7]
     if not final:
         message, gates = made[2:4]
     cap = own_pieces[0].shape[0]
@@ -297,37 +324,22 @@
     other = pl.multiple_of((1 - f) * LANES, LANES)
     width = 2 * LANES
     long = message.shape[1]
-    thin = edge_any.shape[1]
-    pairs = []
+    pairs = [(facts_any, facts)]
     for k in range(nodes):
         at = pl.ds(pl.multiple_of((z ^ k) * cap, cap), cap)
         pairs.append((own_pieces[k], message.at[at, pl.ds(mine, LANES)]))
         pairs.append((other_pieces[k], message.at[at, pl.ds(other, LANES)]))
-    early = [
-        (facts_any, facts),
-        (edge_any.at[batch], edge.at[pl.ds(pl.multiple_of(f * thin, thin), thin), :]),
-        (edge_other_any.at[batch], edge.at[pl.ds(pl.multiple_of((1 - f) * thin, thin), thin), :]),
-    ]
-    late = [(w_in_any, w_in), (w_hid_any, w_hid), (up_any.at[batch], up)]
+    late = [(side_any, message.at[:, 2 * width :]), (w_in_any, w_in), (w_hid_any, w_hid), (up_any.at[batch], up)]
     if prior:
-        before = scratch[8]
+        before = scratch[7]
         late.append((rest[0], before))
     rows_begun = begin(sems, pairs)
-    early_begun = begin(sems, early, len(pairs))
-    late_begun = begin(sems, late, len(pairs) + len(early))
-    end(early_begun)
+    late_begun = begin(sems, late, len(pairs))
+    end(rows_begun)
     lines = events // LANES
     top = facts.shape[0] - 8
     bias_ref = facts[top : top + 4, :]
-    freq, phase = facts[top + 4 : top + 5, :], facts[top + 5 : top + 6, :]
     dst = [facts[2 * lines * batch + j : 2 * lines * batch + j + 1, :] for j in range(lines)]
-    start = 2 * lines * batch + lines
-    for j in range(lines):
-        span = slice(j * LANES, (j + 1) * LANES)
-        angle = down(facts[start + j : start + j + 1, :]) * freq + phase
-        message[span, 2 * width : 2 * width + LANES] = cosine(angle).astype(BF)
-        message[span, 2 * width + LANES :] = jnp.transpose(edge[:, span].astype(F32)).astype(BF)
-    end(rows_begun)
     full = message[:, :width]
     for j in range(events // LANES):
         span = slice(j * LANES, (j + 1) * LANES)
@@ -398,22 +410,41 @@
         made[k][...] = whole[pl.ds(at, chunk), :]
 
 
+def sum_kernel(sems, given, made, scratch):
+    end(begin(sems, list(zip(given, scratch))))
+    total = scratch[0][...].astype(F32)
+    for part in scratch[1:]:
+        total = total + part[...].astype(F32)
+    made[0][...] = total.astype(BF)
+
+
+def widen_kernel(sems, given, made, scratch):
+    (out_ref,), rows = made, given[0].shape[0]
+    end(begin(sems, list(zip(given, scratch))))
+    for x, part in enumerate(scratch):
+        out_ref[x * rows : (x + 1) * rows, :] = part[...].astype(F32)
+
+
 def unpack_kernel(nodes, segs, long, sems, pieces, made, scratch):
     grad_in, grad_hid, grad_bias = made
-    (held,) = scratch
+    held, *far = scratch
     few = nodes // 2
-    chunk = pieces[0].shape[0] // few
+    chunk = pieces[1].shape[0] // few
     z, s = lax.axis_index("node"), lax.axis_index("seg")
-    pairs = []
+
+    def place(x, k):
+        at = pl.multiple_of(((s ^ x) * nodes + (z ^ k)) * chunk, chunk)
+        return pl.ds(at, chunk)
+
+    pairs = list(zip(pieces[1:], far))
     for x in range(segs):
-        for k in range(nodes):
-            at = pl.multiple_of(((s ^ x) * nodes + (z ^ k)) * chunk, chunk)
-            source = pieces[2 * x + k // few]
-            i = k % few
-            pairs.append(
-                (source.at[i * chunk : (i + 1) * chunk, :], held.at[pl.ds(at, chunk), :])
-            )
+        for k in range(few):
+            i = x * few + k
+            pairs.append((pieces[0].at[i * chunk : (i + 1) * chunk, :], held.at[place(x, k), :]))
     end(begin(sems, pairs))
+    for x in range(segs):
+        for k in range(few):
+            held[place(x, few + k), :] = far[x][k * chunk : (k + 1) * chunk, :].astype(F32)
     width = grad_hid.shape[1]
     for g in range(3):
         grad_in[g] = held[g * long : (g + 1) * long, :].astype(F32)
@@ -505,12 +536,18 @@
             )[0]
             handed_memory = seg_next(bundle)
         other_pieces = [feat_swap(p) for p in own_pieces]
-        given = [facts, edge_own, edge_other, w_input, w_hidden, upstream[:, 0]]
+        beside = run(
+            lambda *a, b=b: side_kernel(b, *a),
+            [shape((events, 2 * LANES), BF)],
+            [facts, edge_own, edge_other],
+            [pltpu.VMEM(facts.shape, F32), pltpu.VMEM((2 * edges.shape[-1], events), BF)],
+            3,
+        )[0]
+        given = [facts, beside, w_input, w_hidden, upstream[:, 0]]
         given = given + own_pieces + other_pieces + ([] if totals is None else [totals])
         rooms = [
             pltpu.VMEM((events, long), BF),
             pltpu.VMEM(facts.shape, F32),
-            pltpu.VMEM((2 * edges.shape[-1], events), BF),
             pltpu.VMEM(w_input.shape, BF),
             pltpu.VMEM(w_hidden.shape, BF),
             pltpu.VMEM((events, 4 * half), BF),
@@ -531,7 +568,7 @@
             given,
             rooms,
             copies,
-            (1, 3, 4, 5),
+            (),
         )
         if final:
             fresh, totals = outs[:-1], outs[-1]
@@ -579,13 +616,13 @@
                 narrow = memory_now.astype(BF)
         else:
             returned = exchange(fresh)
-            memory_out = run(
+            memory_out, done = run(
                 lambda *a, b=b: last_kernel(b, *a),
-                [shape((node_rows, half), F32)],
+                [shape((node_rows, half), F32), shape((8, half), F32)],
                 [asked, memory_now] + returned,
                 [numbers, wide_rows, block],
                 2 + nodes,
-            )[0]
+            )
 
     def at(blocks, i):
         return lax.dynamic_index_in_dim(blocks, i, 0, keepdims=False)
@@ -608,18 +645,31 @@
             segs,
         )
     parts = exchange(parts)
-    summed = sum((g.astype(F32) for g in parts[1:]), parts[0].astype(F32)).astype(BF)
+    summed = run(
+        sum_kernel,
+        [shape((chunk, half), BF)],
+        parts + [done],
+        [pltpu.VMEM((chunk, half), BF)] * nodes,
+        nodes,
+    )[0]
     around = [summed] + [node_swap(summed, k) for k in range(1, nodes)]
     sides = [jnp.concatenate(around[:few], axis=0), jnp.concatenate(around[few:], axis=0)]
-    gathered = list(sides)
-    for x in range(1, segs):
-        gathered += [seg_swap(side, x) for side in sides]
+    near, distant = ([side] + [seg_swap(side, x) for x in range(1, segs)] for side in sides)
+    gathered = run(
+        widen_kernel,
+        [shape((segs * few * chunk, half), F32)],
+        near,
+        [share] * segs,
+        segs,
+        flops=0,
+    )
+    gathered = [gathered[0]] + distant
     grads = run(
         lambda *a: unpack_kernel(nodes, segs, long, *a),
         [shape(w_input.shape, F32), shape(w_hidden.shape, F32), shape(bias.shape, F32)],
         gathered,
-        [pltpu.VMEM((total_rows, half), BF)],
-        nodes * segs,
+        [pltpu.VMEM((total_rows, half), F32)] + [share] * segs,
+        segs + few * segs,
     )
     return (memory_out[None], *grads)
 

time: 107 us -> 105 us (0.981)
  waiting for transfers between devices: 33.9 us -> 28.2 us
  starting transfers between devices: 40.6 us -> 43.1 us
  Pallas kernels: 23 us -> 25 us
    ppermute x21, waiting for transfers between devices: 26.9 us -> 22.5 us  [node_swap(): return lax.ppermute(block, 'node', [(i, i ^ k) for i in range(nodes)])]
    ppermute x9, waiting for transfers between devices: 2.79 us -> 0.02 us  [feat_swap(): return lax.ppermute(block, 'feat', [(0, 1), (1, 0)])]
    pallas_call x15 -> x19, Pallas kernels: 23 us -> 25 us  [run(): pl.pallas_call(body, out_shape=list(outs), in_specs=[HBM if i in far else...]
    ppermute x4, waiting for transfers between devices: 1.71 us -> 3.18 us  [seg_swap(): return lax.ppermute(block, 'seg', [(i, i ^ x) for i in range(segs)])]
    ppermute x21, starting transfers between devices: 28.3 us -> 29.8 us  [node_swap(): return lax.ppermute(block, 'node', [(i, i ^ k) for i in range(nodes)])]
  transfers between devices with their start and end apart: 37 -> 37, of which waited for: 19 -> 17; matrix products, arithmetic and copies ran while one was open for 3% -> 3% of each run, Pallas kernels for 12% -> 13%
where the time goes in v7:
time: 105 us
  starting transfers between devices  43.1 us (41%)
  waiting for transfers between devices  28.2 us (27%)
  Pallas kernels  25 us (24%)
  local copies, waits for them, and re-layouts  5.2 us (5%)
  other arithmetic  2.21 us (2%)
  between operations  1.31 us (1%)
    ppermute x21, starting transfers between devices, node_swap(): return lax.ppermute(block, 'node', [(i, i ^ k) for i in range(nodes)])  29.8 us
    pallas_call x19, Pallas kernels, run(): pl.pallas_call(body, out_shape=list(outs), in_specs=[HBM if i in far else...  25 us
    ppermute x21, waiting for transfers between devices, node_swap(): return lax.ppermute(block, 'node', [(i, i ^ k) for i in range(nodes)])  22.5 us
    ppermute x3, starting transfers between devices, seg_next(): return lax.ppermute(block, 'seg', [(i, i + 1) for i in range(segs - 1)])  6.02 us
    ppermute x4, starting transfers between devices, seg_swap(): return lax.ppermute(block, 'seg', [(i, i ^ x) for i in range(segs)])  5.65 us
    unnamed x29, local copies, waits for them, and re-layouts  3.63 us
    ppermute x4, waiting for transfers between devices, seg_swap(): return lax.ppermute(block, 'seg', [(i, i ^ x) for i in range(segs)])  3.18 us
    ppermute x3, waiting for transfers between devices, seg_next(): return lax.ppermute(block, 'seg', [(i, i + 1) for i in range(segs - 1)])  2.49 us
  transfers between devices with their start and end apart: 37, of which 17 were waited for; matrix products, arithmetic and copies ran while one was open for 3% of the time, Pallas kernels for 13%

profile of v7, /device:TPU:0, one launch (start us, length us, event | category | flops | bytes accessed | tf_op | source)
XLA Modules:
  0.0 105.0 jit_solution(6494933618647863542)
XLA Ops:
  1.5 3.1 %collective-permute-start = (s32[2,256]{1,0:T(2,128)S(1)}, s32[2,256]{1,0:T(2,128)S(1)}, u32[]{:S(2)}, u32[]{:S(2)}) collective-permute-start(s32[2,256]{1,0:T(2,128)S(1)} %bitcast.43), channel_id=1, source_target_pairs={{0,4},{4,0},{8,12},{12,8},{1,5},{5,1},{9,13},{13,9},{2,6},{6,2},{1... | collective-permute-start | bytes 6152 | tf_op jit(solution)/shard_map/ppermute | solution.py:474
  4.5 2.6 %collective-permute-start.1 = (s32[2,256]{1,0:T(2,128)S(1)}, s32[2,256]{1,0:T(2,128)S(1)}, u32[]{:S(2)}, u32[]{:S(2)}) collective-permute-start(s32[2,256]{1,0:T(2,128)S(1)} %bitcast.44), channel_id=1, source_target_pairs={{0,8},{4,12},{8,0},{12,4},{1,9},{5,13},{9,1},{13,5},{2,10},{6,14},... | collective-permute-start | bytes 6152 | tf_op jit(solution)/shard_map/ppermute | solution.py:474
  14.1 3.4 %collective-permute-start.3 = (bf16[2064,128]{1,0:T(8,128)(2,1)S(1)}, bf16[2064,128]{1,0:T(8,128)(2,1)S(1)}, u32[]{:S(2)}, u32[]{:S(2)}) collective-permute-start(bf16[2064,128]{1,0:T(8,128)(2,1)S(1)} %shard_map.149), channel_id=1, source_target_pairs={{0,2},{1,3},{4,6},{5,7},{8,10},{9,11},{12,14},{13,15},{16,18},{17,... | collective-permute-start | bytes 1585160 | tf_op jit(solution)/shard_map/ppermute | solution.py:480
  18.7 2.0 %collective-permute-start.7 = (bf16[256,128]{1,0:T(8,128)(2,1)S(1)}, bf16[256,128]{1,0:T(8,128)(2,1)S(1)}, u32[]{:S(2)}, u32[]{:S(2)}) collective-permute-start(bf16[256,128]{1,0:T(8,128)(2,1)S(1)} %get-tuple-element.45), channel_id=1, source_target_pairs={{0,12},{4,8},{8,4},{12,0},{1,13},{5,9},{9,5},{13,1},{2,14},{6,10},... | collective-permute-start | bytes 196616 | tf_op jit(solution)/shard_map/ppermute | solution.py:474
  21.2 5.0 %collective-permute-done.6.refs_7_ = bf16[256,128]{1,0:T(8,128)(2,1)S(1)} collective-permute-done((bf16[256,128]{1,0:T(8,128)(2,1)S(1)}, bf16[256,128]{1,0:T(8,128)(2,1)S(1)}, u32[]{:S(2)}, u32[]{:S(2)}) %collective-permute-start.6) | collective-permute-done | bytes 65568 | tf_op jit(solution)/shard_map/ppermute | solution.py:474
  28.9 3.3 %shard_map.152 = (bf16[512,128]{1,0:T(8,128)(2,1)S(1)}, bf16[512,128]{1,0:T(8,128)(2,1)S(1)}, bf16[1024,768]{1,0:T(8,128)(2,1)S(1)}, bf16[1024,512]{1,0:T(8,128)(2,1)S(1)}, f32[8,128]{1,0:T(8,128)S(1)}) custom-call(f32[40,128]{1,0:T(8,128)S(1)} %concatenate.9.refs_2_.refs_0_, bf16[1024,256]{1,0:T(8,128)(2,1)S(1)} %shard_map.151.refs_1_, ...), custom_call_target="tpu_custom_call" | custom-call | bytes 5267456 | tf_op jit(solution)/shard_map/pallas_call | solution.py:28
  34.8 2.5 %collective-permute-done.14.refs_1_ = bf16[512,128]{1,0:T(8,128)(2,1)S(1)} collective-permute-done((bf16[512,128]{1,0:T(8,128)(2,1)S(1)}, bf16[512,128]{1,0:T(8,128)(2,1)S(1)}, u32[]{:S(2)}, u32[]{:S(2)}) %collective-permute-start.14) | collective-permute-done | bytes 131104 | tf_op jit(solution)/shard_map/ppermute | solution.py:480
  38.8 2.0 %collective-permute-start.16 = (bf16[256,128]{1,0:T(8,128)(2,1)S(1)}, bf16[256,128]{1,0:T(8,128)(2,1)S(1)}, u32[]{:S(2)}, u32[]{:S(2)}) collective-permute-start(bf16[256,128]{1,0:T(8,128)(2,1)S(1)} %get-tuple-element.51), channel_id=1, source_target_pairs={{0,12},{4,8},{8,4},{12,0},{1,13},{5,9},{9,5},{13,1},{2,14},{6,10},... | collective-permute-start | bytes 196616 | tf_op jit(solution)/shard_map/ppermute | solution.py:474
  49.6 2.2 %collective-permute-start.18 = (bf16[256,128]{1,0:T(8,128)(2,1)S(1)}, bf16[256,128]{1,0:T(8,128)(2,1)}, u32[]{:S(2)}, u32[]{:S(2)}) collective-permute-start(bf16[256,128]{1,0:T(8,128)(2,1)S(1)} %get-tuple-element.58), channel_id=1, source_target_pairs={{0,8},{4,12},{8,0},{12,4},{1,9},{5,13},{9,1},{13,5},{2,10},{6,14},... | collective-permute-start | bytes 196616 | tf_op jit(solution)/shard_map/ppermute | solution.py:474
  51.7 2.0 %collective-permute-start.19 = (bf16[256,128]{1,0:T(8,128)(2,1)S(1)}, bf16[256,128]{1,0:T(8,128)(2,1)}, u32[]{:S(2)}, u32[]{:S(2)}) collective-permute-start(bf16[256,128]{1,0:T(8,128)(2,1)S(1)} %get-tuple-element.59), channel_id=1, source_target_pairs={{0,12},{4,8},{8,4},{12,0},{1,13},{5,9},{9,5},{13,1},{2,14},{6,10},... | collective-permute-start | bytes 196616 | tf_op jit(solution)/shard_map/ppermute | solution.py:474
  54.2 2.0 %collective-permute-done.18.refs_7_ = bf16[256,128]{1,0:T(8,128)(2,1)} collective-permute-done((bf16[256,128]{1,0:T(8,128)(2,1)S(1)}, bf16[256,128]{1,0:T(8,128)(2,1)}, u32[]{:S(2)}, u32[]{:S(2)}) %collective-permute-start.18) | collective-permute-done | bytes 65568 | tf_op jit(solution)/shard_map/ppermute | solution.py:474
  60.7 4.5 %shard_map.159 = (bf16[256,128]{1,0:T(8,128)(2,1)S(1)}, bf16[256,128]{1,0:T(8,128)(2,1)S(1)}, bf16[256,128]{1,0:T(8,128)(2,1)S(1)}, bf16[256,128]{1,0:T(8,128)(2,1)S(1)}, bf16[2688,128]{1,0:T(8,128)(2,1)S(1)}) custom-call(f32[40,128]{1,0:T(8,128)S(1)} %copy-done.8, bf16[1024,256]{1,0:T(8,128)(2,1)S(1)} %shard_map.158.refs_1_, ...), custom_call_target="tpu_custom_call" | custom-call | bytes 4706304 | tf_op jit(solution)/shard_map/pallas_call | solution.py:28
  65.2 2.6 %collective-permute-start.29 = (bf16[672,128]{1,0:T(8,128)(2,1)S(1)}, bf16[672,128]{1,0:T(8,128)(2,1)S(1)}, u32[]{:S(2)}, u32[]{:S(2)}) collective-permute-start(bf16[672,128]{1,0:T(8,128)(2,1)S(1)} %get-tuple-element.74), channel_id=1, source_target_pairs={{0,2},{2,0},{1,3},{3,1},{4,6},{6,4},{5,7},{7,5},{8,10},{10,8},{9,1... | collective-permute-start | bytes 516104 | tf_op jit(solution)/shard_map/ppermute | solution.py:477
  67.9 2.6 %collective-permute-start.25 = (bf16[256,128]{1,0:T(8,128)(2,1)S(1)}, bf16[256,128]{1,0:T(8,128)(2,1)S(1)}, u32[]{:S(2)}, u32[]{:S(2)}) collective-permute-start(bf16[256,128]{1,0:T(8,128)(2,1)S(1)} %get-tuple-element.62), channel_id=1, source_target_pairs={{0,8},{4,12},{8,0},{12,4},{1,9},{5,13},{9,1},{13,5},{2,10},{6,14},... | collective-permute-start | bytes 196616 | tf_op jit(solution)/shard_map/ppermute | solution.py:474
  70.5 1.8 %collective-permute-start.26 = (bf16[256,128]{1,0:T(8,128)(2,1)S(1)}, bf16[256,128]{1,0:T(8,128)(2,1)S(1)}, u32[]{:S(2)}, u32[]{:S(2)}) collective-permute-start(bf16[256,128]{1,0:T(8,128)(2,1)S(1)} %get-tuple-element.63), channel_id=1, source_target_pairs={{0,12},{4,8},{8,4},{12,0},{1,13},{5,9},{9,5},{13,1},{2,14},{6,10},... | collective-permute-start | bytes 196616 | tf_op jit(solution)/shard_map/ppermute | solution.py:474
  73.2 2.6 %collective-permute-done.25.refs_4_.refs_3_ = bf16[256,128]{1,0:T(8,128)(2,1)S(1)} collective-permute-done((bf16[256,128]{1,0:T(8,128)(2,1)S(1)}, bf16[256,128]{1,0:T(8,128)(2,1)S(1)}, u32[]{:S(2)}, u32[]{:S(2)}) %collective-permute-start.25) | collective-permute-done | bytes 65568 | tf_op jit(solution)/shard_map/ppermute | solution.py:474
  77.2 1.8 %collective-permute-start.30 = (bf16[336,128]{1,0:T(8,128)(2,1)S(1)}, bf16[336,128]{1,0:T(8,128)(2,1)S(1)}, u32[]{:S(2)}, u32[]{:S(2)}) collective-permute-start(bf16[336,128]{1,0:T(8,128)(2,1)S(1)} %get-tuple-element.68), channel_id=1, source_target_pairs={{0,8},{4,12},{8,0},{12,4},{1,9},{5,13},{9,1},{13,5},{2,10},{6,14},... | collective-permute-start | bytes 258056 | tf_op jit(solution)/shard_map/ppermute | solution.py:474
  78.9 1.9 %collective-permute-start.31 = (bf16[336,128]{1,0:T(8,128)(2,1)S(1)}, bf16[336,128]{1,0:T(8,128)(2,1)S(1)}, u32[]{:S(2)}, u32[]{:S(2)}) collective-permute-start(bf16[336,128]{1,0:T(8,128)(2,1)S(1)} %get-tuple-element.69), channel_id=1, source_target_pairs={{0,12},{4,8},{8,4},{12,0},{1,13},{5,9},{9,5},{13,1},{2,14},{6,10},... | collective-permute-start | bytes 258056 | tf_op jit(solution)/shard_map/ppermute | solution.py:474
  82.8 2.7 %shard_map.160 = (f32[2048,128]{1,0:T(8,128)}, f32[8,128]{1,0:T(8,128)S(1)}) custom-call(s32[2,1024]{1,0:T(2,128)S(1)} %get-tuple-element.39.refs_1_.refs_0_, f32[2048,128]{1,0:T(8,128)S(1)} %shard_map.157.refs_1_, bf16[256,128]{1,0:T(8,128)(2,1)S(1)} %get-tuple-element.60.refs_2_, bf16[256,128]{1,0:T(8,128)(2,1)S(1)} %collective-permute-done.24.refs_3_.refs_2_, ...), custom_call_target="tpu_custom_call" | custom-call | bytes 2371584 | tf_op jit(solution)/shard_map/pallas_call | solution.py:28
  89.8 2.0 %collective-permute-start.35 = (bf16[336,128]{1,0:T(8,128)(2,1)S(1)}, bf16[336,128]{1,0:T(8,128)(2,1)S(1)}, u32[]{:S(2)}, u32[]{:S(2)}) collective-permute-start(bf16[336,128]{1,0:T(8,128)(2,1)S(1)} %shard_map.163), channel_id=1, source_target_pairs={{0,12},{4,8},{8,4},{12,0},{1,13},{5,9},{9,5},{13,1},{2,14},{6,10},... | collective-permute-start | bytes 258056 | tf_op jit(solution)/shard_map/ppermute | solution.py:474
  93.3 3.4 %collective-permute-done.34 = bf16[336,128]{1,0:T(8,128)(2,1)S(1)} collective-permute-done((bf16[336,128]{1,0:T(8,128)(2,1)S(1)}, bf16[336,128]{1,0:T(8,128)(2,1)S(1)}, u32[]{:S(2)}, u32[]{:S(2)}) %collective-permute-start.34) | collective-permute-done | bytes 86048 | tf_op jit(solution)/shard_map/ppermute | solution.py:474
  96.7 1.8 %collective-permute-start.36 = (bf16[672,128]{1,0:T(8,128)(2,1)S(1)}, bf16[672,128]{1,0:T(8,128)(2,1)S(1)}, u32[]{:S(2)}, u32[]{:S(2)}) collective-permute-start(bf16[672,128]{1,0:T(8,128)(2,1)S(1)} %constant_dynamic-update-slice_fusion.refs_1_), channel_id=1, source_target_pairs={{0,2},{2,0},{1,3},{3,1},{4,6},{6,4},{5,7},{7,5},{8,10},{10,8},{9,1... | collective-permute-start | bytes 516104 | tf_op jit(solution)/shard_map/ppermute | solution.py:477
  99.0 3.2 %collective-permute-done.36.refs_2_ = bf16[672,128]{1,0:T(8,128)(2,1)S(1)} collective-permute-done((bf16[672,128]{1,0:T(8,128)(2,1)S(1)}, bf16[672,128]{1,0:T(8,128)(2,1)S(1)}, u32[]{:S(2)}, u32[]{:S(2)}) %collective-permute-start.36) | collective-permute-done | bytes 172064 | tf_op jit(solution)/shard_map/ppermute | solution.py:477
  102.2 2.6 %shard_map.165 = (f32[3,768,128]{2,1,0:T(8,128)}, f32[3,256,128]{2,1,0:T(8,128)}, f32[4,128]{1,0:T(4,128)}) custom-call(f32[1344,128]{1,0:T(8,128)S(1)} %shard_map.164.refs_0_, bf16[672,128]{1,0:T(8,128)(2,1)S(1)} %constant_dynamic-update-slice_fusion.refs_1_, bf16[672,128]{1,0:T(8,128)(2,1)S(1)} %collective-permute-done.36.refs_2_), custom_call_target="tpu_custom_call" | custom-call | bytes 2607104 | tf_op jit(solution)/shard_map/pallas_call | solution.py:28
  (110 shorter events, 40.3 us)
Async XLA Ops:
  1.5 8.7 %collective-permute-start = (s32[2,256]{1,0:T(2,128)S(1)}, s32[2,256]{1,0:T(2,128)S(1)}, u32[]{:S(2)}, u32[]{:S(2)}) collective-permute-start(s32[2,256]{1,0:T(2,128)S(1)} %bitcast.43), channel_id=1, source_target_pairs={{0,4},{4,0},{8,12},{12,8},{1,5},{5,1},{9,13},{13,9},{2,6},{6,2},{1... | collective-permute-start | bytes 6152 | tf_op jit(solution)/shard_map/ppermute | solution.py:474
  4.5 7.0 %collective-permute-start.1 = (s32[2,256]{1,0:T(2,128)S(1)}, s32[2,256]{1,0:T(2,128)S(1)}, u32[]{:S(2)}, u32[]{:S(2)}) collective-permute-start(s32[2,256]{1,0:T(2,128)S(1)} %bitcast.44), channel_id=1, source_target_pairs={{0,8},{4,12},{8,0},{12,4},{1,9},{5,13},{9,1},{13,5},{2,10},{6,14},... | collective-permute-start | bytes 6152 | tf_op jit(solution)/shard_map/ppermute | solution.py:474
  14.1 26.6 %collective-permute-start.3 = (bf16[2064,128]{1,0:T(8,128)(2,1)S(1)}, bf16[2064,128]{1,0:T(8,128)(2,1)S(1)}, u32[]{:S(2)}, u32[]{:S(2)}) collective-permute-start(bf16[2064,128]{1,0:T(8,128)(2,1)S(1)} %shard_map.149), channel_id=1, source_target_pairs={{0,2},{1,3},{4,6},{5,7},{8,10},{9,11},{12,14},{13,15},{16,18},{17,... | collective-permute-start | bytes 1585160 | tf_op jit(solution)/shard_map/ppermute | solution.py:480
  17.6 9.6 %collective-permute-start.4 = (bf16[2,64,1024]{2,1,0:T(8,128)(2,1)S(1)}, bf16[2,64,1024]{2,1,0:T(8,128)(2,1)S(1)}, u32[]{:S(2)}, u32[]{:S(2)}) collective-permute-start(bf16[2,64,1024]{2,1,0:T(8,128)(2,1)S(1)} %bitcast.36), channel_id=1, source_target_pairs={{0,1},{1,0},{2,3},{3,2},{4,5},{5,4},{6,7},{7,6},{8,9},{9,8},{10,11... | collective-permute-start | bytes 786440 | tf_op jit(solution)/shard_map/ppermute | solution.py:483
  17.7 8.6 %collective-permute-start.6 = (bf16[256,128]{1,0:T(8,128)(2,1)S(1)}, bf16[256,128]{1,0:T(8,128)(2,1)S(1)}, u32[]{:S(2)}, u32[]{:S(2)}) collective-permute-start(bf16[256,128]{1,0:T(8,128)(2,1)S(1)} %get-tuple-element.44), channel_id=1, source_target_pairs={{0,8},{4,12},{8,0},{12,4},{1,9},{5,13},{9,1},{13,5},{2,10},{6,14},... | collective-permute-start | bytes 196616 | tf_op jit(solution)/shard_map/ppermute | solution.py:474
  18.7 7.6 %collective-permute-start.7 = (bf16[256,128]{1,0:T(8,128)(2,1)S(1)}, bf16[256,128]{1,0:T(8,128)(2,1)S(1)}, u32[]{:S(2)}, u32[]{:S(2)}) collective-permute-start(bf16[256,128]{1,0:T(8,128)(2,1)S(1)} %get-tuple-element.45), channel_id=1, source_target_pairs={{0,12},{4,8},{8,4},{12,0},{1,13},{5,9},{9,5},{13,1},{2,14},{6,10},... | collective-permute-start | bytes 196616 | tf_op jit(solution)/shard_map/ppermute | solution.py:474
  20.7 6.5 %collective-permute-start.5 = (bf16[256,128]{1,0:T(8,128)(2,1)S(1)}, bf16[256,128]{1,0:T(8,128)(2,1)S(1)}, u32[]{:S(2)}, u32[]{:S(2)}) collective-permute-start(bf16[256,128]{1,0:T(8,128)(2,1)S(1)} %get-tuple-element.43), channel_id=1, source_target_pairs={{0,4},{4,0},{8,12},{12,8},{1,5},{5,1},{9,13},{13,9},{2,6},{6,2},{1... | collective-permute-start | bytes 196616 | tf_op jit(solution)/shard_map/ppermute | solution.py:474
  33.5 8.7 %collective-permute-start.12 = (bf16[512,128]{1,0:T(8,128)(2,1)S(1)}, bf16[512,128]{1,0:T(8,128)(2,1)S(1)}, u32[]{:S(2)}, u32[]{:S(2)}) collective-permute-start(bf16[512,128]{1,0:T(8,128)(2,1)S(1)} %get-tuple-element.46.refs_0_), channel_id=1, source_target_pairs={{0,2},{1,3},{4,6},{5,7},{8,10},{9,11},{12,14},{13,15},{16,18},{17,... | collective-permute-start | bytes 393224 | tf_op jit(solution)/shard_map/ppermute | solution.py:480
  37.4 7.3 %collective-permute-start.15 = (bf16[256,128]{1,0:T(8,128)(2,1)S(1)}, bf16[256,128]{1,0:T(8,128)(2,1)S(1)}, u32[]{:S(2)}, u32[]{:S(2)}) collective-permute-start(bf16[256,128]{1,0:T(8,128)(2,1)S(1)} %get-tuple-element.50), channel_id=1, source_target_pairs={{0,8},{4,12},{8,0},{12,4},{1,9},{5,13},{9,1},{13,5},{2,10},{6,14},... | collective-permute-start | bytes 196616 | tf_op jit(solution)/shard_map/ppermute | solution.py:474
  38.8 6.6 %collective-permute-start.16 = (bf16[256,128]{1,0:T(8,128)(2,1)S(1)}, bf16[256,128]{1,0:T(8,128)(2,1)S(1)}, u32[]{:S(2)}, u32[]{:S(2)}) collective-permute-start(bf16[256,128]{1,0:T(8,128)(2,1)S(1)} %get-tuple-element.51), channel_id=1, source_target_pairs={{0,12},{4,8},{8,4},{12,0},{1,13},{5,9},{9,5},{13,1},{2,14},{6,10},... | collective-permute-start | bytes 196616 | tf_op jit(solution)/shard_map/ppermute | solution.py:474
  49.6 6.7 %collective-permute-start.18 = (bf16[256,128]{1,0:T(8,128)(2,1)S(1)}, bf16[256,128]{1,0:T(8,128)(2,1)}, u32[]{:S(2)}, u32[]{:S(2)}) collective-permute-start(bf16[256,128]{1,0:T(8,128)(2,1)S(1)} %get-tuple-element.58), channel_id=1, source_target_pairs={{0,8},{4,12},{8,0},{12,4},{1,9},{5,13},{9,1},{13,5},{2,10},{6,14},... | collective-permute-start | bytes 196616 | tf_op jit(solution)/shard_map/ppermute | solution.py:474
  51.7 6.2 %collective-permute-start.19 = (bf16[256,128]{1,0:T(8,128)(2,1)S(1)}, bf16[256,128]{1,0:T(8,128)(2,1)}, u32[]{:S(2)}, u32[]{:S(2)}) collective-permute-start(bf16[256,128]{1,0:T(8,128)(2,1)S(1)} %get-tuple-element.59), channel_id=1, source_target_pairs={{0,12},{4,8},{8,4},{12,0},{1,13},{5,9},{9,5},{13,1},{2,14},{6,10},... | collective-permute-start | bytes 196616 | tf_op jit(solution)/shard_map/ppermute | solution.py:474
  53.7 6.0 %collective-permute-start.20 = (bf16[256,128]{1,0:T(8,128)(2,1)}, bf16[256,128]{1,0:T(8,128)(2,1)}, u32[]{:S(2)}, u32[]{:S(2)}) collective-permute-start(bf16[256,128]{1,0:T(8,128)(2,1)} %get-tuple-element.56.refs_5_), channel_id=1, source_target_pairs={{0,1},{1,0},{2,3},{3,2},{4,5},{5,4},{6,7},{7,6},{8,9},{9,8},{10,11... | collective-permute-start | bytes 196616 | tf_op jit(solution)/shard_map/ppermute | solution.py:483
  53.7 6.0 %collective-permute-start.21 = (bf16[256,128]{1,0:T(8,128)(2,1)}, bf16[256,128]{1,0:T(8,128)(2,1)}, u32[]{:S(2)}, u32[]{:S(2)}) collective-permute-start(bf16[256,128]{1,0:T(8,128)(2,1)} %collective-permute-done.17.refs_6_), channel_id=1, source_target_pairs={{0,1},{1,0},{2,3},{3,2},{4,5},{5,4},{6,7},{7,6},{8,9},{9,8},{10,11... | collective-permute-start | bytes 196616 | tf_op jit(solution)/shard_map/ppermute | solution.py:483
  65.2 11.4 %collective-permute-start.29 = (bf16[672,128]{1,0:T(8,128)(2,1)S(1)}, bf16[672,128]{1,0:T(8,128)(2,1)S(1)}, u32[]{:S(2)}, u32[]{:S(2)}) collective-permute-start(bf16[672,128]{1,0:T(8,128)(2,1)S(1)} %get-tuple-element.74), channel_id=1, source_target_pairs={{0,2},{2,0},{1,3},{3,1},{4,6},{6,4},{5,7},{7,5},{8,10},{10,8},{9,1... | collective-permute-start | bytes 516104 | tf_op jit(solution)/shard_map/ppermute | solution.py:477
  67.8 13.0 %collective-permute-start.27 = (bf16[672,128]{1,0:T(8,128)(2,1)S(1)}, bf16[672,128]{1,0:T(8,128)(2,1)S(1)}, u32[]{:S(2)}, u32[]{:S(2)}) collective-permute-start(bf16[672,128]{1,0:T(8,128)(2,1)S(1)} %get-tuple-element.75), channel_id=1, source_target_pairs={{0,2},{2,0},{1,3},{3,1},{4,6},{6,4},{5,7},{7,5},{8,10},{10,8},{9,1... | collective-permute-start | bytes 516104 | tf_op jit(solution)/shard_map/ppermute | solution.py:477
  67.9 7.9 %collective-permute-start.25 = (bf16[256,128]{1,0:T(8,128)(2,1)S(1)}, bf16[256,128]{1,0:T(8,128)(2,1)S(1)}, u32[]{:S(2)}, u32[]{:S(2)}) collective-permute-start(bf16[256,128]{1,0:T(8,128)(2,1)S(1)} %get-tuple-element.62), channel_id=1, source_target_pairs={{0,8},{4,12},{8,0},{12,4},{1,9},{5,13},{9,1},{13,5},{2,10},{6,14},... | collective-permute-start | bytes 196616 | tf_op jit(solution)/shard_map/ppermute | solution.py:474
  70.5 6.2 %collective-permute-start.26 = (bf16[256,128]{1,0:T(8,128)(2,1)S(1)}, bf16[256,128]{1,0:T(8,128)(2,1)S(1)}, u32[]{:S(2)}, u32[]{:S(2)}) collective-permute-start(bf16[256,128]{1,0:T(8,128)(2,1)S(1)} %get-tuple-element.63), channel_id=1, source_target_pairs={{0,12},{4,8},{8,4},{12,0},{1,13},{5,9},{9,5},{13,1},{2,14},{6,10},... | collective-permute-start | bytes 196616 | tf_op jit(solution)/shard_map/ppermute | solution.py:474
  77.2 8.4 %collective-permute-start.30 = (bf16[336,128]{1,0:T(8,128)(2,1)S(1)}, bf16[336,128]{1,0:T(8,128)(2,1)S(1)}, u32[]{:S(2)}, u32[]{:S(2)}) collective-permute-start(bf16[336,128]{1,0:T(8,128)(2,1)S(1)} %get-tuple-element.68), channel_id=1, source_target_pairs={{0,8},{4,12},{8,0},{12,4},{1,9},{5,13},{9,1},{13,5},{2,10},{6,14},... | collective-permute-start | bytes 258056 | tf_op jit(solution)/shard_map/ppermute | solution.py:474
  78.9 7.0 %collective-permute-start.31 = (bf16[336,128]{1,0:T(8,128)(2,1)S(1)}, bf16[336,128]{1,0:T(8,128)(2,1)S(1)}, u32[]{:S(2)}, u32[]{:S(2)}) collective-permute-start(bf16[336,128]{1,0:T(8,128)(2,1)S(1)} %get-tuple-element.69), channel_id=1, source_target_pairs={{0,12},{4,8},{8,4},{12,0},{1,13},{5,9},{9,5},{13,1},{2,14},{6,10},... | collective-permute-start | bytes 258056 | tf_op jit(solution)/shard_map/ppermute | solution.py:474
  81.3 5.5 %collective-permute-start.28 = (bf16[336,128]{1,0:T(8,128)(2,1)S(1)}, bf16[336,128]{1,0:T(8,128)(2,1)S(1)}, u32[]{:S(2)}, u32[]{:S(2)}) collective-permute-start(bf16[336,128]{1,0:T(8,128)(2,1)S(1)} %get-tuple-element.67), channel_id=1, source_target_pairs={{0,4},{4,0},{8,12},{12,8},{1,5},{5,1},{9,13},{13,9},{2,6},{6,2},{1... | collective-permute-start | bytes 258056 | tf_op jit(solution)/shard_map/ppermute | solution.py:474
  88.2 8.5 %collective-permute-start.34 = (bf16[336,128]{1,0:T(8,128)(2,1)S(1)}, bf16[336,128]{1,0:T(8,128)(2,1)S(1)}, u32[]{:S(2)}, u32[]{:S(2)}) collective-permute-start(bf16[336,128]{1,0:T(8,128)(2,1)S(1)} %shard_map.163), channel_id=1, source_target_pairs={{0,8},{4,12},{8,0},{12,4},{1,9},{5,13},{9,1},{13,5},{2,10},{6,14},... | collective-permute-start | bytes 258056 | tf_op jit(solution)/shard_map/ppermute | solution.py:474
  89.8 7.0 %collective-permute-start.35 = (bf16[336,128]{1,0:T(8,128)(2,1)S(1)}, bf16[336,128]{1,0:T(8,128)(2,1)S(1)}, u32[]{:S(2)}, u32[]{:S(2)}) collective-permute-start(bf16[336,128]{1,0:T(8,128)(2,1)S(1)} %shard_map.163), channel_id=1, source_target_pairs={{0,12},{4,8},{8,4},{12,0},{1,13},{5,9},{9,5},{13,1},{2,14},{6,10},... | collective-permute-start | bytes 258056 | tf_op jit(solution)/shard_map/ppermute | solution.py:474
  92.1 6.4 %collective-permute-start.33 = (bf16[672,128]{1,0:T(8,128)(2,1)S(1)}, bf16[672,128]{1,0:T(8,128)(2,1)S(1)}, u32[]{:S(2)}, u32[]{:S(2)}) collective-permute-start(bf16[672,128]{1,0:T(8,128)(2,1)S(1)} %pad_maximum_fusion.refs_0_), channel_id=1, source_target_pairs={{0,2},{2,0},{1,3},{3,1},{4,6},{6,4},{5,7},{7,5},{8,10},{10,8},{9,1... | collective-permute-start | bytes 516104 | tf_op jit(solution)/shard_map/ppermute | solution.py:477
  (24 other events, 161.4 us)

commit v8 on v7

--- a/solution.py
+++ b/solution.py
@@ -311,10 +311,10 @@
 
 
 def batch_kernel(nodes, batch, final, prior, sems, given, made, scratch):
-    facts_any, side_any, w_in_any, w_hid_any, up_any = given[:5]
-    own_pieces, other_pieces = given[5 : 5 + nodes], given[5 + nodes : 5 + 2 * nodes]
-    rest = given[5 + 2 * nodes :]
-    message, facts, w_in, w_hid, gates, up, fresh = scratch[:7]
+    facts_any, side_any, w_any, up_any = given[:4]
+    own_pieces, other_pieces = given[4 : 4 + nodes], given[4 + nodes : 4 + 2 * nodes]
+    rest = given[4 + 2 * nodes :]
+    message, facts, w_ref, gates, up, fresh = scratch[:6]
     if not final:
         message, gates = made[2:4]
     cap = own_pieces[0].shape[0]
@@ -329,9 +329,9 @@
         at = pl.ds(pl.multiple_of((z ^ k) * cap, cap), cap)
         pairs.append((own_pieces[k], message.at[at, pl.ds(mine, LANES)]))
         pairs.append((other_pieces[k], message.at[at, pl.ds(other, LANES)]))
-    late = [(side_any, message.at[:, 2 * width :]), (w_in_any, w_in), (w_hid_any, w_hid), (up_any.at[batch], up)]
+    late = [(side_any, message.at[:, 2 * width :]), (w_any, w_ref), (up_any.at[batch], up)]
     if prior:
-        before = scratch[7]
+        before = scratch[6]
         late.append((rest[0], before))
     rows_begun = begin(sems, pairs)
     late_begun = begin(sems, late, len(pairs))
@@ -345,6 +345,8 @@
         span = slice(j * LANES, (j + 1) * LANES)
         message[span, width : 2 * width] = pick_rows(dst[j].astype(I32), full)
     end(late_begun)
+    w_in = [w_ref[g, :long, :] for g in range(3)]
+    w_hid = [w_ref[g, long:, :] for g in range(3)]
     w_in01 = jnp.concatenate([w_in[0], w_in[1]], axis=1)
     w_hid01 = jnp.concatenate([w_hid[0], w_hid[1]], axis=1)
     sums = [jnp.zeros((1, LANES), F32) for _ in range(4)]
@@ -501,10 +503,11 @@
     rest = jnp.zeros((2, half), F32)
     facts = jnp.concatenate([facts, bias, freq[None], phase[None], rest], axis=0)
 
+    weights = jnp.concatenate([w_input, w_hidden], axis=1)
     narrow = run(
         narrow_kernel,
         [shape((node_rows, half), BF)],
-        [memory_now, wanted[1], facts],
+        [memory_now, wanted[1], facts, weights],
         [pltpu.VMEM((node_rows, half), F32)],
         1,
         (0,),
@@ -543,13 +546,12 @@
             [pltpu.VMEM(facts.shape, F32), pltpu.VMEM((2 * edges.shape[-1], events), BF)],
             3,
         )[0]
-        given = [facts, beside, w_input, w_hidden, upstream[:, 0]]
+        given = [facts, beside, weights, upstream[:, 0]]
         given = given + own_pieces + other_pieces + ([] if totals is None else [totals])
         rooms = [
             pltpu.VMEM((events, long), BF),
             pltpu.VMEM(facts.shape, F32),
-            pltpu.VMEM(w_input.shape, BF),
-            pltpu.VMEM(w_hidden.shape, BF),
+            pltpu.VMEM(weights.shape, BF),
             pltpu.VMEM((events, 4 * half), BF),
             pltpu.VMEM((events, half), BF),
             pltpu.VMEM((events, half), BF),

time: 105 us -> 103 us (0.981)
  local copies, waits for them, and re-layouts: 5.2 us -> 3.75 us
  other arithmetic: 2.21 us -> 0.95 us
    unnamed x29 -> x40, local copies, waits for them, and re-layouts: 3.63 us -> 2.84 us
  transfers between devices with their start and end apart: 37 -> 37, of which waited for: 17 -> 16; matrix products, arithmetic and copies ran while one was open for 3% -> 2% of each run, Pallas kernels for 13% -> 13%
where the time goes in v8:
time: 103 us
  starting transfers between devices  42.6 us (41%)
  waiting for transfers between devices  29.2 us (28%)
  Pallas kernels  24.8 us (24%)
  local copies, waits for them, and re-layouts  3.75 us (4%)
  between operations  1.43 us (1%)
    ppermute x21, starting transfers between devices, node_swap(): return lax.ppermute(block, 'node', [(i, i ^ k) for i in range(nodes)])  29.8 us
    pallas_call x19, Pallas kernels, run(): pl.pallas_call(body, out_shape=list(outs), in_specs=[HBM if i in far else...  24.8 us
    ppermute x21, waiting for transfers between devices, node_swap(): return lax.ppermute(block, 'node', [(i, i ^ k) for i in range(nodes)])  23 us
    ppermute x3, starting transfers between devices, seg_next(): return lax.ppermute(block, 'seg', [(i, i + 1) for i in range(segs - 1)])  6.02 us
    ppermute x4, starting transfers between devices, seg_swap(): return lax.ppermute(block, 'seg', [(i, i ^ x) for i in range(segs)])  5.14 us
    ppermute x4, waiting for transfers between devices, seg_swap(): return lax.ppermute(block, 'seg', [(i, i ^ x) for i in range(segs)])  3.59 us
    unnamed x40, local copies, waits for them, and re-layouts  2.84 us
    ppermute x3, waiting for transfers between devices, seg_next(): return lax.ppermute(block, 'seg', [(i, i + 1) for i in range(segs - 1)])  2.5 us
  transfers between devices with their start and end apart: 37, of which 16 were waited for; matrix products, arithmetic and copies ran while one was open for 2% of the time, Pallas kernels for 13%

profile of v8, /device:TPU:0, one launch (start us, length us, event | category | flops | bytes accessed | tf_op | source)
XLA Modules:
  0.0 102.7 jit_solution(8150864088048875092)
XLA Ops:
  1.7 3.1 %collective-permute-start = (s32[2,256]{1,0:T(2,128)S(1)}, s32[2,256]{1,0:T(2,128)S(1)}, u32[]{:S(2)}, u32[]{:S(2)}) collective-permute-start(s32[2,256]{1,0:T(2,128)S(1)} %bitcast.43), channel_id=1, source_target_pairs={{0,4},{4,0},{8,12},{12,8},{1,5},{5,1},{9,13},{13,9},{2,6},{6,2},{1... | collective-permute-start | bytes 6152 | tf_op jit(solution)/shard_map/ppermute | solution.py:476
  4.7 2.6 %collective-permute-start.1 = (s32[2,256]{1,0:T(2,128)S(1)}, s32[2,256]{1,0:T(2,128)S(1)}, u32[]{:S(2)}, u32[]{:S(2)}) collective-permute-start(s32[2,256]{1,0:T(2,128)S(1)} %bitcast.44), channel_id=1, source_target_pairs={{0,8},{4,12},{8,0},{12,4},{1,9},{5,13},{9,1},{13,5},{2,10},{6,14},... | collective-permute-start | bytes 6152 | tf_op jit(solution)/shard_map/ppermute | solution.py:476
  9.7 3.1 %collective-permute-done.2.refs_3_ = s32[2,256]{1,0:T(2,128)S(1)} collective-permute-done((s32[2,256]{1,0:T(2,128)S(1)}, s32[2,256]{1,0:T(2,128)S(1)}, u32[]{:S(2)}, u32[]{:S(2)}) %collective-permute-start.2) | collective-permute-done | bytes 2080 | tf_op jit(solution)/shard_map/ppermute | solution.py:476
  14.4 3.4 %collective-permute-start.3 = (bf16[2064,128]{1,0:T(8,128)(2,1)S(1)}, bf16[2064,128]{1,0:T(8,128)(2,1)S(1)}, u32[]{:S(2)}, u32[]{:S(2)}) collective-permute-start(bf16[2064,128]{1,0:T(8,128)(2,1)S(1)} %shard_map.149), channel_id=1, source_target_pairs={{0,2},{1,3},{4,6},{5,7},{8,10},{9,11},{12,14},{13,15},{16,18},{17,... | collective-permute-start | bytes 1585160 | tf_op jit(solution)/shard_map/ppermute | solution.py:482
  19.0 2.5 %collective-permute-start.5 = (bf16[256,128]{1,0:T(8,128)(2,1)S(1)}, bf16[256,128]{1,0:T(8,128)(2,1)S(1)}, u32[]{:S(2)}, u32[]{:S(2)}) collective-permute-start(bf16[256,128]{1,0:T(8,128)(2,1)S(1)} %get-tuple-element.43), channel_id=1, source_target_pairs={{0,4},{4,0},{8,12},{12,8},{1,5},{5,1},{9,13},{13,9},{2,6},{6,2},{1... | collective-permute-start | bytes 196616 | tf_op jit(solution)/shard_map/ppermute | solution.py:476
  21.4 3.7 %collective-permute-done.6.refs_6_ = bf16[256,128]{1,0:T(8,128)(2,1)S(1)} collective-permute-done((bf16[256,128]{1,0:T(8,128)(2,1)S(1)}, bf16[256,128]{1,0:T(8,128)(2,1)S(1)}, u32[]{:S(2)}, u32[]{:S(2)}) %collective-permute-start.6) | collective-permute-done | bytes 65568 | tf_op jit(solution)/shard_map/ppermute | solution.py:476
  27.7 2.9 %shard_map.152 = (bf16[512,128]{1,0:T(8,128)(2,1)S(1)}, bf16[512,128]{1,0:T(8,128)(2,1)S(1)}, bf16[1024,768]{1,0:T(8,128)(2,1)S(1)}, bf16[1024,512]{1,0:T(8,128)(2,1)S(1)}, f32[8,128]{1,0:T(8,128)S(1)}) custom-call(f32[40,128]{1,0:T(8,128)S(1)} %concatenate.12.refs_2_.refs_0_, bf16[1024,256]{1,0:T(8,128)(2,1)S(1)} %shard_map.151.refs_1_, ...), custom_call_target="tpu_custom_call" | custom-call | bytes 5267456 | tf_op jit(solution)/shard_map/pallas_call | solution.py:28
  33.3 2.5 %collective-permute-done.14.refs_1_ = bf16[512,128]{1,0:T(8,128)(2,1)S(1)} collective-permute-done((bf16[512,128]{1,0:T(8,128)(2,1)S(1)}, bf16[512,128]{1,0:T(8,128)(2,1)S(1)}, u32[]{:S(2)}, u32[]{:S(2)}) %collective-permute-start.14) | collective-permute-done | bytes 131104 | tf_op jit(solution)/shard_map/ppermute | solution.py:482
  45.3 1.7 %shard_map.156 = (bf16[1024,128]{1,0:T(8,128)(2,1)S(1)}, bf16[256,128]{1,0:T(8,128)(2,1)}, bf16[256,128]{1,0:T(8,128)(2,1)S(1)}, bf16[256,128]{1,0:T(8,128)(2,1)S(1)}, bf16[256,128]{1,0:T(8,128)(2,1)S(1)}) custom-call(s32[2,1024]{1,0:T(2,128)S(1)} %get-tuple-element.39.refs_1_.refs_0_, s32[1,1024]{1,0:T(1,128)S(1)} %get-tuple-element.40.refs_1_.refs_0_, ...), custom_call_target="tpu_custom_call" | custom-call | bytes 2437120 | tf_op jit(solution)/shard_map/pallas_call | solution.py:28
  48.1 2.4 %collective-permute-start.18 = (bf16[256,128]{1,0:T(8,128)(2,1)S(1)}, bf16[256,128]{1,0:T(8,128)(2,1)}, u32[]{:S(2)}, u32[]{:S(2)}) collective-permute-start(bf16[256,128]{1,0:T(8,128)(2,1)S(1)} %get-tuple-element.58), channel_id=1, source_target_pairs={{0,8},{4,12},{8,0},{12,4},{1,9},{5,13},{9,1},{13,5},{2,10},{6,14},... | collective-permute-start | bytes 196616 | tf_op jit(solution)/shard_map/ppermute | solution.py:476
  52.6 2.2 %collective-permute-done.18.refs_6_ = bf16[256,128]{1,0:T(8,128)(2,1)} collective-permute-done((bf16[256,128]{1,0:T(8,128)(2,1)S(1)}, bf16[256,128]{1,0:T(8,128)(2,1)}, u32[]{:S(2)}, u32[]{:S(2)}) %collective-permute-start.18) | collective-permute-done | bytes 65568 | tf_op jit(solution)/shard_map/ppermute | solution.py:476
  54.8 1.9 %collective-permute-done.19.refs_7_ = bf16[256,128]{1,0:T(8,128)(2,1)} collective-permute-done((bf16[256,128]{1,0:T(8,128)(2,1)S(1)}, bf16[256,128]{1,0:T(8,128)(2,1)}, u32[]{:S(2)}, u32[]{:S(2)}) %collective-permute-start.19) | collective-permute-done | bytes 65568 | tf_op jit(solution)/shard_map/ppermute | solution.py:476
  58.7 4.5 %shard_map.159 = (bf16[256,128]{1,0:T(8,128)(2,1)S(1)}, bf16[256,128]{1,0:T(8,128)(2,1)S(1)}, bf16[256,128]{1,0:T(8,128)(2,1)S(1)}, bf16[256,128]{1,0:T(8,128)(2,1)S(1)}, bf16[2688,128]{1,0:T(8,128)(2,1)S(1)}) custom-call(f32[40,128]{1,0:T(8,128)S(1)} %concatenate.12.refs_2_.refs_0_, bf16[1024,256]{1,0:T(8,128)(2,1)S(1)} %shard_map.158.refs_1_, ...), custom_call_target="tpu_custom_call" | custom-call | bytes 4706304 | tf_op jit(solution)/shard_map/pallas_call | solution.py:28
  63.3 2.6 %collective-permute-start.29 = (bf16[672,128]{1,0:T(8,128)(2,1)S(1)}, bf16[672,128]{1,0:T(8,128)(2,1)S(1)}, u32[]{:S(2)}, u32[]{:S(2)}) collective-permute-start(bf16[672,128]{1,0:T(8,128)(2,1)S(1)} %get-tuple-element.74), channel_id=1, source_target_pairs={{0,2},{2,0},{1,3},{3,1},{4,6},{6,4},{5,7},{7,5},{8,10},{10,8},{9,1... | collective-permute-start | bytes 516104 | tf_op jit(solution)/shard_map/ppermute | solution.py:479
  66.0 2.2 %collective-permute-start.25 = (bf16[256,128]{1,0:T(8,128)(2,1)S(1)}, bf16[256,128]{1,0:T(8,128)(2,1)S(1)}, u32[]{:S(2)}, u32[]{:S(2)}) collective-permute-start(bf16[256,128]{1,0:T(8,128)(2,1)S(1)} %get-tuple-element.62), channel_id=1, source_target_pairs={{0,8},{4,12},{8,0},{12,4},{1,9},{5,13},{9,1},{13,5},{2,10},{6,14},... | collective-permute-start | bytes 196616 | tf_op jit(solution)/shard_map/ppermute | solution.py:476
  68.2 2.2 %collective-permute-start.26 = (bf16[256,128]{1,0:T(8,128)(2,1)S(1)}, bf16[256,128]{1,0:T(8,128)(2,1)S(1)}, u32[]{:S(2)}, u32[]{:S(2)}) collective-permute-start(bf16[256,128]{1,0:T(8,128)(2,1)S(1)} %get-tuple-element.63), channel_id=1, source_target_pairs={{0,12},{4,8},{8,4},{12,0},{1,13},{5,9},{9,5},{13,1},{2,14},{6,10},... | collective-permute-start | bytes 196616 | tf_op jit(solution)/shard_map/ppermute | solution.py:476
  71.3 3.4 %collective-permute-done.25.refs_4_.refs_3_ = bf16[256,128]{1,0:T(8,128)(2,1)S(1)} collective-permute-done((bf16[256,128]{1,0:T(8,128)(2,1)S(1)}, bf16[256,128]{1,0:T(8,128)(2,1)S(1)}, u32[]{:S(2)}, u32[]{:S(2)}) %collective-permute-start.25) | collective-permute-done | bytes 65568 | tf_op jit(solution)/shard_map/ppermute | solution.py:476
  76.7 2.1 %collective-permute-start.31 = (bf16[336,128]{1,0:T(8,128)(2,1)S(1)}, bf16[336,128]{1,0:T(8,128)(2,1)S(1)}, u32[]{:S(2)}, u32[]{:S(2)}) collective-permute-start(bf16[336,128]{1,0:T(8,128)(2,1)S(1)} %get-tuple-element.69), channel_id=1, source_target_pairs={{0,12},{4,8},{8,4},{12,0},{1,13},{5,9},{9,5},{13,1},{2,14},{6,10},... | collective-permute-start | bytes 258056 | tf_op jit(solution)/shard_map/ppermute | solution.py:476
  80.9 2.7 %shard_map.160 = (f32[2048,128]{1,0:T(8,128)}, f32[8,128]{1,0:T(8,128)S(1)}) custom-call(s32[2,1024]{1,0:T(2,128)S(1)} %get-tuple-element.39.refs_1_.refs_0_, f32[2048,128]{1,0:T(8,128)S(1)} %shard_map.157.refs_1_, bf16[256,128]{1,0:T(8,128)(2,1)S(1)} %get-tuple-element.60.refs_2_, bf16[256,128]{1,0:T(8,128)(2,1)S(1)} %collective-permute-done.24.refs_3_.refs_2_, ...), custom_call_target="tpu_custom_call" | custom-call | bytes 2371584 | tf_op jit(solution)/shard_map/pallas_call | solution.py:28
  86.2 1.7 %collective-permute-start.34 = (bf16[336,128]{1,0:T(8,128)(2,1)S(1)}, bf16[336,128]{1,0:T(8,128)(2,1)S(1)}, u32[]{:S(2)}, u32[]{:S(2)}) collective-permute-start(bf16[336,128]{1,0:T(8,128)(2,1)S(1)} %shard_map.163), channel_id=1, source_target_pairs={{0,8},{4,12},{8,0},{12,4},{1,9},{5,13},{9,1},{13,5},{2,10},{6,14},... | collective-permute-start | bytes 258056 | tf_op jit(solution)/shard_map/ppermute | solution.py:476
  88.0 1.7 %collective-permute-start.35 = (bf16[336,128]{1,0:T(8,128)(2,1)S(1)}, bf16[336,128]{1,0:T(8,128)(2,1)S(1)}, u32[]{:S(2)}, u32[]{:S(2)}) collective-permute-start(bf16[336,128]{1,0:T(8,128)(2,1)S(1)} %shard_map.163), channel_id=1, source_target_pairs={{0,12},{4,8},{8,4},{12,0},{1,13},{5,9},{9,5},{13,1},{2,14},{6,10},... | collective-permute-start | bytes 258056 | tf_op jit(solution)/shard_map/ppermute | solution.py:476
  91.1 3.3 %collective-permute-done.34 = bf16[336,128]{1,0:T(8,128)(2,1)S(1)} collective-permute-done((bf16[336,128]{1,0:T(8,128)(2,1)S(1)}, bf16[336,128]{1,0:T(8,128)(2,1)S(1)}, u32[]{:S(2)}, u32[]{:S(2)}) %collective-permute-start.34) | collective-permute-done | bytes 86048 | tf_op jit(solution)/shard_map/ppermute | solution.py:476
  96.3 3.6 %collective-permute-done.36.refs_2_ = bf16[672,128]{1,0:T(8,128)(2,1)S(1)} collective-permute-done((bf16[672,128]{1,0:T(8,128)(2,1)S(1)}, bf16[672,128]{1,0:T(8,128)(2,1)S(1)}, u32[]{:S(2)}, u32[]{:S(2)}) %collective-permute-start.36) | collective-permute-done | bytes 172064 | tf_op jit(solution)/shard_map/ppermute | solution.py:479
  99.9 2.6 %shard_map.165 = (f32[3,768,128]{2,1,0:T(8,128)}, f32[3,256,128]{2,1,0:T(8,128)}, f32[4,128]{1,0:T(4,128)}) custom-call(f32[1344,128]{1,0:T(8,128)S(1)} %shard_map.164.refs_0_, bf16[672,128]{1,0:T(8,128)(2,1)S(1)} %constant_dynamic-update-slice_fusion.2.refs_1_, bf16[672,128]{1,0:T(8,128)(2,1)S(1)} %collective-permute-done.36.refs_2_), custom_call_target="tpu_custom_call" | custom-call | bytes 2607104 | tf_op jit(solution)/shard_map/pallas_call | solution.py:28
  (122 shorter events, 36.6 us)
Async XLA Ops:
  1.7 7.8 %collective-permute-start = (s32[2,256]{1,0:T(2,128)S(1)}, s32[2,256]{1,0:T(2,128)S(1)}, u32[]{:S(2)}, u32[]{:S(2)}) collective-permute-start(s32[2,256]{1,0:T(2,128)S(1)} %bitcast.43), channel_id=1, source_target_pairs={{0,4},{4,0},{8,12},{12,8},{1,5},{5,1},{9,13},{13,9},{2,6},{6,2},{1... | collective-permute-start | bytes 6152 | tf_op jit(solution)/shard_map/ppermute | solution.py:476
  7.3 5.4 %collective-permute-start.2 = (s32[2,256]{1,0:T(2,128)S(1)}, s32[2,256]{1,0:T(2,128)S(1)}, u32[]{:S(2)}, u32[]{:S(2)}) collective-permute-start(s32[2,256]{1,0:T(2,128)S(1)} %bitcast.45), channel_id=1, source_target_pairs={{0,12},{4,8},{8,4},{12,0},{1,13},{5,9},{9,5},{13,1},{2,14},{6,10},... | collective-permute-start | bytes 6152 | tf_op jit(solution)/shard_map/ppermute | solution.py:476
  14.4 24.8 %collective-permute-start.3 = (bf16[2064,128]{1,0:T(8,128)(2,1)S(1)}, bf16[2064,128]{1,0:T(8,128)(2,1)S(1)}, u32[]{:S(2)}, u32[]{:S(2)}) collective-permute-start(bf16[2064,128]{1,0:T(8,128)(2,1)S(1)} %shard_map.149), channel_id=1, source_target_pairs={{0,2},{1,3},{4,6},{5,7},{8,10},{9,11},{12,14},{13,15},{16,18},{17,... | collective-permute-start | bytes 1585160 | tf_op jit(solution)/shard_map/ppermute | solution.py:482
  17.8 8.3 %collective-permute-start.4 = (bf16[2,64,1024]{2,1,0:T(8,128)(2,1)S(1)}, bf16[2,64,1024]{2,1,0:T(8,128)(2,1)S(1)}, u32[]{:S(2)}, u32[]{:S(2)}) collective-permute-start(bf16[2,64,1024]{2,1,0:T(8,128)(2,1)S(1)} %bitcast.36), channel_id=1, source_target_pairs={{0,1},{1,0},{2,3},{3,2},{4,5},{5,4},{6,7},{7,6},{8,9},{9,8},{10,11... | collective-permute-start | bytes 786440 | tf_op jit(solution)/shard_map/ppermute | solution.py:485
  17.9 7.3 %collective-permute-start.6 = (bf16[256,128]{1,0:T(8,128)(2,1)S(1)}, bf16[256,128]{1,0:T(8,128)(2,1)S(1)}, u32[]{:S(2)}, u32[]{:S(2)}) collective-permute-start(bf16[256,128]{1,0:T(8,128)(2,1)S(1)} %get-tuple-element.44), channel_id=1, source_target_pairs={{0,8},{4,12},{8,0},{12,4},{1,9},{5,13},{9,1},{13,5},{2,10},{6,14},... | collective-permute-start | bytes 196616 | tf_op jit(solution)/shard_map/ppermute | solution.py:476
  18.0 7.2 %collective-permute-start.7 = (bf16[256,128]{1,0:T(8,128)(2,1)S(1)}, bf16[256,128]{1,0:T(8,128)(2,1)S(1)}, u32[]{:S(2)}, u32[]{:S(2)}) collective-permute-start(bf16[256,128]{1,0:T(8,128)(2,1)S(1)} %get-tuple-element.45), channel_id=1, source_target_pairs={{0,12},{4,8},{8,4},{12,0},{1,13},{5,9},{9,5},{13,1},{2,14},{6,10},... | collective-permute-start | bytes 196616 | tf_op jit(solution)/shard_map/ppermute | solution.py:476
  19.0 7.1 %collective-permute-start.5 = (bf16[256,128]{1,0:T(8,128)(2,1)S(1)}, bf16[256,128]{1,0:T(8,128)(2,1)S(1)}, u32[]{:S(2)}, u32[]{:S(2)}) collective-permute-start(bf16[256,128]{1,0:T(8,128)(2,1)S(1)} %get-tuple-element.43), channel_id=1, source_target_pairs={{0,4},{4,0},{8,12},{12,8},{1,5},{5,1},{9,13},{13,9},{2,6},{6,2},{1... | collective-permute-start | bytes 196616 | tf_op jit(solution)/shard_map/ppermute | solution.py:476
  32.0 8.6 %collective-permute-start.12 = (bf16[512,128]{1,0:T(8,128)(2,1)S(1)}, bf16[512,128]{1,0:T(8,128)(2,1)S(1)}, u32[]{:S(2)}, u32[]{:S(2)}) collective-permute-start(bf16[512,128]{1,0:T(8,128)(2,1)S(1)} %get-tuple-element.46.refs_0_), channel_id=1, source_target_pairs={{0,2},{1,3},{4,6},{5,7},{8,10},{9,11},{12,14},{13,15},{16,18},{17,... | collective-permute-start | bytes 393224 | tf_op jit(solution)/shard_map/ppermute | solution.py:482
  35.9 6.9 %collective-permute-start.15 = (bf16[256,128]{1,0:T(8,128)(2,1)S(1)}, bf16[256,128]{1,0:T(8,128)(2,1)S(1)}, u32[]{:S(2)}, u32[]{:S(2)}) collective-permute-start(bf16[256,128]{1,0:T(8,128)(2,1)S(1)} %get-tuple-element.50), channel_id=1, source_target_pairs={{0,8},{4,12},{8,0},{12,4},{1,9},{5,13},{9,1},{13,5},{2,10},{6,14},... | collective-permute-start | bytes 196616 | tf_op jit(solution)/shard_map/ppermute | solution.py:476
  37.5 6.6 %collective-permute-start.16 = (bf16[256,128]{1,0:T(8,128)(2,1)S(1)}, bf16[256,128]{1,0:T(8,128)(2,1)S(1)}, u32[]{:S(2)}, u32[]{:S(2)}) collective-permute-start(bf16[256,128]{1,0:T(8,128)(2,1)S(1)} %get-tuple-element.51), channel_id=1, source_target_pairs={{0,12},{4,8},{8,4},{12,0},{1,13},{5,9},{9,5},{13,1},{2,14},{6,10},... | collective-permute-start | bytes 196616 | tf_op jit(solution)/shard_map/ppermute | solution.py:476
  48.1 6.7 %collective-permute-start.18 = (bf16[256,128]{1,0:T(8,128)(2,1)S(1)}, bf16[256,128]{1,0:T(8,128)(2,1)}, u32[]{:S(2)}, u32[]{:S(2)}) collective-permute-start(bf16[256,128]{1,0:T(8,128)(2,1)S(1)} %get-tuple-element.58), channel_id=1, source_target_pairs={{0,8},{4,12},{8,0},{12,4},{1,9},{5,13},{9,1},{13,5},{2,10},{6,14},... | collective-permute-start | bytes 196616 | tf_op jit(solution)/shard_map/ppermute | solution.py:476
  50.5 6.2 %collective-permute-start.19 = (bf16[256,128]{1,0:T(8,128)(2,1)S(1)}, bf16[256,128]{1,0:T(8,128)(2,1)}, u32[]{:S(2)}, u32[]{:S(2)}) collective-permute-start(bf16[256,128]{1,0:T(8,128)(2,1)S(1)} %get-tuple-element.59), channel_id=1, source_target_pairs={{0,12},{4,8},{8,4},{12,0},{1,13},{5,9},{9,5},{13,1},{2,14},{6,10},... | collective-permute-start | bytes 196616 | tf_op jit(solution)/shard_map/ppermute | solution.py:476
  52.1 6.6 %collective-permute-start.20 = (bf16[256,128]{1,0:T(8,128)(2,1)}, bf16[256,128]{1,0:T(8,128)(2,1)}, u32[]{:S(2)}, u32[]{:S(2)}) collective-permute-start(bf16[256,128]{1,0:T(8,128)(2,1)} %get-tuple-element.56.refs_4_), channel_id=1, source_target_pairs={{0,1},{1,0},{2,3},{3,2},{4,5},{5,4},{6,7},{7,6},{8,9},{9,8},{10,11... | collective-permute-start | bytes 196616 | tf_op jit(solution)/shard_map/ppermute | solution.py:485
  52.1 6.6 %collective-permute-start.21 = (bf16[256,128]{1,0:T(8,128)(2,1)}, bf16[256,128]{1,0:T(8,128)(2,1)}, u32[]{:S(2)}, u32[]{:S(2)}) collective-permute-start(bf16[256,128]{1,0:T(8,128)(2,1)} %collective-permute-done.17.refs_5_), channel_id=1, source_target_pairs={{0,1},{1,0},{2,3},{3,2},{4,5},{5,4},{6,7},{7,6},{8,9},{9,8},{10,11... | collective-permute-start | bytes 196616 | tf_op jit(solution)/shard_map/ppermute | solution.py:485
  63.3 11.3 %collective-permute-start.29 = (bf16[672,128]{1,0:T(8,128)(2,1)S(1)}, bf16[672,128]{1,0:T(8,128)(2,1)S(1)}, u32[]{:S(2)}, u32[]{:S(2)}) collective-permute-start(bf16[672,128]{1,0:T(8,128)(2,1)S(1)} %get-tuple-element.74), channel_id=1, source_target_pairs={{0,2},{2,0},{1,3},{3,1},{4,6},{6,4},{5,7},{7,5},{8,10},{10,8},{9,1... | collective-permute-start | bytes 516104 | tf_op jit(solution)/shard_map/ppermute | solution.py:479
  65.9 12.9 %collective-permute-start.27 = (bf16[672,128]{1,0:T(8,128)(2,1)S(1)}, bf16[672,128]{1,0:T(8,128)(2,1)S(1)}, u32[]{:S(2)}, u32[]{:S(2)}) collective-permute-start(bf16[672,128]{1,0:T(8,128)(2,1)S(1)} %get-tuple-element.75), channel_id=1, source_target_pairs={{0,2},{2,0},{1,3},{3,1},{4,6},{6,4},{5,7},{7,5},{8,10},{10,8},{9,1... | collective-permute-start | bytes 516104 | tf_op jit(solution)/shard_map/ppermute | solution.py:479
  66.0 8.6 %collective-permute-start.25 = (bf16[256,128]{1,0:T(8,128)(2,1)S(1)}, bf16[256,128]{1,0:T(8,128)(2,1)S(1)}, u32[]{:S(2)}, u32[]{:S(2)}) collective-permute-start(bf16[256,128]{1,0:T(8,128)(2,1)S(1)} %get-tuple-element.62), channel_id=1, source_target_pairs={{0,8},{4,12},{8,0},{12,4},{1,9},{5,13},{9,1},{13,5},{2,10},{6,14},... | collective-permute-start | bytes 196616 | tf_op jit(solution)/shard_map/ppermute | solution.py:476
  68.2 6.4 %collective-permute-start.26 = (bf16[256,128]{1,0:T(8,128)(2,1)S(1)}, bf16[256,128]{1,0:T(8,128)(2,1)S(1)}, u32[]{:S(2)}, u32[]{:S(2)}) collective-permute-start(bf16[256,128]{1,0:T(8,128)(2,1)S(1)} %get-tuple-element.63), channel_id=1, source_target_pairs={{0,12},{4,8},{8,4},{12,0},{1,13},{5,9},{9,5},{13,1},{2,14},{6,10},... | collective-permute-start | bytes 196616 | tf_op jit(solution)/shard_map/ppermute | solution.py:476
  75.2 8.4 %collective-permute-start.30 = (bf16[336,128]{1,0:T(8,128)(2,1)S(1)}, bf16[336,128]{1,0:T(8,128)(2,1)S(1)}, u32[]{:S(2)}, u32[]{:S(2)}) collective-permute-start(bf16[336,128]{1,0:T(8,128)(2,1)S(1)} %get-tuple-element.68), channel_id=1, source_target_pairs={{0,8},{4,12},{8,0},{12,4},{1,9},{5,13},{9,1},{13,5},{2,10},{6,14},... | collective-permute-start | bytes 258056 | tf_op jit(solution)/shard_map/ppermute | solution.py:476
  76.7 7.3 %collective-permute-start.31 = (bf16[336,128]{1,0:T(8,128)(2,1)S(1)}, bf16[336,128]{1,0:T(8,128)(2,1)S(1)}, u32[]{:S(2)}, u32[]{:S(2)}) collective-permute-start(bf16[336,128]{1,0:T(8,128)(2,1)S(1)} %get-tuple-element.69), channel_id=1, source_target_pairs={{0,12},{4,8},{8,4},{12,0},{1,13},{5,9},{9,5},{13,1},{2,14},{6,10},... | collective-permute-start | bytes 258056 | tf_op jit(solution)/shard_map/ppermute | solution.py:476
  86.2 8.2 %collective-permute-start.34 = (bf16[336,128]{1,0:T(8,128)(2,1)S(1)}, bf16[336,128]{1,0:T(8,128)(2,1)S(1)}, u32[]{:S(2)}, u32[]{:S(2)}) collective-permute-start(bf16[336,128]{1,0:T(8,128)(2,1)S(1)} %shard_map.163), channel_id=1, source_target_pairs={{0,8},{4,12},{8,0},{12,4},{1,9},{5,13},{9,1},{13,5},{2,10},{6,14},... | collective-permute-start | bytes 258056 | tf_op jit(solution)/shard_map/ppermute | solution.py:476
  88.0 6.4 %collective-permute-start.35 = (bf16[336,128]{1,0:T(8,128)(2,1)S(1)}, bf16[336,128]{1,0:T(8,128)(2,1)S(1)}, u32[]{:S(2)}, u32[]{:S(2)}) collective-permute-start(bf16[336,128]{1,0:T(8,128)(2,1)S(1)} %shard_map.163), channel_id=1, source_target_pairs={{0,12},{4,8},{8,4},{12,0},{1,13},{5,9},{9,5},{13,1},{2,14},{6,10},... | collective-permute-start | bytes 258056 | tf_op jit(solution)/shard_map/ppermute | solution.py:476
  90.0 5.8 %collective-permute-start.33 = (bf16[672,128]{1,0:T(8,128)(2,1)S(1)}, bf16[672,128]{1,0:T(8,128)(2,1)S(1)}, u32[]{:S(2)}, u32[]{:S(2)}) collective-permute-start(bf16[672,128]{1,0:T(8,128)(2,1)S(1)} %pad_maximum_fusion.refs_0_), channel_id=1, source_target_pairs={{0,2},{2,0},{1,3},{3,1},{4,6},{6,4},{5,7},{7,5},{8,10},{10,8},{9,1... | collective-permute-start | bytes 516104 | tf_op jit(solution)/shard_map/ppermute | solution.py:479
  94.4 5.5 %collective-permute-start.36 = (bf16[672,128]{1,0:T(8,128)(2,1)S(1)}, bf16[672,128]{1,0:T(8,128)(2,1)S(1)}, u32[]{:S(2)}, u32[]{:S(2)}) collective-permute-start(bf16[672,128]{1,0:T(8,128)(2,1)S(1)} %constant_dynamic-update-slice_fusion.2.refs_1_), channel_id=1, source_target_pairs={{0,2},{2,0},{1,3},{3,1},{4,6},{6,4},{5,7},{7,5},{8,10},{10,8},{9,1... | collective-permute-start | bytes 516104 | tf_op jit(solution)/shard_map/ppermute | solution.py:479
  (29 other events, 178.4 us)

commit v9 on v8

--- a/solution.py
+++ b/solution.py
@@ -422,14 +422,13 @@
 
 def widen_kernel(sems, given, made, scratch):
     (out_ref,), rows = made, given[0].shape[0]
-    end(begin(sems, list(zip(given, scratch))))
-    for x, part in enumerate(scratch):
+    for x, part in enumerate(given):
         out_ref[x * rows : (x + 1) * rows, :] = part[...].astype(F32)
 
 
 def unpack_kernel(nodes, segs, long, sems, pieces, made, scratch):
     grad_in, grad_hid, grad_bias = made
-    held, *far = scratch
+    (held,), far = scratch, pieces[1:]
     few = nodes // 2
     chunk = pieces[1].shape[0] // few
     z, s = lax.axis_index("node"), lax.axis_index("seg")
@@ -438,12 +437,10 @@
         at = pl.multiple_of(((s ^ x) * nodes + (z ^ k)) * chunk, chunk)
         return pl.ds(at, chunk)
 
-    pairs = list(zip(pieces[1:], far))
     for x in range(segs):
         for k in range(few):
             i = x * few + k
-            pairs.append((pieces[0].at[i * chunk : (i + 1) * chunk, :], held.at[place(x, k), :]))
-    end(begin(sems, pairs))
+            held[place(x, k), :] = pieces[0][i * chunk : (i + 1) * chunk, :]
     for x in range(segs):
         for k in range(few):
             held[place(x, few + k), :] = far[x][k * chunk : (k + 1) * chunk, :].astype(F32)
@@ -661,8 +658,8 @@
         widen_kernel,
         [shape((segs * few * chunk, half), F32)],
         near,
-        [share] * segs,
-        segs,
+        [],
+        here=tuple(range(segs)),
         flops=0,
     )
     gathered = [gathered[0]] + distant
@@ -670,8 +667,8 @@
         lambda *a: unpack_kernel(nodes, segs, long, *a),
         [shape(w_input.shape, F32), shape(w_hidden.shape, F32), shape(bias.shape, F32)],
         gathered,
-        [pltpu.VMEM((total_rows, half), F32)] + [share] * segs,
-        segs + few * segs,
+        [pltpu.VMEM((total_rows, half), F32)],
+        here=tuple(range(segs + 1)),
     )
     return (memory_out[None], *grads)
 

time: 103 us -> 102 us (level)
  Pallas kernels: 24.8 us -> 23 us
    pallas_call x19, Pallas kernels: 24.8 us -> 23 us  [run(): pl.pallas_call(body, out_shape=list(outs), in_specs=[HBM if i in far else...]
where the time goes in v9:
time: 102 us; the launch traced here: 101 us
  starting transfers between devices  42.6 us (42%)
  waiting for transfers between devices  29.6 us (29%)
  Pallas kernels  23 us (23%)
  local copies, waits for them, and re-layouts  3.75 us (4%)
  between operations  1.43 us (1%)
    ppermute x21, starting transfers between devices, node_swap(): return lax.ppermute(block, 'node', [(i, i ^ k) for i in range(nodes)])  29.8 us
    pallas_call x19, Pallas kernels, run(): pl.pallas_call(body, out_shape=list(outs), in_specs=[HBM if i in far else...  23 us
    ppermute x21, waiting for transfers between devices, node_swap(): return lax.ppermute(block, 'node', [(i, i ^ k) for i in range(nodes)])  23 us
    ppermute x3, starting transfers between devices, seg_next(): return lax.ppermute(block, 'seg', [(i, i + 1) for i in range(segs - 1)])  6.02 us
    ppermute x4, starting transfers between devices, seg_swap(): return lax.ppermute(block, 'seg', [(i, i ^ x) for i in range(segs)])  5.14 us
    ppermute x4, waiting for transfers between devices, seg_swap(): return lax.ppermute(block, 'seg', [(i, i ^ x) for i in range(segs)])  4.02 us
    unnamed x40, local copies, waits for them, and re-layouts  2.84 us
    ppermute x3, waiting for transfers between devices, seg_next(): return lax.ppermute(block, 'seg', [(i, i + 1) for i in range(segs - 1)])  2.5 us
  transfers between devices with their start and end apart: 37, of which 16 were waited for; matrix products, arithmetic and copies ran while one was open for 2% of the time, Pallas kernels for 13%

profile of v9, /device:TPU:0, one launch (start us, length us, event | category | flops | bytes accessed | tf_op | source)
XLA Modules:
  0.0 101.4 jit_solution(1892335590225154200)
XLA Ops:
  1.7 3.1 %collective-permute-start = (s32[2,256]{1,0:T(2,128)S(1)}, s32[2,256]{1,0:T(2,128)S(1)}, u32[]{:S(2)}, u32[]{:S(2)}) collective-permute-start(s32[2,256]{1,0:T(2,128)S(1)} %bitcast.43), channel_id=1, source_target_pairs={{0,4},{4,0},{8,12},{12,8},{1,5},{5,1},{9,13},{13,9},{2,6},{6,2},{1... | collective-permute-start | bytes 6152 | tf_op jit(solution)/shard_map/ppermute | solution.py:473
  4.7 2.6 %collective-permute-start.1 = (s32[2,256]{1,0:T(2,128)S(1)}, s32[2,256]{1,0:T(2,128)S(1)}, u32[]{:S(2)}, u32[]{:S(2)}) collective-permute-start(s32[2,256]{1,0:T(2,128)S(1)} %bitcast.44), channel_id=1, source_target_pairs={{0,8},{4,12},{8,0},{12,4},{1,9},{5,13},{9,1},{13,5},{2,10},{6,14},... | collective-permute-start | bytes 6152 | tf_op jit(solution)/shard_map/ppermute | solution.py:473
  9.7 3.1 %collective-permute-done.2.refs_3_ = s32[2,256]{1,0:T(2,128)S(1)} collective-permute-done((s32[2,256]{1,0:T(2,128)S(1)}, s32[2,256]{1,0:T(2,128)S(1)}, u32[]{:S(2)}, u32[]{:S(2)}) %collective-permute-start.2) | collective-permute-done | bytes 2080 | tf_op jit(solution)/shard_map/ppermute | solution.py:473
  14.4 3.4 %collective-permute-start.3 = (bf16[2064,128]{1,0:T(8,128)(2,1)S(1)}, bf16[2064,128]{1,0:T(8,128)(2,1)S(1)}, u32[]{:S(2)}, u32[]{:S(2)}) collective-permute-start(bf16[2064,128]{1,0:T(8,128)(2,1)S(1)} %shard_map.149), channel_id=1, source_target_pairs={{0,2},{1,3},{4,6},{5,7},{8,10},{9,11},{12,14},{13,15},{16,18},{17,... | collective-permute-start | bytes 1585160 | tf_op jit(solution)/shard_map/ppermute | solution.py:479
  19.0 2.5 %collective-permute-start.5 = (bf16[256,128]{1,0:T(8,128)(2,1)S(1)}, bf16[256,128]{1,0:T(8,128)(2,1)S(1)}, u32[]{:S(2)}, u32[]{:S(2)}) collective-permute-start(bf16[256,128]{1,0:T(8,128)(2,1)S(1)} %get-tuple-element.43), channel_id=1, source_target_pairs={{0,4},{4,0},{8,12},{12,8},{1,5},{5,1},{9,13},{13,9},{2,6},{6,2},{1... | collective-permute-start | bytes 196616 | tf_op jit(solution)/shard_map/ppermute | solution.py:473
  21.4 3.7 %collective-permute-done.6.refs_6_ = bf16[256,128]{1,0:T(8,128)(2,1)S(1)} collective-permute-done((bf16[256,128]{1,0:T(8,128)(2,1)S(1)}, bf16[256,128]{1,0:T(8,128)(2,1)S(1)}, u32[]{:S(2)}, u32[]{:S(2)}) %collective-permute-start.6) | collective-permute-done | bytes 65568 | tf_op jit(solution)/shard_map/ppermute | solution.py:473
  27.7 2.9 %shard_map.152 = (bf16[512,128]{1,0:T(8,128)(2,1)S(1)}, bf16[512,128]{1,0:T(8,128)(2,1)S(1)}, bf16[1024,768]{1,0:T(8,128)(2,1)S(1)}, bf16[1024,512]{1,0:T(8,128)(2,1)S(1)}, f32[8,128]{1,0:T(8,128)S(1)}) custom-call(f32[40,128]{1,0:T(8,128)S(1)} %concatenate.12.refs_2_.refs_0_, bf16[1024,256]{1,0:T(8,128)(2,1)S(1)} %shard_map.151.refs_1_, ...), custom_call_target="tpu_custom_call" | custom-call | bytes 5267456 | tf_op jit(solution)/shard_map/pallas_call | solution.py:28
  33.3 2.5 %collective-permute-done.14.refs_1_ = bf16[512,128]{1,0:T(8,128)(2,1)S(1)} collective-permute-done((bf16[512,128]{1,0:T(8,128)(2,1)S(1)}, bf16[512,128]{1,0:T(8,128)(2,1)S(1)}, u32[]{:S(2)}, u32[]{:S(2)}) %collective-permute-start.14) | collective-permute-done | bytes 131104 | tf_op jit(solution)/shard_map/ppermute | solution.py:479
  37.5 1.6 %collective-permute-start.16 = (bf16[256,128]{1,0:T(8,128)(2,1)S(1)}, bf16[256,128]{1,0:T(8,128)(2,1)S(1)}, u32[]{:S(2)}, u32[]{:S(2)}) collective-permute-start(bf16[256,128]{1,0:T(8,128)(2,1)S(1)} %get-tuple-element.51), channel_id=1, source_target_pairs={{0,12},{4,8},{8,4},{12,0},{1,13},{5,9},{9,5},{13,1},{2,14},{6,10},... | collective-permute-start | bytes 196616 | tf_op jit(solution)/shard_map/ppermute | solution.py:473
  45.3 1.7 %shard_map.156 = (bf16[1024,128]{1,0:T(8,128)(2,1)S(1)}, bf16[256,128]{1,0:T(8,128)(2,1)}, bf16[256,128]{1,0:T(8,128)(2,1)S(1)}, bf16[256,128]{1,0:T(8,128)(2,1)S(1)}, bf16[256,128]{1,0:T(8,128)(2,1)S(1)}) custom-call(s32[2,1024]{1,0:T(2,128)S(1)} %get-tuple-element.39.refs_1_.refs_0_, s32[1,1024]{1,0:T(1,128)S(1)} %get-tuple-element.40.refs_1_.refs_0_, ...), custom_call_target="tpu_custom_call" | custom-call | bytes 2437120 | tf_op jit(solution)/shard_map/pallas_call | solution.py:28
  48.1 2.4 %collective-permute-start.18 = (bf16[256,128]{1,0:T(8,128)(2,1)S(1)}, bf16[256,128]{1,0:T(8,128)(2,1)}, u32[]{:S(2)}, u32[]{:S(2)}) collective-permute-start(bf16[256,128]{1,0:T(8,128)(2,1)S(1)} %get-tuple-element.58), channel_id=1, source_target_pairs={{0,8},{4,12},{8,0},{12,4},{1,9},{5,13},{9,1},{13,5},{2,10},{6,14},... | collective-permute-start | bytes 196616 | tf_op jit(solution)/shard_map/ppermute | solution.py:473
  52.6 2.2 %collective-permute-done.18.refs_6_ = bf16[256,128]{1,0:T(8,128)(2,1)} collective-permute-done((bf16[256,128]{1,0:T(8,128)(2,1)S(1)}, bf16[256,128]{1,0:T(8,128)(2,1)}, u32[]{:S(2)}, u32[]{:S(2)}) %collective-permute-start.18) | collective-permute-done | bytes 65568 | tf_op jit(solution)/shard_map/ppermute | solution.py:473
  54.8 1.9 %collective-permute-done.19.refs_7_ = bf16[256,128]{1,0:T(8,128)(2,1)} collective-permute-done((bf16[256,128]{1,0:T(8,128)(2,1)S(1)}, bf16[256,128]{1,0:T(8,128)(2,1)}, u32[]{:S(2)}, u32[]{:S(2)}) %collective-permute-start.19) | collective-permute-done | bytes 65568 | tf_op jit(solution)/shard_map/ppermute | solution.py:473
  58.7 4.5 %shard_map.159 = (bf16[256,128]{1,0:T(8,128)(2,1)S(1)}, bf16[256,128]{1,0:T(8,128)(2,1)S(1)}, bf16[256,128]{1,0:T(8,128)(2,1)S(1)}, bf16[256,128]{1,0:T(8,128)(2,1)S(1)}, bf16[2688,128]{1,0:T(8,128)(2,1)S(1)}) custom-call(f32[40,128]{1,0:T(8,128)S(1)} %concatenate.12.refs_2_.refs_0_, bf16[1024,256]{1,0:T(8,128)(2,1)S(1)} %shard_map.158.refs_1_, ...), custom_call_target="tpu_custom_call" | custom-call | bytes 4706304 | tf_op jit(solution)/shard_map/pallas_call | solution.py:28
  63.3 2.6 %collective-permute-start.29 = (bf16[672,128]{1,0:T(8,128)(2,1)S(1)}, bf16[672,128]{1,0:T(8,128)(2,1)S(1)}, u32[]{:S(2)}, u32[]{:S(2)}) collective-permute-start(bf16[672,128]{1,0:T(8,128)(2,1)S(1)} %get-tuple-element.74), channel_id=1, source_target_pairs={{0,2},{2,0},{1,3},{3,1},{4,6},{6,4},{5,7},{7,5},{8,10},{10,8},{9,1... | collective-permute-start | bytes 516104 | tf_op jit(solution)/shard_map/ppermute | solution.py:476
  66.0 2.2 %collective-permute-start.25 = (bf16[256,128]{1,0:T(8,128)(2,1)S(1)}, bf16[256,128]{1,0:T(8,128)(2,1)S(1)}, u32[]{:S(2)}, u32[]{:S(2)}) collective-permute-start(bf16[256,128]{1,0:T(8,128)(2,1)S(1)} %get-tuple-element.62), channel_id=1, source_target_pairs={{0,8},{4,12},{8,0},{12,4},{1,9},{5,13},{9,1},{13,5},{2,10},{6,14},... | collective-permute-start | bytes 196616 | tf_op jit(solution)/shard_map/ppermute | solution.py:473
  68.2 2.2 %collective-permute-start.26 = (bf16[256,128]{1,0:T(8,128)(2,1)S(1)}, bf16[256,128]{1,0:T(8,128)(2,1)S(1)}, u32[]{:S(2)}, u32[]{:S(2)}) collective-permute-start(bf16[256,128]{1,0:T(8,128)(2,1)S(1)} %get-tuple-element.63), channel_id=1, source_target_pairs={{0,12},{4,8},{8,4},{12,0},{1,13},{5,9},{9,5},{13,1},{2,14},{6,10},... | collective-permute-start | bytes 196616 | tf_op jit(solution)/shard_map/ppermute | solution.py:473
  71.3 3.4 %collective-permute-done.25.refs_4_.refs_3_ = bf16[256,128]{1,0:T(8,128)(2,1)S(1)} collective-permute-done((bf16[256,128]{1,0:T(8,128)(2,1)S(1)}, bf16[256,128]{1,0:T(8,128)(2,1)S(1)}, u32[]{:S(2)}, u32[]{:S(2)}) %collective-permute-start.25) | collective-permute-done | bytes 65568 | tf_op jit(solution)/shard_map/ppermute | solution.py:473
  76.7 2.1 %collective-permute-start.31 = (bf16[336,128]{1,0:T(8,128)(2,1)S(1)}, bf16[336,128]{1,0:T(8,128)(2,1)S(1)}, u32[]{:S(2)}, u32[]{:S(2)}) collective-permute-start(bf16[336,128]{1,0:T(8,128)(2,1)S(1)} %get-tuple-element.69), channel_id=1, source_target_pairs={{0,12},{4,8},{8,4},{12,0},{1,13},{5,9},{9,5},{13,1},{2,14},{6,10},... | collective-permute-start | bytes 258056 | tf_op jit(solution)/shard_map/ppermute | solution.py:473
  80.9 2.7 %shard_map.160 = (f32[2048,128]{1,0:T(8,128)}, f32[8,128]{1,0:T(8,128)S(1)}) custom-call(s32[2,1024]{1,0:T(2,128)S(1)} %get-tuple-element.39.refs_1_.refs_0_, f32[2048,128]{1,0:T(8,128)S(1)} %shard_map.157.refs_1_, bf16[256,128]{1,0:T(8,128)(2,1)S(1)} %get-tuple-element.60.refs_2_, bf16[256,128]{1,0:T(8,128)(2,1)S(1)} %collective-permute-done.24.refs_3_.refs_2_, ...), custom_call_target="tpu_custom_call" | custom-call | bytes 2371584 | tf_op jit(solution)/shard_map/pallas_call | solution.py:28
  86.2 1.7 %collective-permute-start.34 = (bf16[336,128]{1,0:T(8,128)(2,1)S(1)}, bf16[336,128]{1,0:T(8,128)(2,1)S(1)}, u32[]{:S(2)}, u32[]{:S(2)}) collective-permute-start(bf16[336,128]{1,0:T(8,128)(2,1)S(1)} %shard_map.163), channel_id=1, source_target_pairs={{0,8},{4,12},{8,0},{12,4},{1,9},{5,13},{9,1},{13,5},{2,10},{6,14},... | collective-permute-start | bytes 258056 | tf_op jit(solution)/shard_map/ppermute | solution.py:473
  88.0 1.7 %collective-permute-start.35 = (bf16[336,128]{1,0:T(8,128)(2,1)S(1)}, bf16[336,128]{1,0:T(8,128)(2,1)S(1)}, u32[]{:S(2)}, u32[]{:S(2)}) collective-permute-start(bf16[336,128]{1,0:T(8,128)(2,1)S(1)} %shard_map.163), channel_id=1, source_target_pairs={{0,12},{4,8},{8,4},{12,0},{1,13},{5,9},{9,5},{13,1},{2,14},{6,10},... | collective-permute-start | bytes 258056 | tf_op jit(solution)/shard_map/ppermute | solution.py:473
  91.1 3.3 %collective-permute-done.34 = bf16[336,128]{1,0:T(8,128)(2,1)S(1)} collective-permute-done((bf16[336,128]{1,0:T(8,128)(2,1)S(1)}, bf16[336,128]{1,0:T(8,128)(2,1)S(1)}, u32[]{:S(2)}, u32[]{:S(2)}) %collective-permute-start.34) | collective-permute-done | bytes 86048 | tf_op jit(solution)/shard_map/ppermute | solution.py:473
  95.9 4.0 %collective-permute-done.36.refs_2_ = bf16[672,128]{1,0:T(8,128)(2,1)S(1)} collective-permute-done((bf16[672,128]{1,0:T(8,128)(2,1)S(1)}, bf16[672,128]{1,0:T(8,128)(2,1)S(1)}, u32[]{:S(2)}, u32[]{:S(2)}) %collective-permute-start.36) | collective-permute-done | bytes 172064 | tf_op jit(solution)/shard_map/ppermute | solution.py:476
  (122 shorter events, 35.9 us)
Async XLA Ops:
  1.7 7.8 %collective-permute-start = (s32[2,256]{1,0:T(2,128)S(1)}, s32[2,256]{1,0:T(2,128)S(1)}, u32[]{:S(2)}, u32[]{:S(2)}) collective-permute-start(s32[2,256]{1,0:T(2,128)S(1)} %bitcast.43), channel_id=1, source_target_pairs={{0,4},{4,0},{8,12},{12,8},{1,5},{5,1},{9,13},{13,9},{2,6},{6,2},{1... | collective-permute-start | bytes 6152 | tf_op jit(solution)/shard_map/ppermute | solution.py:473
  7.3 5.4 %collective-permute-start.2 = (s32[2,256]{1,0:T(2,128)S(1)}, s32[2,256]{1,0:T(2,128)S(1)}, u32[]{:S(2)}, u32[]{:S(2)}) collective-permute-start(s32[2,256]{1,0:T(2,128)S(1)} %bitcast.45), channel_id=1, source_target_pairs={{0,12},{4,8},{8,4},{12,0},{1,13},{5,9},{9,5},{13,1},{2,14},{6,10},... | collective-permute-start | bytes 6152 | tf_op jit(solution)/shard_map/ppermute | solution.py:473
  14.4 24.8 %collective-permute-start.3 = (bf16[2064,128]{1,0:T(8,128)(2,1)S(1)}, bf16[2064,128]{1,0:T(8,128)(2,1)S(1)}, u32[]{:S(2)}, u32[]{:S(2)}) collective-permute-start(bf16[2064,128]{1,0:T(8,128)(2,1)S(1)} %shard_map.149), channel_id=1, source_target_pairs={{0,2},{1,3},{4,6},{5,7},{8,10},{9,11},{12,14},{13,15},{16,18},{17,... | collective-permute-start | bytes 1585160 | tf_op jit(solution)/shard_map/ppermute | solution.py:479
  17.8 8.3 %collective-permute-start.4 = (bf16[2,64,1024]{2,1,0:T(8,128)(2,1)S(1)}, bf16[2,64,1024]{2,1,0:T(8,128)(2,1)S(1)}, u32[]{:S(2)}, u32[]{:S(2)}) collective-permute-start(bf16[2,64,1024]{2,1,0:T(8,128)(2,1)S(1)} %bitcast.36), channel_id=1, source_target_pairs={{0,1},{1,0},{2,3},{3,2},{4,5},{5,4},{6,7},{7,6},{8,9},{9,8},{10,11... | collective-permute-start | bytes 786440 | tf_op jit(solution)/shard_map/ppermute | solution.py:482
  17.9 7.3 %collective-permute-start.6 = (bf16[256,128]{1,0:T(8,128)(2,1)S(1)}, bf16[256,128]{1,0:T(8,128)(2,1)S(1)}, u32[]{:S(2)}, u32[]{:S(2)}) collective-permute-start(bf16[256,128]{1,0:T(8,128)(2,1)S(1)} %get-tuple-element.44), channel_id=1, source_target_pairs={{0,8},{4,12},{8,0},{12,4},{1,9},{5,13},{9,1},{13,5},{2,10},{6,14},... | collective-permute-start | bytes 196616 | tf_op jit(solution)/shard_map/ppermute | solution.py:473
  18.0 7.2 %collective-permute-start.7 = (bf16[256,128]{1,0:T(8,128)(2,1)S(1)}, bf16[256,128]{1,0:T(8,128)(2,1)S(1)}, u32[]{:S(2)}, u32[]{:S(2)}) collective-permute-start(bf16[256,128]{1,0:T(8,128)(2,1)S(1)} %get-tuple-element.45), channel_id=1, source_target_pairs={{0,12},{4,8},{8,4},{12,0},{1,13},{5,9},{9,5},{13,1},{2,14},{6,10},... | collective-permute-start | bytes 196616 | tf_op jit(solution)/shard_map/ppermute | solution.py:473
  19.0 7.1 %collective-permute-start.5 = (bf16[256,128]{1,0:T(8,128)(2,1)S(1)}, bf16[256,128]{1,0:T(8,128)(2,1)S(1)}, u32[]{:S(2)}, u32[]{:S(2)}) collective-permute-start(bf16[256,128]{1,0:T(8,128)(2,1)S(1)} %get-tuple-element.43), channel_id=1, source_target_pairs={{0,4},{4,0},{8,12},{12,8},{1,5},{5,1},{9,13},{13,9},{2,6},{6,2},{1... | collective-permute-start | bytes 196616 | tf_op jit(solution)/shard_map/ppermute | solution.py:473
  32.0 8.6 %collective-permute-start.12 = (bf16[512,128]{1,0:T(8,128)(2,1)S(1)}, bf16[512,128]{1,0:T(8,128)(2,1)S(1)}, u32[]{:S(2)}, u32[]{:S(2)}) collective-permute-start(bf16[512,128]{1,0:T(8,128)(2,1)S(1)} %get-tuple-element.46.refs_0_), channel_id=1, source_target_pairs={{0,2},{1,3},{4,6},{5,7},{8,10},{9,11},{12,14},{13,15},{16,18},{17,... | collective-permute-start | bytes 393224 | tf_op jit(solution)/shard_map/ppermute | solution.py:479
  35.9 6.9 %collective-permute-start.15 = (bf16[256,128]{1,0:T(8,128)(2,1)S(1)}, bf16[256,128]{1,0:T(8,128)(2,1)S(1)}, u32[]{:S(2)}, u32[]{:S(2)}) collective-permute-start(bf16[256,128]{1,0:T(8,128)(2,1)S(1)} %get-tuple-element.50), channel_id=1, source_target_pairs={{0,8},{4,12},{8,0},{12,4},{1,9},{5,13},{9,1},{13,5},{2,10},{6,14},... | collective-permute-start | bytes 196616 | tf_op jit(solution)/shard_map/ppermute | solution.py:473
  37.5 6.6 %collective-permute-start.16 = (bf16[256,128]{1,0:T(8,128)(2,1)S(1)}, bf16[256,128]{1,0:T(8,128)(2,1)S(1)}, u32[]{:S(2)}, u32[]{:S(2)}) collective-permute-start(bf16[256,128]{1,0:T(8,128)(2,1)S(1)} %get-tuple-element.51), channel_id=1, source_target_pairs={{0,12},{4,8},{8,4},{12,0},{1,13},{5,9},{9,5},{13,1},{2,14},{6,10},... | collective-permute-start | bytes 196616 | tf_op jit(solution)/shard_map/ppermute | solution.py:473
  48.1 6.7 %collective-permute-start.18 = (bf16[256,128]{1,0:T(8,128)(2,1)S(1)}, bf16[256,128]{1,0:T(8,128)(2,1)}, u32[]{:S(2)}, u32[]{:S(2)}) collective-permute-start(bf16[256,128]{1,0:T(8,128)(2,1)S(1)} %get-tuple-element.58), channel_id=1, source_target_pairs={{0,8},{4,12},{8,0},{12,4},{1,9},{5,13},{9,1},{13,5},{2,10},{6,14},... | collective-permute-start | bytes 196616 | tf_op jit(solution)/shard_map/ppermute | solution.py:473
  50.5 6.2 %collective-permute-start.19 = (bf16[256,128]{1,0:T(8,128)(2,1)S(1)}, bf16[256,128]{1,0:T(8,128)(2,1)}, u32[]{:S(2)}, u32[]{:S(2)}) collective-permute-start(bf16[256,128]{1,0:T(8,128)(2,1)S(1)} %get-tuple-element.59), channel_id=1, source_target_pairs={{0,12},{4,8},{8,4},{12,0},{1,13},{5,9},{9,5},{13,1},{2,14},{6,10},... | collective-permute-start | bytes 196616 | tf_op jit(solution)/shard_map/ppermute | solution.py:473
  52.1 6.6 %collective-permute-start.20 = (bf16[256,128]{1,0:T(8,128)(2,1)}, bf16[256,128]{1,0:T(8,128)(2,1)}, u32[]{:S(2)}, u32[]{:S(2)}) collective-permute-start(bf16[256,128]{1,0:T(8,128)(2,1)} %get-tuple-element.56.refs_4_), channel_id=1, source_target_pairs={{0,1},{1,0},{2,3},{3,2},{4,5},{5,4},{6,7},{7,6},{8,9},{9,8},{10,11... | collective-permute-start | bytes 196616 | tf_op jit(solution)/shard_map/ppermute | solution.py:482
  52.1 6.6 %collective-permute-start.21 = (bf16[256,128]{1,0:T(8,128)(2,1)}, bf16[256,128]{1,0:T(8,128)(2,1)}, u32[]{:S(2)}, u32[]{:S(2)}) collective-permute-start(bf16[256,128]{1,0:T(8,128)(2,1)} %collective-permute-done.17.refs_5_), channel_id=1, source_target_pairs={{0,1},{1,0},{2,3},{3,2},{4,5},{5,4},{6,7},{7,6},{8,9},{9,8},{10,11... | collective-permute-start | bytes 196616 | tf_op jit(solution)/shard_map/ppermute | solution.py:482
  63.3 11.3 %collective-permute-start.29 = (bf16[672,128]{1,0:T(8,128)(2,1)S(1)}, bf16[672,128]{1,0:T(8,128)(2,1)S(1)}, u32[]{:S(2)}, u32[]{:S(2)}) collective-permute-start(bf16[672,128]{1,0:T(8,128)(2,1)S(1)} %get-tuple-element.74), channel_id=1, source_target_pairs={{0,2},{2,0},{1,3},{3,1},{4,6},{6,4},{5,7},{7,5},{8,10},{10,8},{9,1... | collective-permute-start | bytes 516104 | tf_op jit(solution)/shard_map/ppermute | solution.py:476
  65.9 12.9 %collective-permute-start.27 = (bf16[672,128]{1,0:T(8,128)(2,1)S(1)}, bf16[672,128]{1,0:T(8,128)(2,1)S(1)}, u32[]{:S(2)}, u32[]{:S(2)}) collective-permute-start(bf16[672,128]{1,0:T(8,128)(2,1)S(1)} %get-tuple-element.75), channel_id=1, source_target_pairs={{0,2},{2,0},{1,3},{3,1},{4,6},{6,4},{5,7},{7,5},{8,10},{10,8},{9,1... | collective-permute-start | bytes 516104 | tf_op jit(solution)/shard_map/ppermute | solution.py:476
  66.0 8.6 %collective-permute-start.25 = (bf16[256,128]{1,0:T(8,128)(2,1)S(1)}, bf16[256,128]{1,0:T(8,128)(2,1)S(1)}, u32[]{:S(2)}, u32[]{:S(2)}) collective-permute-start(bf16[256,128]{1,0:T(8,128)(2,1)S(1)} %get-tuple-element.62), channel_id=1, source_target_pairs={{0,8},{4,12},{8,0},{12,4},{1,9},{5,13},{9,1},{13,5},{2,10},{6,14},... | collective-permute-start | bytes 196616 | tf_op jit(solution)/shard_map/ppermute | solution.py:473
  68.2 6.4 %collective-permute-start.26 = (bf16[256,128]{1,0:T(8,128)(2,1)S(1)}, bf16[256,128]{1,0:T(8,128)(2,1)S(1)}, u32[]{:S(2)}, u32[]{:S(2)}) collective-permute-start(bf16[256,128]{1,0:T(8,128)(2,1)S(1)} %get-tuple-element.63), channel_id=1, source_target_pairs={{0,12},{4,8},{8,4},{12,0},{1,13},{5,9},{9,5},{13,1},{2,14},{6,10},... | collective-permute-start | bytes 196616 | tf_op jit(solution)/shard_map/ppermute | solution.py:473
  75.2 8.4 %collective-permute-start.30 = (bf16[336,128]{1,0:T(8,128)(2,1)S(1)}, bf16[336,128]{1,0:T(8,128)(2,1)S(1)}, u32[]{:S(2)}, u32[]{:S(2)}) collective-permute-start(bf16[336,128]{1,0:T(8,128)(2,1)S(1)} %get-tuple-element.68), channel_id=1, source_target_pairs={{0,8},{4,12},{8,0},{12,4},{1,9},{5,13},{9,1},{13,5},{2,10},{6,14},... | collective-permute-start | bytes 258056 | tf_op jit(solution)/shard_map/ppermute | solution.py:473
  76.7 7.3 %collective-permute-start.31 = (bf16[336,128]{1,0:T(8,128)(2,1)S(1)}, bf16[336,128]{1,0:T(8,128)(2,1)S(1)}, u32[]{:S(2)}, u32[]{:S(2)}) collective-permute-start(bf16[336,128]{1,0:T(8,128)(2,1)S(1)} %get-tuple-element.69), channel_id=1, source_target_pairs={{0,12},{4,8},{8,4},{12,0},{1,13},{5,9},{9,5},{13,1},{2,14},{6,10},... | collective-permute-start | bytes 258056 | tf_op jit(solution)/shard_map/ppermute | solution.py:473
  86.2 8.2 %collective-permute-start.34 = (bf16[336,128]{1,0:T(8,128)(2,1)S(1)}, bf16[336,128]{1,0:T(8,128)(2,1)S(1)}, u32[]{:S(2)}, u32[]{:S(2)}) collective-permute-start(bf16[336,128]{1,0:T(8,128)(2,1)S(1)} %shard_map.163), channel_id=1, source_target_pairs={{0,8},{4,12},{8,0},{12,4},{1,9},{5,13},{9,1},{13,5},{2,10},{6,14},... | collective-permute-start | bytes 258056 | tf_op jit(solution)/shard_map/ppermute | solution.py:473
  88.0 6.4 %collective-permute-start.35 = (bf16[336,128]{1,0:T(8,128)(2,1)S(1)}, bf16[336,128]{1,0:T(8,128)(2,1)S(1)}, u32[]{:S(2)}, u32[]{:S(2)}) collective-permute-start(bf16[336,128]{1,0:T(8,128)(2,1)S(1)} %shard_map.163), channel_id=1, source_target_pairs={{0,12},{4,8},{8,4},{12,0},{1,13},{5,9},{9,5},{13,1},{2,14},{6,10},... | collective-permute-start | bytes 258056 | tf_op jit(solution)/shard_map/ppermute | solution.py:473
  90.0 5.8 %collective-permute-start.33 = (bf16[672,128]{1,0:T(8,128)(2,1)S(1)}, bf16[672,128]{1,0:T(8,128)(2,1)S(1)}, u32[]{:S(2)}, u32[]{:S(2)}) collective-permute-start(bf16[672,128]{1,0:T(8,128)(2,1)S(1)} %pad_maximum_fusion.refs_0_), channel_id=1, source_target_pairs={{0,2},{2,0},{1,3},{3,1},{4,6},{6,4},{5,7},{7,5},{8,10},{10,8},{9,1... | collective-permute-start | bytes 516104 | tf_op jit(solution)/shard_map/ppermute | solution.py:476
  94.4 5.5 %collective-permute-start.36 = (bf16[672,128]{1,0:T(8,128)(2,1)S(1)}, bf16[672,128]{1,0:T(8,128)(2,1)S(1)}, u32[]{:S(2)}, u32[]{:S(2)}) collective-permute-start(bf16[672,128]{1,0:T(8,128)(2,1)S(1)} %constant_dynamic-update-slice_fusion.2.refs_1_), channel_id=1, source_target_pairs={{0,2},{2,0},{1,3},{3,1},{4,6},{6,4},{5,7},{7,5},{8,10},{10,8},{9,1... | collective-permute-start | bytes 516104 | tf_op jit(solution)/shard_map/ppermute | solution.py:476
  (29 other events, 178.4 us)
